TPU v7x, 32 devices: a whole 2x2x4 slice. The times are simulated.
32 devices in a mesh: tx: 4 (over y, core), ty: 8 (over z, x).
Axes of the slice: x: 2, y: 2, z: 4, core: 2. Of those that a mesh axis runs over, the one named last changes fastest.
Arguments:
- schur_slab: bfloat16 [8192, 4096], P(('tx', 'ty')), may hold values from -2.5 to 2.5
- pivot_inverse: bfloat16 [4, 256, 256], replicated
- block_pattern: int32 [4, 2, 32], replicated, may hold values 0 or 1
- column_order: int32 [4, 32], replicated, may hold values from 0 to 31, each once within a row
- pivot_blocks: int32 [4, 32], replicated, may hold values from 0 to 31, each once within a row
Outputs:
- factored_slab: bfloat16 [8192, 4096], P(('tx', 'ty'))
Inputs may be any that keep to these rules, and one draw needn't show every extreme that they name: `column_order`: each level's entry is a permutation of the column blocks. `pivot_blocks`: each level's entry is a permutation of the column blocks.
All inputs are finite; a program needn't handle non-finite values.
Results may differ from a plain program's by a relative error of at most 0.0095.
Values may be sent and summed in bfloat16 or wider, within the bound.
No kernel may reach another device: no remote copies, remote signals or barrier semaphores. Data moves between devices by JAX's collectives and lax.ppermute only.
A program may use at most 64 MiB of HBM per device.

v0:
```python
import jax
import jax.numpy as jnp
from jax import lax
from jax.sharding import PartitionSpec as P

BLOCK = 128
LEVELS = 4


def swapped(block, axis, stride):
    count = lax.axis_size(axis)
    route = []
    for low in range(count):
        high = low | 1 << stride
        if high != low and high < count:
            route += [(low, high), (high, low)]
    return lax.ppermute(block, axis, route)


def high_bit(axis_count, tier_index):
    return axis_count.bit_length() - 2 - tier_index // 2


def trade_whole(current, tier_index):
    if tier_index % 2 == 0:
        return swapped(current, "tx", high_bit(lax.axis_size("tx"), tier_index))
    return swapped(current, "ty", high_bit(lax.axis_size("ty"), tier_index))


def trade_panel(piece, step):
    if step % 2 == 0:
        return swapped(piece, "tx", high_bit(lax.axis_size("tx"), step))
    return swapped(piece, "ty", high_bit(lax.axis_size("ty"), step))


def on_device(schur_slab, pivot_inverse, block_pattern, column_order, pivot_blocks):
    slab_rows, sep_width = schur_slab.shape
    block_count = sep_width // BLOCK
    pivot_total = pivot_inverse.shape[1]
    pivot_count = pivot_total // BLOCK
    current = schur_slab
    for tier_index in range(LEVELS):
        share = pivot_total // 2 ** (tier_index + 1)
        partner = trade_whole(current, tier_index)
        block_order = column_order[tier_index]
        moved = partner.reshape(slab_rows, block_count, BLOCK)[:, block_order].reshape(
            slab_rows, sep_width
        )
        merged = current.astype(jnp.float32) + moved.astype(jnp.float32)
        collected = merged[:share].astype(jnp.bfloat16)
        for step in range(tier_index + 1):
            other_piece = trade_panel(collected, step)
            if step % 2 == 0:
                my_bit = jnp.bitwise_and(
                    jnp.right_shift(lax.axis_index("tx"), high_bit(lax.axis_size("tx"), step)), 1
                )
            else:
                my_bit = jnp.bitwise_and(
                    jnp.right_shift(lax.axis_index("ty"), high_bit(lax.axis_size("ty"), step)), 1
                )
            low_first = jnp.concatenate([collected, other_piece], axis=0)
            high_first = jnp.concatenate([other_piece, collected], axis=0)
            collected = jnp.where(my_bit == 0, low_first, high_first)
        mask_rows = jnp.repeat(block_pattern[tier_index], BLOCK, axis=0).astype(jnp.bfloat16)
        panel = (
            collected.reshape(pivot_total, block_count, BLOCK) * mask_rows[:, :, None]
        ).reshape(pivot_total, sep_width)
        chosen_blocks = pivot_blocks[tier_index, :pivot_count]
        coupling = merged.reshape(slab_rows, block_count, BLOCK)[:, chosen_blocks]
        coupling = coupling.reshape(slab_rows, pivot_total).astype(jnp.bfloat16)
        weights = jnp.dot(
            coupling, pivot_inverse[tier_index], preferred_element_type=jnp.float32
        ).astype(jnp.bfloat16)
        update = jnp.dot(weights, panel, preferred_element_type=jnp.float32)
        current = (merged - update).astype(jnp.bfloat16)
    return current


def solution(mesh):
    return jax.shard_map(
        on_device,
        mesh=mesh,
        in_specs=(P(("tx", "ty"), None), P(), P(), P(), P()),
        out_specs=P(("tx", "ty"), None),
        check_vma=False,
    )
```

profile of v0, /device:TPU:0, one launch (start us, length us, event | category | flops | bytes accessed | tf_op | source)
XLA Modules:
  0.0 429.5 jit_solution(5881274820933665093)
XLA Ops:
  0.0 3.3 copy.17
  3.3 3.0 collective-permute-start
  6.3 45.6 %collective-permute-done = bf16[256,4096]{0,1:T(8,128)(2,1)S(1)} collective-permute-done((bf16[256,4096]{0,1:T(8,128)(2,1)S(1)}, bf16[256,4096]{0,1:T(8,128)(2,1)S(1)}, u32[]{:S(2)}, u32[]{:S(2)}) %collective-permute-start) | collective-permute-done | bytes 2097184 | tf_op jit(solution)/shard_map/ppermute | solution.py:17
  53.3 3.2 copy.18
  56.5 2.1 gather_fusion
  58.6 2.8 bitcast_add_fusion.3
  65.4 2.7 copy_bitcast_fusion.3
  68.8 19.3 %collective-permute-done.1 = bf16[128,4096]{1,0:T(8,128)(2,1)} collective-permute-done((bf16[128,4096]{1,0:T(8,128)(2,1)S(1)}, bf16[128,4096]{1,0:T(8,128)(2,1)}, u32[]{:S(2)}, u32[]{:S(2)}) %collective-permute-start.1) | collective-permute-done | bytes 1048608 | tf_op jit(solution)/shard_map/ppermute | solution.py:17
  90.0 5.9 %fusion = bf16[256,4096]{1,0:T(8,128)(2,1)} fusion(f32[256,4096]{1,0:T(8,128)} %copy-done, bf16[32,8,32,128]{3,2,1,0:T(8,128)(2,1)S(1)} %bitcast.158, bf16[128,4096]{1,0:T(8,128)(2,1)} %collective-permute-done.1, bf16[128,4096]{1,0:T(8,128)(2,1)S(1)} %slice.148, pred[]{:T(512)S(6)} %eq.8, bf16[256,256]{0,1:T(8,128)(2,1)S(1)} %bitcast.170, ...), kind=kOutput, calls=%fused_computation.12 | convolution fusion | flops 586219520 | bytes 10747905 | tf_op jit(solution)/shard_map/dot_general | solution.py:74
  95.8 2.5 collective-permute-start.2
  98.3 89.4 %collective-permute-done.2 = bf16[256,4096]{1,0:T(8,128)(2,1)S(1)} collective-permute-done((bf16[256,4096]{1,0:T(8,128)(2,1)}, bf16[256,4096]{1,0:T(8,128)(2,1)S(1)}, u32[]{:S(2)}, u32[]{:S(2)}) %collective-permute-start.2) | collective-permute-done | bytes 2097184 | tf_op jit(solution)/shard_map/ppermute | solution.py:17
  188.3 2.1 gather_fusion.2
  190.5 2.8 bitcast_add_fusion.2
  196.5 12.1 %collective-permute-done.3 = bf16[64,4096]{1,0:T(8,128)(2,1)S(1)} collective-permute-done((bf16[64,4096]{1,0:T(8,128)(2,1)S(1)}, bf16[64,4096]{1,0:T(8,128)(2,1)S(1)}, u32[]{:S(2)}, u32[]{:S(2)}) %collective-permute-start.3) | collective-permute-done | bytes 524320 | tf_op jit(solution)/shard_map/ppermute | solution.py:17
  208.8 2.7 copy_bitcast_fusion.2
  212.2 43.5 %collective-permute-done.4 = bf16[128,4096]{1,0:T(8,128)(2,1)} collective-permute-done((bf16[128,4096]{1,0:T(8,128)(2,1)S(1)}, bf16[128,4096]{1,0:T(8,128)(2,1)}, u32[]{:S(2)}, u32[]{:S(2)}) %collective-permute-start.4) | collective-permute-done | bytes 1048608 | tf_op jit(solution)/shard_map/ppermute | solution.py:17
  257.7 5.8 %fusion.1 = bf16[256,4096]{1,0:T(8,128)(2,1)} fusion(f32[256,4096]{1,0:T(8,128)} %copy-done.1, bf16[32,8,32,128]{3,2,1,0:T(8,128)(2,1)S(1)} %bitcast.159, bf16[128,4096]{1,0:T(8,128)(2,1)} %collective-permute-done.4, bf16[128,4096]{1,0:T(8,128)(2,1)S(1)} %maximum_select_fusion.8, pred[]{:T(512)S(6)} %eq.9, bf16[256,256]{0,1:T(8,128)(2,1)S(1)} %bitcast.171, ...), kind=kOutput, calls=%fused_computation.13 | convolution fusion | flops 586219520 | bytes 10747905 | tf_op jit(solution)/shard_map/dot_general | solution.py:74
  263.6 4.4 %collective-permute-done.5 = bf16[256,4096]{1,0:T(8,128)(2,1)S(1)} collective-permute-done((bf16[256,4096]{1,0:T(8,128)(2,1)}, bf16[256,4096]{1,0:T(8,128)(2,1)S(1)}, u32[]{:S(2)}, u32[]{:S(2)}) %collective-permute-start.5) | collective-permute-done | bytes 2097184 | tf_op jit(solution)/shard_map/ppermute | solution.py:17
  268.5 2.1 gather_fusion.4
  270.6 2.8 bitcast_add_fusion.1
  275.8 8.1 %collective-permute-done.6 = bf16[32,4096]{1,0:T(8,128)(2,1)S(1)} collective-permute-done((bf16[32,4096]{1,0:T(8,128)(2,1)S(1)}, bf16[32,4096]{1,0:T(8,128)(2,1)S(1)}, u32[]{:S(2)}, u32[]{:S(2)}) %collective-permute-start.6) | collective-permute-done | bytes 262176 | tf_op jit(solution)/shard_map/ppermute | solution.py:17
  284.0 23.8 %collective-permute-done.7 = bf16[64,4096]{1,0:T(8,128)(2,1)S(1)} collective-permute-done((bf16[64,4096]{1,0:T(8,128)(2,1)S(1)}, bf16[64,4096]{1,0:T(8,128)(2,1)S(1)}, u32[]{:S(2)}, u32[]{:S(2)}) %collective-permute-start.7) | collective-permute-done | bytes 524320 | tf_op jit(solution)/shard_map/ppermute | solution.py:17
  308.1 2.7 copy_bitcast_fusion.1
  313.7 5.9 %fusion.2 = bf16[256,4096]{1,0:T(8,128)(2,1)} fusion(f32[256,4096]{1,0:T(8,128)} %copy-done.2, bf16[32,8,32,128]{3,2,1,0:T(8,128)(2,1)S(1)} %bitcast.160, bf16[128,4096]{1,0:T(8,128)(2,1)} %collective-permute-done.8, bf16[128,4096]{1,0:T(8,128)(2,1)S(1)} %maximum_select_fusion.9, pred[]{:T(512)S(6)} %eq.20, bf16[256,256]{0,1:T(8,128)(2,1)S(1)} %bitcast.172, ...), kind=kOutput, calls=%fused_computation.14 | convolution fusion | flops 586219520 | bytes 10747905 | tf_op jit(solution)/shard_map/dot_general | solution.py:74
  319.5 48.2 %collective-permute-done.9 = bf16[256,4096]{1,0:T(8,128)(2,1)S(1)} collective-permute-done((bf16[256,4096]{1,0:T(8,128)(2,1)}, bf16[256,4096]{1,0:T(8,128)(2,1)S(1)}, u32[]{:S(2)}, u32[]{:S(2)}) %collective-permute-start.9) | collective-permute-done | bytes 2097184 | tf_op jit(solution)/shard_map/ppermute | solution.py:17
  368.3 2.1 gather_fusion.6
  370.5 2.8 bitcast_add_fusion
  375.6 4.8 %collective-permute-done.10 = bf16[16,4096]{1,0:T(8,128)(2,1)S(1)} collective-permute-done((bf16[16,4096]{1,0:T(8,128)(2,1)S(1)}, bf16[16,4096]{1,0:T(8,128)(2,1)S(1)}, u32[]{:S(2)}, u32[]{:S(2)}) %collective-permute-start.10) | collective-permute-done | bytes 131104 | tf_op jit(solution)/shard_map/ppermute | solution.py:17
  382.2 11.9 %collective-permute-done.11 = bf16[32,4096]{1,0:T(8,128)(2,1)S(1)} collective-permute-done((bf16[32,4096]{1,0:T(8,128)(2,1)S(1)}, bf16[32,4096]{1,0:T(8,128)(2,1)S(1)}, u32[]{:S(2)}, u32[]{:S(2)}) %collective-permute-start.11) | collective-permute-done | bytes 262176 | tf_op jit(solution)/shard_map/ppermute | solution.py:17
  396.4 2.7 copy_bitcast_fusion
  399.8 21.9 %collective-permute-done.13 = bf16[128,4096]{1,0:T(8,128)(2,1)} collective-permute-done((bf16[128,4096]{1,0:T(8,128)(2,1)S(1)}, bf16[128,4096]{1,0:T(8,128)(2,1)}, u32[]{:S(2)}, u32[]{:S(2)}) %collective-permute-start.13) | collective-permute-done | bytes 1048608 | tf_op jit(solution)/shard_map/ppermute | solution.py:17
  423.6 5.9 %fusion.3 = bf16[256,4096]{1,0:T(8,128)(2,1)} fusion(f32[256,4096]{1,0:T(8,128)} %copy-done.3, bf16[32,8,32,128]{3,2,1,0:T(8,128)(2,1)S(1)} %bitcast.157, bf16[128,4096]{1,0:T(8,128)(2,1)} %collective-permute-done.13, bf16[128,4096]{1,0:T(8,128)(2,1)S(1)} %maximum_select_fusion.10, pred[]{:T(512)S(6)} %eq.21, bf16[256,256]{0,1:T(8,128)(2,1)S(1)} %bitcast.169, ...), kind=kOutput, calls=%fused_computation.15 | convolution fusion | flops 586219520 | bytes 10747905 | tf_op jit(solution)/shard_map/dot_general | solution.py:74
  (69 shorter events, 30.1 us)
Async XLA Ops:
  0.0 6.3 %copy-start.6 = (s32[4,32]{1,0:T(4,128)S(1)}, s32[4,32]{1,0:T(4,128)}, u32[]{:S(2)}) copy-start(s32[4,32]{1,0:T(4,128)} %param.8) | copy-start | bytes 1540
  3.3 48.7 %collective-permute-start = (bf16[256,4096]{0,1:T(8,128)(2,1)S(1)}, bf16[256,4096]{0,1:T(8,128)(2,1)S(1)}, u32[]{:S(2)}, u32[]{:S(2)}) collective-permute-start(bf16[256,4096]{0,1:T(8,128)(2,1)S(1)} %copy.17), channel_id=1, source_target_pairs={{0,16},{16,0},{8,24},{24,8},{1,17},{17,1},{9,25},{25,9},{2,18},{18... | collective-permute-start | bytes 6291464 | tf_op jit(solution)/shard_map/ppermute | solution.py:17
  52.0 1.3 copy-start.4
  61.4 1.9 copy-start
  63.4 1.9 copy-start.5
  63.4 1.9 copy-start.7
  63.5 24.5 %collective-permute-start.1 = (bf16[128,4096]{1,0:T(8,128)(2,1)S(1)}, bf16[128,4096]{1,0:T(8,128)(2,1)}, u32[]{:S(2)}, u32[]{:S(2)}) collective-permute-start(bf16[128,4096]{1,0:T(8,128)(2,1)S(1)} %slice.148), channel_id=1, source_target_pairs={{0,16},{16,0},{8,24},{24,8},{1,17},{17,1},{9,25},{25,9},{2,18},{18... | collective-permute-start | bytes 3145736 | tf_op jit(solution)/shard_map/ppermute | solution.py:17
  95.8 91.9 %collective-permute-start.2 = (bf16[256,4096]{1,0:T(8,128)(2,1)}, bf16[256,4096]{1,0:T(8,128)(2,1)S(1)}, u32[]{:S(2)}, u32[]{:S(2)}) collective-permute-start(bf16[256,4096]{1,0:T(8,128)(2,1)} %fusion), channel_id=1, source_target_pairs={{0,4},{4,0},{1,5},{5,1},{2,6},{6,2},{3,7},{7,3},{8,12},{12,8},{9,1... | collective-permute-start | bytes 6291464 | tf_op jit(solution)/shard_map/ppermute | solution.py:17
  193.3 1.9 copy-start.1
  195.3 13.2 %collective-permute-start.3 = (bf16[64,4096]{1,0:T(8,128)(2,1)S(1)}, bf16[64,4096]{1,0:T(8,128)(2,1)S(1)}, u32[]{:S(2)}, u32[]{:S(2)}) collective-permute-start(bf16[64,4096]{1,0:T(8,128)(2,1)S(1)} %slice.149), channel_id=1, source_target_pairs={{0,16},{16,0},{8,24},{24,8},{1,17},{17,1},{9,25},{25,9},{2,18},{18... | collective-permute-start | bytes 1572872 | tf_op jit(solution)/shard_map/ppermute | solution.py:17
  208.7 47.0 %collective-permute-start.4 = (bf16[128,4096]{1,0:T(8,128)(2,1)S(1)}, bf16[128,4096]{1,0:T(8,128)(2,1)}, u32[]{:S(2)}, u32[]{:S(2)}) collective-permute-start(bf16[128,4096]{1,0:T(8,128)(2,1)S(1)} %maximum_select_fusion.8), channel_id=1, source_target_pairs={{0,4},{4,0},{1,5},{5,1},{2,6},{6,2},{3,7},{7,3},{8,12},{12,8},{9,1... | collective-permute-start | bytes 3145736 | tf_op jit(solution)/shard_map/ppermute | solution.py:17
  263.5 4.4 %collective-permute-start.5 = (bf16[256,4096]{1,0:T(8,128)(2,1)}, bf16[256,4096]{1,0:T(8,128)(2,1)S(1)}, u32[]{:S(2)}, u32[]{:S(2)}) collective-permute-start(bf16[256,4096]{1,0:T(8,128)(2,1)} %fusion.1), channel_id=1, source_target_pairs={{0,8},{8,0},{16,24},{24,16},{1,9},{9,1},{17,25},{25,17},{2,10},{10... | collective-permute-start | bytes 6291464 | tf_op jit(solution)/shard_map/ppermute | solution.py:17
  273.5 1.9 copy-start.2
  275.4 8.4 %collective-permute-start.6 = (bf16[32,4096]{1,0:T(8,128)(2,1)S(1)}, bf16[32,4096]{1,0:T(8,128)(2,1)S(1)}, u32[]{:S(2)}, u32[]{:S(2)}) collective-permute-start(bf16[32,4096]{1,0:T(8,128)(2,1)S(1)} %slice.150), channel_id=1, source_target_pairs={{0,16},{16,0},{8,24},{24,8},{1,17},{17,1},{9,25},{25,9},{2,18},{18... | collective-permute-start | bytes 786440 | tf_op jit(solution)/shard_map/ppermute | solution.py:17
  283.9 23.9 %collective-permute-start.7 = (bf16[64,4096]{1,0:T(8,128)(2,1)S(1)}, bf16[64,4096]{1,0:T(8,128)(2,1)S(1)}, u32[]{:S(2)}, u32[]{:S(2)}) collective-permute-start(bf16[64,4096]{1,0:T(8,128)(2,1)S(1)} %maximum_select_fusion.11), channel_id=1, source_target_pairs={{0,4},{4,0},{1,5},{5,1},{2,6},{6,2},{3,7},{7,3},{8,12},{12,8},{9,1... | collective-permute-start | bytes 1572872 | tf_op jit(solution)/shard_map/ppermute | solution.py:17
  308.0 3.5 collective-permute-start.8
  319.5 48.2 %collective-permute-start.9 = (bf16[256,4096]{1,0:T(8,128)(2,1)}, bf16[256,4096]{1,0:T(8,128)(2,1)S(1)}, u32[]{:S(2)}, u32[]{:S(2)}) collective-permute-start(bf16[256,4096]{1,0:T(8,128)(2,1)} %fusion.2), channel_id=1, source_target_pairs={{0,2},{2,0},{1,3},{3,1},{4,6},{6,4},{5,7},{7,5},{8,10},{10,8},{9,1... | collective-permute-start | bytes 6291464 | tf_op jit(solution)/shard_map/ppermute | solution.py:17
  373.3 1.9 copy-start.3
  375.2 5.2 %collective-permute-start.10 = (bf16[16,4096]{1,0:T(8,128)(2,1)S(1)}, bf16[16,4096]{1,0:T(8,128)(2,1)S(1)}, u32[]{:S(2)}, u32[]{:S(2)}) collective-permute-start(bf16[16,4096]{1,0:T(8,128)(2,1)S(1)} %slice.151), channel_id=1, source_target_pairs={{0,16},{16,0},{8,24},{24,8},{1,17},{17,1},{9,25},{25,9},{2,18},{18... | collective-permute-start | bytes 393224 | tf_op jit(solution)/shard_map/ppermute | solution.py:17
  380.4 13.6 %collective-permute-start.11 = (bf16[32,4096]{1,0:T(8,128)(2,1)S(1)}, bf16[32,4096]{1,0:T(8,128)(2,1)S(1)}, u32[]{:S(2)}, u32[]{:S(2)}) collective-permute-start(bf16[32,4096]{1,0:T(8,128)(2,1)S(1)} %maximum_select_fusion.13), channel_id=1, source_target_pairs={{0,4},{4,0},{1,5},{5,1},{2,6},{6,2},{3,7},{7,3},{8,12},{12,8},{9,1... | collective-permute-start | bytes 786440 | tf_op jit(solution)/shard_map/ppermute | solution.py:17
  394.1 2.0 collective-permute-start.12
  396.3 25.4 %collective-permute-start.13 = (bf16[128,4096]{1,0:T(8,128)(2,1)S(1)}, bf16[128,4096]{1,0:T(8,128)(2,1)}, u32[]{:S(2)}, u32[]{:S(2)}) collective-permute-start(bf16[128,4096]{1,0:T(8,128)(2,1)S(1)} %maximum_select_fusion.10), channel_id=1, source_target_pairs={{0,2},{2,0},{1,3},{3,1},{4,6},{6,4},{5,7},{7,5},{8,10},{10,8},{9,1... | collective-permute-start | bytes 3145736 | tf_op jit(solution)/shard_map/ppermute | solution.py:17
where the time goes:
time: 430 us; the launch traced here: 429 us
  waiting for transfers between devices  335 us (78%)
  local copies, waits for them, and re-layouts  47.4 us (11%)
  matrix products  23.4 us (5%)
  other arithmetic  12.1 us (3%)
  starting transfers between devices  11.3 us (3%)
    ppermute x14, waiting for transfers between devices, swapped(): return lax.ppermute(block, axis, route)  335 us
    dot_general x4, matrix products, on_device(): update = jnp.dot(weights, panel, preferred_element_type=jnp.float32)  23.4 us
    unnamed x17, local copies, waits for them, and re-layouts  12.3 us
    ppermute x14, starting transfers between devices, swapped(): return lax.ppermute(block, axis, route)  11.3 us
    add x4, other arithmetic, on_device(): merged = current.astype(jnp.float32) + moved.astype(jnp.float32)  11.2 us
    reshape x4, local copies, waits for them, and re-layouts, on_device(): coupling = merged.reshape(slab_rows, block_count, BLOCK)[:, chosen_blocks]  10.8 us
  transfers between devices with their start and end apart: 14, of which 13 were waited for; matrix products, arithmetic and copies ran while one was open for 3% of the time, Pallas kernels for 0%

commit v1 on v0

v1 whole, which is shorter than its diff:
```python
import functools

import jax
import jax.numpy as jnp
from jax import lax
from jax.experimental import pallas as pl
from jax.experimental.pallas import tpu as pltpu
from jax.sharding import PartitionSpec as P

BLOCK = 128
LEVELS = 4
TILE = 2 * BLOCK
F32 = jnp.float32
BF16 = jnp.bfloat16


def stride_bit(axis, level):
    return lax.axis_size(axis).bit_length() - 2 - level // 2


def level_axis(level):
    return "tx" if level % 2 == 0 else "ty"


def trade(block, level):
    axis = level_axis(level)
    flip = 1 << stride_bit(axis, level)
    return lax.ppermute(block, axis, [(i, i ^ flip) for i in range(lax.axis_size(axis))])


def my_bit(level):
    axis = level_axis(level)
    place = lax.axis_index(axis).astype(jnp.int32)
    return jnp.bitwise_and(jnp.right_shift(place, stride_bit(axis, level)), 1)


def cut(pieces, start, rows):
    for ref, low, count in pieces:
        if start < count:
            assert start + rows <= count
            return ref, low + start
        start -= count
    raise ValueError


def segments(one, other):
    edges = {0}
    for pieces in (one, other):
        at = 0
        for _, _, count in pieces:
            at += count
            edges.add(at)
    edges = sorted(edges)
    return [(a, b - a) for a, b in zip(edges[:-1], edges[1:])]


def level_kernel(meta, *refs, base, blocks, n_in, top, pairs, outs, keeps):
    ins, out_refs, rest = refs[:n_in], refs[n_in : n_in + len(outs)], refs[n_in + len(outs) :]
    width = blocks * BLOCK

    def stack(spec):
        return [(ins[i], low, count) for i, low, count in spec]

    def at(j):
        return pl.ds(pl.multiple_of(j * BLOCK, BLOCK), BLOCK)

    def read(pieces, start, rows, j):
        ref, low = cut(pieces, start, rows)
        return ref[pl.ds(low, rows), at(j)].astype(F32)

    def order(j):
        return meta[base + j]

    if top is not None:
        inv, (panel, inv_rel, merged) = ins[0], rest
        a, b = stack(top[0]), stack(top[1])
        half = sum(count for _, _, count in a)
        shift = meta[base + 4 * blocks]
        row_id = lax.broadcasted_iota(jnp.int32, inv.shape, 0)
        col_id = lax.broadcasted_iota(jnp.int32, inv.shape, 1)
        swap = jnp.where(row_id == jnp.bitwise_xor(col_id, shift), 1.0, 0.0).astype(BF16)
        inv_rel[...] = jnp.dot(inv[...], swap, preferred_element_type=F32).astype(BF16)

        def merge_block(j, carry):
            other = order(j)
            keep_a = meta[base + blocks + j].astype(F32)
            keep_b = meta[base + 2 * blocks + j].astype(F32)
            for start, rows in segments(a, b):
                from_a = read(a, start, rows, j) + read(b, start, rows, other)
                from_b = read(b, start, rows, j) + read(a, start, rows, other)
                low, high = pl.ds(start, rows), pl.ds(half + start, rows)
                merged[low, at(j)] = from_a
                merged[high, at(j)] = from_b
                panel[low, at(j)] = (from_a * keep_a).astype(BF16)
                panel[high, at(j)] = (from_b * keep_b).astype(BF16)
            return carry

        lax.fori_loop(0, blocks, merge_block, 0, unroll=4)
    else:
        panel, inv_rel = ins[0], ins[1]

    def columns(job, j):
        source, start, rows = job
        if source == "top":
            return merged[pl.ds(start, rows), at(j)]
        a, b = (stack(s) for s in pairs[source])
        return read(a, start, rows, j) + read(b, start, rows, order(j))

    jobs = [job for dest in outs for job in dest]
    pivots = [meta[base + 3 * blocks + i] for i in range(inv_rel.shape[0] // BLOCK)]
    coupling = jnp.concatenate(
        [jnp.concatenate([columns(job, p) for p in pivots], axis=1).astype(BF16) for job in jobs],
        axis=0,
    )
    weights = jnp.dot(coupling, inv_rel[...], preferred_element_type=F32).astype(BF16)

    def finish_tile(t, carry):
        lanes = pl.ds(pl.multiple_of(t * TILE, TILE), TILE)
        update = jnp.dot(weights, panel[:, lanes], preferred_element_type=F32)
        done = 0
        for out, dest in zip(out_refs, outs):
            put = 0
            for job in dest:
                rows = job[2]
                for i in range(TILE // BLOCK):
                    j = (TILE // BLOCK) * t + i
                    part = update[done : done + rows, i * BLOCK : (i + 1) * BLOCK]
                    out[pl.ds(put, rows), at(j)] = (columns(job, j) - part).astype(BF16)
                put += rows
                done += rows
        return carry

    lax.fori_loop(0, width // TILE, finish_tile, 0, unroll=4)


def run_level(level, meta, held, outs, pairs=(), top=None, keeps=False):
    arrays = list(held)

    def spec(stack):
        named = []
        for x, low, rows in stack:
            found = [i for i, seen in enumerate(arrays) if seen is x]
            if not found:
                arrays.append(x)
            named.append((found[0] if found else len(arrays) - 1, low, rows))
        return tuple(named)

    top_spec = None if top is None else (spec(top[0]), spec(top[1]))
    pair_specs = tuple((spec(a), spec(b)) for a, b in pairs)
    width = arrays[-1].shape[1]
    size = held[-1].shape[0]
    shapes = [jax.ShapeDtypeStruct((sum(job[2] for job in dest), width), BF16) for dest in outs]
    rows = sum(shape.shape[0] for shape in shapes)
    scratch = []
    if top is not None:
        tails = [(size, width), (size, size)]
        if keeps:
            shapes += [jax.ShapeDtypeStruct(s, BF16) for s in tails]
        else:
            scratch += [pltpu.VMEM(s, BF16) for s in tails]
        scratch.append(pltpu.VMEM((size, width), F32))
    blocks = width // BLOCK
    kernel = functools.partial(
        level_kernel,
        base=level * meta.shape[0] // LEVELS,
        blocks=blocks,
        n_in=len(arrays),
        top=top_spec,
        pairs=pair_specs,
        outs=tuple(tuple(dest) for dest in outs),
        keeps=keeps,
    )
    return pl.pallas_call(
        kernel,
        out_shape=shapes,
        in_specs=[pl.BlockSpec(memory_space=pltpu.SMEM)]
        + [pl.BlockSpec(memory_space=pltpu.VMEM)] * len(arrays),
        out_specs=[pl.BlockSpec(memory_space=pltpu.VMEM)] * len(shapes),
        scratch_shapes=scratch,
        compiler_params=pltpu.CompilerParams(vmem_limit_bytes=30 * 2**20),
        cost_estimate=pl.CostEstimate(
            flops=2 * rows * size * (width + size),
            bytes_accessed=sum(x.size * 2 for x in arrays) + sum(s.size * 2 for s in shapes),
            transcendentals=0,
        ),
        name=f"level{level}_rows{rows}",
    )(meta, *arrays)


def on_device(schur_slab, pivot_inverse, block_pattern, column_order, pivot_blocks):
    size = pivot_inverse.shape[1]
    blocks = schur_slab.shape[1] // BLOCK
    half = size // 2
    quarter = half // 2
    eighth = quarter // 2
    rank = jnp.int32(0)
    meta = []
    for level in range(LEVELS):
        bit = my_bit(level)
        rank = rank + bit * (1 << level)
        shift = rank * (size >> (level + 1))
        meta += [
            column_order[level],
            jnp.where(bit == 0, block_pattern[level, 0], block_pattern[level, 1]),
            jnp.where(bit == 0, block_pattern[level, 1], block_pattern[level, 0]),
            pivot_blocks[level],
            jnp.zeros((blocks,), jnp.int32) + shift,
        ]
    meta = jnp.concatenate(meta)

    first = schur_slab[:half]
    first_1, first_2 = schur_slab[:quarter], schur_slab[quarter:half]
    rest_1, rest_2 = schur_slab[half : half + quarter], schur_slab[half + quarter :]

    first_y = trade(first, 0)
    first_z1 = trade(first_1, 1)
    first_z2 = trade(first_2, 1)
    first_yz1 = trade(first_z1, 0)
    rest_y1 = trade(rest_1, 0)
    first_yz2 = trade(first_z2, 0)
    rest_y2 = trade(rest_2, 0)

    tops = [("top", 0, quarter), ("top", half, quarter)]
    near, near_x, panel, inv = run_level(
        0,
        meta,
        (pivot_inverse[0],),
        [tops, [("top", quarter, quarter)]],
        top=([(first, 0, half)], [(first_y, 0, half)]),
        keeps=True,
    )
    (after_1,) = run_level(
        0, meta, (panel, inv), [[(0, 0, quarter)]], pairs=[([(rest_1, 0, quarter)], [(rest_y1, 0, quarter)])]
    )
    (after_2,) = run_level(
        0, meta, (panel, inv), [[(0, 0, quarter)]], pairs=[([(rest_2, 0, quarter)], [(rest_y2, 0, quarter)])]
    )
    far, far_x = run_level(
        0,
        meta,
        (pivot_inverse[0],),
        [tops, [("top", quarter, quarter)]],
        top=(
            [(first_z1, 0, quarter), (first_z2, 0, quarter)],
            [(first_yz1, 0, quarter), (first_yz2, 0, quarter)],
        ),
    )

    after_z1 = trade(after_1, 1)
    after_z2 = trade(after_2, 1)
    tops = [("top", low, eighth) for low in range(0, size, quarter)]
    head, panel, inv = run_level(
        1,
        meta,
        (pivot_inverse[1],),
        [tops + [("top", eighth, eighth), (0, 0, quarter)]],
        top=([(near, 0, half)], [(far, 0, half)]),
        pairs=[([(near_x, 0, quarter)], [(far_x, 0, quarter)])],
        keeps=True,
    )
    (next_1,) = run_level(
        1, meta, (panel, inv), [[(0, 0, quarter)]], pairs=[([(after_1, 0, quarter)], [(after_z1, 0, quarter)])]
    )
    (next_2,) = run_level(
        1, meta, (panel, inv), [[(0, 0, quarter)]], pairs=[([(after_2, 0, quarter)], [(after_z2, 0, quarter)])]
    )

    head_c = trade(head, 2)
    next_c1 = trade(next_1, 2)
    next_c2 = trade(next_2, 2)
    more = head.shape[0] - half
    share = eighth // 2
    tops_a = [("top", low, share) for low in range(0, half, eighth)]
    tops_b = [("top", half + low, share) for low in range(0, half, eighth)]
    lead, other_tops, panel, inv = run_level(
        2,
        meta,
        (pivot_inverse[2],),
        [tops_a + [("top", share, share), (0, 0, more)], tops_b],
        top=([(head, 0, half)], [(head_c, 0, half)]),
        pairs=[([(head, half, more)], [(head_c, half, more)])],
        keeps=True,
    )
    (last_1,) = run_level(
        2, meta, (panel, inv), [[(0, 0, quarter)]], pairs=[([(next_1, 0, quarter)], [(next_c1, 0, quarter)])]
    )
    (last_2,) = run_level(
        2, meta, (panel, inv), [[(0, 0, quarter)]], pairs=[([(next_2, 0, quarter)], [(next_c2, 0, quarter)])]
    )

    lead_w = trade(lead, 3)
    tops_cw = trade(lead_w[:quarter], 2)
    last_w1 = trade(last_1, 3)
    last_w2 = trade(last_2, 3)
    more = lead.shape[0] - quarter
    (out,) = run_level(
        3,
        meta,
        (pivot_inverse[3],),
        [[("top", 0, share), (0, 0, more), (1, 0, quarter), (2, 0, quarter)]],
        top=([(lead, 0, quarter), (other_tops, 0, quarter)], [(lead_w, 0, quarter), (tops_cw, 0, quarter)]),
        pairs=[
            ([(lead, quarter, more)], [(lead_w, quarter, more)]),
            ([(last_1, 0, quarter)], [(last_w1, 0, quarter)]),
            ([(last_2, 0, quarter)], [(last_w2, 0, quarter)]),
        ],
    )
    return out


def solution(mesh):
    return jax.shard_map(
        on_device,
        mesh=mesh,
        in_specs=(P(("tx", "ty"), None), P(), P(), P(), P()),
        out_specs=P(("tx", "ty"), None),
        check_vma=False,
    )
```

time: 430 us -> 177 us (0.41)
  waiting for transfers between devices: 335 us -> 120 us
  local copies, waits for them, and re-layouts: 47.4 us -> 4.19 us
  Pallas kernels: 0 us -> 34.2 us
  matrix products: 23.4 us -> 0 us
  other arithmetic: 12.1 us -> 0.01 us
  starting transfers between devices: 11.3 us -> 17.9 us
    ppermute x14 -> x16, waiting for transfers between devices: 335 us -> 120 us  [trade(): lax.ppermute(block, axis, [(i, i ^ flip) for i in range(lax.axis_size(axi...]
    pallas_call x0 -> x11, Pallas kernels: none -> 34.2 us  [run_level(): pl.pallas_call(kernel, out_shape=shapes, in_specs=[pl.BlockSpec(memory_sp...]
    dot_general x4 -> x0, matrix products: 23.4 us -> none  [on_device(): update = jnp.dot(weights, panel, preferred_element_type=jnp.float32)]
    reshape x8 -> x0, local copies, waits for them, and re-layouts: 15.7 us -> none  [the longest x4 10.8 us: on_device(): coupling = merged.reshape(slab_rows, block_count, BLOCK)[:, chosen_blocks]]
    unnamed x17 -> x8, local copies, waits for them, and re-layouts: 12.3 us -> 0.01 us
    add x4 -> x0, other arithmetic: 11.2 us -> none  [on_device(): merged = current.astype(jnp.float32) + moved.astype(jnp.float32)]
    gather x8 -> x0, local copies, waits for them, and re-layouts: 10.9 us -> none  [the longest x4 8.57 us: on_device(): partner.reshape(slab_rows, block_count, BLOCK)[:, block_order]]
    mul x4 -> x0, local copies, waits for them, and re-layouts: 7.78 us -> none  [on_device(): collected.reshape(pivot_total, block_count, BLOCK) * mask_rows[:, :, None]]
  transfers between devices with their start and end apart: 14 -> 16, of which waited for: 13 -> 10; matrix products, arithmetic and copies ran while one was open for 3% -> 1% of each run, Pallas kernels for 0% -> 10%
where the time goes in v1:
time: 177 us
  waiting for transfers between devices  120 us (68%)
  Pallas kernels  34.2 us (19%)
  starting transfers between devices  17.9 us (10%)
  local copies, waits for them, and re-layouts  4.19 us (2%)
    ppermute x16, waiting for transfers between devices, trade(): lax.ppermute(block, axis, [(i, i ^ flip) for i in range(lax.axis_size(axi...  120 us
    pallas_call x11, Pallas kernels, run_level(): pl.pallas_call(kernel, out_shape=shapes, in_specs=[pl.BlockSpec(memory_sp...  34.2 us
    ppermute x16, starting transfers between devices, trade(): lax.ppermute(block, axis, [(i, i ^ flip) for i in range(lax.axis_size(axi...  17.9 us
  transfers between devices with their start and end apart: 16, of which 10 were waited for; matrix products, arithmetic and copies ran while one was open for 1% of the time, Pallas kernels for 10%

profile of v1, /device:TPU:0, one launch (start us, length us, event | category | flops | bytes accessed | tf_op | source)
XLA Modules:
  0.0 177.0 jit_solution(3423354561141098595)
XLA Ops:
  0.0 2.8 %fusion.8 = (bf16[64,4096]{1,0:T(8,128)(2,1)S(1)}, bf16[64,4096]{1,0:T(8,128)(2,1)}, bf16[64,4096]{1,0:T(8,128)(2,1)}, bf16[64,4096]{1,0:T(8,128)(2,1)S(1)}) fusion(bf16[256,4096]{1,0:T(8,128)(2,1)} %param.5), kind=kLoop, calls=%fused_computation.28 | loop fusion | bytes 4194304 | tf_op jit(solution)/shard_map/slice | solution.py:213
  2.8 4.1 %collective-permute-start.2 = (bf16[64,4096]{1,0:T(8,128)(2,1)}, bf16[64,4096]{1,0:T(8,128)(2,1)}, u32[]{:S(2)}, u32[]{:S(2)}) collective-permute-start(bf16[64,4096]{1,0:T(8,128)(2,1)} %get-tuple-element.32), channel_id=1, source_target_pairs={{0,4},{1,5},{2,6},{3,7},{4,0},{5,1},{6,2},{7,3},{8,12},{9,13},{10,... | collective-permute-start | bytes 1572872 | tf_op jit(solution)/shard_map/ppermute | solution.py:28
  7.1 1.8 %collective-permute-start = (bf16[128,4096]{1,0:T(8,128)(2,1)S(1)}, bf16[128,4096]{1,0:T(8,128)(2,1)S(1)}, u32[]{:S(2)}, u32[]{:S(2)}) collective-permute-start(bf16[128,4096]{1,0:T(8,128)(2,1)S(1)} %slice.107.refs_1_), channel_id=1, source_target_pairs={{0,16},{8,24},{16,0},{24,8},{1,17},{9,25},{17,1},{25,9},{2,18},{10... | collective-permute-start | bytes 3145736 | tf_op jit(solution)/shard_map/ppermute | solution.py:28
  8.9 33.5 %collective-permute-done.2.refs_2_ = bf16[64,4096]{1,0:T(8,128)(2,1)} collective-permute-done((bf16[64,4096]{1,0:T(8,128)(2,1)}, bf16[64,4096]{1,0:T(8,128)(2,1)}, u32[]{:S(2)}, u32[]{:S(2)}) %collective-permute-start.2) | collective-permute-done | bytes 524320 | tf_op jit(solution)/shard_map/ppermute | solution.py:28
  42.5 1.9 %collective-permute-start.4 = (bf16[64,4096]{1,0:T(8,128)(2,1)}, bf16[64,4096]{1,0:T(8,128)(2,1)}, u32[]{:S(2)}, u32[]{:S(2)}) collective-permute-start(bf16[64,4096]{1,0:T(8,128)(2,1)} %collective-permute-done.2.refs_2_), channel_id=1, source_target_pairs={{0,16},{8,24},{16,0},{24,8},{1,17},{9,25},{17,1},{25,9},{2,18},{10... | collective-permute-start | bytes 1572872 | tf_op jit(solution)/shard_map/ppermute | solution.py:28
  44.3 8.5 %collective-permute-done.1.refs_1_ = bf16[64,4096]{1,0:T(8,128)(2,1)} collective-permute-done((bf16[64,4096]{1,0:T(8,128)(2,1)}, bf16[64,4096]{1,0:T(8,128)(2,1)}, u32[]{:S(2)}, u32[]{:S(2)}) %collective-permute-start.1) | collective-permute-done | bytes 524320 | tf_op jit(solution)/shard_map/ppermute | solution.py:28
  52.9 1.6 collective-permute-start.3
  54.6 1.1 slice_bitcast_fusion
  55.8 4.2 %level0_rows192.2 = (bf16[128,4096]{1,0:T(8,128)(2,1)S(1)}, bf16[64,4096]{1,0:T(8,128)(2,1)S(1)}, bf16[256,4096]{1,0:T(8,128)(2,1)S(1)}, bf16[256,256]{1,0:T(8,128)(2,1)S(1)}) custom-call(s32[640]{0:T(1024)S(1)} %concatenate.3.meta, bf16[256,256]{1,0:T(8,128)(2,1)S(1)} %get-tuple-element.35.refs_0_, bf16[128,4096]{1,0:T(8,128)(2,1)S(1)} %slice.107.refs_1_, ...), custom_call_target="tpu_custom_call" | custom-call | flops 427819008 | bytes 6029312 | tf_op jit(solution)/shard_map/level0_rows192/pallas_call | solution.py:173
  59.9 6.4 %collective-permute-done.3.refs_3_ = bf16[64,4096]{1,0:T(8,128)(2,1)} collective-permute-done((bf16[64,4096]{1,0:T(8,128)(2,1)}, bf16[64,4096]{1,0:T(8,128)(2,1)}, u32[]{:S(2)}, u32[]{:S(2)}) %collective-permute-start.3) | collective-permute-done | bytes 524320 | tf_op jit(solution)/shard_map/ppermute | solution.py:28
  66.3 5.1 %level0_rows192.3 = (bf16[128,4096]{1,0:T(8,128)(2,1)S(1)}, bf16[64,4096]{1,0:T(8,128)(2,1)S(1)}) custom-call(s32[640]{0:T(1024)S(1)} %concatenate.3.meta, bf16[256,256]{1,0:T(8,128)(2,1)S(1)} %get-tuple-element.35.refs_0_, bf16[64,4096]{1,0:T(8,128)(2,1)} %collective-permute-done.1.refs_1_, bf16[64,4096]{1,0:T(8,128)(2,1)} %collective-permute-done.2.refs_2_, ...), custom_call_target="tpu_custom_call" | custom-call | flops 427819008 | bytes 3801088 | tf_op jit(solution)/shard_map/level0_rows192/pallas_call | solution.py:173
  71.4 4.5 %level1_rows224.1 = (bf16[224,4096]{1,0:T(8,128)(2,1)S(1)}, bf16[256,4096]{1,0:T(8,128)(2,1)S(1)}, bf16[256,256]{1,0:T(8,128)(2,1)S(1)}) custom-call(s32[640]{0:T(1024)S(1)} %concatenate.3.meta, bf16[256,256]{1,0:T(8,128)(2,1)S(1)} %get-tuple-element.38.refs_0_, bf16[128,4096]{1,0:T(8,128)(2,1)S(1)} %get-tuple-element.18.refs_1_, ...), custom_call_target="tpu_custom_call" | custom-call | flops 499122176 | bytes 7340032 | tf_op jit(solution)/shard_map/level1_rows224/pallas_call | solution.py:173
  76.0 1.3 collective-permute-start.8
  77.3 0.8 collective-permute-start.12
  78.0 1.7 collective-permute-done.5.refs_2_
  79.7 4.6 %level2_rows240.1 = (bf16[176,4096]{1,0:T(8,128)(2,1)S(1)}, bf16[64,4096]{1,0:T(8,128)(2,1)S(1)}, bf16[256,4096]{1,0:T(8,128)(2,1)S(1)}, bf16[256,256]{1,0:T(8,128)(2,1)S(1)}) custom-call(s32[640]{0:T(1024)S(1)} %concatenate.3.meta, bf16[256,256]{1,0:T(8,128)(2,1)S(1)} %get-tuple-element.36.refs_0_, bf16[224,4096]{1,0:T(8,128)(2,1)S(1)} %get-tuple-element.22.refs_1_, ...), custom_call_target="tpu_custom_call" | custom-call | flops 534773760 | bytes 7995392 | tf_op jit(solution)/shard_map/level2_rows240/pallas_call | solution.py:173
  84.3 1.5 collective-permute-start.6
  85.8 4.9 %collective-permute-done.8.refs_3_ = bf16[64,4096]{1,0:T(8,128)(2,1)S(1)} collective-permute-done((bf16[64,4096]{1,0:T(8,128)(2,1)S(1)}, bf16[64,4096]{1,0:T(8,128)(2,1)S(1)}, u32[]{:S(2)}, u32[]{:S(2)}) %collective-permute-start.8) | collective-permute-done | bytes 524320 | tf_op jit(solution)/shard_map/ppermute | solution.py:28
  90.7 1.6 level0_rows64.2.refs_2_
  92.4 9.1 %collective-permute-done.12.refs_3_ = bf16[64,4096]{1,0:T(8,128)(2,1)S(1)} collective-permute-done((bf16[64,4096]{1,0:T(8,128)(2,1)S(1)}, bf16[64,4096]{1,0:T(8,128)(2,1)S(1)}, u32[]{:S(2)}, u32[]{:S(2)}) %collective-permute-start.12) | collective-permute-done | bytes 524320 | tf_op jit(solution)/shard_map/ppermute | solution.py:28
  101.5 1.6 level0_rows64.3.refs_2_
  103.2 25.8 %collective-permute-done.9.refs_3_ = bf16[64,4096]{1,0:T(8,128)(2,1)S(1)} collective-permute-done((bf16[64,4096]{1,0:T(8,128)(2,1)S(1)}, bf16[64,4096]{1,0:T(8,128)(2,1)S(1)}, u32[]{:S(2)}, u32[]{:S(2)}) %collective-permute-start.9) | collective-permute-done | bytes 524320 | tf_op jit(solution)/shard_map/ppermute | solution.py:28
  129.0 1.6 level1_rows64.2.refs_2_
  130.7 8.7 %collective-permute-done.13.refs_3_ = bf16[64,4096]{1,0:T(8,128)(2,1)S(1)} collective-permute-done((bf16[64,4096]{1,0:T(8,128)(2,1)S(1)}, bf16[64,4096]{1,0:T(8,128)(2,1)S(1)}, u32[]{:S(2)}, u32[]{:S(2)}) %collective-permute-start.13) | collective-permute-done | bytes 524320 | tf_op jit(solution)/shard_map/ppermute | solution.py:28
  139.5 1.6 level1_rows64.3.refs_2_
  141.2 1.6 level2_rows64.2.refs_5_
  142.8 4.1 %collective-permute-start.11 = (bf16[64,4096]{1,0:T(8,128)(2,1)S(1)}, bf16[64,4096]{1,0:T(8,128)(2,1)S(1)}, u32[]{:S(2)}, u32[]{:S(2)}) collective-permute-start(bf16[64,4096]{1,0:T(8,128)(2,1)S(1)} %level2_rows64.2.refs_5_), channel_id=1, source_target_pairs={{0,2},{1,3},{2,0},{3,1},{4,6},{5,7},{6,4},{7,5},{8,10},{9,11},{10,... | collective-permute-start | bytes 1572872 | tf_op jit(solution)/shard_map/ppermute | solution.py:28
  146.9 1.6 level2_rows64.3.refs_7_
  148.6 0.3 collective-permute-start.15
  149.0 10.7 %collective-permute-done.11.refs_6_ = bf16[64,4096]{1,0:T(8,128)(2,1)S(1)} collective-permute-done((bf16[64,4096]{1,0:T(8,128)(2,1)S(1)}, bf16[64,4096]{1,0:T(8,128)(2,1)S(1)}, u32[]{:S(2)}, u32[]{:S(2)}) %collective-permute-start.11) | collective-permute-done | bytes 524320 | tf_op jit(solution)/shard_map/ppermute | solution.py:28
  159.7 11.0 %collective-permute-done.15.refs_8_ = bf16[64,4096]{1,0:T(8,128)(2,1)S(1)} collective-permute-done((bf16[64,4096]{1,0:T(8,128)(2,1)S(1)}, bf16[64,4096]{1,0:T(8,128)(2,1)S(1)}, u32[]{:S(2)}, u32[]{:S(2)}) %collective-permute-start.15) | collective-permute-done | bytes 524320 | tf_op jit(solution)/shard_map/ppermute | solution.py:28
  170.8 6.2 %level3_rows256.1 = bf16[256,4096]{1,0:T(8,128)(2,1)} custom-call(s32[640]{0:T(1024)S(1)} %concatenate.3.meta, bf16[256,256]{1,0:T(8,128)(2,1)S(1)} %get-tuple-element.37.refs_0_, bf16[176,4096]{1,0:T(8,128)(2,1)S(1)} %get-tuple-element.23.refs_1_, bf16[64,4096]{1,0:T(8,128)(2,1)S(1)} %get-tuple-element.24.refs_2_, ...), custom_call_target="tpu_custom_call" | custom-call | flops 570425344 | bytes 8257536 | tf_op jit(solution)/shard_map/level3_rows256/pallas_call | solution.py:173
  (31 shorter events, 0.8 us)
Async XLA Ops:
  0.0 7.0 %copy-start = (bf16[256,4096]{1,0:T(8,128)(2,1)S(1)}, bf16[256,4096]{1,0:T(8,128)(2,1)}, u32[]{:S(2)}) copy-start(bf16[256,4096]{1,0:T(8,128)(2,1)} %param.5) | copy-start | bytes 6291460
  2.8 6.1 %copy-start.1 = (s32[4,2,32]{2,1,0:T(2,128)S(1)}, s32[4,2,32]{2,1,0:T(2,128)}, u32[]{:S(2)}) copy-start(s32[4,2,32]{2,1,0:T(2,128)} %param.7) | copy-start | bytes 3076
  2.8 51.6 %copy-start.2 = (s32[4,32]{1,0:T(4,128)S(1)}, s32[4,32]{1,0:T(4,128)}, u32[]{:S(2)}) copy-start(s32[4,32]{1,0:T(4,128)} %param.9) | copy-start | bytes 1540
  2.8 51.6 %copy-start.3 = (s32[4,32]{1,0:T(4,128)S(1)}, s32[4,32]{1,0:T(4,128)}, u32[]{:S(2)}) copy-start(s32[4,32]{1,0:T(4,128)} %param.8) | copy-start | bytes 1540
  2.8 39.6 %collective-permute-start.2 = (bf16[64,4096]{1,0:T(8,128)(2,1)}, bf16[64,4096]{1,0:T(8,128)(2,1)}, u32[]{:S(2)}, u32[]{:S(2)}) collective-permute-start(bf16[64,4096]{1,0:T(8,128)(2,1)} %get-tuple-element.32), channel_id=1, source_target_pairs={{0,4},{1,5},{2,6},{3,7},{4,0},{5,1},{6,2},{7,3},{8,12},{9,13},{10,... | collective-permute-start | bytes 1572872 | tf_op jit(solution)/shard_map/ppermute | solution.py:28
  6.9 45.9 %collective-permute-start.1 = (bf16[64,4096]{1,0:T(8,128)(2,1)}, bf16[64,4096]{1,0:T(8,128)(2,1)}, u32[]{:S(2)}, u32[]{:S(2)}) collective-permute-start(bf16[64,4096]{1,0:T(8,128)(2,1)} %get-tuple-element.33), channel_id=1, source_target_pairs={{0,4},{1,5},{2,6},{3,7},{4,0},{5,1},{6,2},{7,3},{8,12},{9,13},{10,... | collective-permute-start | bytes 1572872 | tf_op jit(solution)/shard_map/ppermute | solution.py:28
  7.1 48.7 %collective-permute-start = (bf16[128,4096]{1,0:T(8,128)(2,1)S(1)}, bf16[128,4096]{1,0:T(8,128)(2,1)S(1)}, u32[]{:S(2)}, u32[]{:S(2)}) collective-permute-start(bf16[128,4096]{1,0:T(8,128)(2,1)S(1)} %slice.107.refs_1_), channel_id=1, source_target_pairs={{0,16},{8,24},{16,0},{24,8},{1,17},{9,25},{17,1},{25,9},{2,18},{10... | collective-permute-start | bytes 3145736 | tf_op jit(solution)/shard_map/ppermute | solution.py:28
  42.5 17.5 %collective-permute-start.4 = (bf16[64,4096]{1,0:T(8,128)(2,1)}, bf16[64,4096]{1,0:T(8,128)(2,1)}, u32[]{:S(2)}, u32[]{:S(2)}) collective-permute-start(bf16[64,4096]{1,0:T(8,128)(2,1)} %collective-permute-done.2.refs_2_), channel_id=1, source_target_pairs={{0,16},{8,24},{16,0},{24,8},{1,17},{9,25},{17,1},{25,9},{2,18},{10... | collective-permute-start | bytes 1572872 | tf_op jit(solution)/shard_map/ppermute | solution.py:28
  52.9 13.4 %collective-permute-start.3 = (bf16[64,4096]{1,0:T(8,128)(2,1)}, bf16[64,4096]{1,0:T(8,128)(2,1)}, u32[]{:S(2)}, u32[]{:S(2)}) collective-permute-start(bf16[64,4096]{1,0:T(8,128)(2,1)} %collective-permute-done.1.refs_1_), channel_id=1, source_target_pairs={{0,16},{8,24},{16,0},{24,8},{1,17},{9,25},{17,1},{25,9},{2,18},{10... | collective-permute-start | bytes 1572872 | tf_op jit(solution)/shard_map/ppermute | solution.py:28
  75.9 3.9 %collective-permute-start.5 = (bf16[224,4096]{1,0:T(8,128)(2,1)S(1)}, bf16[224,4096]{1,0:T(8,128)(2,1)S(1)}, u32[]{:S(2)}, u32[]{:S(2)}) collective-permute-start(bf16[224,4096]{1,0:T(8,128)(2,1)S(1)} %get-tuple-element.22.refs_1_), channel_id=1, source_target_pairs={{0,8},{8,0},{16,24},{24,16},{1,9},{9,1},{17,25},{25,17},{2,10},{10... | collective-permute-start | bytes 5505032 | tf_op jit(solution)/shard_map/ppermute | solution.py:28
  76.0 14.8 %collective-permute-start.8 = (bf16[64,4096]{1,0:T(8,128)(2,1)S(1)}, bf16[64,4096]{1,0:T(8,128)(2,1)S(1)}, u32[]{:S(2)}, u32[]{:S(2)}) collective-permute-start(bf16[64,4096]{1,0:T(8,128)(2,1)S(1)} %get-tuple-element.34.refs_2_), channel_id=1, source_target_pairs={{0,16},{8,24},{16,0},{24,8},{1,17},{9,25},{17,1},{25,9},{2,18},{10... | collective-permute-start | bytes 1572872 | tf_op jit(solution)/shard_map/ppermute | solution.py:28
  77.3 24.2 %collective-permute-start.12 = (bf16[64,4096]{1,0:T(8,128)(2,1)S(1)}, bf16[64,4096]{1,0:T(8,128)(2,1)S(1)}, u32[]{:S(2)}, u32[]{:S(2)}) collective-permute-start(bf16[64,4096]{1,0:T(8,128)(2,1)S(1)} %get-tuple-element.31.refs_2_), channel_id=1, source_target_pairs={{0,16},{8,24},{16,0},{24,8},{1,17},{9,25},{17,1},{25,9},{2,18},{10... | collective-permute-start | bytes 1572872 | tf_op jit(solution)/shard_map/ppermute | solution.py:28
  84.3 64.5 %collective-permute-start.6 = (bf16[176,4096]{1,0:T(8,128)(2,1)S(1)}, bf16[176,4096]{1,0:T(8,128)(2,1)S(1)}, u32[]{:S(2)}, u32[]{:S(2)}) collective-permute-start(bf16[176,4096]{1,0:T(8,128)(2,1)S(1)} %get-tuple-element.23.refs_1_), channel_id=1, source_target_pairs={{0,2},{1,3},{2,0},{3,1},{4,6},{5,7},{6,4},{7,5},{8,10},{9,11},{10,... | collective-permute-start | bytes 4325384 | tf_op jit(solution)/shard_map/ppermute | solution.py:28
  92.4 36.7 %collective-permute-start.9 = (bf16[64,4096]{1,0:T(8,128)(2,1)S(1)}, bf16[64,4096]{1,0:T(8,128)(2,1)S(1)}, u32[]{:S(2)}, u32[]{:S(2)}) collective-permute-start(bf16[64,4096]{1,0:T(8,128)(2,1)S(1)} %level0_rows64.2.refs_2_), channel_id=1, source_target_pairs={{0,4},{1,5},{2,6},{3,7},{4,0},{5,1},{6,2},{7,3},{8,12},{9,13},{10,... | collective-permute-start | bytes 1572872 | tf_op jit(solution)/shard_map/ppermute | solution.py:28
  103.1 36.3 %collective-permute-start.13 = (bf16[64,4096]{1,0:T(8,128)(2,1)S(1)}, bf16[64,4096]{1,0:T(8,128)(2,1)S(1)}, u32[]{:S(2)}, u32[]{:S(2)}) collective-permute-start(bf16[64,4096]{1,0:T(8,128)(2,1)S(1)} %level0_rows64.3.refs_2_), channel_id=1, source_target_pairs={{0,4},{1,5},{2,6},{3,7},{4,0},{5,1},{6,2},{7,3},{8,12},{9,13},{10,... | collective-permute-start | bytes 1572872 | tf_op jit(solution)/shard_map/ppermute | solution.py:28
  130.7 10.5 %collective-permute-start.10 = (bf16[64,4096]{1,0:T(8,128)(2,1)S(1)}, bf16[64,4096]{1,0:T(8,128)(2,1)S(1)}, u32[]{:S(2)}, u32[]{:S(2)}) collective-permute-start(bf16[64,4096]{1,0:T(8,128)(2,1)S(1)} %level1_rows64.2.refs_2_), channel_id=1, source_target_pairs={{0,8},{8,0},{16,24},{24,16},{1,9},{9,1},{17,25},{25,17},{2,10},{10... | collective-permute-start | bytes 1572872 | tf_op jit(solution)/shard_map/ppermute | solution.py:28
  141.1 5.8 %collective-permute-start.14 = (bf16[64,4096]{1,0:T(8,128)(2,1)S(1)}, bf16[64,4096]{1,0:T(8,128)(2,1)S(1)}, u32[]{:S(2)}, u32[]{:S(2)}) collective-permute-start(bf16[64,4096]{1,0:T(8,128)(2,1)S(1)} %level1_rows64.3.refs_2_), channel_id=1, source_target_pairs={{0,8},{8,0},{16,24},{24,16},{1,9},{9,1},{17,25},{25,17},{2,10},{10... | collective-permute-start | bytes 1572872 | tf_op jit(solution)/shard_map/ppermute | solution.py:28
  142.8 16.9 %collective-permute-start.11 = (bf16[64,4096]{1,0:T(8,128)(2,1)S(1)}, bf16[64,4096]{1,0:T(8,128)(2,1)S(1)}, u32[]{:S(2)}, u32[]{:S(2)}) collective-permute-start(bf16[64,4096]{1,0:T(8,128)(2,1)S(1)} %level2_rows64.2.refs_5_), channel_id=1, source_target_pairs={{0,2},{1,3},{2,0},{3,1},{4,6},{5,7},{6,4},{7,5},{8,10},{9,11},{10,... | collective-permute-start | bytes 1572872 | tf_op jit(solution)/shard_map/ppermute | solution.py:28
  148.6 22.2 %collective-permute-start.15 = (bf16[64,4096]{1,0:T(8,128)(2,1)S(1)}, bf16[64,4096]{1,0:T(8,128)(2,1)S(1)}, u32[]{:S(2)}, u32[]{:S(2)}) collective-permute-start(bf16[64,4096]{1,0:T(8,128)(2,1)S(1)} %level2_rows64.3.refs_7_), channel_id=1, source_target_pairs={{0,2},{1,3},{2,0},{3,1},{4,6},{5,7},{6,4},{7,5},{8,10},{9,11},{10,... | collective-permute-start | bytes 1572872 | tf_op jit(solution)/shard_map/ppermute | solution.py:28
  148.9 21.9 %collective-permute-start.7 = (bf16[64,4096]{1,0:T(8,128)(2,1)S(1)}, bf16[64,4096]{1,0:T(8,128)(2,1)S(1)}, u32[]{:S(2)}, u32[]{:S(2)}) collective-permute-start(bf16[64,4096]{1,0:T(8,128)(2,1)S(1)} %slice.113), channel_id=1, source_target_pairs={{0,8},{8,0},{16,24},{24,16},{1,9},{9,1},{17,25},{25,17},{2,10},{10... | collective-permute-start | bytes 1572872 | tf_op jit(solution)/shard_map/ppermute | solution.py:28

commit v2 on v1

v2 whole, which is shorter than its diff:
```python
import functools

import jax
import jax.numpy as jnp
from jax import lax
from jax.experimental import pallas as pl
from jax.experimental.pallas import tpu as pltpu
from jax.sharding import PartitionSpec as P

BLOCK = 128
LEVELS = 4
TILE = 2 * BLOCK
F32 = jnp.float32
BF16 = jnp.bfloat16


def stride_bit(axis, level):
    return lax.axis_size(axis).bit_length() - 2 - level // 2


def level_axis(level):
    return "tx" if level % 2 == 0 else "ty"


def trade(block, level):
    axis = level_axis(level)
    flip = 1 << stride_bit(axis, level)
    return lax.ppermute(block, axis, [(i, i ^ flip) for i in range(lax.axis_size(axis))])


def my_bit(level):
    axis = level_axis(level)
    place = lax.axis_index(axis).astype(jnp.int32)
    return jnp.bitwise_and(jnp.right_shift(place, stride_bit(axis, level)), 1)


def after(x, *others):
    return lax.optimization_barrier((x, *others))


def cut(pieces, start, rows):
    for ref, low, count in pieces:
        if start < count:
            assert start + rows <= count
            return ref, low + start
        start -= count
    raise ValueError


def segments(one, other):
    edges = {0}
    for pieces in (one, other):
        at = 0
        for _, _, count in pieces:
            at += count
            edges.add(at)
    edges = sorted(edges)
    return [(a, b - a) for a, b in zip(edges[:-1], edges[1:])]


def reorder_kernel(meta, inv, out, *, step):
    for level in range(LEVELS):
        shape = inv.shape[1:]
        row_id = lax.broadcasted_iota(jnp.int32, shape, 0)
        col_id = lax.broadcasted_iota(jnp.int32, shape, 1)
        source = jnp.bitwise_xor(col_id, meta[step * (level + 1) - 1])
        swap = jnp.where(row_id == source, 1.0, 0.0).astype(BF16)
        out[level] = jnp.dot(inv[level], swap, preferred_element_type=F32).astype(BF16)


def level_kernel(meta, *refs, base, level, blocks, n_in, top, pairs, outs, n_hidden):
    ins, rest = refs[:n_in], refs[n_in + n_hidden :]
    out_refs, rest = rest[: len(outs)], rest[len(outs) :]
    width = blocks * BLOCK

    def stack(spec):
        return [(ins[i], low, count) for i, low, count in spec]

    def at(j):
        return pl.ds(pl.multiple_of(j * BLOCK, BLOCK), BLOCK)

    def read(pieces, start, rows, j):
        ref, low = cut(pieces, start, rows)
        return ref[pl.ds(low, rows), at(j)].astype(F32)

    def order(j):
        return meta[base + j]

    inv = ins[0]
    if top is not None:
        panel, merged = rest
        a, b = stack(top[0]), stack(top[1])
        half = sum(count for _, _, count in a)

        def merge_block(j, carry):
            other = order(j)
            keep_a = meta[base + blocks + j].astype(F32)
            keep_b = meta[base + 2 * blocks + j].astype(F32)
            for start, rows in segments(a, b):
                from_a = read(a, start, rows, j) + read(b, start, rows, other)
                from_b = read(b, start, rows, j) + read(a, start, rows, other)
                low, high = pl.ds(start, rows), pl.ds(half + start, rows)
                merged[low, at(j)] = from_a
                merged[high, at(j)] = from_b
                panel[low, at(j)] = (from_a * keep_a).astype(BF16)
                panel[high, at(j)] = (from_b * keep_b).astype(BF16)
            return carry

        lax.fori_loop(0, blocks, merge_block, 0, unroll=4)
    else:
        panel = ins[1]

    def columns(job, j):
        source, start, rows = job
        if source == "top":
            return merged[pl.ds(start, rows), at(j)]
        a, b = (stack(s) for s in pairs[source])
        return read(a, start, rows, j) + read(b, start, rows, order(j))

    jobs = [job for dest in outs for job in dest]
    pivots = [meta[base + 3 * blocks + i] for i in range(inv.shape[1] // BLOCK)]
    coupling = jnp.concatenate(
        [jnp.concatenate([columns(job, p) for p in pivots], axis=1).astype(BF16) for job in jobs],
        axis=0,
    )
    weights = jnp.dot(coupling, inv[level], preferred_element_type=F32).astype(BF16)

    def finish_tile(t, carry):
        lanes = pl.ds(pl.multiple_of(t * TILE, TILE), TILE)
        update = jnp.dot(weights, panel[:, lanes], preferred_element_type=F32)
        done = 0
        for out, dest in zip(out_refs, outs):
            put = 0
            for job in dest:
                rows = job[2]
                for i in range(TILE // BLOCK):
                    j = (TILE // BLOCK) * t + i
                    part = update[done : done + rows, i * BLOCK : (i + 1) * BLOCK]
                    out[pl.ds(put, rows), at(j)] = (columns(job, j) - part).astype(BF16)
                put += rows
                done += rows
        return carry

    lax.fori_loop(0, width // TILE, finish_tile, 0, unroll=4)


def run_level(level, meta, held, outs, pairs=(), top=None, keeps=False, part=None, cost=0):
    arrays = list(held)

    def spec(stack):
        named = []
        for x, low, rows in stack:
            found = [i for i, seen in enumerate(arrays) if seen is x]
            if not found:
                arrays.append(x)
            named.append((found[0] if found else len(arrays) - 1, low, rows))
        return tuple(named)

    top_spec = None if top is None else (spec(top[0]), spec(top[1]))
    pair_specs = tuple((spec(a), spec(b)) for a, b in pairs)
    n_in = len(arrays)
    width = arrays[-1].shape[1]
    size = held[0].shape[1]
    counts = [sum(job[2] for job in dest) for dest in outs]
    shapes = [jax.ShapeDtypeStruct((rows, width), BF16) for rows in counts]
    whole = pl.BlockSpec(memory_space=pltpu.VMEM)
    in_specs = [pl.BlockSpec(memory_space=pltpu.SMEM)] + [whole] * n_in
    out_specs = [whole] * len(shapes)
    aliases = {}
    hidden = []
    if part is not None:
        all_rows, block, old = part
        shapes[0] = jax.ShapeDtypeStruct((all_rows, width), BF16)
        out_specs[0] = pl.BlockSpec((counts[0], width), lambda i: (block, 0))
        if old is not None:
            hidden = [old]
            in_specs.append(pl.BlockSpec(memory_space=pl.ANY))
            aliases = {1 + n_in: 0}
    scratch = []
    if top is not None:
        if keeps:
            shapes.append(jax.ShapeDtypeStruct((size, width), BF16))
            out_specs.append(whole)
        else:
            scratch.append(pltpu.VMEM((size, width), BF16))
        scratch.append(pltpu.VMEM((size, width), F32))
    kernel = functools.partial(
        level_kernel,
        base=level * meta.shape[0] // LEVELS,
        level=level,
        blocks=width // BLOCK,
        n_in=n_in,
        top=top_spec,
        pairs=pair_specs,
        outs=tuple(tuple(dest) for dest in outs),
        n_hidden=len(hidden),
    )
    return pl.pallas_call(
        kernel,
        grid=(1,) if part is not None else (),
        out_shape=shapes,
        in_specs=in_specs,
        out_specs=out_specs,
        scratch_shapes=scratch,
        input_output_aliases=aliases,
        compiler_params=pltpu.CompilerParams(vmem_limit_bytes=30 * 2**20),
        cost_estimate=pl.CostEstimate(flops=cost, bytes_accessed=0, transcendentals=0),
        name=f"level{level}_rows{sum(counts)}",
    )(meta, *arrays, *hidden)


def reorder(meta, pivot_inverse):
    step = meta.shape[0] // LEVELS
    return pl.pallas_call(
        functools.partial(reorder_kernel, step=step),
        out_shape=jax.ShapeDtypeStruct(pivot_inverse.shape, BF16),
        in_specs=[pl.BlockSpec(memory_space=pltpu.SMEM), pl.BlockSpec(memory_space=pltpu.VMEM)],
        out_specs=pl.BlockSpec(memory_space=pltpu.VMEM),
        compiler_params=pltpu.CompilerParams(vmem_limit_bytes=30 * 2**20),
        cost_estimate=pl.CostEstimate(flops=0, bytes_accessed=0, transcendentals=0),
        name="reorder",
    )(meta, pivot_inverse)


def make_meta(size, block_pattern, column_order, pivot_blocks):
    blocks = column_order.shape[1]
    rank = jnp.int32(0)
    meta = []
    for level in range(LEVELS):
        bit = my_bit(level)
        rank = rank + bit * (1 << level)
        shift = rank * (size >> (level + 1))
        meta += [
            column_order[level],
            jnp.where(bit == 0, block_pattern[level, 0], block_pattern[level, 1]),
            jnp.where(bit == 0, block_pattern[level, 1], block_pattern[level, 0]),
            pivot_blocks[level],
            jnp.zeros((blocks,), jnp.int32) + shift,
        ]
    return jnp.concatenate(meta)


def on_device(schur_slab, pivot_inverse, block_pattern, column_order, pivot_blocks):
    all_rows = schur_slab.shape[0]
    size = pivot_inverse.shape[1]
    half, quarter, eighth, share = size // 2, size // 4, size // 8, size // 16
    meta = make_meta(size, block_pattern, column_order, pivot_blocks)

    def rows_of(x):
        return [(x, 0, x.shape[0])]

    def chunk(level, panel, own, other, **more):
        (out,) = run_level(
            level, meta, (inv, panel), [[(0, 0, own.shape[0])]], pairs=[(rows_of(own), rows_of(other))], **more
        )
        return out

    first_1 = schur_slab[:quarter]
    first_z1 = trade(first_1, 1)
    slab, first_1 = after(schur_slab, first_1)
    first = slab[:half]
    first_y = trade(first, 0)
    slab, first = after(slab, first)
    first_2 = slab[quarter:half]
    rest_1, rest_2 = slab[half : half + quarter], slab[half + quarter :]
    inv = reorder(meta, pivot_inverse)

    first_yz1 = trade(first_z1, 0)
    first_2, first_z1 = after(first_2, first_z1)
    first_z2 = trade(first_2, 1)
    rest_1, first_y = after(rest_1, first_y)
    rest_y1 = trade(rest_1, 0)

    tops = [("top", 0, quarter), ("top", half, quarter)]
    near, near_x, panel_0 = run_level(
        0, meta, (inv,), [tops, [("top", quarter, quarter)]], top=(rows_of(first), rows_of(first_y)), keeps=True
    )
    after_1 = chunk(0, panel_0, rest_1, rest_y1)
    first_z2, after_1, first_yz1 = after(first_z2, after_1, first_yz1)
    first_yz2 = trade(first_z2, 0)
    after_z1 = trade(after_1, 1)
    rest_2, first_yz2 = after(rest_2, first_yz2)
    rest_y2 = trade(rest_2, 0)
    far, far_x = run_level(
        0,
        meta,
        (inv,),
        [tops, [("top", quarter, quarter)]],
        top=(rows_of(first_z1) + rows_of(first_z2), rows_of(first_yz1) + rows_of(first_yz2)),
    )

    tops = [("top", low, eighth) for low in range(0, size, quarter)]
    head, panel_1 = run_level(1, meta, (inv,), [tops], top=(rows_of(near), rows_of(far)), keeps=True)
    head_c = trade(head, 2)
    rest_y2, after_z1 = after(rest_y2, after_z1)
    after_2 = chunk(0, panel_0, rest_2, rest_y2, cost=10**10)
    after_z2 = trade(after_2, 1)
    head_c, after_2 = after(head_c, after_2)

    tops = [("top", low, share) for low in range(0, size, eighth)]
    mine, others, panel_2 = run_level(
        2,
        meta,
        (inv,),
        [[tops[0], tops[2]], [tops[i] for i in (1, 3, 4, 5, 6, 7)]],
        top=(rows_of(head), rows_of(head_c)),
        keeps=True,
    )
    mine_w = trade(mine, 3)
    after_z1, mine = after(after_z1, mine)
    (next_1,) = run_level(
        1,
        meta,
        (inv, panel_1),
        [[(0, 0, eighth), (1, 0, quarter), (2, 0, quarter)]],
        pairs=[
            ([(near, eighth, eighth)], [(far, eighth, eighth)]),
            (rows_of(near_x), rows_of(far_x)),
            (rows_of(after_1), rows_of(after_z1)),
        ],
    )
    next_c1 = trade(next_1, 2)
    (last_1,) = run_level(
        2,
        meta,
        (inv, panel_2),
        [[(0, 0, share), (1, 0, next_1.shape[0])]],
        pairs=[
            ([(head, share, share)], [(head_c, share, share)]),
            (rows_of(next_1), rows_of(next_c1)),
        ],
    )
    last_w1 = trade(last_1, 3)
    mine_wy = trade(mine_w, 0)
    mine_wc = trade(mine_w, 2)
    after_z2, mine_w, last_1 = after(after_z2, mine_w, last_1)
    next_2 = chunk(1, panel_1, after_2, after_z2)
    last_2 = chunk(2, panel_2, next_2, trade(next_2, 2))
    last_w2 = trade(last_2, 3)
    mine_wy, last_2 = after(mine_wy, last_2)
    mine_wyc = trade(mine_wy, 2)

    last_w1, mine_wyc, last_2 = after(last_w1, mine_wyc, last_2)
    tops = [(mine, 0, share), (others, 0, share), (mine, share, share)]
    tops += [(others, share * i, share) for i in range(1, 6)]
    tops_w = [(x, low, share) for low in (0, share) for x in (mine_w, mine_wy)]
    tops_w += [(x, low, share) for low in (0, share) for x in (mine_wc, mine_wyc)]
    out, panel_3 = run_level(
        3,
        meta,
        (inv,),
        [[("top", 0, share), (0, 0, last_1.shape[0])]],
        top=(tops, tops_w),
        pairs=[(rows_of(last_1), rows_of(last_w1))],
        keeps=True,
        part=(all_rows, 0, None),
    )
    return chunk(3, panel_3, last_2, last_w2, part=(all_rows, all_rows // quarter - 1, out))


def solution(mesh):
    return jax.shard_map(
        on_device,
        mesh=mesh,
        in_specs=(P(("tx", "ty"), None), P(), P(), P(), P()),
        out_specs=P(("tx", "ty"), None),
        check_vma=False,
    )
```

time: 177 us -> 168 us (0.949)
  waiting for transfers between devices: 120 us -> 103 us
  starting transfers between devices: 17.9 us -> 20.6 us
  local copies, waits for them, and re-layouts: 4.19 us -> 6.82 us
  Pallas kernels: 34.2 us -> 36 us
    ppermute x16 -> x18, waiting for transfers between devices: 120 us -> 103 us  [trade(): lax.ppermute(block, axis, [(i, i ^ flip) for i in range(lax.axis_size(axi...]
    slice x3, local copies, waits for them, and re-layouts: 2.92 us -> 5.64 us  [the longest x1 2.48 us: on_device(): rest_1, rest_2 = (slab[half:half + quarter], slab[half + quarter:])]
    ppermute x16 -> x18, starting transfers between devices: 17.9 us -> 20.6 us  [trade(): lax.ppermute(block, axis, [(i, i ^ flip) for i in range(lax.axis_size(axi...]
    pallas_call x11 -> x13, Pallas kernels: 34.2 us -> 36 us  [the longest x12 35 us: run_level(): pl.pallas_call(kernel, grid=(1,) if part is not None else (), out_shape=s...]
  transfers between devices with their start and end apart: 16 -> 18, of which waited for: 10 -> 12; matrix products, arithmetic and copies ran while one was open for 1% -> 2% of each run, Pallas kernels for 10% -> 17%
where the time goes in v2:
time: 168 us; the launch traced here: 166 us
  waiting for transfers between devices  103 us (61%)
  Pallas kernels  36 us (21%)
  starting transfers between devices  20.6 us (12%)
  local copies, waits for them, and re-layouts  6.82 us (4%)
    ppermute x18, waiting for transfers between devices, trade(): lax.ppermute(block, axis, [(i, i ^ flip) for i in range(lax.axis_size(axi...  103 us
    pallas_call x12, Pallas kernels, run_level(): pl.pallas_call(kernel, grid=(1,) if part is not None else (), out_shape=s...  35 us
    ppermute x18, starting transfers between devices, trade(): lax.ppermute(block, axis, [(i, i ^ flip) for i in range(lax.axis_size(axi...  20.6 us
  transfers between devices with their start and end apart: 18, of which 12 were waited for; matrix products, arithmetic and copies ran while one was open for 2% of the time, Pallas kernels for 17%

profile of v2, /device:TPU:0, one launch (start us, length us, event | category | flops | bytes accessed | tf_op | source)
XLA Modules:
  0.0 166.2 jit_solution(6614790076094836994)
XLA Ops:
  0.0 1.9 %slice.87 = bf16[64,4096]{1,0:T(8,128)(2,1)} slice(bf16[256,4096]{1,0:T(8,128)(2,1)} %param.5), slice={[0:64], [0:4096]} | slice | bytes 1048576 | tf_op jit(solution)/shard_map/slice | solution.py:258
  1.9 1.3 slice.88.refs_1_
  3.2 3.0 %collective-permute-start.2 = (bf16[128,4096]{1,0:T(8,128)(2,1)S(1)}, bf16[128,4096]{1,0:T(8,128)(2,1)S(1)}, u32[]{:S(2)}, u32[]{:S(2)}) collective-permute-start(bf16[128,4096]{1,0:T(8,128)(2,1)S(1)} %slice.88.refs_1_), channel_id=1, source_target_pairs={{0,16},{8,24},{16,0},{24,8},{1,17},{9,25},{17,1},{25,9},{2,18},{10... | collective-permute-start | bytes 3145736 | tf_op jit(solution)/shard_map/ppermute | solution.py:28
  6.2 2.6 %collective-permute-start = (bf16[64,4096]{1,0:T(8,128)(2,1)}, bf16[64,4096]{1,0:T(8,128)(2,1)S(1)}, u32[]{:S(2)}, u32[]{:S(2)}) collective-permute-start(bf16[64,4096]{1,0:T(8,128)(2,1)} %slice.87), channel_id=1, source_target_pairs={{0,4},{1,5},{2,6},{3,7},{4,0},{5,1},{6,2},{7,3},{8,12},{9,13},{10,... | collective-permute-start | bytes 1572872 | tf_op jit(solution)/shard_map/ppermute | solution.py:28
  8.8 2.5 %fusion.8 = (bf16[64,4096]{1,0:T(8,128)(2,1)S(1)}, bf16[64,4096]{1,0:T(8,128)(2,1)}, bf16[64,4096]{1,0:T(8,128)(2,1)}) fusion(bf16[256,4096]{1,0:T(8,128)(2,1)} %param.5), kind=kLoop, calls=%fused_computation.24 | loop fusion | bytes 3145728 | tf_op jit(solution)/shard_map/slice | solution.py:265
  11.3 20.7 %collective-permute-done.refs_1_ = bf16[64,4096]{1,0:T(8,128)(2,1)S(1)} collective-permute-done((bf16[64,4096]{1,0:T(8,128)(2,1)}, bf16[64,4096]{1,0:T(8,128)(2,1)S(1)}, u32[]{:S(2)}, u32[]{:S(2)}) %collective-permute-start) | collective-permute-done | bytes 524320 | tf_op jit(solution)/shard_map/ppermute | solution.py:28
  32.4 1.6 collective-permute-start.3
  34.2 1.0 copy-done
  36.2 3.9 %level0_rows192.2 = (bf16[128,4096]{1,0:T(8,128)(2,1)S(1)}, bf16[64,4096]{1,0:T(8,128)(2,1)S(1)}, bf16[256,4096]{1,0:T(8,128)(2,1)S(1)}) custom-call(s32[640]{0:T(1024)S(1)} %concatenate.3.meta, bf16[4,256,256]{2,1,0:T(8,128)(2,1)S(1)} %reorder.1.refs_0_, bf16[128,4096]{1,0:T(8,128)(2,1)S(1)} %slice.88.refs_1_, ...), custom_call_target="tpu_custom_call" | custom-call | tf_op jit(solution)/shard_map/level0_rows192/pallas_call | solution.py:198
  40.1 16.0 %collective-permute-done.3.refs_3_ = bf16[64,4096]{1,0:T(8,128)(2,1)} collective-permute-done((bf16[64,4096]{1,0:T(8,128)(2,1)S(1)}, bf16[64,4096]{1,0:T(8,128)(2,1)}, u32[]{:S(2)}, u32[]{:S(2)}) %collective-permute-start.3) | collective-permute-done | bytes 524320 | tf_op jit(solution)/shard_map/ppermute | solution.py:28
  56.1 2.1 %level0_rows64.2.refs_6_ = bf16[64,4096]{1,0:T(8,128)(2,1)S(1)} custom-call(s32[640]{0:T(1024)S(1)} %concatenate.3.meta, bf16[4,256,256]{2,1,0:T(8,128)(2,1)S(1)} %reorder.1.refs_0_, bf16[256,4096]{1,0:T(8,128)(2,1)S(1)} %get-tuple-element.48.refs_1_, bf16[64,4096]{1,0:T(8,128)(2,1)S(1)} %get-tuple-element.49.refs_2_, ...), custom_call_target="tpu_custom_call" | custom-call | tf_op jit(solution)/shard_map/level0_rows64/pallas_call | solution.py:198
  58.8 2.6 %collective-permute-start.7 = (bf16[64,4096]{1,0:T(8,128)(2,1)S(1)}, bf16[64,4096]{1,0:T(8,128)(2,1)S(1)}, u32[]{:S(2)}, u32[]{:S(2)}) collective-permute-start(bf16[64,4096]{1,0:T(8,128)(2,1)S(1)} %level0_rows64.2.refs_6_), channel_id=1, source_target_pairs={{0,4},{1,5},{2,6},{3,7},{4,0},{5,1},{6,2},{7,3},{8,12},{9,13},{10,... | collective-permute-start | bytes 1572872 | tf_op jit(solution)/shard_map/ppermute | solution.py:28
  61.4 9.2 %collective-permute-done.5.refs_4_ = bf16[64,4096]{1,0:T(8,128)(2,1)S(1)} collective-permute-done((bf16[64,4096]{1,0:T(8,128)(2,1)}, bf16[64,4096]{1,0:T(8,128)(2,1)S(1)}, u32[]{:S(2)}, u32[]{:S(2)}) %collective-permute-start.5) | collective-permute-done | bytes 524320 | tf_op jit(solution)/shard_map/ppermute | solution.py:28
  71.1 4.5 %level0_rows192.3 = (bf16[128,4096]{1,0:T(8,128)(2,1)S(1)}, bf16[64,4096]{1,0:T(8,128)(2,1)S(1)}) custom-call(s32[640]{0:T(1024)S(1)} %concatenate.3.meta, bf16[4,256,256]{2,1,0:T(8,128)(2,1)S(1)} %reorder.1.refs_0_, bf16[64,4096]{1,0:T(8,128)(2,1)S(1)} %collective-permute-done.refs_1_, bf16[64,4096]{1,0:T(8,128)(2,1)} %collective-permute-done.1.refs_2_, ...), custom_call_target="tpu_custom_call" | custom-call | tf_op jit(solution)/shard_map/level0_rows192/pallas_call | solution.py:198
  75.6 3.8 %level1_rows128.1 = (bf16[128,4096]{1,0:T(8,128)(2,1)S(1)}, bf16[256,4096]{1,0:T(8,128)(2,1)S(1)}) custom-call(s32[640]{0:T(1024)S(1)} %concatenate.3.meta, bf16[4,256,256]{2,1,0:T(8,128)(2,1)S(1)} %reorder.1.refs_0_, bf16[128,4096]{1,0:T(8,128)(2,1)S(1)} %get-tuple-element.54.refs_1_.refs_2_, bf16[128,4096]{1,0:T(8,128)(2,1)S(1)} %get-tuple-element.58.refs_2_.refs_3_), custom_call_target="tpu_custom_call" | custom-call | tf_op jit(solution)/shard_map/level1_rows128/pallas_call | solution.py:198
  79.5 3.1 %collective-permute-done.7.refs_7_ = bf16[64,4096]{1,0:T(8,128)(2,1)S(1)} collective-permute-done((bf16[64,4096]{1,0:T(8,128)(2,1)S(1)}, bf16[64,4096]{1,0:T(8,128)(2,1)S(1)}, u32[]{:S(2)}, u32[]{:S(2)}) %collective-permute-start.7) | collective-permute-done | bytes 524320 | tf_op jit(solution)/shard_map/ppermute | solution.py:28
  82.5 1.6 level0_rows64.3.refs_2_
  84.2 3.8 %level2_rows128.1 = (bf16[32,4096]{1,0:T(8,128)(2,1)S(1)}, bf16[96,4096]{1,0:T(8,128)(2,1)S(1)}, bf16[256,4096]{1,0:T(8,128)(2,1)S(1)}) custom-call(s32[640]{0:T(1024)S(1)} %concatenate.3.meta, bf16[4,256,256]{2,1,0:T(8,128)(2,1)S(1)} %reorder.1.refs_0_, bf16[128,4096]{1,0:T(8,128)(2,1)S(1)} %get-tuple-element.59.refs_1_.refs_2_, ...), custom_call_target="tpu_custom_call" | custom-call | tf_op jit(solution)/shard_map/level2_rows128/pallas_call | solution.py:198
  87.9 2.1 %level1_rows160.1.refs_4_ = bf16[160,4096]{1,0:T(8,128)(2,1)S(1)} custom-call(s32[640]{0:T(1024)S(1)} %concatenate.3.meta, bf16[4,256,256]{2,1,0:T(8,128)(2,1)S(1)} %reorder.1.refs_0_, bf16[256,4096]{1,0:T(8,128)(2,1)S(1)} %get-tuple-element.66.refs_1_, bf16[128,4096]{1,0:T(8,128)(2,1)S(1)} %get-tuple-element.54.refs_1_.refs_2_, ...), custom_call_target="tpu_custom_call" | custom-call | tf_op jit(solution)/shard_map/level1_rows160/pallas_call | solution.py:198
  90.1 1.5 collective-permute-start.9
  91.6 1.5 collective-permute-done.11.refs_5_
  93.1 2.2 %level2_rows176.1.refs_7_ = bf16[176,4096]{1,0:T(8,128)(2,1)S(1)} custom-call(s32[640]{0:T(1024)S(1)} %concatenate.3.meta, bf16[4,256,256]{2,1,0:T(8,128)(2,1)S(1)} %reorder.1.refs_0_, bf16[256,4096]{1,0:T(8,128)(2,1)S(1)} %get-tuple-element.65.refs_1_, bf16[128,4096]{1,0:T(8,128)(2,1)S(1)} %get-tuple-element.59.refs_1_.refs_2_, ...), custom_call_target="tpu_custom_call" | custom-call | tf_op jit(solution)/shard_map/level2_rows176/pallas_call | solution.py:198
  95.3 5.3 %collective-permute-start.15 = (bf16[176,4096]{1,0:T(8,128)(2,1)S(1)}, bf16[176,4096]{1,0:T(8,128)(2,1)S(1)}, u32[]{:S(2)}, u32[]{:S(2)}) collective-permute-start(bf16[176,4096]{1,0:T(8,128)(2,1)S(1)} %level2_rows176.1.refs_7_), channel_id=1, source_target_pairs={{0,2},{1,3},{2,0},{3,1},{4,6},{5,7},{6,4},{7,5},{8,10},{9,11},{10,... | collective-permute-start | bytes 4325384 | tf_op jit(solution)/shard_map/ppermute | solution.py:28
  100.7 15.9 %collective-permute-done.9.refs_3_ = bf16[64,4096]{1,0:T(8,128)(2,1)S(1)} collective-permute-done((bf16[64,4096]{1,0:T(8,128)(2,1)S(1)}, bf16[64,4096]{1,0:T(8,128)(2,1)S(1)}, u32[]{:S(2)}, u32[]{:S(2)}) %collective-permute-start.9) | collective-permute-done | bytes 524320 | tf_op jit(solution)/shard_map/ppermute | solution.py:28
  116.7 28.0 %collective-permute-done.10.refs_3_ = bf16[32,4096]{1,0:T(8,128)(2,1)S(1)} collective-permute-done((bf16[32,4096]{1,0:T(8,128)(2,1)S(1)}, bf16[32,4096]{1,0:T(8,128)(2,1)S(1)}, u32[]{:S(2)}, u32[]{:S(2)}) %collective-permute-start.10) | collective-permute-done | bytes 262176 | tf_op jit(solution)/shard_map/ppermute | solution.py:28
  144.6 1.6 level1_rows64.1.refs_2_
  146.3 1.6 collective-permute-start.12
  148.2 1.6 level2_rows64.1.refs_2_
  149.9 5.1 %collective-permute-done.12.refs_4_ = bf16[32,4096]{1,0:T(8,128)(2,1)S(1)} collective-permute-done((bf16[32,4096]{1,0:T(8,128)(2,1)S(1)}, bf16[32,4096]{1,0:T(8,128)(2,1)S(1)}, u32[]{:S(2)}, u32[]{:S(2)}) %collective-permute-start.12) | collective-permute-done | bytes 262176 | tf_op jit(solution)/shard_map/ppermute | solution.py:28
  156.9 5.4 %level3_rows192.1 = (bf16[256,4096]{1,0:T(8,128)(2,1)}, bf16[256,4096]{1,0:T(8,128)(2,1)S(1)}) custom-call(s32[640]{0:T(1024)S(1)} %concatenate.3.meta, bf16[4,256,256]{2,1,0:T(8,128)(2,1)S(1)} %reorder.1.refs_0_, bf16[32,4096]{1,0:T(8,128)(2,1)S(1)} %get-tuple-element.63.refs_1_, bf16[96,4096]{1,0:T(8,128)(2,1)S(1)} %get-tuple-element.64.refs_2_, ...), custom_call_target="tpu_custom_call" | custom-call | tf_op jit(solution)/shard_map/level3_rows192/pallas_call | solution.py:198
  162.4 1.5 collective-permute-done.17.refs_3_
  163.8 2.4 %level3_rows64.1 = bf16[256,4096]{1,0:T(8,128)(2,1)} custom-call(s32[640]{0:T(1024)S(1)} %concatenate.3.meta, bf16[4,256,256]{2,1,0:T(8,128)(2,1)S(1)} %reorder.1.refs_0_, bf16[256,4096]{1,0:T(8,128)(2,1)S(1)} %get-tuple-element.78.refs_1_, bf16[64,4096]{1,0:T(8,128)(2,1)S(1)} %level2_rows64.1.refs_2_, ...), custom_call_target="tpu_custom_call", output_to_operand_aliasing={{}: (5, {})} | custom-call | tf_op jit(solution)/shard_map/level3_rows64/pallas_call | solution.py:198
  (38 shorter events, 5.2 us)
Async XLA Ops:
  3.2 30.8 %copy-start.2 = (s32[4,2,32]{2,1,0:T(2,128)S(1)}, s32[4,2,32]{2,1,0:T(2,128)}, u32[]{:S(2)}) copy-start(s32[4,2,32]{2,1,0:T(2,128)} %param.7) | copy-start | bytes 3076
  3.2 30.8 %copy-start.3 = (s32[4,32]{1,0:T(4,128)S(1)}, s32[4,32]{1,0:T(4,128)}, u32[]{:S(2)}) copy-start(s32[4,32]{1,0:T(4,128)} %param.9) | copy-start | bytes 1540
  3.2 30.8 %copy-start.4 = (s32[4,32]{1,0:T(4,128)S(1)}, s32[4,32]{1,0:T(4,128)}, u32[]{:S(2)}) copy-start(s32[4,32]{1,0:T(4,128)} %param.8) | copy-start | bytes 1540
  3.2 29.2 %collective-permute-start.2 = (bf16[128,4096]{1,0:T(8,128)(2,1)S(1)}, bf16[128,4096]{1,0:T(8,128)(2,1)S(1)}, u32[]{:S(2)}, u32[]{:S(2)}) collective-permute-start(bf16[128,4096]{1,0:T(8,128)(2,1)S(1)} %slice.88.refs_1_), channel_id=1, source_target_pairs={{0,16},{8,24},{16,0},{24,8},{1,17},{9,25},{17,1},{25,9},{2,18},{10... | collective-permute-start | bytes 3145736 | tf_op jit(solution)/shard_map/ppermute | solution.py:28
  6.2 25.7 %collective-permute-start = (bf16[64,4096]{1,0:T(8,128)(2,1)}, bf16[64,4096]{1,0:T(8,128)(2,1)S(1)}, u32[]{:S(2)}, u32[]{:S(2)}) collective-permute-start(bf16[64,4096]{1,0:T(8,128)(2,1)} %slice.87), channel_id=1, source_target_pairs={{0,4},{1,5},{2,6},{3,7},{4,0},{5,1},{6,2},{7,3},{8,12},{9,13},{10,... | collective-permute-start | bytes 1572872 | tf_op jit(solution)/shard_map/ppermute | solution.py:28
  32.0 26.3 %collective-permute-start.1 = (bf16[64,4096]{1,0:T(8,128)(2,1)}, bf16[64,4096]{1,0:T(8,128)(2,1)}, u32[]{:S(2)}, u32[]{:S(2)}) collective-permute-start(bf16[64,4096]{1,0:T(8,128)(2,1)} %get-tuple-element.45), channel_id=1, source_target_pairs={{0,4},{1,5},{2,6},{3,7},{4,0},{5,1},{6,2},{7,3},{8,12},{9,13},{10,... | collective-permute-start | bytes 1572872 | tf_op jit(solution)/shard_map/ppermute | solution.py:28
  32.0 26.3 %collective-permute-start.4 = (bf16[64,4096]{1,0:T(8,128)(2,1)S(1)}, bf16[64,4096]{1,0:T(8,128)(2,1)}, u32[]{:S(2)}, u32[]{:S(2)}) collective-permute-start(bf16[64,4096]{1,0:T(8,128)(2,1)S(1)} %collective-permute-done.refs_1_), channel_id=1, source_target_pairs={{0,16},{8,24},{16,0},{24,8},{1,17},{9,25},{17,1},{25,9},{2,18},{10... | collective-permute-start | bytes 1572872 | tf_op jit(solution)/shard_map/ppermute | solution.py:28
  32.4 23.7 %collective-permute-start.3 = (bf16[64,4096]{1,0:T(8,128)(2,1)S(1)}, bf16[64,4096]{1,0:T(8,128)(2,1)}, u32[]{:S(2)}, u32[]{:S(2)}) collective-permute-start(bf16[64,4096]{1,0:T(8,128)(2,1)S(1)} %get-tuple-element.49.refs_2_), channel_id=1, source_target_pairs={{0,16},{8,24},{16,0},{24,8},{1,17},{9,25},{17,1},{25,9},{2,18},{10... | collective-permute-start | bytes 1572872 | tf_op jit(solution)/shard_map/ppermute | solution.py:28
  34.2 1.0 copy-start
  56.1 14.5 %copy-start.1 = (bf16[64,4096]{1,0:T(8,128)(2,1)S(1)}, bf16[64,4096]{1,0:T(8,128)(2,1)}, u32[]{:S(2)}) copy-start(bf16[64,4096]{1,0:T(8,128)(2,1)} %get-tuple-element.51.refs_2_) | copy-start | bytes 1572868
  58.3 12.4 %collective-permute-start.5 = (bf16[64,4096]{1,0:T(8,128)(2,1)}, bf16[64,4096]{1,0:T(8,128)(2,1)S(1)}, u32[]{:S(2)}, u32[]{:S(2)}) collective-permute-start(bf16[64,4096]{1,0:T(8,128)(2,1)} %collective-permute-done.1.refs_2_), channel_id=1, source_target_pairs={{0,16},{8,24},{16,0},{24,8},{1,17},{9,25},{17,1},{25,9},{2,18},{10... | collective-permute-start | bytes 1572872 | tf_op jit(solution)/shard_map/ppermute | solution.py:28
  58.8 23.7 %collective-permute-start.7 = (bf16[64,4096]{1,0:T(8,128)(2,1)S(1)}, bf16[64,4096]{1,0:T(8,128)(2,1)S(1)}, u32[]{:S(2)}, u32[]{:S(2)}) collective-permute-start(bf16[64,4096]{1,0:T(8,128)(2,1)S(1)} %level0_rows64.2.refs_6_), channel_id=1, source_target_pairs={{0,4},{1,5},{2,6},{3,7},{4,0},{5,1},{6,2},{7,3},{8,12},{9,13},{10,... | collective-permute-start | bytes 1572872 | tf_op jit(solution)/shard_map/ppermute | solution.py:28
  70.6 11.9 %collective-permute-start.6 = (bf16[64,4096]{1,0:T(8,128)(2,1)S(1)}, bf16[64,4096]{1,0:T(8,128)(2,1)S(1)}, u32[]{:S(2)}, u32[]{:S(2)}) collective-permute-start(bf16[64,4096]{1,0:T(8,128)(2,1)S(1)} %copy-done.1), channel_id=1, source_target_pairs={{0,16},{8,24},{16,0},{24,8},{1,17},{9,25},{17,1},{25,9},{2,18},{10... | collective-permute-start | bytes 1572872 | tf_op jit(solution)/shard_map/ppermute | solution.py:28
  79.4 4.8 %collective-permute-start.8 = (bf16[128,4096]{1,0:T(8,128)(2,1)S(1)}, bf16[128,4096]{1,0:T(8,128)(2,1)S(1)}, u32[]{:S(2)}, u32[]{:S(2)}) collective-permute-start(bf16[128,4096]{1,0:T(8,128)(2,1)S(1)} %get-tuple-element.59.refs_1_.refs_2_), channel_id=1, source_target_pairs={{0,8},{8,0},{16,24},{24,16},{1,9},{9,1},{17,25},{25,17},{2,10},{10... | collective-permute-start | bytes 3145736 | tf_op jit(solution)/shard_map/ppermute | solution.py:28
  90.0 3.1 %collective-permute-start.11 = (bf16[160,4096]{1,0:T(8,128)(2,1)S(1)}, bf16[160,4096]{1,0:T(8,128)(2,1)S(1)}, u32[]{:S(2)}, u32[]{:S(2)}) collective-permute-start(bf16[160,4096]{1,0:T(8,128)(2,1)S(1)} %level1_rows160.1.refs_4_), channel_id=1, source_target_pairs={{0,8},{8,0},{16,24},{24,16},{1,9},{9,1},{17,25},{25,17},{2,10},{10... | collective-permute-start | bytes 3932168 | tf_op jit(solution)/shard_map/ppermute | solution.py:28
  90.1 26.6 %collective-permute-start.9 = (bf16[64,4096]{1,0:T(8,128)(2,1)S(1)}, bf16[64,4096]{1,0:T(8,128)(2,1)S(1)}, u32[]{:S(2)}, u32[]{:S(2)}) collective-permute-start(bf16[64,4096]{1,0:T(8,128)(2,1)S(1)} %level0_rows64.3.refs_2_), channel_id=1, source_target_pairs={{0,4},{1,5},{2,6},{3,7},{4,0},{5,1},{6,2},{7,3},{8,12},{9,13},{10,... | collective-permute-start | bytes 1572872 | tf_op jit(solution)/shard_map/ppermute | solution.py:28
  95.3 61.2 %collective-permute-start.15 = (bf16[176,4096]{1,0:T(8,128)(2,1)S(1)}, bf16[176,4096]{1,0:T(8,128)(2,1)S(1)}, u32[]{:S(2)}, u32[]{:S(2)}) collective-permute-start(bf16[176,4096]{1,0:T(8,128)(2,1)S(1)} %level2_rows176.1.refs_7_), channel_id=1, source_target_pairs={{0,2},{1,3},{2,0},{3,1},{4,6},{5,7},{6,4},{7,5},{8,10},{9,11},{10,... | collective-permute-start | bytes 4325384 | tf_op jit(solution)/shard_map/ppermute | solution.py:28
  100.7 43.9 %collective-permute-start.10 = (bf16[32,4096]{1,0:T(8,128)(2,1)S(1)}, bf16[32,4096]{1,0:T(8,128)(2,1)S(1)}, u32[]{:S(2)}, u32[]{:S(2)}) collective-permute-start(bf16[32,4096]{1,0:T(8,128)(2,1)S(1)} %get-tuple-element.63.refs_1_), channel_id=1, source_target_pairs={{0,2},{1,3},{2,0},{3,1},{4,6},{5,7},{6,4},{7,5},{8,10},{9,11},{10,... | collective-permute-start | bytes 786440 | tf_op jit(solution)/shard_map/ppermute | solution.py:28
  146.2 2.0 %collective-permute-start.13 = (bf16[64,4096]{1,0:T(8,128)(2,1)S(1)}, bf16[64,4096]{1,0:T(8,128)(2,1)S(1)}, u32[]{:S(2)}, u32[]{:S(2)}) collective-permute-start(bf16[64,4096]{1,0:T(8,128)(2,1)S(1)} %level1_rows64.1.refs_2_), channel_id=1, source_target_pairs={{0,8},{8,0},{16,24},{24,16},{1,9},{9,1},{17,25},{25,17},{2,10},{10... | collective-permute-start | bytes 1572872 | tf_op jit(solution)/shard_map/ppermute | solution.py:28
  146.3 8.7 %collective-permute-start.12 = (bf16[32,4096]{1,0:T(8,128)(2,1)S(1)}, bf16[32,4096]{1,0:T(8,128)(2,1)S(1)}, u32[]{:S(2)}, u32[]{:S(2)}) collective-permute-start(bf16[32,4096]{1,0:T(8,128)(2,1)S(1)} %collective-permute-done.10.refs_3_), channel_id=1, source_target_pairs={{0,16},{8,24},{16,0},{24,8},{1,17},{9,25},{17,1},{25,9},{2,18},{10... | collective-permute-start | bytes 786440 | tf_op jit(solution)/shard_map/ppermute | solution.py:28
  149.8 14.0 %collective-permute-start.17 = (bf16[64,4096]{1,0:T(8,128)(2,1)S(1)}, bf16[64,4096]{1,0:T(8,128)(2,1)S(1)}, u32[]{:S(2)}, u32[]{:S(2)}) collective-permute-start(bf16[64,4096]{1,0:T(8,128)(2,1)S(1)} %level2_rows64.1.refs_2_), channel_id=1, source_target_pairs={{0,2},{1,3},{2,0},{3,1},{4,6},{5,7},{6,4},{7,5},{8,10},{9,11},{10,... | collective-permute-start | bytes 1572872 | tf_op jit(solution)/shard_map/ppermute | solution.py:28
  155.0 1.5 collective-permute-start.16
  155.0 1.9 %collective-permute-start.14 = (bf16[32,4096]{1,0:T(8,128)(2,1)S(1)}, bf16[32,4096]{1,0:T(8,128)(2,1)S(1)}, u32[]{:S(2)}, u32[]{:S(2)}) collective-permute-start(bf16[32,4096]{1,0:T(8,128)(2,1)S(1)} %collective-permute-done.10.refs_3_), channel_id=1, source_target_pairs={{0,8},{8,0},{16,24},{24,16},{1,9},{9,1},{17,25},{25,17},{2,10},{10... | collective-permute-start | bytes 786440 | tf_op jit(solution)/shard_map/ppermute | solution.py:28

commit v3 on v2

--- a/solution.py
+++ b/solution.py
@@ -290,68 +290,74 @@
     )
 
     tops = [("top", low, eighth) for low in range(0, size, quarter)]
-    head, panel_1 = run_level(1, meta, (inv,), [tops], top=(rows_of(near), rows_of(far)), keeps=True)
+    head, panel_1 = run_level(
+        1,
+        meta,
+        (inv,),
+        [tops + [("top", eighth, eighth), (0, 0, quarter)]],
+        top=(rows_of(near), rows_of(far)),
+        pairs=[(rows_of(near_x), rows_of(far_x))],
+        keeps=True,
+    )
     head_c = trade(head, 2)
     rest_y2, after_z1 = after(rest_y2, after_z1)
-    after_2 = chunk(0, panel_0, rest_2, rest_y2, cost=10**10)
+    after_2 = chunk(0, panel_0, rest_2, rest_y2, cost=3 * 10**10)
     after_z2 = trade(after_2, 1)
     head_c, after_2 = after(head_c, after_2)
 
+    more = head.shape[0] - half
     tops = [("top", low, share) for low in range(0, size, eighth)]
-    mine, others, panel_2 = run_level(
+    lead, others, panel_2 = run_level(
         2,
         meta,
         (inv,),
-        [[tops[0], tops[2]], [tops[i] for i in (1, 3, 4, 5, 6, 7)]],
-        top=(rows_of(head), rows_of(head_c)),
+        [
+            [tops[0], tops[2], ("top", share, share), (0, 0, more)],
+            [tops[i] for i in (1, 3, 4, 5, 6, 7)],
+        ],
+        top=([(head, 0, half)], [(head_c, 0, half)]),
+        pairs=[([(head, half, more)], [(head_c, half, more)])],
         keeps=True,
     )
-    mine_w = trade(mine, 3)
-    after_z1, mine = after(after_z1, mine)
-    (next_1,) = run_level(
+    lead_w = trade(lead, 3)
+    after_z1, lead = after(after_z1, lead)
+    next_1a, next_1b = run_level(
         1,
         meta,
         (inv, panel_1),
-        [[(0, 0, eighth), (1, 0, quarter), (2, 0, quarter)]],
-        pairs=[
-            ([(near, eighth, eighth)], [(far, eighth, eighth)]),
-            (rows_of(near_x), rows_of(far_x)),
-            (rows_of(after_1), rows_of(after_z1)),
-        ],
-    )
-    next_c1 = trade(next_1, 2)
+        [[(0, 0, eighth)], [(0, eighth, eighth)]],
+        pairs=[(rows_of(after_1), rows_of(after_z1))],
+    )
     (last_1,) = run_level(
         2,
         meta,
         (inv, panel_2),
-        [[(0, 0, share), (1, 0, next_1.shape[0])]],
-        pairs=[
-            ([(head, share, share)], [(head_c, share, share)]),
-            (rows_of(next_1), rows_of(next_c1)),
-        ],
+        [[(0, 0, eighth), (1, 0, eighth)]],
+        pairs=[(rows_of(x), rows_of(trade(x, 2))) for x in (next_1a, next_1b)],
     )
     last_w1 = trade(last_1, 3)
-    mine_wy = trade(mine_w, 0)
-    mine_wc = trade(mine_w, 2)
-    after_z2, mine_w, last_1 = after(after_z2, mine_w, last_1)
-    next_2 = chunk(1, panel_1, after_2, after_z2)
+    after_z2, last_1 = after(after_z2, last_1)
+    next_2 = chunk(1, panel_1, after_2, after_z2, cost=25 * 10**8)
     last_2 = chunk(2, panel_2, next_2, trade(next_2, 2))
     last_w2 = trade(last_2, 3)
-    mine_wy, last_2 = after(mine_wy, last_2)
-    mine_wyc = trade(mine_wy, 2)
-
-    last_w1, mine_wyc, last_2 = after(last_w1, mine_wyc, last_2)
-    tops = [(mine, 0, share), (others, 0, share), (mine, share, share)]
+    lead_w, last_2 = after(lead_w, last_2)
+    tops_w = lead_w[:eighth]
+    tops_wc = trade(tops_w, 2)
+    tops_wy = trade(tops_w, 0)
+    tops_wyc = trade(tops_wy, 2)
+
+    more = lead.shape[0] - eighth
+    tops = [(lead, 0, share), (others, 0, share), (lead, share, share)]
     tops += [(others, share * i, share) for i in range(1, 6)]
-    tops_w = [(x, low, share) for low in (0, share) for x in (mine_w, mine_wy)]
-    tops_w += [(x, low, share) for low in (0, share) for x in (mine_wc, mine_wyc)]
+    tops_other = [(x, low, share) for low in (0, share) for x in (tops_w, tops_wy)]
+    tops_other += [(x, low, share) for low in (0, share) for x in (tops_wc, tops_wyc)]
     out, panel_3 = run_level(
         3,
         meta,
         (inv,),
-        [[("top", 0, share), (0, 0, last_1.shape[0])]],
-        top=(tops, tops_w),
-        pairs=[(rows_of(last_1), rows_of(last_w1))],
+        [[("top", 0, share), (0, 0, more), (1, 0, quarter)]],
+        top=(tops, tops_other),
+        pairs=[([(lead, eighth, more)], [(lead_w, eighth, more)]), (rows_of(last_1), rows_of(last_w1))],
         keeps=True,
         part=(all_rows, 0, None),
     )

time: 168 us -> 153 us (0.911)
  waiting for transfers between devices: 103 us -> 88.4 us
    ppermute x18 -> x19, waiting for transfers between devices: 103 us -> 88.4 us  [trade(): lax.ppermute(block, axis, [(i, i ^ flip) for i in range(lax.axis_size(axi...]
    ppermute x18 -> x19, starting transfers between devices: 20.6 us -> 19.6 us  [trade(): lax.ppermute(block, axis, [(i, i ^ flip) for i in range(lax.axis_size(axi...]
  transfers between devices with their start and end apart: 18 -> 19, of which waited for: 12 -> 12; matrix products, arithmetic and copies ran while one was open for 2% -> 2% of each run, Pallas kernels for 17% -> 22%
where the time goes in v3:
time: 153 us; the launch traced here: 151 us
  waiting for transfers between devices  88.4 us (58%)
  Pallas kernels  35.9 us (23%)
  starting transfers between devices  19.6 us (13%)
  local copies, waits for them, and re-layouts  6.83 us (4%)
    ppermute x19, waiting for transfers between devices, trade(): lax.ppermute(block, axis, [(i, i ^ flip) for i in range(lax.axis_size(axi...  88.4 us
    pallas_call x12, Pallas kernels, run_level(): pl.pallas_call(kernel, grid=(1,) if part is not None else (), out_shape=s...  34.9 us
    ppermute x19, starting transfers between devices, trade(): lax.ppermute(block, axis, [(i, i ^ flip) for i in range(lax.axis_size(axi...  19.6 us
  transfers between devices with their start and end apart: 19, of which 12 were waited for; matrix products, arithmetic and copies ran while one was open for 2% of the time, Pallas kernels for 22%

profile of v3, /device:TPU:0, one launch (start us, length us, event | category | flops | bytes accessed | tf_op | source)
XLA Modules:
  0.0 150.9 jit_solution(7581983606514365459)
XLA Ops:
  0.0 1.9 %slice.90 = bf16[64,4096]{1,0:T(8,128)(2,1)} slice(bf16[256,4096]{1,0:T(8,128)(2,1)} %param.5), slice={[0:64], [0:4096]} | slice | bytes 1048576 | tf_op jit(solution)/shard_map/slice | solution.py:258
  1.9 1.3 slice.91.refs_1_
  3.2 3.0 %collective-permute-start.2 = (bf16[128,4096]{1,0:T(8,128)(2,1)S(1)}, bf16[128,4096]{1,0:T(8,128)(2,1)S(1)}, u32[]{:S(2)}, u32[]{:S(2)}) collective-permute-start(bf16[128,4096]{1,0:T(8,128)(2,1)S(1)} %slice.91.refs_1_), channel_id=1, source_target_pairs={{0,16},{8,24},{16,0},{24,8},{1,17},{9,25},{17,1},{25,9},{2,18},{10... | collective-permute-start | bytes 3145736 | tf_op jit(solution)/shard_map/ppermute | solution.py:28
  6.2 2.6 %collective-permute-start = (bf16[64,4096]{1,0:T(8,128)(2,1)}, bf16[64,4096]{1,0:T(8,128)(2,1)S(1)}, u32[]{:S(2)}, u32[]{:S(2)}) collective-permute-start(bf16[64,4096]{1,0:T(8,128)(2,1)} %slice.90), channel_id=1, source_target_pairs={{0,4},{1,5},{2,6},{3,7},{4,0},{5,1},{6,2},{7,3},{8,12},{9,13},{10,... | collective-permute-start | bytes 1572872 | tf_op jit(solution)/shard_map/ppermute | solution.py:28
  8.8 2.5 %fusion.8 = (bf16[64,4096]{1,0:T(8,128)(2,1)S(1)}, bf16[64,4096]{1,0:T(8,128)(2,1)}, bf16[64,4096]{1,0:T(8,128)(2,1)}) fusion(bf16[256,4096]{1,0:T(8,128)(2,1)} %param.5), kind=kLoop, calls=%fused_computation.24 | loop fusion | bytes 3145728 | tf_op jit(solution)/shard_map/slice | solution.py:265
  11.3 20.7 %collective-permute-done.refs_1_ = bf16[64,4096]{1,0:T(8,128)(2,1)S(1)} collective-permute-done((bf16[64,4096]{1,0:T(8,128)(2,1)}, bf16[64,4096]{1,0:T(8,128)(2,1)S(1)}, u32[]{:S(2)}, u32[]{:S(2)}) %collective-permute-start) | collective-permute-done | bytes 524320 | tf_op jit(solution)/shard_map/ppermute | solution.py:28
  32.4 1.6 %collective-permute-start.3 = (bf16[64,4096]{1,0:T(8,128)(2,1)S(1)}, bf16[64,4096]{1,0:T(8,128)(2,1)}, u32[]{:S(2)}, u32[]{:S(2)}) collective-permute-start(bf16[64,4096]{1,0:T(8,128)(2,1)S(1)} %get-tuple-element.47.refs_2_), channel_id=1, source_target_pairs={{0,16},{8,24},{16,0},{24,8},{1,17},{9,25},{17,1},{25,9},{2,18},{10... | collective-permute-start | bytes 1572872 | tf_op jit(solution)/shard_map/ppermute | solution.py:28
  34.2 1.0 copy-done
  36.2 3.9 %level0_rows192.2 = (bf16[128,4096]{1,0:T(8,128)(2,1)S(1)}, bf16[64,4096]{1,0:T(8,128)(2,1)S(1)}, bf16[256,4096]{1,0:T(8,128)(2,1)S(1)}) custom-call(s32[640]{0:T(1024)S(1)} %concatenate.3.meta, bf16[4,256,256]{2,1,0:T(8,128)(2,1)S(1)} %reorder.1.refs_0_, bf16[128,4096]{1,0:T(8,128)(2,1)S(1)} %slice.91.refs_1_, ...), custom_call_target="tpu_custom_call" | custom-call | tf_op jit(solution)/shard_map/level0_rows192/pallas_call | solution.py:198
  40.1 16.0 %collective-permute-done.3.refs_3_ = bf16[64,4096]{1,0:T(8,128)(2,1)} collective-permute-done((bf16[64,4096]{1,0:T(8,128)(2,1)S(1)}, bf16[64,4096]{1,0:T(8,128)(2,1)}, u32[]{:S(2)}, u32[]{:S(2)}) %collective-permute-start.3) | collective-permute-done | bytes 524320 | tf_op jit(solution)/shard_map/ppermute | solution.py:28
  56.1 2.1 %level0_rows64.2.refs_2_ = bf16[64,4096]{1,0:T(8,128)(2,1)S(1)} custom-call(s32[640]{0:T(1024)S(1)} %concatenate.3.meta, bf16[4,256,256]{2,1,0:T(8,128)(2,1)S(1)} %reorder.1.refs_0_, bf16[256,4096]{1,0:T(8,128)(2,1)S(1)} %get-tuple-element.46.refs_1_, bf16[64,4096]{1,0:T(8,128)(2,1)S(1)} %get-tuple-element.47.refs_2_, ...), custom_call_target="tpu_custom_call" | custom-call | tf_op jit(solution)/shard_map/level0_rows64/pallas_call | solution.py:198
  58.8 2.6 %collective-permute-start.7 = (bf16[64,4096]{1,0:T(8,128)(2,1)S(1)}, bf16[64,4096]{1,0:T(8,128)(2,1)S(1)}, u32[]{:S(2)}, u32[]{:S(2)}) collective-permute-start(bf16[64,4096]{1,0:T(8,128)(2,1)S(1)} %level0_rows64.2.refs_2_), channel_id=1, source_target_pairs={{0,4},{1,5},{2,6},{3,7},{4,0},{5,1},{6,2},{7,3},{8,12},{9,13},{10,... | collective-permute-start | bytes 1572872 | tf_op jit(solution)/shard_map/ppermute | solution.py:28
  61.4 9.2 %collective-permute-done.5.refs_4_ = bf16[64,4096]{1,0:T(8,128)(2,1)S(1)} collective-permute-done((bf16[64,4096]{1,0:T(8,128)(2,1)}, bf16[64,4096]{1,0:T(8,128)(2,1)S(1)}, u32[]{:S(2)}, u32[]{:S(2)}) %collective-permute-start.5) | collective-permute-done | bytes 524320 | tf_op jit(solution)/shard_map/ppermute | solution.py:28
  71.1 4.5 %level0_rows192.3 = (bf16[128,4096]{1,0:T(8,128)(2,1)S(1)}, bf16[64,4096]{1,0:T(8,128)(2,1)S(1)}) custom-call(s32[640]{0:T(1024)S(1)} %concatenate.3.meta, bf16[4,256,256]{2,1,0:T(8,128)(2,1)S(1)} %reorder.1.refs_0_, bf16[64,4096]{1,0:T(8,128)(2,1)S(1)} %collective-permute-done.refs_1_, bf16[64,4096]{1,0:T(8,128)(2,1)} %collective-permute-done.1.refs_2_, ...), custom_call_target="tpu_custom_call" | custom-call | tf_op jit(solution)/shard_map/level0_rows192/pallas_call | solution.py:198
  75.6 4.3 %level1_rows224.1 = (bf16[224,4096]{1,0:T(8,128)(2,1)S(1)}, bf16[256,4096]{1,0:T(8,128)(2,1)S(1)}) custom-call(s32[640]{0:T(1024)S(1)} %concatenate.3.meta, bf16[4,256,256]{2,1,0:T(8,128)(2,1)S(1)} %reorder.1.refs_0_, bf16[128,4096]{1,0:T(8,128)(2,1)S(1)} %get-tuple-element.52.refs_1_, bf16[128,4096]{1,0:T(8,128)(2,1)S(1)} %get-tuple-element.56.refs_2_, ...), custom_call_target="tpu_custom_call" | custom-call | tf_op jit(solution)/shard_map/level1_rows224/pallas_call | solution.py:198
  80.0 2.6 %collective-permute-done.7.refs_3_ = bf16[64,4096]{1,0:T(8,128)(2,1)S(1)} collective-permute-done((bf16[64,4096]{1,0:T(8,128)(2,1)S(1)}, bf16[64,4096]{1,0:T(8,128)(2,1)S(1)}, u32[]{:S(2)}, u32[]{:S(2)}) %collective-permute-start.7) | collective-permute-done | bytes 524320 | tf_op jit(solution)/shard_map/ppermute | solution.py:28
  82.5 1.6 %level0_rows64.3.refs_2_ = bf16[64,4096]{1,0:T(8,128)(2,1)S(1)} custom-call(s32[640]{0:T(1024)S(1)} %concatenate.3.meta, bf16[4,256,256]{2,1,0:T(8,128)(2,1)S(1)} %reorder.1.refs_0_, bf16[256,4096]{1,0:T(8,128)(2,1)S(1)} %get-tuple-element.46.refs_1_, bf16[64,4096]{1,0:T(8,128)(2,1)S(1)} %copy-done.1, bf16[64,4096]{1,0:T(8,128)(2,1)S(1)} %collective-permute-done.6.refs_3_), custom_call_target="tpu_custom_call" | custom-call | flops 30000001024 | tf_op jit(solution)/shard_map/level0_rows64/pallas_call | solution.py:198
  84.2 1.5 collective-permute-start.10
  85.7 4.3 %level2_rows240.1 = (bf16[144,4096]{1,0:T(8,128)(2,1)S(1)}, bf16[96,4096]{1,0:T(8,128)(2,1)S(1)}, bf16[256,4096]{1,0:T(8,128)(2,1)S(1)}) custom-call(s32[640]{0:T(1024)S(1)} %concatenate.3.meta, bf16[4,256,256]{2,1,0:T(8,128)(2,1)S(1)} %reorder.1.refs_0_, bf16[224,4096]{1,0:T(8,128)(2,1)S(1)} %get-tuple-element.59.refs_1_, ...), custom_call_target="tpu_custom_call" | custom-call | tf_op jit(solution)/shard_map/level2_rows240/pallas_call | solution.py:198
  90.0 4.8 %collective-permute-start.9 = (bf16[144,4096]{1,0:T(8,128)(2,1)S(1)}, bf16[144,4096]{1,0:T(8,128)(2,1)S(1)}, u32[]{:S(2)}, u32[]{:S(2)}) collective-permute-start(bf16[144,4096]{1,0:T(8,128)(2,1)S(1)} %get-tuple-element.63.refs_1_), channel_id=1, source_target_pairs={{0,2},{1,3},{2,0},{3,1},{4,6},{5,7},{6,4},{7,5},{8,10},{9,11},{10,... | collective-permute-start | bytes 3538952 | tf_op jit(solution)/shard_map/ppermute | solution.py:28
  94.8 1.6 %level1_rows64.2 = (bf16[32,4096]{1,0:T(8,128)(2,1)S(1)}, bf16[32,4096]{1,0:T(8,128)(2,1)S(1)}) custom-call(s32[640]{0:T(1024)S(1)} %concatenate.3.meta, bf16[4,256,256]{2,1,0:T(8,128)(2,1)S(1)} %reorder.1.refs_0_, bf16[256,4096]{1,0:T(8,128)(2,1)S(1)} %get-tuple-element.66.refs_1_, bf16[64,4096]{1,0:T(8,128)(2,1)S(1)} %level0_rows64.2.refs_2_, ...), custom_call_target="tpu_custom_call" | custom-call | tf_op jit(solution)/shard_map/level1_rows64/pallas_call | solution.py:198
  98.4 1.6 %level2_rows64.2.refs_8_ = bf16[64,4096]{1,0:T(8,128)(2,1)S(1)} custom-call(s32[640]{0:T(1024)S(1)} %concatenate.3.meta, bf16[4,256,256]{2,1,0:T(8,128)(2,1)S(1)} %reorder.1.refs_0_, bf16[256,4096]{1,0:T(8,128)(2,1)S(1)} %get-tuple-element.65.refs_1_, bf16[32,4096]{1,0:T(8,128)(2,1)S(1)} %get-tuple-element.69.refs_2_, ...), custom_call_target="tpu_custom_call" | custom-call | tf_op jit(solution)/shard_map/level2_rows64/pallas_call | solution.py:198
  100.0 8.2 %collective-permute-done.10.refs_3_ = bf16[64,4096]{1,0:T(8,128)(2,1)S(1)} collective-permute-done((bf16[64,4096]{1,0:T(8,128)(2,1)S(1)}, bf16[64,4096]{1,0:T(8,128)(2,1)S(1)}, u32[]{:S(2)}, u32[]{:S(2)}) %collective-permute-start.10) | collective-permute-done | bytes 524320 | tf_op jit(solution)/shard_map/ppermute | solution.py:28
  108.2 1.6 %level1_rows64.3.refs_2_ = bf16[64,4096]{1,0:T(8,128)(2,1)S(1)} custom-call(s32[640]{0:T(1024)S(1)} %concatenate.3.meta, bf16[4,256,256]{2,1,0:T(8,128)(2,1)S(1)} %reorder.1.refs_0_, bf16[256,4096]{1,0:T(8,128)(2,1)S(1)} %get-tuple-element.66.refs_1_, bf16[64,4096]{1,0:T(8,128)(2,1)S(1)} %level0_rows64.3.refs_2_, ...), custom_call_target="tpu_custom_call" | custom-call | flops 2500000000 | tf_op jit(solution)/shard_map/level1_rows64/pallas_call | solution.py:198
  110.6 1.2 collective-permute-done.13.refs_3_
  111.8 1.6 %level2_rows64.3.refs_2_ = bf16[64,4096]{1,0:T(8,128)(2,1)S(1)} custom-call(s32[640]{0:T(1024)S(1)} %concatenate.3.meta, bf16[4,256,256]{2,1,0:T(8,128)(2,1)S(1)} %reorder.1.refs_0_, bf16[256,4096]{1,0:T(8,128)(2,1)S(1)} %get-tuple-element.65.refs_1_, bf16[64,4096]{1,0:T(8,128)(2,1)S(1)} %level1_rows64.3.refs_2_, ...), custom_call_target="tpu_custom_call" | custom-call | tf_op jit(solution)/shard_map/level2_rows64/pallas_call | solution.py:198
  113.4 14.5 %collective-permute-done.9.refs_7_ = bf16[144,4096]{1,0:T(8,128)(2,1)S(1)} collective-permute-done((bf16[144,4096]{1,0:T(8,128)(2,1)S(1)}, bf16[144,4096]{1,0:T(8,128)(2,1)S(1)}, u32[]{:S(2)}, u32[]{:S(2)}) %collective-permute-start.9) | collective-permute-done | bytes 1179680 | tf_op jit(solution)/shard_map/ppermute | solution.py:28
  128.5 5.9 %collective-permute-done.14.refs_4_ = bf16[32,4096]{1,0:T(8,128)(2,1)S(1)} collective-permute-done((bf16[32,4096]{1,0:T(8,128)(2,1)S(1)}, bf16[32,4096]{1,0:T(8,128)(2,1)S(1)}, u32[]{:S(2)}, u32[]{:S(2)}) %collective-permute-start.14) | collective-permute-done | bytes 262176 | tf_op jit(solution)/shard_map/ppermute | solution.py:28
  134.4 4.8 %collective-permute-done.17.refs_9_ = bf16[64,4096]{1,0:T(8,128)(2,1)S(1)} collective-permute-done((bf16[64,4096]{1,0:T(8,128)(2,1)S(1)}, bf16[64,4096]{1,0:T(8,128)(2,1)S(1)}, u32[]{:S(2)}, u32[]{:S(2)}) %collective-permute-start.17) | collective-permute-done | bytes 524320 | tf_op jit(solution)/shard_map/ppermute | solution.py:28
  139.2 5.4 %level3_rows192.1 = (bf16[256,4096]{1,0:T(8,128)(2,1)}, bf16[256,4096]{1,0:T(8,128)(2,1)S(1)}) custom-call(s32[640]{0:T(1024)S(1)} %concatenate.3.meta, bf16[4,256,256]{2,1,0:T(8,128)(2,1)S(1)} %reorder.1.refs_0_, bf16[144,4096]{1,0:T(8,128)(2,1)S(1)} %get-tuple-element.63.refs_1_, bf16[96,4096]{1,0:T(8,128)(2,1)S(1)} %get-tuple-element.64.refs_2_, ...), custom_call_target="tpu_custom_call" | custom-call | tf_op jit(solution)/shard_map/level3_rows192/pallas_call | solution.py:198
  144.5 4.0 %collective-permute-done.18.refs_3_ = bf16[64,4096]{1,0:T(8,128)(2,1)S(1)} collective-permute-done((bf16[64,4096]{1,0:T(8,128)(2,1)S(1)}, bf16[64,4096]{1,0:T(8,128)(2,1)S(1)}, u32[]{:S(2)}, u32[]{:S(2)}) %collective-permute-start.18) | collective-permute-done | bytes 524320 | tf_op jit(solution)/shard_map/ppermute | solution.py:28
  148.5 2.4 %level3_rows64.1 = bf16[256,4096]{1,0:T(8,128)(2,1)} custom-call(s32[640]{0:T(1024)S(1)} %concatenate.3.meta, bf16[4,256,256]{2,1,0:T(8,128)(2,1)S(1)} %reorder.1.refs_0_, bf16[256,4096]{1,0:T(8,128)(2,1)S(1)} %get-tuple-element.74.refs_1_, bf16[64,4096]{1,0:T(8,128)(2,1)S(1)} %level2_rows64.3.refs_2_, ...), custom_call_target="tpu_custom_call", output_to_operand_aliasing={{}: (5, {})} | custom-call | tf_op jit(solution)/shard_map/level3_rows64/pallas_call | solution.py:198
  (41 shorter events, 5.9 us)
Async XLA Ops:
  3.2 30.8 %copy-start.2 = (s32[4,2,32]{2,1,0:T(2,128)S(1)}, s32[4,2,32]{2,1,0:T(2,128)}, u32[]{:S(2)}) copy-start(s32[4,2,32]{2,1,0:T(2,128)} %param.7) | copy-start | bytes 3076
  3.2 30.8 %copy-start.3 = (s32[4,32]{1,0:T(4,128)S(1)}, s32[4,32]{1,0:T(4,128)}, u32[]{:S(2)}) copy-start(s32[4,32]{1,0:T(4,128)} %param.9) | copy-start | bytes 1540
  3.2 30.8 %copy-start.4 = (s32[4,32]{1,0:T(4,128)S(1)}, s32[4,32]{1,0:T(4,128)}, u32[]{:S(2)}) copy-start(s32[4,32]{1,0:T(4,128)} %param.8) | copy-start | bytes 1540
  3.2 29.2 %collective-permute-start.2 = (bf16[128,4096]{1,0:T(8,128)(2,1)S(1)}, bf16[128,4096]{1,0:T(8,128)(2,1)S(1)}, u32[]{:S(2)}, u32[]{:S(2)}) collective-permute-start(bf16[128,4096]{1,0:T(8,128)(2,1)S(1)} %slice.91.refs_1_), channel_id=1, source_target_pairs={{0,16},{8,24},{16,0},{24,8},{1,17},{9,25},{17,1},{25,9},{2,18},{10... | collective-permute-start | bytes 3145736 | tf_op jit(solution)/shard_map/ppermute | solution.py:28
  6.2 25.7 %collective-permute-start = (bf16[64,4096]{1,0:T(8,128)(2,1)}, bf16[64,4096]{1,0:T(8,128)(2,1)S(1)}, u32[]{:S(2)}, u32[]{:S(2)}) collective-permute-start(bf16[64,4096]{1,0:T(8,128)(2,1)} %slice.90), channel_id=1, source_target_pairs={{0,4},{1,5},{2,6},{3,7},{4,0},{5,1},{6,2},{7,3},{8,12},{9,13},{10,... | collective-permute-start | bytes 1572872 | tf_op jit(solution)/shard_map/ppermute | solution.py:28
  32.0 26.3 %collective-permute-start.1 = (bf16[64,4096]{1,0:T(8,128)(2,1)}, bf16[64,4096]{1,0:T(8,128)(2,1)}, u32[]{:S(2)}, u32[]{:S(2)}) collective-permute-start(bf16[64,4096]{1,0:T(8,128)(2,1)} %get-tuple-element.43), channel_id=1, source_target_pairs={{0,4},{1,5},{2,6},{3,7},{4,0},{5,1},{6,2},{7,3},{8,12},{9,13},{10,... | collective-permute-start | bytes 1572872 | tf_op jit(solution)/shard_map/ppermute | solution.py:28
  32.0 26.3 %collective-permute-start.4 = (bf16[64,4096]{1,0:T(8,128)(2,1)S(1)}, bf16[64,4096]{1,0:T(8,128)(2,1)}, u32[]{:S(2)}, u32[]{:S(2)}) collective-permute-start(bf16[64,4096]{1,0:T(8,128)(2,1)S(1)} %collective-permute-done.refs_1_), channel_id=1, source_target_pairs={{0,16},{8,24},{16,0},{24,8},{1,17},{9,25},{17,1},{25,9},{2,18},{10... | collective-permute-start | bytes 1572872 | tf_op jit(solution)/shard_map/ppermute | solution.py:28
  32.4 23.7 %collective-permute-start.3 = (bf16[64,4096]{1,0:T(8,128)(2,1)S(1)}, bf16[64,4096]{1,0:T(8,128)(2,1)}, u32[]{:S(2)}, u32[]{:S(2)}) collective-permute-start(bf16[64,4096]{1,0:T(8,128)(2,1)S(1)} %get-tuple-element.47.refs_2_), channel_id=1, source_target_pairs={{0,16},{8,24},{16,0},{24,8},{1,17},{9,25},{17,1},{25,9},{2,18},{10... | collective-permute-start | bytes 1572872 | tf_op jit(solution)/shard_map/ppermute | solution.py:28
  34.2 1.0 copy-start
  56.1 14.5 %copy-start.1 = (bf16[64,4096]{1,0:T(8,128)(2,1)S(1)}, bf16[64,4096]{1,0:T(8,128)(2,1)}, u32[]{:S(2)}) copy-start(bf16[64,4096]{1,0:T(8,128)(2,1)} %get-tuple-element.49.refs_2_) | copy-start | bytes 1572868
  58.3 12.4 %collective-permute-start.5 = (bf16[64,4096]{1,0:T(8,128)(2,1)}, bf16[64,4096]{1,0:T(8,128)(2,1)S(1)}, u32[]{:S(2)}, u32[]{:S(2)}) collective-permute-start(bf16[64,4096]{1,0:T(8,128)(2,1)} %collective-permute-done.1.refs_2_), channel_id=1, source_target_pairs={{0,16},{8,24},{16,0},{24,8},{1,17},{9,25},{17,1},{25,9},{2,18},{10... | collective-permute-start | bytes 1572872 | tf_op jit(solution)/shard_map/ppermute | solution.py:28
  58.8 23.7 %collective-permute-start.7 = (bf16[64,4096]{1,0:T(8,128)(2,1)S(1)}, bf16[64,4096]{1,0:T(8,128)(2,1)S(1)}, u32[]{:S(2)}, u32[]{:S(2)}) collective-permute-start(bf16[64,4096]{1,0:T(8,128)(2,1)S(1)} %level0_rows64.2.refs_2_), channel_id=1, source_target_pairs={{0,4},{1,5},{2,6},{3,7},{4,0},{5,1},{6,2},{7,3},{8,12},{9,13},{10,... | collective-permute-start | bytes 1572872 | tf_op jit(solution)/shard_map/ppermute | solution.py:28
  70.6 11.9 %collective-permute-start.6 = (bf16[64,4096]{1,0:T(8,128)(2,1)S(1)}, bf16[64,4096]{1,0:T(8,128)(2,1)S(1)}, u32[]{:S(2)}, u32[]{:S(2)}) collective-permute-start(bf16[64,4096]{1,0:T(8,128)(2,1)S(1)} %copy-done.1), channel_id=1, source_target_pairs={{0,16},{8,24},{16,0},{24,8},{1,17},{9,25},{17,1},{25,9},{2,18},{10... | collective-permute-start | bytes 1572872 | tf_op jit(solution)/shard_map/ppermute | solution.py:28
  79.9 5.8 %collective-permute-start.8 = (bf16[224,4096]{1,0:T(8,128)(2,1)S(1)}, bf16[224,4096]{1,0:T(8,128)(2,1)S(1)}, u32[]{:S(2)}, u32[]{:S(2)}) collective-permute-start(bf16[224,4096]{1,0:T(8,128)(2,1)S(1)} %get-tuple-element.59.refs_1_), channel_id=1, source_target_pairs={{0,8},{8,0},{16,24},{24,16},{1,9},{9,1},{17,25},{25,17},{2,10},{10... | collective-permute-start | bytes 5505032 | tf_op jit(solution)/shard_map/ppermute | solution.py:28
  84.2 24.1 %collective-permute-start.10 = (bf16[64,4096]{1,0:T(8,128)(2,1)S(1)}, bf16[64,4096]{1,0:T(8,128)(2,1)S(1)}, u32[]{:S(2)}, u32[]{:S(2)}) collective-permute-start(bf16[64,4096]{1,0:T(8,128)(2,1)S(1)} %level0_rows64.3.refs_2_), channel_id=1, source_target_pairs={{0,4},{1,5},{2,6},{3,7},{4,0},{5,1},{6,2},{7,3},{8,12},{9,13},{10,... | collective-permute-start | bytes 1572872 | tf_op jit(solution)/shard_map/ppermute | solution.py:28
  90.0 37.9 %collective-permute-start.9 = (bf16[144,4096]{1,0:T(8,128)(2,1)S(1)}, bf16[144,4096]{1,0:T(8,128)(2,1)S(1)}, u32[]{:S(2)}, u32[]{:S(2)}) collective-permute-start(bf16[144,4096]{1,0:T(8,128)(2,1)S(1)} %get-tuple-element.63.refs_1_), channel_id=1, source_target_pairs={{0,2},{1,3},{2,0},{3,1},{4,6},{5,7},{6,4},{7,5},{8,10},{9,11},{10,... | collective-permute-start | bytes 3538952 | tf_op jit(solution)/shard_map/ppermute | solution.py:28
  96.4 1.6 %collective-permute-start.11 = (bf16[32,4096]{1,0:T(8,128)(2,1)S(1)}, bf16[32,4096]{1,0:T(8,128)(2,1)S(1)}, u32[]{:S(2)}, u32[]{:S(2)}) collective-permute-start(bf16[32,4096]{1,0:T(8,128)(2,1)S(1)} %get-tuple-element.69.refs_2_), channel_id=1, source_target_pairs={{0,8},{8,0},{16,24},{24,16},{1,9},{9,1},{17,25},{25,17},{2,10},{10... | collective-permute-start | bytes 786440 | tf_op jit(solution)/shard_map/ppermute | solution.py:28
  96.5 1.9 %collective-permute-start.12 = (bf16[32,4096]{1,0:T(8,128)(2,1)S(1)}, bf16[32,4096]{1,0:T(8,128)(2,1)S(1)}, u32[]{:S(2)}, u32[]{:S(2)}) collective-permute-start(bf16[32,4096]{1,0:T(8,128)(2,1)S(1)} %get-tuple-element.70.refs_4_), channel_id=1, source_target_pairs={{0,8},{8,0},{16,24},{24,16},{1,9},{9,1},{17,25},{25,17},{2,10},{10... | collective-permute-start | bytes 786440 | tf_op jit(solution)/shard_map/ppermute | solution.py:28
  109.8 2.0 %collective-permute-start.13 = (bf16[64,4096]{1,0:T(8,128)(2,1)S(1)}, bf16[64,4096]{1,0:T(8,128)(2,1)S(1)}, u32[]{:S(2)}, u32[]{:S(2)}) collective-permute-start(bf16[64,4096]{1,0:T(8,128)(2,1)S(1)} %level1_rows64.3.refs_2_), channel_id=1, source_target_pairs={{0,8},{8,0},{16,24},{24,16},{1,9},{9,1},{17,25},{25,17},{2,10},{10... | collective-permute-start | bytes 1572872 | tf_op jit(solution)/shard_map/ppermute | solution.py:28
  109.9 29.2 %collective-permute-start.17 = (bf16[64,4096]{1,0:T(8,128)(2,1)S(1)}, bf16[64,4096]{1,0:T(8,128)(2,1)S(1)}, u32[]{:S(2)}, u32[]{:S(2)}) collective-permute-start(bf16[64,4096]{1,0:T(8,128)(2,1)S(1)} %level2_rows64.2.refs_8_), channel_id=1, source_target_pairs={{0,2},{1,3},{2,0},{3,1},{4,6},{5,7},{6,4},{7,5},{8,10},{9,11},{10,... | collective-permute-start | bytes 1572872 | tf_op jit(solution)/shard_map/ppermute | solution.py:28
  127.9 6.4 %collective-permute-start.14 = (bf16[32,4096]{1,0:T(8,128)(2,1)S(1)}, bf16[32,4096]{1,0:T(8,128)(2,1)S(1)}, u32[]{:S(2)}, u32[]{:S(2)}) collective-permute-start(bf16[32,4096]{1,0:T(8,128)(2,1)S(1)} %slice.95.refs_3_), channel_id=1, source_target_pairs={{0,16},{8,24},{16,0},{24,8},{1,17},{9,25},{17,1},{25,9},{2,18},{10... | collective-permute-start | bytes 786440 | tf_op jit(solution)/shard_map/ppermute | solution.py:28
  128.4 20.1 %collective-permute-start.18 = (bf16[64,4096]{1,0:T(8,128)(2,1)S(1)}, bf16[64,4096]{1,0:T(8,128)(2,1)S(1)}, u32[]{:S(2)}, u32[]{:S(2)}) collective-permute-start(bf16[64,4096]{1,0:T(8,128)(2,1)S(1)} %level2_rows64.3.refs_2_), channel_id=1, source_target_pairs={{0,2},{1,3},{2,0},{3,1},{4,6},{5,7},{6,4},{7,5},{8,10},{9,11},{10,... | collective-permute-start | bytes 1572872 | tf_op jit(solution)/shard_map/ppermute | solution.py:28
  128.4 10.7 %collective-permute-start.15 = (bf16[32,4096]{1,0:T(8,128)(2,1)S(1)}, bf16[32,4096]{1,0:T(8,128)(2,1)S(1)}, u32[]{:S(2)}, u32[]{:S(2)}) collective-permute-start(bf16[32,4096]{1,0:T(8,128)(2,1)S(1)} %slice.95.refs_3_), channel_id=1, source_target_pairs={{0,8},{8,0},{16,24},{24,16},{1,9},{9,1},{17,25},{25,17},{2,10},{10... | collective-permute-start | bytes 786440 | tf_op jit(solution)/shard_map/ppermute | solution.py:28
  134.4 4.8 %collective-permute-start.16 = (bf16[32,4096]{1,0:T(8,128)(2,1)S(1)}, bf16[32,4096]{1,0:T(8,128)(2,1)S(1)}, u32[]{:S(2)}, u32[]{:S(2)}) collective-permute-start(bf16[32,4096]{1,0:T(8,128)(2,1)S(1)} %collective-permute-done.14.refs_4_), channel_id=1, source_target_pairs={{0,8},{8,0},{16,24},{24,16},{1,9},{9,1},{17,25},{25,17},{2,10},{10... | collective-permute-start | bytes 786440 | tf_op jit(solution)/shard_map/ppermute | solution.py:28

commit v4 on v3

--- a/solution.py
+++ b/solution.py
@@ -68,13 +68,9 @@
         out[level] = jnp.dot(inv[level], swap, preferred_element_type=F32).astype(BF16)
 
 
-def level_kernel(meta, *refs, base, level, blocks, n_in, top, pairs, outs, n_hidden):
-    ins, rest = refs[:n_in], refs[n_in + n_hidden :]
-    out_refs, rest = rest[: len(outs)], rest[len(outs) :]
+def eliminate(meta, inv, panel, merged, top, pairs, outs, level, blocks):
     width = blocks * BLOCK
-
-    def stack(spec):
-        return [(ins[i], low, count) for i, low, count in spec]
+    base = level * meta.shape[0] // LEVELS
 
     def at(j):
         return pl.ds(pl.multiple_of(j * BLOCK, BLOCK), BLOCK)
@@ -86,10 +82,8 @@
     def order(j):
         return meta[base + j]
 
-    inv = ins[0]
     if top is not None:
-        panel, merged = rest
-        a, b = stack(top[0]), stack(top[1])
+        a, b = top
         half = sum(count for _, _, count in a)
 
         def merge_block(j, carry):
@@ -107,17 +101,15 @@
             return carry
 
         lax.fori_loop(0, blocks, merge_block, 0, unroll=4)
-    else:
-        panel = ins[1]
 
     def columns(job, j):
         source, start, rows = job
         if source == "top":
             return merged[pl.ds(start, rows), at(j)]
-        a, b = (stack(s) for s in pairs[source])
+        a, b = pairs[source]
         return read(a, start, rows, j) + read(b, start, rows, order(j))
 
-    jobs = [job for dest in outs for job in dest]
+    jobs = [job for _, dest in outs for job in dest]
     pivots = [meta[base + 3 * blocks + i] for i in range(inv.shape[1] // BLOCK)]
     coupling = jnp.concatenate(
         [jnp.concatenate([columns(job, p) for p in pivots], axis=1).astype(BF16) for job in jobs],
@@ -129,7 +121,7 @@
         lanes = pl.ds(pl.multiple_of(t * TILE, TILE), TILE)
         update = jnp.dot(weights, panel[:, lanes], preferred_element_type=F32)
         done = 0
-        for out, dest in zip(out_refs, outs):
+        for out, dest in outs:
             put = 0
             for job in dest:
                 rows = job[2]
@@ -142,6 +134,72 @@
         return carry
 
     lax.fori_loop(0, width // TILE, finish_tile, 0, unroll=4)
+
+
+def level_kernel(meta, *refs, level, blocks, n_in, top, pairs, outs, n_hidden):
+    ins, rest = refs[:n_in], refs[n_in + n_hidden :]
+    out_refs, rest = rest[: len(outs)], rest[len(outs) :]
+
+    def stack(spec):
+        return [(ins[i], low, count) for i, low, count in spec]
+
+    panel, merged = rest if top is not None else (ins[1], None)
+    eliminate(
+        meta,
+        ins[0],
+        panel,
+        merged,
+        None if top is None else tuple(stack(s) for s in top),
+        [tuple(stack(s) for s in pair) for pair in pairs],
+        list(zip(out_refs, outs)),
+        level,
+        blocks,
+    )
+
+
+def two_level_kernel(meta, inv, *refs, blocks, counts, first_outs, second_outs):
+    n = len(counts)
+    ours, theirs, (near, near_x, out, panel, other_panel, merged, far, far_x) = (
+        refs[:n],
+        refs[n : 2 * n],
+        refs[2 * n :],
+    )
+    stacks = tuple([(ref, 0, count) for ref, count in zip(group, counts)] for group in (ours, theirs))
+    made = list(zip((far, far_x), first_outs))
+    eliminate(meta, inv, other_panel, merged, stacks, [], made, 0, blocks)
+
+    def whole(ref):
+        return [(ref, 0, ref.shape[0])]
+
+    pair = [(whole(near_x), whole(far_x))]
+    eliminate(
+        meta, inv, panel, merged, (whole(near), whole(far)), pair, [(out, second_outs)], 1, blocks
+    )
+
+
+def split_kernel(slab, *refs, starts):
+    outs, sems = refs[:-1], refs[-1]
+    copies = [
+        pltpu.make_async_copy(slab.at[pl.ds(start, out.shape[0])], out, sems.at[i])
+        for i, (start, out) in enumerate(zip(starts, outs))
+    ]
+    for copy in copies:
+        copy.start()
+    for copy in copies:
+        copy.wait()
+
+
+def split(slab, pieces):
+    return pl.pallas_call(
+        functools.partial(split_kernel, starts=[start for start, _ in pieces]),
+        out_shape=[jax.ShapeDtypeStruct((rows, slab.shape[1]), BF16) for _, rows in pieces],
+        in_specs=[pl.BlockSpec(memory_space=pltpu.HBM)],
+        out_specs=[pl.BlockSpec(memory_space=pltpu.HBM)] * len(pieces),
+        scratch_shapes=[pltpu.SemaphoreType.DMA((len(pieces),))],
+        compiler_params=pltpu.CompilerParams(vmem_limit_bytes=60 * 2**20),
+        cost_estimate=pl.CostEstimate(flops=0, bytes_accessed=0, transcendentals=0),
+        name="split",
+    )(slab)
 
 
 def run_level(level, meta, held, outs, pairs=(), top=None, keeps=False, part=None, cost=0):
@@ -186,7 +244,6 @@
         scratch.append(pltpu.VMEM((size, width), F32))
     kernel = functools.partial(
         level_kernel,
-        base=level * meta.shape[0] // LEVELS,
         level=level,
         blocks=width // BLOCK,
         n_in=n_in,
@@ -207,6 +264,34 @@
         cost_estimate=pl.CostEstimate(flops=cost, bytes_accessed=0, transcendentals=0),
         name=f"level{level}_rows{sum(counts)}",
     )(meta, *arrays, *hidden)
+
+
+def run_two_levels(meta, inv, ours, theirs, near, near_x, first_outs, second_outs):
+    width, size = near.shape[1], inv.shape[1]
+    rows = sum(job[2] for job in second_outs)
+    vmem = pl.BlockSpec(memory_space=pltpu.VMEM)
+    kernel = functools.partial(
+        two_level_kernel,
+        blocks=width // BLOCK,
+        counts=tuple(x.shape[0] for x in ours),
+        first_outs=first_outs,
+        second_outs=second_outs,
+    )
+    return pl.pallas_call(
+        kernel,
+        out_shape=[jax.ShapeDtypeStruct((n, width), BF16) for n in (rows, size)],
+        in_specs=[pl.BlockSpec(memory_space=pltpu.SMEM)] + [vmem] * (3 + 2 * len(ours)),
+        out_specs=[vmem, vmem],
+        scratch_shapes=[
+            pltpu.VMEM((size, width), BF16),
+            pltpu.VMEM((size, width), F32),
+            pltpu.VMEM(near.shape, BF16),
+            pltpu.VMEM(near_x.shape, BF16),
+        ],
+        compiler_params=pltpu.CompilerParams(vmem_limit_bytes=30 * 2**20),
+        cost_estimate=pl.CostEstimate(flops=0, bytes_accessed=0, transcendentals=0),
+        name="level0_level1",
+    )(meta, inv, *ours, *theirs, near, near_x)
 
 
 def reorder(meta, pivot_inverse):
@@ -255,49 +340,43 @@
         )
         return out
 
-    first_1 = schur_slab[:quarter]
+    cut_1 = quarter + share
+    first_1, begin = split(schur_slab, [(0, cut_1), (0, half + quarter)])
     first_z1 = trade(first_1, 1)
-    slab, first_1 = after(schur_slab, first_1)
-    first = slab[:half]
-    first_y = trade(first, 0)
-    slab, first = after(slab, first)
-    first_2 = slab[quarter:half]
-    rest_1, rest_2 = slab[half : half + quarter], slab[half + quarter :]
+    begin_y = trade(begin, 0)
+    slab, begin = after(schur_slab, begin)
+    first_2, rest_2 = slab[cut_1:half], slab[half + quarter :]
     inv = reorder(meta, pivot_inverse)
 
     first_yz1 = trade(first_z1, 0)
     first_2, first_z1 = after(first_2, first_z1)
     first_z2 = trade(first_2, 1)
-    rest_1, first_y = after(rest_1, first_y)
-    rest_y1 = trade(rest_1, 0)
 
     tops = [("top", 0, quarter), ("top", half, quarter)]
-    near, near_x, panel_0 = run_level(
-        0, meta, (inv,), [tops, [("top", quarter, quarter)]], top=(rows_of(first), rows_of(first_y)), keeps=True
-    )
-    after_1 = chunk(0, panel_0, rest_1, rest_y1)
+    near, near_x, after_1, panel_0 = run_level(
+        0,
+        meta,
+        (inv,),
+        [tops, [("top", quarter, quarter)], [(0, 0, quarter)]],
+        top=([(begin, 0, half)], [(begin_y, 0, half)]),
+        pairs=[([(begin, half, quarter)], [(begin_y, half, quarter)])],
+        keeps=True,
+    )
     first_z2, after_1, first_yz1 = after(first_z2, after_1, first_yz1)
     first_yz2 = trade(first_z2, 0)
     after_z1 = trade(after_1, 1)
     rest_2, first_yz2 = after(rest_2, first_yz2)
     rest_y2 = trade(rest_2, 0)
-    far, far_x = run_level(
-        0,
-        meta,
-        (inv,),
-        [tops, [("top", quarter, quarter)]],
-        top=(rows_of(first_z1) + rows_of(first_z2), rows_of(first_yz1) + rows_of(first_yz2)),
-    )
-
-    tops = [("top", low, eighth) for low in range(0, size, quarter)]
-    head, panel_1 = run_level(
-        1,
-        meta,
-        (inv,),
-        [tops + [("top", eighth, eighth), (0, 0, quarter)]],
-        top=(rows_of(near), rows_of(far)),
-        pairs=[(rows_of(near_x), rows_of(far_x))],
-        keeps=True,
+
+    head, panel_1 = run_two_levels(
+        meta,
+        inv,
+        (first_z1, first_z2),
+        (first_yz1, first_yz2),
+        near,
+        near_x,
+        (tuple(tops), (("top", quarter, quarter),)),
+        tuple([("top", low, eighth) for low in range(0, size, quarter)] + [("top", eighth, eighth), (0, 0, quarter)]),
     )
     head_c = trade(head, 2)
     rest_y2, after_z1 = after(rest_y2, after_z1)

time: 153 us -> 220 us (1.44)
  Pallas kernels: 35.9 us -> 102 us
  starting transfers between devices: 19.6 us -> 12.9 us
  waiting for transfers between devices: 88.4 us -> 95.1 us
    pallas_call x0 -> x2, Pallas kernels: none -> 76.9 us  [the longest x1 68.6 us: split(): pl.pallas_call(functools.partial(split_kernel, starts=[start for start, _...]
    pallas_call x12 -> x9, Pallas kernels: 34.9 us -> 24.4 us  [run_level(): pl.pallas_call(kernel, grid=(1,) if part is not None else (), out_shape=s...]
    ppermute x19 -> x18, waiting for transfers between devices: 88.4 us -> 95.1 us  [trade(): lax.ppermute(block, axis, [(i, i ^ flip) for i in range(lax.axis_size(axi...]
    ppermute x19 -> x18, starting transfers between devices: 19.6 us -> 12.9 us  [trade(): lax.ppermute(block, axis, [(i, i ^ flip) for i in range(lax.axis_size(axi...]
    slice x3 -> x2, local copies, waits for them, and re-layouts: 5.63 us -> 2.84 us  [on_device(): first_2, rest_2 = (slab[cut_1:half], slab[half + quarter:])]
  transfers between devices with their start and end apart: 19 -> 18, of which waited for: 12 -> 12; matrix products, arithmetic and copies ran while one was open for 2% -> 4% of each run, Pallas kernels for 22% -> 14%
where the time goes in v4:
time: 220 us
  Pallas kernels  102 us (46%)
  waiting for transfers between devices  95.1 us (43%)
  starting transfers between devices  12.9 us (6%)
  local copies, waits for them, and re-layouts  8.36 us (4%)
    ppermute x18, waiting for transfers between devices, trade(): lax.ppermute(block, axis, [(i, i ^ flip) for i in range(lax.axis_size(axi...  95.1 us
    pallas_call x1, Pallas kernels, split(): pl.pallas_call(functools.partial(split_kernel, starts=[start for start, _...  68.6 us
    pallas_call x9, Pallas kernels, run_level(): pl.pallas_call(kernel, grid=(1,) if part is not None else (), out_shape=s...  24.4 us
    ppermute x18, starting transfers between devices, trade(): lax.ppermute(block, axis, [(i, i ^ flip) for i in range(lax.axis_size(axi...  12.9 us
    pallas_call x1, Pallas kernels, run_two_levels(): pl.pallas_call(kernel, out_shape=[jax.ShapeDtypeStruct((n, width), BF16)...  8.27 us
  transfers between devices with their start and end apart: 18, of which 12 were waited for; matrix products, arithmetic and copies ran while one was open for 4% of the time, Pallas kernels for 14%

profile of v4, /device:TPU:0, one launch (start us, length us, event | category | flops | bytes accessed | tf_op | source)
XLA Modules:
  0.0 220.0 jit_solution(17072264410882451914)
XLA Ops:
  0.0 68.6 %split.1 = (bf16[80,4096]{1,0:T(8,128)(2,1)}, bf16[192,4096]{1,0:T(8,128)(2,1)}) custom-call(bf16[256,4096]{1,0:T(8,128)(2,1)} %slab.1), custom_call_target="tpu_custom_call" | custom-call | tf_op jit(solution)/shard_map/split/pallas_call | solution.py:193
  68.6 3.0 %collective-permute-start.2 = (bf16[192,4096]{1,0:T(8,128)(2,1)}, bf16[192,4096]{1,0:T(8,128)(2,1)S(1)}, u32[]{:S(2)}, u32[]{:S(2)}) collective-permute-start(bf16[192,4096]{1,0:T(8,128)(2,1)} %get-tuple-element.43.refs_1_), channel_id=1, source_target_pairs={{0,16},{8,24},{16,0},{24,8},{1,17},{9,25},{17,1},{25,9},{2,18},{10... | collective-permute-start | bytes 4718600 | tf_op jit(solution)/shard_map/ppermute | solution.py:28
  71.7 2.6 %collective-permute-start = (bf16[80,4096]{1,0:T(8,128)(2,1)}, bf16[80,4096]{1,0:T(8,128)(2,1)}, u32[]{:S(2)}, u32[]{:S(2)}) collective-permute-start(bf16[80,4096]{1,0:T(8,128)(2,1)} %get-tuple-element.41), channel_id=1, source_target_pairs={{0,4},{1,5},{2,6},{3,7},{4,0},{5,1},{6,2},{7,3},{8,12},{9,13},{10,... | collective-permute-start | bytes 1966088 | tf_op jit(solution)/shard_map/ppermute | solution.py:28
  74.3 1.8 slice.82
  76.0 27.1 %collective-permute-done.refs_0_ = bf16[80,4096]{1,0:T(8,128)(2,1)} collective-permute-done((bf16[80,4096]{1,0:T(8,128)(2,1)}, bf16[80,4096]{1,0:T(8,128)(2,1)}, u32[]{:S(2)}, u32[]{:S(2)}) %collective-permute-start) | collective-permute-done | bytes 655392 | tf_op jit(solution)/shard_map/ppermute | solution.py:28
  104.7 1.5 slice_bitcast_fusion
  109.2 1.0 copy-done.1
  110.2 0.9 reorder.1.refs_0_.inv
  111.2 4.3 %level0_rows256.1 = (bf16[128,4096]{1,0:T(8,128)(2,1)S(1)}, bf16[64,4096]{1,0:T(8,128)(2,1)S(1)}, bf16[64,4096]{1,0:T(8,128)(2,1)S(1)}, bf16[256,4096]{1,0:T(8,128)(2,1)S(1)}) custom-call(s32[640]{0:T(1024)S(1)} %concatenate.3.meta, bf16[4,256,256]{2,1,0:T(8,128)(2,1)S(1)} %reorder.1.refs_0_.inv, bf16[192,4096]{1,0:T(8,128)(2,1)S(1)} %copy-done, ...), custom_call_target="tpu_custom_call" | custom-call | tf_op jit(solution)/shard_map/level0_rows256/pallas_call | solution.py:255
  115.5 7.9 %collective-permute-done.1.refs_1_ = bf16[48,4096]{1,0:T(8,128)(2,1)S(1)} collective-permute-done((bf16[48,4096]{1,0:T(8,128)(2,1)}, bf16[48,4096]{1,0:T(8,128)(2,1)S(1)}, u32[]{:S(2)}, u32[]{:S(2)}) %collective-permute-start.1) | collective-permute-done | bytes 393248 | tf_op jit(solution)/shard_map/ppermute | solution.py:28
  123.4 1.5 collective-permute-start.4
  124.9 1.1 slice.81.refs_2_
  126.1 6.6 %collective-permute-done.4.refs_3_ = bf16[48,4096]{1,0:T(8,128)(2,1)S(1)} collective-permute-done((bf16[48,4096]{1,0:T(8,128)(2,1)S(1)}, bf16[48,4096]{1,0:T(8,128)(2,1)S(1)}, u32[]{:S(2)}, u32[]{:S(2)}) %collective-permute-start.4) | collective-permute-done | bytes 393248 | tf_op jit(solution)/shard_map/ppermute | solution.py:28
  132.7 1.5 collective-permute-start.5
  134.2 8.3 %level0_level1.1 = (bf16[224,4096]{1,0:T(8,128)(2,1)S(1)}, bf16[256,4096]{1,0:T(8,128)(2,1)S(1)}) custom-call(s32[640]{0:T(1024)S(1)} %concatenate.3.meta, bf16[4,256,256]{2,1,0:T(8,128)(2,1)S(1)} %reorder.1.refs_0_.inv, bf16[80,4096]{1,0:T(8,128)(2,1)} %collective-permute-done.refs_0_, bf16[48,4096]{1,0:T(8,128)(2,1)S(1)} %collective-permute-done.1.refs_1_, ...), custom_call_target="tpu_custom_call" | custom-call | tf_op jit(solution)/shard_map/level0_level1/pallas_call | solution.py:280
  142.6 7.2 %collective-permute-done.6.refs_3_ = bf16[64,4096]{1,0:T(8,128)(2,1)S(1)} collective-permute-done((bf16[64,4096]{1,0:T(8,128)(2,1)S(1)}, bf16[64,4096]{1,0:T(8,128)(2,1)S(1)}, u32[]{:S(2)}, u32[]{:S(2)}) %collective-permute-start.6) | collective-permute-done | bytes 524320 | tf_op jit(solution)/shard_map/ppermute | solution.py:28
  149.8 1.6 level0_rows64.1.refs_2_
  151.5 4.3 %level2_rows240.1 = (bf16[144,4096]{1,0:T(8,128)(2,1)S(1)}, bf16[96,4096]{1,0:T(8,128)(2,1)S(1)}, bf16[256,4096]{1,0:T(8,128)(2,1)S(1)}) custom-call(s32[640]{0:T(1024)S(1)} %concatenate.3.meta, bf16[4,256,256]{2,1,0:T(8,128)(2,1)S(1)} %reorder.1.refs_0_.inv, bf16[224,4096]{1,0:T(8,128)(2,1)S(1)} %get-tuple-element.54.refs_1_, ...), custom_call_target="tpu_custom_call" | custom-call | tf_op jit(solution)/shard_map/level2_rows240/pallas_call | solution.py:255
  155.8 2.3 %collective-permute-start.8 = (bf16[144,4096]{1,0:T(8,128)(2,1)S(1)}, bf16[144,4096]{1,0:T(8,128)(2,1)S(1)}, u32[]{:S(2)}, u32[]{:S(2)}) collective-permute-start(bf16[144,4096]{1,0:T(8,128)(2,1)S(1)} %get-tuple-element.59.refs_1_), channel_id=1, source_target_pairs={{0,2},{1,3},{2,0},{3,1},{4,6},{5,7},{6,4},{7,5},{8,10},{9,11},{10,... | collective-permute-start | bytes 3538952 | tf_op jit(solution)/shard_map/ppermute | solution.py:28
  158.1 1.6 level1_rows64.2
  160.3 1.0 collective-permute-done.10.refs_3_
  161.7 1.6 level2_rows64.2.refs_8_
  163.3 13.3 %collective-permute-done.9.refs_3_ = bf16[64,4096]{1,0:T(8,128)(2,1)S(1)} collective-permute-done((bf16[64,4096]{1,0:T(8,128)(2,1)S(1)}, bf16[64,4096]{1,0:T(8,128)(2,1)S(1)}, u32[]{:S(2)}, u32[]{:S(2)}) %collective-permute-start.9) | collective-permute-done | bytes 524320 | tf_op jit(solution)/shard_map/ppermute | solution.py:28
  176.6 1.6 level1_rows64.3.refs_2_
  178.3 1.8 collective-permute-done.12.refs_3_
  180.2 1.6 level2_rows64.3.refs_2_
  181.8 14.2 %collective-permute-done.8.refs_7_ = bf16[144,4096]{1,0:T(8,128)(2,1)S(1)} collective-permute-done((bf16[144,4096]{1,0:T(8,128)(2,1)S(1)}, bf16[144,4096]{1,0:T(8,128)(2,1)S(1)}, u32[]{:S(2)}, u32[]{:S(2)}) %collective-permute-start.8) | collective-permute-done | bytes 1179680 | tf_op jit(solution)/shard_map/ppermute | solution.py:28
  196.6 5.9 %collective-permute-done.13.refs_4_ = bf16[32,4096]{1,0:T(8,128)(2,1)S(1)} collective-permute-done((bf16[32,4096]{1,0:T(8,128)(2,1)S(1)}, bf16[32,4096]{1,0:T(8,128)(2,1)S(1)}, u32[]{:S(2)}, u32[]{:S(2)}) %collective-permute-start.13) | collective-permute-done | bytes 262176 | tf_op jit(solution)/shard_map/ppermute | solution.py:28
  202.6 4.7 %collective-permute-done.16.refs_9_ = bf16[64,4096]{1,0:T(8,128)(2,1)S(1)} collective-permute-done((bf16[64,4096]{1,0:T(8,128)(2,1)S(1)}, bf16[64,4096]{1,0:T(8,128)(2,1)S(1)}, u32[]{:S(2)}, u32[]{:S(2)}) %collective-permute-start.16) | collective-permute-done | bytes 524320 | tf_op jit(solution)/shard_map/ppermute | solution.py:28
  207.3 5.4 %level3_rows192.1 = (bf16[256,4096]{1,0:T(8,128)(2,1)}, bf16[256,4096]{1,0:T(8,128)(2,1)S(1)}) custom-call(s32[640]{0:T(1024)S(1)} %concatenate.3.meta, bf16[4,256,256]{2,1,0:T(8,128)(2,1)S(1)} %reorder.1.refs_0_.inv, bf16[144,4096]{1,0:T(8,128)(2,1)S(1)} %get-tuple-element.59.refs_1_, bf16[96,4096]{1,0:T(8,128)(2,1)S(1)} %get-tuple-element.60.refs_2_, ...), custom_call_target="tpu_custom_call" | custom-call | tf_op jit(solution)/shard_map/level3_rows192/pallas_call | solution.py:255
  212.6 4.9 %collective-permute-done.17.refs_3_ = bf16[64,4096]{1,0:T(8,128)(2,1)S(1)} collective-permute-done((bf16[64,4096]{1,0:T(8,128)(2,1)S(1)}, bf16[64,4096]{1,0:T(8,128)(2,1)S(1)}, u32[]{:S(2)}, u32[]{:S(2)}) %collective-permute-start.17) | collective-permute-done | bytes 524320 | tf_op jit(solution)/shard_map/ppermute | solution.py:28
  217.5 2.4 %level3_rows64.1 = bf16[256,4096]{1,0:T(8,128)(2,1)} custom-call(s32[640]{0:T(1024)S(1)} %concatenate.3.meta, bf16[4,256,256]{2,1,0:T(8,128)(2,1)S(1)} %reorder.1.refs_0_.inv, bf16[256,4096]{1,0:T(8,128)(2,1)S(1)} %get-tuple-element.70.refs_1_, bf16[64,4096]{1,0:T(8,128)(2,1)S(1)} %level2_rows64.3.refs_2_, ...), custom_call_target="tpu_custom_call", output_to_operand_aliasing={{}: (5, {})} | custom-call | tf_op jit(solution)/shard_map/level3_rows64/pallas_call | solution.py:255
  (33 shorter events, 6.5 us)
Async XLA Ops:
  0.0 103.6 %copy-start.2 = (s32[4,2,32]{2,1,0:T(2,128)S(1)}, s32[4,2,32]{2,1,0:T(2,128)}, u32[]{:S(2)}) copy-start(s32[4,2,32]{2,1,0:T(2,128)} %param.7) | copy-start | bytes 3076
  68.6 42.5 %copy-start = (bf16[192,4096]{1,0:T(8,128)(2,1)S(1)}, bf16[192,4096]{1,0:T(8,128)(2,1)}, u32[]{:S(2)}) copy-start(bf16[192,4096]{1,0:T(8,128)(2,1)} %get-tuple-element.43.refs_1_) | copy-start | bytes 4718596
  68.6 42.5 %collective-permute-start.2 = (bf16[192,4096]{1,0:T(8,128)(2,1)}, bf16[192,4096]{1,0:T(8,128)(2,1)S(1)}, u32[]{:S(2)}, u32[]{:S(2)}) collective-permute-start(bf16[192,4096]{1,0:T(8,128)(2,1)} %get-tuple-element.43.refs_1_), channel_id=1, source_target_pairs={{0,16},{8,24},{16,0},{24,8},{1,17},{9,25},{17,1},{25,9},{2,18},{10... | collective-permute-start | bytes 4718600 | tf_op jit(solution)/shard_map/ppermute | solution.py:28
  71.7 31.5 %collective-permute-start = (bf16[80,4096]{1,0:T(8,128)(2,1)}, bf16[80,4096]{1,0:T(8,128)(2,1)}, u32[]{:S(2)}, u32[]{:S(2)}) collective-permute-start(bf16[80,4096]{1,0:T(8,128)(2,1)} %get-tuple-element.41), channel_id=1, source_target_pairs={{0,4},{1,5},{2,6},{3,7},{4,0},{5,1},{6,2},{7,3},{8,12},{9,13},{10,... | collective-permute-start | bytes 1966088 | tf_op jit(solution)/shard_map/ppermute | solution.py:28
  103.1 20.3 %collective-permute-start.3 = (bf16[80,4096]{1,0:T(8,128)(2,1)}, bf16[80,4096]{1,0:T(8,128)(2,1)}, u32[]{:S(2)}, u32[]{:S(2)}) collective-permute-start(bf16[80,4096]{1,0:T(8,128)(2,1)} %collective-permute-done.refs_0_), channel_id=1, source_target_pairs={{0,16},{8,24},{16,0},{24,8},{1,17},{9,25},{17,1},{25,9},{2,18},{10... | collective-permute-start | bytes 1966088 | tf_op jit(solution)/shard_map/ppermute | solution.py:28
  104.1 19.2 %collective-permute-start.1 = (bf16[48,4096]{1,0:T(8,128)(2,1)}, bf16[48,4096]{1,0:T(8,128)(2,1)S(1)}, u32[]{:S(2)}, u32[]{:S(2)}) collective-permute-start(bf16[48,4096]{1,0:T(8,128)(2,1)} %slice.82), channel_id=1, source_target_pairs={{0,4},{1,5},{2,6},{3,7},{4,0},{5,1},{6,2},{7,3},{8,12},{9,13},{10,... | collective-permute-start | bytes 1179656 | tf_op jit(solution)/shard_map/ppermute | solution.py:28
  109.2 1.0 copy-start.1
  123.4 9.3 %collective-permute-start.4 = (bf16[48,4096]{1,0:T(8,128)(2,1)S(1)}, bf16[48,4096]{1,0:T(8,128)(2,1)S(1)}, u32[]{:S(2)}, u32[]{:S(2)}) collective-permute-start(bf16[48,4096]{1,0:T(8,128)(2,1)S(1)} %collective-permute-done.1.refs_1_), channel_id=1, source_target_pairs={{0,16},{8,24},{16,0},{24,8},{1,17},{9,25},{17,1},{25,9},{2,18},{10... | collective-permute-start | bytes 1179656 | tf_op jit(solution)/shard_map/ppermute | solution.py:28
  126.0 23.8 %collective-permute-start.6 = (bf16[64,4096]{1,0:T(8,128)(2,1)S(1)}, bf16[64,4096]{1,0:T(8,128)(2,1)S(1)}, u32[]{:S(2)}, u32[]{:S(2)}) collective-permute-start(bf16[64,4096]{1,0:T(8,128)(2,1)S(1)} %get-tuple-element.47.refs_2_), channel_id=1, source_target_pairs={{0,4},{1,5},{2,6},{3,7},{4,0},{5,1},{6,2},{7,3},{8,12},{9,13},{10,... | collective-permute-start | bytes 1572872 | tf_op jit(solution)/shard_map/ppermute | solution.py:28
  132.7 17.1 %collective-permute-start.5 = (bf16[64,4096]{1,0:T(8,128)(2,1)S(1)}, bf16[64,4096]{1,0:T(8,128)(2,1)S(1)}, u32[]{:S(2)}, u32[]{:S(2)}) collective-permute-start(bf16[64,4096]{1,0:T(8,128)(2,1)S(1)} %slice.81.refs_2_), channel_id=1, source_target_pairs={{0,16},{8,24},{16,0},{24,8},{1,17},{9,25},{17,1},{25,9},{2,18},{10... | collective-permute-start | bytes 1572872 | tf_op jit(solution)/shard_map/ppermute | solution.py:28
  142.5 9.0 %collective-permute-start.7 = (bf16[224,4096]{1,0:T(8,128)(2,1)S(1)}, bf16[224,4096]{1,0:T(8,128)(2,1)S(1)}, u32[]{:S(2)}, u32[]{:S(2)}) collective-permute-start(bf16[224,4096]{1,0:T(8,128)(2,1)S(1)} %get-tuple-element.54.refs_1_), channel_id=1, source_target_pairs={{0,8},{8,0},{16,24},{24,16},{1,9},{9,1},{17,25},{25,17},{2,10},{10... | collective-permute-start | bytes 5505032 | tf_op jit(solution)/shard_map/ppermute | solution.py:28
  151.4 25.2 %collective-permute-start.9 = (bf16[64,4096]{1,0:T(8,128)(2,1)S(1)}, bf16[64,4096]{1,0:T(8,128)(2,1)S(1)}, u32[]{:S(2)}, u32[]{:S(2)}) collective-permute-start(bf16[64,4096]{1,0:T(8,128)(2,1)S(1)} %level0_rows64.1.refs_2_), channel_id=1, source_target_pairs={{0,4},{1,5},{2,6},{3,7},{4,0},{5,1},{6,2},{7,3},{8,12},{9,13},{10,... | collective-permute-start | bytes 1572872 | tf_op jit(solution)/shard_map/ppermute | solution.py:28
  155.8 40.2 %collective-permute-start.8 = (bf16[144,4096]{1,0:T(8,128)(2,1)S(1)}, bf16[144,4096]{1,0:T(8,128)(2,1)S(1)}, u32[]{:S(2)}, u32[]{:S(2)}) collective-permute-start(bf16[144,4096]{1,0:T(8,128)(2,1)S(1)} %get-tuple-element.59.refs_1_), channel_id=1, source_target_pairs={{0,2},{1,3},{2,0},{3,1},{4,6},{5,7},{6,4},{7,5},{8,10},{9,11},{10,... | collective-permute-start | bytes 3538952 | tf_op jit(solution)/shard_map/ppermute | solution.py:28
  159.7 1.6 collective-permute-start.10
  159.8 1.9 collective-permute-start.11
  178.2 2.0 collective-permute-start.12
  178.3 29.0 %collective-permute-start.16 = (bf16[64,4096]{1,0:T(8,128)(2,1)S(1)}, bf16[64,4096]{1,0:T(8,128)(2,1)S(1)}, u32[]{:S(2)}, u32[]{:S(2)}) collective-permute-start(bf16[64,4096]{1,0:T(8,128)(2,1)S(1)} %level2_rows64.2.refs_8_), channel_id=1, source_target_pairs={{0,2},{1,3},{2,0},{3,1},{4,6},{5,7},{6,4},{7,5},{8,10},{9,11},{10,... | collective-permute-start | bytes 1572872 | tf_op jit(solution)/shard_map/ppermute | solution.py:28
  196.0 6.5 %collective-permute-start.13 = (bf16[32,4096]{1,0:T(8,128)(2,1)S(1)}, bf16[32,4096]{1,0:T(8,128)(2,1)S(1)}, u32[]{:S(2)}, u32[]{:S(2)}) collective-permute-start(bf16[32,4096]{1,0:T(8,128)(2,1)S(1)} %slice.83.refs_3_), channel_id=1, source_target_pairs={{0,16},{8,24},{16,0},{24,8},{1,17},{9,25},{17,1},{25,9},{2,18},{10... | collective-permute-start | bytes 786440 | tf_op jit(solution)/shard_map/ppermute | solution.py:28
  196.6 20.9 %collective-permute-start.17 = (bf16[64,4096]{1,0:T(8,128)(2,1)S(1)}, bf16[64,4096]{1,0:T(8,128)(2,1)S(1)}, u32[]{:S(2)}, u32[]{:S(2)}) collective-permute-start(bf16[64,4096]{1,0:T(8,128)(2,1)S(1)} %level2_rows64.3.refs_2_), channel_id=1, source_target_pairs={{0,2},{1,3},{2,0},{3,1},{4,6},{5,7},{6,4},{7,5},{8,10},{9,11},{10,... | collective-permute-start | bytes 1572872 | tf_op jit(solution)/shard_map/ppermute | solution.py:28
  196.6 10.6 %collective-permute-start.14 = (bf16[32,4096]{1,0:T(8,128)(2,1)S(1)}, bf16[32,4096]{1,0:T(8,128)(2,1)S(1)}, u32[]{:S(2)}, u32[]{:S(2)}) collective-permute-start(bf16[32,4096]{1,0:T(8,128)(2,1)S(1)} %slice.83.refs_3_), channel_id=1, source_target_pairs={{0,8},{8,0},{16,24},{24,16},{1,9},{9,1},{17,25},{25,17},{2,10},{10... | collective-permute-start | bytes 786440 | tf_op jit(solution)/shard_map/ppermute | solution.py:28
  202.5 4.7 %collective-permute-start.15 = (bf16[32,4096]{1,0:T(8,128)(2,1)S(1)}, bf16[32,4096]{1,0:T(8,128)(2,1)S(1)}, u32[]{:S(2)}, u32[]{:S(2)}) collective-permute-start(bf16[32,4096]{1,0:T(8,128)(2,1)S(1)} %collective-permute-done.13.refs_4_), channel_id=1, source_target_pairs={{0,8},{8,0},{16,24},{24,16},{1,9},{9,1},{17,25},{25,17},{2,10},{10... | collective-permute-start | bytes 786440 | tf_op jit(solution)/shard_map/ppermute | solution.py:28

commit v5 on v4

--- a/solution.py
+++ b/solution.py
@@ -159,47 +159,13 @@
 
 def two_level_kernel(meta, inv, *refs, blocks, counts, first_outs, second_outs):
     n = len(counts)
-    ours, theirs, (near, near_x, out, panel, other_panel, merged, far, far_x) = (
-        refs[:n],
-        refs[n : 2 * n],
-        refs[2 * n :],
-    )
+    ours, theirs, near, far, far_x = refs[:n], refs[n : 2 * n], *refs[2 * n : 2 * n + 3]
+    outs, panel, other_panel, merged = refs[2 * n + 3 : -3], *refs[-3:]
     stacks = tuple([(ref, 0, count) for ref, count in zip(group, counts)] for group in (ours, theirs))
     made = list(zip((far, far_x), first_outs))
     eliminate(meta, inv, other_panel, merged, stacks, [], made, 0, blocks)
-
-    def whole(ref):
-        return [(ref, 0, ref.shape[0])]
-
-    pair = [(whole(near_x), whole(far_x))]
-    eliminate(
-        meta, inv, panel, merged, (whole(near), whole(far)), pair, [(out, second_outs)], 1, blocks
-    )
-
-
-def split_kernel(slab, *refs, starts):
-    outs, sems = refs[:-1], refs[-1]
-    copies = [
-        pltpu.make_async_copy(slab.at[pl.ds(start, out.shape[0])], out, sems.at[i])
-        for i, (start, out) in enumerate(zip(starts, outs))
-    ]
-    for copy in copies:
-        copy.start()
-    for copy in copies:
-        copy.wait()
-
-
-def split(slab, pieces):
-    return pl.pallas_call(
-        functools.partial(split_kernel, starts=[start for start, _ in pieces]),
-        out_shape=[jax.ShapeDtypeStruct((rows, slab.shape[1]), BF16) for _, rows in pieces],
-        in_specs=[pl.BlockSpec(memory_space=pltpu.HBM)],
-        out_specs=[pl.BlockSpec(memory_space=pltpu.HBM)] * len(pieces),
-        scratch_shapes=[pltpu.SemaphoreType.DMA((len(pieces),))],
-        compiler_params=pltpu.CompilerParams(vmem_limit_bytes=60 * 2**20),
-        cost_estimate=pl.CostEstimate(flops=0, bytes_accessed=0, transcendentals=0),
-        name="split",
-    )(slab)
+    top = tuple([(ref, 0, ref.shape[0])] for ref in (near, far))
+    eliminate(meta, inv, panel, merged, top, [], list(zip(outs, second_outs)), 1, blocks)
 
 
 def run_level(level, meta, held, outs, pairs=(), top=None, keeps=False, part=None, cost=0):
@@ -266,9 +232,9 @@
     )(meta, *arrays, *hidden)
 
 
-def run_two_levels(meta, inv, ours, theirs, near, near_x, first_outs, second_outs):
+def run_two_levels(meta, inv, ours, theirs, near, first_outs, second_outs):
     width, size = near.shape[1], inv.shape[1]
-    rows = sum(job[2] for job in second_outs)
+    rows = [sum(job[2] for job in dest) for dest in (*first_outs, *second_outs)] + [size]
     vmem = pl.BlockSpec(memory_space=pltpu.VMEM)
     kernel = functools.partial(
         two_level_kernel,
@@ -279,19 +245,14 @@
     )
     return pl.pallas_call(
         kernel,
-        out_shape=[jax.ShapeDtypeStruct((n, width), BF16) for n in (rows, size)],
-        in_specs=[pl.BlockSpec(memory_space=pltpu.SMEM)] + [vmem] * (3 + 2 * len(ours)),
-        out_specs=[vmem, vmem],
-        scratch_shapes=[
-            pltpu.VMEM((size, width), BF16),
-            pltpu.VMEM((size, width), F32),
-            pltpu.VMEM(near.shape, BF16),
-            pltpu.VMEM(near_x.shape, BF16),
-        ],
+        out_shape=[jax.ShapeDtypeStruct((n, width), BF16) for n in rows],
+        in_specs=[pl.BlockSpec(memory_space=pltpu.SMEM)] + [vmem] * (2 + 2 * len(ours)),
+        out_specs=[vmem] * len(rows),
+        scratch_shapes=[pltpu.VMEM((size, width), BF16), pltpu.VMEM((size, width), F32)],
         compiler_params=pltpu.CompilerParams(vmem_limit_bytes=30 * 2**20),
         cost_estimate=pl.CostEstimate(flops=0, bytes_accessed=0, transcendentals=0),
         name="level0_level1",
-    )(meta, inv, *ours, *theirs, near, near_x)
+    )(meta, inv, *ours, *theirs, near)
 
 
 def reorder(meta, pivot_inverse):
@@ -340,12 +301,15 @@
         )
         return out
 
-    cut_1 = quarter + share
-    first_1, begin = split(schur_slab, [(0, cut_1), (0, half + quarter)])
-    first_z1 = trade(first_1, 1)
-    begin_y = trade(begin, 0)
-    slab, begin = after(schur_slab, begin)
-    first_2, rest_2 = slab[cut_1:half], slab[half + quarter :]
+    three = half - eighth
+    begin_1 = schur_slab[:three]
+    first_z1 = trade(begin_1, 1)
+    begin_y1 = trade(begin_1, 0)
+    slab, begin_1 = after(schur_slab, begin_1)
+    begin_2 = slab[three : 2 * three]
+    begin_y2 = trade(begin_2, 0)
+    slab, begin_2 = after(slab, begin_2)
+    first_2, rest_2 = slab[three:half], slab[2 * three :]
     inv = reorder(meta, pivot_inverse)
 
     first_yz1 = trade(first_z1, 0)
@@ -353,13 +317,14 @@
     first_z2 = trade(first_2, 1)
 
     tops = [("top", 0, quarter), ("top", half, quarter)]
+    begun = ((begin_1, begin_2), (begin_y1, begin_y2))
     near, near_x, after_1, panel_0 = run_level(
         0,
         meta,
         (inv,),
         [tops, [("top", quarter, quarter)], [(0, 0, quarter)]],
-        top=([(begin, 0, half)], [(begin_y, 0, half)]),
-        pairs=[([(begin, half, quarter)], [(begin_y, half, quarter)])],
+        top=tuple([(x, 0, three), (y, 0, eighth)] for x, y in begun),
+        pairs=[tuple([(y, eighth, quarter)] for _, y in begun)],
         keeps=True,
     )
     first_z2, after_1, first_yz1 = after(first_z2, after_1, first_yz1)
@@ -368,55 +333,61 @@
     rest_2, first_yz2 = after(rest_2, first_yz2)
     rest_y2 = trade(rest_2, 0)
 
-    head, panel_1 = run_two_levels(
+    e, y, z, yz = (("top", low, eighth) for low in range(0, size, quarter))
+    jobs = [[e, (*y[:2], share)], [("top", quarter + share, share), z], [yz]]
+    far, far_x, *head, panel_1 = run_two_levels(
         meta,
         inv,
         (first_z1, first_z2),
         (first_yz1, first_yz2),
         near,
-        near_x,
         (tuple(tops), (("top", quarter, quarter),)),
-        tuple([("top", low, eighth) for low in range(0, size, quarter)] + [("top", eighth, eighth), (0, 0, quarter)]),
-    )
-    head_c = trade(head, 2)
-    rest_y2, after_z1 = after(rest_y2, after_z1)
-    after_2 = chunk(0, panel_0, rest_2, rest_y2, cost=3 * 10**10)
-    after_z2 = trade(after_2, 1)
-    head_c, after_2 = after(head_c, after_2)
-
-    more = head.shape[0] - half
+        jobs,
+    )
+    head_c = [trade(x, 2) for x in head]
+
     tops = [("top", low, share) for low in range(0, size, eighth)]
     lead, others, panel_2 = run_level(
         2,
         meta,
         (inv,),
-        [
-            [tops[0], tops[2], ("top", share, share), (0, 0, more)],
-            [tops[i] for i in (1, 3, 4, 5, 6, 7)],
+        [[tops[0], tops[2], ("top", share, share)], [tops[i] for i in (1, 3, 4, 5, 6, 7)]],
+        top=tuple(sum((rows_of(x) for x in group), []) for group in (head, head_c)),
+        keeps=True,
+    )
+    rest_y2, after_z1, far_x, lead = after(rest_y2, after_z1, far_x, lead)
+    after_2 = chunk(0, panel_0, rest_2, rest_y2, cost=0)
+    after_z2 = trade(after_2, 1)
+    (next_0,) = run_level(
+        1,
+        meta,
+        (inv, panel_1),
+        [[(0, 0, eighth), (1, 0, quarter)]],
+        pairs=[
+            ([(near, eighth, eighth)], [(far, eighth, eighth)]),
+            (rows_of(near_x), rows_of(far_x)),
         ],
-        top=([(head, 0, half)], [(head_c, 0, half)]),
-        pairs=[([(head, half, more)], [(head_c, half, more)])],
-        keeps=True,
     )
     lead_w = trade(lead, 3)
-    after_z1, lead = after(after_z1, lead)
-    next_1a, next_1b = run_level(
+    after_z1, after_2 = after(after_z1, after_2)
+    next_1 = run_level(
         1,
         meta,
         (inv, panel_1),
         [[(0, 0, eighth)], [(0, eighth, eighth)]],
         pairs=[(rows_of(after_1), rows_of(after_z1))],
     )
+    next_1 = [next_0, *next_1]
     (last_1,) = run_level(
         2,
         meta,
         (inv, panel_2),
-        [[(0, 0, eighth), (1, 0, eighth)]],
-        pairs=[(rows_of(x), rows_of(trade(x, 2))) for x in (next_1a, next_1b)],
+        [[(i, 0, x.shape[0]) for i, x in enumerate(next_1)]],
+        pairs=[(rows_of(x), rows_of(trade(x, 2))) for x in next_1],
     )
     last_w1 = trade(last_1, 3)
-    after_z2, last_1 = after(after_z2, last_1)
-    next_2 = chunk(1, panel_1, after_2, after_z2, cost=25 * 10**8)
+    after_z2, last_1, lead_w = after(after_z2, last_1, lead_w)
+    next_2 = chunk(1, panel_1, after_2, after_z2, cost=15 * 10**8)
     last_2 = chunk(2, panel_2, next_2, trade(next_2, 2))
     last_w2 = trade(last_2, 3)
     lead_w, last_2 = after(lead_w, last_2)
@@ -434,7 +405,7 @@
         3,
         meta,
         (inv,),
-        [[("top", 0, share), (0, 0, more), (1, 0, quarter)]],
+        [[("top", 0, share), (0, 0, more), (1, 0, last_1.shape[0])]],
         top=(tops, tops_other),
         pairs=[([(lead, eighth, more)], [(lead_w, eighth, more)]), (rows_of(last_1), rows_of(last_w1))],
         keeps=True,

time: 220 us -> 155 us (0.70)
  Pallas kernels: 102 us -> 34.7 us
  waiting for transfers between devices: 95.1 us -> 98.1 us
  starting transfers between devices: 12.9 us -> 15.4 us
    pallas_call x1 -> x0, Pallas kernels: 68.6 us -> none  [split(): pl.pallas_call(functools.partial(split_kernel, starts=[start for start, _...]
    ppermute x18 -> x22, waiting for transfers between devices: 95.1 us -> 98.1 us  [trade(): lax.ppermute(block, axis, [(i, i ^ flip) for i in range(lax.axis_size(axi...]
    ppermute x18 -> x22, starting transfers between devices: 12.9 us -> 15.4 us  [trade(): lax.ppermute(block, axis, [(i, i ^ flip) for i in range(lax.axis_size(axi...]
    pallas_call x9 -> x10, Pallas kernels: 24.4 us -> 26.7 us  [run_level(): pl.pallas_call(kernel, grid=(1,) if part is not None else (), out_shape=s...]
    slice x2 -> x4, local copies, waits for them, and re-layouts: 2.84 us -> 5.15 us  [the longest x2 2.74 us: on_device(): first_2, rest_2 = (slab[three:half], slab[2 * three:])]
  transfers between devices with their start and end apart: 18 -> 22, of which waited for: 12 -> 15; matrix products, arithmetic and copies ran while one was open for 4% -> 3% of each run, Pallas kernels for 14% -> 20%
where the time goes in v5:
time: 155 us
  waiting for transfers between devices  98.1 us (63%)
  Pallas kernels  34.7 us (22%)
  starting transfers between devices  15.4 us (10%)
  local copies, waits for them, and re-layouts  6.34 us (4%)
    ppermute x22, waiting for transfers between devices, trade(): lax.ppermute(block, axis, [(i, i ^ flip) for i in range(lax.axis_size(axi...  98.1 us
    pallas_call x10, Pallas kernels, run_level(): pl.pallas_call(kernel, grid=(1,) if part is not None else (), out_shape=s...  26.7 us
    ppermute x22, starting transfers between devices, trade(): lax.ppermute(block, axis, [(i, i ^ flip) for i in range(lax.axis_size(axi...  15.4 us
    pallas_call x1, Pallas kernels, run_two_levels(): pl.pallas_call(kernel, out_shape=[jax.ShapeDtypeStruct((n, width), BF16)...  7.01 us
  transfers between devices with their start and end apart: 22, of which 15 were waited for; matrix products, arithmetic and copies ran while one was open for 3% of the time, Pallas kernels for 20%

profile of v5, /device:TPU:0, one launch (start us, length us, event | category | flops | bytes accessed | tf_op | source)
XLA Modules:
  0.0 154.8 jit_solution(15270166311419913972)
XLA Ops:
  0.0 1.2 slice.87.refs_1_
  1.2 4.1 %collective-permute-start = (bf16[96,4096]{1,0:T(8,128)(2,1)S(1)}, bf16[96,4096]{1,0:T(8,128)(2,1)S(1)}, u32[]{:S(2)}, u32[]{:S(2)}) collective-permute-start(bf16[96,4096]{1,0:T(8,128)(2,1)S(1)} %slice.87.refs_1_), channel_id=1, source_target_pairs={{0,4},{1,5},{2,6},{3,7},{4,0},{5,1},{6,2},{7,3},{8,12},{9,13},{10,... | collective-permute-start | bytes 2359304 | tf_op jit(solution)/shard_map/ppermute | solution.py:28
  6.5 1.6 %collective-permute-start.3 = (bf16[96,4096]{1,0:T(8,128)(2,1)S(1)}, bf16[96,4096]{1,0:T(8,128)(2,1)}, u32[]{:S(2)}, u32[]{:S(2)}) collective-permute-start(bf16[96,4096]{1,0:T(8,128)(2,1)S(1)} %slice.88.refs_2_), channel_id=1, source_target_pairs={{0,16},{8,24},{16,0},{24,8},{1,17},{9,25},{17,1},{25,9},{2,18},{10... | collective-permute-start | bytes 2359304 | tf_op jit(solution)/shard_map/ppermute | solution.py:28
  8.6 31.1 %collective-permute-done.refs_0_ = bf16[96,4096]{1,0:T(8,128)(2,1)S(1)} collective-permute-done((bf16[96,4096]{1,0:T(8,128)(2,1)S(1)}, bf16[96,4096]{1,0:T(8,128)(2,1)S(1)}, u32[]{:S(2)}, u32[]{:S(2)}) %collective-permute-start) | collective-permute-done | bytes 786464 | tf_op jit(solution)/shard_map/ppermute | solution.py:28
  39.7 1.6 %collective-permute-start.4 = (bf16[96,4096]{1,0:T(8,128)(2,1)S(1)}, bf16[96,4096]{1,0:T(8,128)(2,1)S(1)}, u32[]{:S(2)}, u32[]{:S(2)}) collective-permute-start(bf16[96,4096]{1,0:T(8,128)(2,1)S(1)} %collective-permute-done.refs_0_), channel_id=1, source_target_pairs={{0,16},{8,24},{16,0},{24,8},{1,17},{9,25},{17,1},{25,9},{2,18},{10... | collective-permute-start | bytes 2359304 | tf_op jit(solution)/shard_map/ppermute | solution.py:28
  41.3 1.7 %slice.90 = bf16[32,4096]{1,0:T(8,128)(2,1)} slice(bf16[256,4096]{1,0:T(8,128)(2,1)} %param.5), slice={[96:128], [0:4096]} | slice | bytes 524288 | tf_op jit(solution)/shard_map/slice | solution.py:312
  45.3 5.0 %level0_rows256.1 = (bf16[128,4096]{1,0:T(8,128)(2,1)S(1)}, bf16[64,4096]{1,0:T(8,128)(2,1)S(1)}, bf16[64,4096]{1,0:T(8,128)(2,1)S(1)}, bf16[256,4096]{1,0:T(8,128)(2,1)S(1)}) custom-call(s32[640]{0:T(1024)S(1)} %concatenate.3.meta, bf16[4,256,256]{2,1,0:T(8,128)(2,1)S(1)} %reorder.1.refs_0_.inv, bf16[96,4096]{1,0:T(8,128)(2,1)S(1)} %slice.87.refs_1_, ...), custom_call_target="tpu_custom_call" | custom-call | tf_op jit(solution)/shard_map/level0_rows256/pallas_call | solution.py:221
  50.3 6.4 %collective-permute-done.1.refs_1_ = bf16[32,4096]{1,0:T(8,128)(2,1)S(1)} collective-permute-done((bf16[32,4096]{1,0:T(8,128)(2,1)}, bf16[32,4096]{1,0:T(8,128)(2,1)S(1)}, u32[]{:S(2)}, u32[]{:S(2)}) %collective-permute-start.1) | collective-permute-done | bytes 262176 | tf_op jit(solution)/shard_map/ppermute | solution.py:28
  56.7 2.6 %collective-permute-done.4.refs_2_ = bf16[96,4096]{1,0:T(8,128)(2,1)S(1)} collective-permute-done((bf16[96,4096]{1,0:T(8,128)(2,1)S(1)}, bf16[96,4096]{1,0:T(8,128)(2,1)S(1)}, u32[]{:S(2)}, u32[]{:S(2)}) %collective-permute-start.4) | collective-permute-done | bytes 786464 | tf_op jit(solution)/shard_map/ppermute | solution.py:28
  59.3 1.5 collective-permute-start.5
  62.3 4.4 %collective-permute-done.5.refs_3_ = bf16[32,4096]{1,0:T(8,128)(2,1)S(1)} collective-permute-done((bf16[32,4096]{1,0:T(8,128)(2,1)S(1)}, bf16[32,4096]{1,0:T(8,128)(2,1)S(1)}, u32[]{:S(2)}, u32[]{:S(2)}) %collective-permute-start.5) | collective-permute-done | bytes 262176 | tf_op jit(solution)/shard_map/ppermute | solution.py:28
  66.7 1.4 collective-permute-start.6
  68.1 7.0 %level0_level1.1 = (bf16[128,4096]{1,0:T(8,128)(2,1)S(1)}, bf16[64,4096]{1,0:T(8,128)(2,1)S(1)}, bf16[48,4096]{1,0:T(8,128)(2,1)S(1)}, bf16[48,4096]{1,0:T(8,128...) custom-call(s32[640]{0:T(1024)S(1)} %concatenate.3.meta, ...), custom_call_target="tpu_custom_call" | custom-call | tf_op jit(solution)/shard_map/level0_level1/pallas_call | solution.py:246
  75.8 2.1 %collective-permute-done.10.refs_6_ = bf16[32,4096]{1,0:T(8,128)(2,1)S(1)} collective-permute-done((bf16[32,4096]{1,0:T(8,128)(2,1)S(1)}, bf16[32,4096]{1,0:T(8,128)(2,1)S(1)}, u32[]{:S(2)}, u32[]{:S(2)}) %collective-permute-start.10) | collective-permute-done | bytes 262176 | tf_op jit(solution)/shard_map/ppermute | solution.py:28
  77.9 3.7 %level2_rows144.1 = (bf16[48,4096]{1,0:T(8,128)(2,1)S(1)}, bf16[96,4096]{1,0:T(8,128)(2,1)S(1)}, bf16[256,4096]{1,0:T(8,128)(2,1)S(1)}) custom-call(s32[640]{0:T(1024)S(1)} %concatenate.3.meta, bf16[4,256,256]{2,1,0:T(8,128)(2,1)S(1)} %reorder.1.refs_0_.inv, bf16[48,4096]{1,0:T(8,128)(2,1)S(1)} %get-tuple-element.58.refs_1_, ...), custom_call_target="tpu_custom_call" | custom-call | tf_op jit(solution)/shard_map/level2_rows144/pallas_call | solution.py:221
  81.6 5.2 %collective-permute-done.7.refs_3_ = bf16[64,4096]{1,0:T(8,128)(2,1)S(1)} collective-permute-done((bf16[64,4096]{1,0:T(8,128)(2,1)S(1)}, bf16[64,4096]{1,0:T(8,128)(2,1)S(1)}, u32[]{:S(2)}, u32[]{:S(2)}) %collective-permute-start.7) | collective-permute-done | bytes 524320 | tf_op jit(solution)/shard_map/ppermute | solution.py:28
  86.7 1.8 %level1_rows96.1.refs_2_ = bf16[96,4096]{1,0:T(8,128)(2,1)S(1)} custom-call(s32[640]{0:T(1024)S(1)} %concatenate.3.meta, bf16[4,256,256]{2,1,0:T(8,128)(2,1)S(1)} %reorder.1.refs_0_.inv, bf16[256,4096]{1,0:T(8,128)(2,1)S(1)} %get-tuple-element.67.refs_1_, bf16[128,4096]{1,0:T(8,128)(2,1)S(1)} %get-tuple-element.56.refs_4_.refs_2_, ...), custom_call_target="tpu_custom_call" | custom-call | tf_op jit(solution)/shard_map/level1_rows96/pallas_call | solution.py:221
  88.6 1.6 %level0_rows64.1.refs_2_ = bf16[64,4096]{1,0:T(8,128)(2,1)S(1)} custom-call(s32[640]{0:T(1024)S(1)} %concatenate.3.meta, bf16[4,256,256]{2,1,0:T(8,128)(2,1)S(1)} %reorder.1.refs_0_.inv, bf16[256,4096]{1,0:T(8,128)(2,1)S(1)} %get-tuple-element.64.refs_1_, bf16[64,4096]{1,0:T(8,128)(2,1)S(1)} %slice.89.refs_2_, ...), custom_call_target="tpu_custom_call" | custom-call | tf_op jit(solution)/shard_map/level0_rows64/pallas_call | solution.py:221
  90.3 1.7 %collective-permute-start.15 = (bf16[48,4096]{1,0:T(8,128)(2,1)S(1)}, bf16[48,4096]{1,0:T(8,128)(2,1)S(1)}, u32[]{:S(2)}, u32[]{:S(2)}) collective-permute-start(bf16[48,4096]{1,0:T(8,128)(2,1)S(1)} %get-tuple-element.62.refs_1_), channel_id=1, source_target_pairs={{0,2},{1,3},{2,0},{3,1},{4,6},{5,7},{6,4},{7,5},{8,10},{9,11},{10,... | collective-permute-start | bytes 1179656 | tf_op jit(solution)/shard_map/ppermute | solution.py:28
  92.0 1.6 %level1_rows64.2 = (bf16[32,4096]{1,0:T(8,128)(2,1)S(1)}, bf16[32,4096]{1,0:T(8,128)(2,1)S(1)}) custom-call(s32[640]{0:T(1024)S(1)} %concatenate.3.meta, bf16[4,256,256]{2,1,0:T(8,128)(2,1)S(1)} %reorder.1.refs_0_.inv, bf16[256,4096]{1,0:T(8,128)(2,1)S(1)} %get-tuple-element.67.refs_1_, bf16[64,4096]{1,0:T(8,128)(2,1)S(1)} %get-tuple-element.52.refs_2_, ...), custom_call_target="tpu_custom_call" | custom-call | tf_op jit(solution)/shard_map/level1_rows64/pallas_call | solution.py:221
  95.6 2.1 %level2_rows160.1.refs_8_ = bf16[160,4096]{1,0:T(8,128)(2,1)S(1)} custom-call(s32[640]{0:T(1024)S(1)} %concatenate.3.meta, bf16[4,256,256]{2,1,0:T(8,128)(2,1)S(1)} %reorder.1.refs_0_.inv, bf16[256,4096]{1,0:T(8,128)(2,1)S(1)} %get-tuple-element.66.refs_1_, bf16[96,4096]{1,0:T(8,128)(2,1)S(1)} %level1_rows96.1.refs_2_, ...), custom_call_target="tpu_custom_call" | custom-call | tf_op jit(solution)/shard_map/level2_rows160/pallas_call | solution.py:221
  98.1 13.0 %collective-permute-done.15.refs_7_ = bf16[48,4096]{1,0:T(8,128)(2,1)S(1)} collective-permute-done((bf16[48,4096]{1,0:T(8,128)(2,1)S(1)}, bf16[48,4096]{1,0:T(8,128)(2,1)S(1)}, u32[]{:S(2)}, u32[]{:S(2)}) %collective-permute-start.15) | collective-permute-done | bytes 393248 | tf_op jit(solution)/shard_map/ppermute | solution.py:28
  111.1 4.3 %collective-permute-done.11.refs_3_ = bf16[64,4096]{1,0:T(8,128)(2,1)S(1)} collective-permute-done((bf16[64,4096]{1,0:T(8,128)(2,1)S(1)}, bf16[64,4096]{1,0:T(8,128)(2,1)S(1)}, u32[]{:S(2)}, u32[]{:S(2)}) %collective-permute-start.11) | collective-permute-done | bytes 524320 | tf_op jit(solution)/shard_map/ppermute | solution.py:28
  115.4 1.6 %level1_rows64.3.refs_2_ = bf16[64,4096]{1,0:T(8,128)(2,1)S(1)} custom-call(s32[640]{0:T(1024)S(1)} %concatenate.3.meta, bf16[4,256,256]{2,1,0:T(8,128)(2,1)S(1)} %reorder.1.refs_0_.inv, bf16[256,4096]{1,0:T(8,128)(2,1)S(1)} %get-tuple-element.67.refs_1_, bf16[64,4096]{1,0:T(8,128)(2,1)S(1)} %level0_rows64.1.refs_2_, ...), custom_call_target="tpu_custom_call" | custom-call | flops 1500000000 | tf_op jit(solution)/shard_map/level1_rows64/pallas_call | solution.py:221
  117.1 1.9 %collective-permute-done.16.refs_3_ = bf16[64,4096]{1,0:T(8,128)(2,1)S(1)} collective-permute-done((bf16[64,4096]{1,0:T(8,128)(2,1)S(1)}, bf16[64,4096]{1,0:T(8,128)(2,1)S(1)}, u32[]{:S(2)}, u32[]{:S(2)}) %collective-permute-start.16) | collective-permute-done | bytes 524320 | tf_op jit(solution)/shard_map/ppermute | solution.py:28
  119.0 1.6 %level2_rows64.1.refs_2_ = bf16[64,4096]{1,0:T(8,128)(2,1)S(1)} custom-call(s32[640]{0:T(1024)S(1)} %concatenate.3.meta, bf16[4,256,256]{2,1,0:T(8,128)(2,1)S(1)} %reorder.1.refs_0_.inv, bf16[256,4096]{1,0:T(8,128)(2,1)S(1)} %get-tuple-element.66.refs_1_, bf16[64,4096]{1,0:T(8,128)(2,1)S(1)} %level1_rows64.3.refs_2_, ...), custom_call_target="tpu_custom_call" | custom-call | tf_op jit(solution)/shard_map/level2_rows64/pallas_call | solution.py:221
  121.3 7.7 %collective-permute-done.17.refs_4_ = bf16[32,4096]{1,0:T(8,128)(2,1)S(1)} collective-permute-done((bf16[32,4096]{1,0:T(8,128)(2,1)S(1)}, bf16[32,4096]{1,0:T(8,128)(2,1)S(1)}, u32[]{:S(2)}, u32[]{:S(2)}) %collective-permute-start.17) | collective-permute-done | bytes 262176 | tf_op jit(solution)/shard_map/ppermute | solution.py:28
  129.0 1.5 collective-permute-done.19.refs_6_
  130.6 11.0 %collective-permute-done.20.refs_9_ = bf16[160,4096]{1,0:T(8,128)(2,1)S(1)} collective-permute-done((bf16[160,4096]{1,0:T(8,128)(2,1)S(1)}, bf16[160,4096]{1,0:T(8,128)(2,1)S(1)}, u32[]{:S(2)}, u32[]{:S(2)}) %collective-permute-start.20) | collective-permute-done | bytes 1310752 | tf_op jit(solution)/shard_map/ppermute | solution.py:28
  141.6 5.4 %level3_rows192.1 = (bf16[256,4096]{1,0:T(8,128)(2,1)}, bf16[256,4096]{1,0:T(8,128)(2,1)S(1)}) custom-call(s32[640]{0:T(1024)S(1)} %concatenate.3.meta, bf16[4,256,256]{2,1,0:T(8,128)(2,1)S(1)} %reorder.1.refs_0_.inv, bf16[48,4096]{1,0:T(8,128)(2,1)S(1)} %get-tuple-element.62.refs_1_, bf16[96,4096]{1,0:T(8,128)(2,1)S(1)} %get-tuple-element.63.refs_2_, ...), custom_call_target="tpu_custom_call" | custom-call | tf_op jit(solution)/shard_map/level3_rows192/pallas_call | solution.py:221
  147.0 5.4 %collective-permute-done.21.refs_3_ = bf16[64,4096]{1,0:T(8,128)(2,1)S(1)} collective-permute-done((bf16[64,4096]{1,0:T(8,128)(2,1)S(1)}, bf16[64,4096]{1,0:T(8,128)(2,1)S(1)}, u32[]{:S(2)}, u32[]{:S(2)}) %collective-permute-start.21) | collective-permute-done | bytes 524320 | tf_op jit(solution)/shard_map/ppermute | solution.py:28
  152.4 2.4 %level3_rows64.1 = bf16[256,4096]{1,0:T(8,128)(2,1)} custom-call(s32[640]{0:T(1024)S(1)} %concatenate.3.meta, bf16[4,256,256]{2,1,0:T(8,128)(2,1)S(1)} %reorder.1.refs_0_.inv, bf16[256,4096]{1,0:T(8,128)(2,1)S(1)} %get-tuple-element.80.refs_1_, bf16[64,4096]{1,0:T(8,128)(2,1)S(1)} %level2_rows64.1.refs_2_, ...), custom_call_target="tpu_custom_call", output_to_operand_aliasing={{}: (5, {})} | custom-call | tf_op jit(solution)/shard_map/level3_rows64/pallas_call | solution.py:221
  (45 shorter events, 9.3 us)
Async XLA Ops:
  0.0 43.0 %copy-start.1 = (s32[4,2,32]{2,1,0:T(2,128)S(1)}, s32[4,2,32]{2,1,0:T(2,128)}, u32[]{:S(2)}) copy-start(s32[4,2,32]{2,1,0:T(2,128)} %param.7) | copy-start | bytes 3076
  0.0 43.1 %copy-start.3 = (s32[4,32]{1,0:T(4,128)S(1)}, s32[4,32]{1,0:T(4,128)}, u32[]{:S(2)}) copy-start(s32[4,32]{1,0:T(4,128)} %param.8) | copy-start | bytes 1540
  0.0 43.1 %copy-start.2 = (s32[4,32]{1,0:T(4,128)S(1)}, s32[4,32]{1,0:T(4,128)}, u32[]{:S(2)}) copy-start(s32[4,32]{1,0:T(4,128)} %param.9) | copy-start | bytes 1540
  1.2 38.5 %collective-permute-start = (bf16[96,4096]{1,0:T(8,128)(2,1)S(1)}, bf16[96,4096]{1,0:T(8,128)(2,1)S(1)}, u32[]{:S(2)}, u32[]{:S(2)}) collective-permute-start(bf16[96,4096]{1,0:T(8,128)(2,1)S(1)} %slice.87.refs_1_), channel_id=1, source_target_pairs={{0,4},{1,5},{2,6},{3,7},{4,0},{5,1},{6,2},{7,3},{8,12},{9,13},{10,... | collective-permute-start | bytes 2359304 | tf_op jit(solution)/shard_map/ppermute | solution.py:28
  6.5 38.7 %collective-permute-start.3 = (bf16[96,4096]{1,0:T(8,128)(2,1)S(1)}, bf16[96,4096]{1,0:T(8,128)(2,1)}, u32[]{:S(2)}, u32[]{:S(2)}) collective-permute-start(bf16[96,4096]{1,0:T(8,128)(2,1)S(1)} %slice.88.refs_2_), channel_id=1, source_target_pairs={{0,16},{8,24},{16,0},{24,8},{1,17},{9,25},{17,1},{25,9},{2,18},{10... | collective-permute-start | bytes 2359304 | tf_op jit(solution)/shard_map/ppermute | solution.py:28
  8.1 37.2 %collective-permute-start.2 = (bf16[96,4096]{1,0:T(8,128)(2,1)S(1)}, bf16[96,4096]{1,0:T(8,128)(2,1)}, u32[]{:S(2)}, u32[]{:S(2)}) collective-permute-start(bf16[96,4096]{1,0:T(8,128)(2,1)S(1)} %slice.87.refs_1_), channel_id=1, source_target_pairs={{0,16},{8,24},{16,0},{24,8},{1,17},{9,25},{17,1},{25,9},{2,18},{10... | collective-permute-start | bytes 2359304 | tf_op jit(solution)/shard_map/ppermute | solution.py:28
  39.7 19.6 %collective-permute-start.4 = (bf16[96,4096]{1,0:T(8,128)(2,1)S(1)}, bf16[96,4096]{1,0:T(8,128)(2,1)S(1)}, u32[]{:S(2)}, u32[]{:S(2)}) collective-permute-start(bf16[96,4096]{1,0:T(8,128)(2,1)S(1)} %collective-permute-done.refs_0_), channel_id=1, source_target_pairs={{0,16},{8,24},{16,0},{24,8},{1,17},{9,25},{17,1},{25,9},{2,18},{10... | collective-permute-start | bytes 2359304 | tf_op jit(solution)/shard_map/ppermute | solution.py:28
  43.0 13.7 %collective-permute-start.1 = (bf16[32,4096]{1,0:T(8,128)(2,1)}, bf16[32,4096]{1,0:T(8,128)(2,1)S(1)}, u32[]{:S(2)}, u32[]{:S(2)}) collective-permute-start(bf16[32,4096]{1,0:T(8,128)(2,1)} %slice.90), channel_id=1, source_target_pairs={{0,4},{1,5},{2,6},{3,7},{4,0},{5,1},{6,2},{7,3},{8,12},{9,13},{10,... | collective-permute-start | bytes 786440 | tf_op jit(solution)/shard_map/ppermute | solution.py:28
  43.3 1.0 copy-start
  59.3 7.4 %collective-permute-start.5 = (bf16[32,4096]{1,0:T(8,128)(2,1)S(1)}, bf16[32,4096]{1,0:T(8,128)(2,1)S(1)}, u32[]{:S(2)}, u32[]{:S(2)}) collective-permute-start(bf16[32,4096]{1,0:T(8,128)(2,1)S(1)} %collective-permute-done.1.refs_1_), channel_id=1, source_target_pairs={{0,16},{8,24},{16,0},{24,8},{1,17},{9,25},{17,1},{25,9},{2,18},{10... | collective-permute-start | bytes 786440 | tf_op jit(solution)/shard_map/ppermute | solution.py:28
  61.9 24.8 %collective-permute-start.7 = (bf16[64,4096]{1,0:T(8,128)(2,1)S(1)}, bf16[64,4096]{1,0:T(8,128)(2,1)S(1)}, u32[]{:S(2)}, u32[]{:S(2)}) collective-permute-start(bf16[64,4096]{1,0:T(8,128)(2,1)S(1)} %get-tuple-element.52.refs_2_), channel_id=1, source_target_pairs={{0,4},{1,5},{2,6},{3,7},{4,0},{5,1},{6,2},{7,3},{8,12},{9,13},{10,... | collective-permute-start | bytes 1572872 | tf_op jit(solution)/shard_map/ppermute | solution.py:28
  66.7 20.0 %collective-permute-start.6 = (bf16[64,4096]{1,0:T(8,128)(2,1)S(1)}, bf16[64,4096]{1,0:T(8,128)(2,1)S(1)}, u32[]{:S(2)}, u32[]{:S(2)}) collective-permute-start(bf16[64,4096]{1,0:T(8,128)(2,1)S(1)} %slice.89.refs_2_), channel_id=1, source_target_pairs={{0,16},{8,24},{16,0},{24,8},{1,17},{9,25},{17,1},{25,9},{2,18},{10... | collective-permute-start | bytes 1572872 | tf_op jit(solution)/shard_map/ppermute | solution.py:28
  75.1 2.7 %collective-permute-start.8 = (bf16[48,4096]{1,0:T(8,128)(2,1)S(1)}, bf16[48,4096]{1,0:T(8,128)(2,1)S(1)}, u32[]{:S(2)}, u32[]{:S(2)}) collective-permute-start(bf16[48,4096]{1,0:T(8,128)(2,1)S(1)} %get-tuple-element.58.refs_1_), channel_id=1, source_target_pairs={{0,8},{8,0},{16,24},{24,16},{1,9},{9,1},{17,25},{25,17},{2,10},{10... | collective-permute-start | bytes 1179656 | tf_op jit(solution)/shard_map/ppermute | solution.py:28
  75.2 2.7 %collective-permute-start.9 = (bf16[48,4096]{1,0:T(8,128)(2,1)S(1)}, bf16[48,4096]{1,0:T(8,128)(2,1)S(1)}, u32[]{:S(2)}, u32[]{:S(2)}) collective-permute-start(bf16[48,4096]{1,0:T(8,128)(2,1)S(1)} %get-tuple-element.59.refs_2_), channel_id=1, source_target_pairs={{0,8},{8,0},{16,24},{24,16},{1,9},{9,1},{17,25},{25,17},{2,10},{10... | collective-permute-start | bytes 1179656 | tf_op jit(solution)/shard_map/ppermute | solution.py:28
  75.7 2.1 %collective-permute-start.10 = (bf16[32,4096]{1,0:T(8,128)(2,1)S(1)}, bf16[32,4096]{1,0:T(8,128)(2,1)S(1)}, u32[]{:S(2)}, u32[]{:S(2)}) collective-permute-start(bf16[32,4096]{1,0:T(8,128)(2,1)S(1)} %get-tuple-element.60.refs_3_), channel_id=1, source_target_pairs={{0,8},{8,0},{16,24},{24,16},{1,9},{9,1},{17,25},{25,17},{2,10},{10... | collective-permute-start | bytes 786440 | tf_op jit(solution)/shard_map/ppermute | solution.py:28
  88.5 7.1 %collective-permute-start.12 = (bf16[96,4096]{1,0:T(8,128)(2,1)S(1)}, bf16[96,4096]{1,0:T(8,128)(2,1)S(1)}, u32[]{:S(2)}, u32[]{:S(2)}) collective-permute-start(bf16[96,4096]{1,0:T(8,128)(2,1)S(1)} %level1_rows96.1.refs_2_), channel_id=1, source_target_pairs={{0,8},{8,0},{16,24},{24,16},{1,9},{9,1},{17,25},{25,17},{2,10},{10... | collective-permute-start | bytes 2359304 | tf_op jit(solution)/shard_map/ppermute | solution.py:28
  90.2 25.2 %collective-permute-start.11 = (bf16[64,4096]{1,0:T(8,128)(2,1)S(1)}, bf16[64,4096]{1,0:T(8,128)(2,1)S(1)}, u32[]{:S(2)}, u32[]{:S(2)}) collective-permute-start(bf16[64,4096]{1,0:T(8,128)(2,1)S(1)} %level0_rows64.1.refs_2_), channel_id=1, source_target_pairs={{0,4},{1,5},{2,6},{3,7},{4,0},{5,1},{6,2},{7,3},{8,12},{9,13},{10,... | collective-permute-start | bytes 1572872 | tf_op jit(solution)/shard_map/ppermute | solution.py:28
  90.3 20.8 %collective-permute-start.15 = (bf16[48,4096]{1,0:T(8,128)(2,1)S(1)}, bf16[48,4096]{1,0:T(8,128)(2,1)S(1)}, u32[]{:S(2)}, u32[]{:S(2)}) collective-permute-start(bf16[48,4096]{1,0:T(8,128)(2,1)S(1)} %get-tuple-element.62.refs_1_), channel_id=1, source_target_pairs={{0,2},{1,3},{2,0},{3,1},{4,6},{5,7},{6,4},{7,5},{8,10},{9,11},{10,... | collective-permute-start | bytes 1179656 | tf_op jit(solution)/shard_map/ppermute | solution.py:28
  93.6 1.6 %collective-permute-start.13 = (bf16[32,4096]{1,0:T(8,128)(2,1)S(1)}, bf16[32,4096]{1,0:T(8,128)(2,1)S(1)}, u32[]{:S(2)}, u32[]{:S(2)}) collective-permute-start(bf16[32,4096]{1,0:T(8,128)(2,1)S(1)} %get-tuple-element.73.refs_4_), channel_id=1, source_target_pairs={{0,8},{8,0},{16,24},{24,16},{1,9},{9,1},{17,25},{25,17},{2,10},{10... | collective-permute-start | bytes 786440 | tf_op jit(solution)/shard_map/ppermute | solution.py:28
  93.7 1.9 %collective-permute-start.14 = (bf16[32,4096]{1,0:T(8,128)(2,1)S(1)}, bf16[32,4096]{1,0:T(8,128)(2,1)S(1)}, u32[]{:S(2)}, u32[]{:S(2)}) collective-permute-start(bf16[32,4096]{1,0:T(8,128)(2,1)S(1)} %get-tuple-element.74.refs_6_), channel_id=1, source_target_pairs={{0,8},{8,0},{16,24},{24,16},{1,9},{9,1},{17,25},{25,17},{2,10},{10... | collective-permute-start | bytes 786440 | tf_op jit(solution)/shard_map/ppermute | solution.py:28
  97.7 43.9 %collective-permute-start.20 = (bf16[160,4096]{1,0:T(8,128)(2,1)S(1)}, bf16[160,4096]{1,0:T(8,128)(2,1)S(1)}, u32[]{:S(2)}, u32[]{:S(2)}) collective-permute-start(bf16[160,4096]{1,0:T(8,128)(2,1)S(1)} %level2_rows160.1.refs_8_), channel_id=1, source_target_pairs={{0,2},{1,3},{2,0},{3,1},{4,6},{5,7},{6,4},{7,5},{8,10},{9,11},{10,... | collective-permute-start | bytes 3932168 | tf_op jit(solution)/shard_map/ppermute | solution.py:28
  117.0 2.0 %collective-permute-start.16 = (bf16[64,4096]{1,0:T(8,128)(2,1)S(1)}, bf16[64,4096]{1,0:T(8,128)(2,1)S(1)}, u32[]{:S(2)}, u32[]{:S(2)}) collective-permute-start(bf16[64,4096]{1,0:T(8,128)(2,1)S(1)} %level1_rows64.3.refs_2_), channel_id=1, source_target_pairs={{0,8},{8,0},{16,24},{24,16},{1,9},{9,1},{17,25},{25,17},{2,10},{10... | collective-permute-start | bytes 1572872 | tf_op jit(solution)/shard_map/ppermute | solution.py:28
  120.6 8.4 %collective-permute-start.17 = (bf16[32,4096]{1,0:T(8,128)(2,1)S(1)}, bf16[32,4096]{1,0:T(8,128)(2,1)S(1)}, u32[]{:S(2)}, u32[]{:S(2)}) collective-permute-start(bf16[32,4096]{1,0:T(8,128)(2,1)S(1)} %slice.91.refs_3_), channel_id=1, source_target_pairs={{0,16},{8,24},{16,0},{24,8},{1,17},{9,25},{17,1},{25,9},{2,18},{10... | collective-permute-start | bytes 786440 | tf_op jit(solution)/shard_map/ppermute | solution.py:28
  121.3 31.1 %collective-permute-start.21 = (bf16[64,4096]{1,0:T(8,128)(2,1)S(1)}, bf16[64,4096]{1,0:T(8,128)(2,1)S(1)}, u32[]{:S(2)}, u32[]{:S(2)}) collective-permute-start(bf16[64,4096]{1,0:T(8,128)(2,1)S(1)} %level2_rows64.1.refs_2_), channel_id=1, source_target_pairs={{0,2},{1,3},{2,0},{3,1},{4,6},{5,7},{6,4},{7,5},{8,10},{9,11},{10,... | collective-permute-start | bytes 1572872 | tf_op jit(solution)/shard_map/ppermute | solution.py:28
  121.3 7.7 %collective-permute-start.18 = (bf16[32,4096]{1,0:T(8,128)(2,1)S(1)}, bf16[32,4096]{1,0:T(8,128)(2,1)S(1)}, u32[]{:S(2)}, u32[]{:S(2)}) collective-permute-start(bf16[32,4096]{1,0:T(8,128)(2,1)S(1)} %slice.91.refs_3_), channel_id=1, source_target_pairs={{0,8},{8,0},{16,24},{24,16},{1,9},{9,1},{17,25},{25,17},{2,10},{10... | collective-permute-start | bytes 786440 | tf_op jit(solution)/shard_map/ppermute | solution.py:28
  129.0 1.5 collective-permute-start.19

commit v6 on v5

--- a/solution.py
+++ b/solution.py
@@ -301,35 +301,36 @@
         )
         return out
 
-    three = half - eighth
-    begin_1 = schur_slab[:three]
+    cut_1 = quarter + share
+    cut_2 = half + quarter
+    begin_1 = schur_slab[:cut_1]
     first_z1 = trade(begin_1, 1)
     begin_y1 = trade(begin_1, 0)
     slab, begin_1 = after(schur_slab, begin_1)
-    begin_2 = slab[three : 2 * three]
-    begin_y2 = trade(begin_2, 0)
-    slab, begin_2 = after(slab, begin_2)
-    first_2, rest_2 = slab[three:half], slab[2 * three :]
+    begin_2, begin_3, rest_2 = slab[cut_1:half], slab[half:cut_2], slab[cut_2:]
+    begin_y2, begin_y3 = trade(begin_2, 0), trade(begin_3, 0)
     inv = reorder(meta, pivot_inverse)
 
     first_yz1 = trade(first_z1, 0)
-    first_2, first_z1 = after(first_2, first_z1)
+    first_2, first_z1 = after(begin_2, first_z1)
     first_z2 = trade(first_2, 1)
+    rest_2, begin_y3 = after(rest_2, begin_y3)
 
     tops = [("top", 0, quarter), ("top", half, quarter)]
-    begun = ((begin_1, begin_2), (begin_y1, begin_y2))
+    begun = ((begin_1, begin_2, begin_3), (begin_y1, begin_y2, begin_y3))
     near, near_x, after_1, panel_0 = run_level(
         0,
         meta,
         (inv,),
         [tops, [("top", quarter, quarter)], [(0, 0, quarter)]],
-        top=tuple([(x, 0, three), (y, 0, eighth)] for x, y in begun),
-        pairs=[tuple([(y, eighth, quarter)] for _, y in begun)],
+        top=tuple(rows_of(x) + rows_of(y) for x, y, _ in begun),
+        pairs=[tuple(rows_of(x) for *_, x in begun)],
         keeps=True,
     )
-    first_z2, after_1, first_yz1 = after(first_z2, after_1, first_yz1)
+    first_z2, after_1 = after(first_z2, after_1)
+    after_z1 = trade(after_1, 1)
+    first_z2, first_yz1 = after(first_z2, first_yz1)
     first_yz2 = trade(first_z2, 0)
-    after_z1 = trade(after_1, 1)
     rest_2, first_yz2 = after(rest_2, first_yz2)
     rest_y2 = trade(rest_2, 0)
 

time: 155 us -> 150 us (0.968)
  waiting for transfers between devices: 98.1 us -> 92 us
  starting transfers between devices: 15.4 us -> 17.5 us
  local copies, waits for them, and re-layouts: 6.34 us -> 4.65 us
    ppermute x22 -> x23, waiting for transfers between devices: 98.1 us -> 92 us  [trade(): lax.ppermute(block, axis, [(i, i ^ flip) for i in range(lax.axis_size(axi...]
    ppermute x22 -> x23, starting transfers between devices: 15.4 us -> 17.5 us  [trade(): lax.ppermute(block, axis, [(i, i ^ flip) for i in range(lax.axis_size(axi...]
    slice x4 -> x3, local copies, waits for them, and re-layouts: 5.15 us -> 3.46 us  [the longest x1 1.27 us: on_device(): slab[half:cut_2]]
  transfers between devices with their start and end apart: 22 -> 23, of which waited for: 15 -> 15; matrix products, arithmetic and copies ran while one was open for 3% -> 2% of each run, Pallas kernels for 20% -> 21%
where the time goes in v6:
time: 150 us; the launch traced here: 149 us
  waiting for transfers between devices  92 us (61%)
  Pallas kernels  35.1 us (23%)
  starting transfers between devices  17.5 us (12%)
  local copies, waits for them, and re-layouts  4.65 us (3%)
    ppermute x23, waiting for transfers between devices, trade(): lax.ppermute(block, axis, [(i, i ^ flip) for i in range(lax.axis_size(axi...  92 us
    pallas_call x10, Pallas kernels, run_level(): pl.pallas_call(kernel, grid=(1,) if part is not None else (), out_shape=s...  26.5 us
    ppermute x23, starting transfers between devices, trade(): lax.ppermute(block, axis, [(i, i ^ flip) for i in range(lax.axis_size(axi...  17.5 us
    pallas_call x1, Pallas kernels, run_two_levels(): pl.pallas_call(kernel, out_shape=[jax.ShapeDtypeStruct((n, width), BF16)...  7.65 us
  transfers between devices with their start and end apart: 23, of which 15 were waited for; matrix products, arithmetic and copies ran while one was open for 2% of the time, Pallas kernels for 21%

profile of v6, /device:TPU:0, one launch (start us, length us, event | category | flops | bytes accessed | tf_op | source)
XLA Modules:
  0.0 149.4 jit_solution(16693099684768866978)
XLA Ops:
  0.0 1.2 slice.87.refs_1_
  1.2 3.0 %collective-permute-start.3 = (bf16[80,4096]{1,0:T(8,128)(2,1)S(1)}, bf16[80,4096]{1,0:T(8,128)(2,1)S(1)}, u32[]{:S(2)}, u32[]{:S(2)}) collective-permute-start(bf16[80,4096]{1,0:T(8,128)(2,1)S(1)} %slice.87.refs_1_), channel_id=1, source_target_pairs={{0,16},{8,24},{16,0},{24,8},{1,17},{9,25},{17,1},{25,9},{2,18},{10... | collective-permute-start | bytes 1966088 | tf_op jit(solution)/shard_map/ppermute | solution.py:28
  4.2 2.6 %collective-permute-start.1 = (bf16[80,4096]{1,0:T(8,128)(2,1)S(1)}, bf16[80,4096]{1,0:T(8,128)(2,1)S(1)}, u32[]{:S(2)}, u32[]{:S(2)}) collective-permute-start(bf16[80,4096]{1,0:T(8,128)(2,1)S(1)} %slice.87.refs_1_), channel_id=1, source_target_pairs={{0,4},{1,5},{2,6},{3,7},{4,0},{5,1},{6,2},{7,3},{8,12},{9,13},{10,... | collective-permute-start | bytes 1966088 | tf_op jit(solution)/shard_map/ppermute | solution.py:28
  6.8 1.3 fusion.8
  9.7 1.6 %collective-permute-start.4 = (bf16[48,4096]{1,0:T(8,128)(2,1)S(1)}, bf16[48,4096]{1,0:T(8,128)(2,1)}, u32[]{:S(2)}, u32[]{:S(2)}) collective-permute-start(bf16[48,4096]{1,0:T(8,128)(2,1)S(1)} %slice.90.refs_2_), channel_id=1, source_target_pairs={{0,16},{8,24},{16,0},{24,8},{1,17},{9,25},{17,1},{25,9},{2,18},{10... | collective-permute-start | bytes 1179656 | tf_op jit(solution)/shard_map/ppermute | solution.py:28
  11.3 24.1 %collective-permute-done.1.refs_0_ = bf16[80,4096]{1,0:T(8,128)(2,1)S(1)} collective-permute-done((bf16[80,4096]{1,0:T(8,128)(2,1)S(1)}, bf16[80,4096]{1,0:T(8,128)(2,1)S(1)}, u32[]{:S(2)}, u32[]{:S(2)}) %collective-permute-start.1) | collective-permute-done | bytes 655392 | tf_op jit(solution)/shard_map/ppermute | solution.py:28
  38.1 1.4 collective-permute-done.4.refs_4_
  39.5 4.8 %level0_rows256.1 = (bf16[128,4096]{1,0:T(8,128)(2,1)S(1)}, bf16[64,4096]{1,0:T(8,128)(2,1)S(1)}, bf16[64,4096]{1,0:T(8,128)(2,1)S(1)}, bf16[256,4096]{1,0:T(8,128)(2,1)S(1)}) custom-call(s32[640]{0:T(1024)S(1)} %concatenate.3.meta, bf16[4,256,256]{2,1,0:T(8,128)(2,1)S(1)} %reorder.1.refs_0_.inv, bf16[80,4096]{1,0:T(8,128)(2,1)S(1)} %slice.87.refs_1_, ...), custom_call_target="tpu_custom_call" | custom-call | tf_op jit(solution)/shard_map/level0_rows256/pallas_call | solution.py:221
  44.3 10.7 %collective-permute-done.2.refs_1_ = bf16[48,4096]{1,0:T(8,128)(2,1)} collective-permute-done((bf16[48,4096]{1,0:T(8,128)(2,1)S(1)}, bf16[48,4096]{1,0:T(8,128)(2,1)}, u32[]{:S(2)}, u32[]{:S(2)}) %collective-permute-start.2) | collective-permute-done | bytes 393248 | tf_op jit(solution)/shard_map/ppermute | solution.py:28
  55.0 1.5 %collective-permute-start.6 = (bf16[48,4096]{1,0:T(8,128)(2,1)}, bf16[48,4096]{1,0:T(8,128)(2,1)S(1)}, u32[]{:S(2)}, u32[]{:S(2)}) collective-permute-start(bf16[48,4096]{1,0:T(8,128)(2,1)} %collective-permute-done.2.refs_1_), channel_id=1, source_target_pairs={{0,16},{8,24},{16,0},{24,8},{1,17},{9,25},{17,1},{25,9},{2,18},{10... | collective-permute-start | bytes 1179656 | tf_op jit(solution)/shard_map/ppermute | solution.py:28
  57.1 7.5 %collective-permute-done.6.refs_3_ = bf16[48,4096]{1,0:T(8,128)(2,1)S(1)} collective-permute-done((bf16[48,4096]{1,0:T(8,128)(2,1)}, bf16[48,4096]{1,0:T(8,128)(2,1)S(1)}, u32[]{:S(2)}, u32[]{:S(2)}) %collective-permute-start.6) | collective-permute-done | bytes 393248 | tf_op jit(solution)/shard_map/ppermute | solution.py:28
  64.5 1.5 %collective-permute-start.7 = (bf16[64,4096]{1,0:T(8,128)(2,1)S(1)}, bf16[64,4096]{1,0:T(8,128)(2,1)S(1)}, u32[]{:S(2)}, u32[]{:S(2)}) collective-permute-start(bf16[64,4096]{1,0:T(8,128)(2,1)S(1)} %get-tuple-element.53.refs_2_), channel_id=1, source_target_pairs={{0,16},{8,24},{16,0},{24,8},{1,17},{9,25},{17,1},{25,9},{2,18},{10... | collective-permute-start | bytes 1572872 | tf_op jit(solution)/shard_map/ppermute | solution.py:28
  66.1 7.7 %level0_level1.1 = (bf16[128,4096]{1,0:T(8,128)(2,1)S(1)}, bf16[64,4096]{1,0:T(8,128)(2,1)S(1)}, bf16[48,4096]{1,0:T(8,128)(2,1)S(1)}, bf16[48,4096]{1,0:T(8,128...) custom-call(s32[640]{0:T(1024)S(1)} %concatenate.3.meta, ...), custom_call_target="tpu_custom_call" | custom-call | tf_op jit(solution)/shard_map/level0_level1/pallas_call | solution.py:246
  74.4 2.1 %collective-permute-done.11.refs_6_ = bf16[32,4096]{1,0:T(8,128)(2,1)S(1)} collective-permute-done((bf16[32,4096]{1,0:T(8,128)(2,1)S(1)}, bf16[32,4096]{1,0:T(8,128)(2,1)S(1)}, u32[]{:S(2)}, u32[]{:S(2)}) %collective-permute-start.11) | collective-permute-done | bytes 262176 | tf_op jit(solution)/shard_map/ppermute | solution.py:28
  76.5 3.7 %level2_rows144.1 = (bf16[48,4096]{1,0:T(8,128)(2,1)S(1)}, bf16[96,4096]{1,0:T(8,128)(2,1)S(1)}, bf16[256,4096]{1,0:T(8,128)(2,1)S(1)}) custom-call(s32[640]{0:T(1024)S(1)} %concatenate.3.meta, bf16[4,256,256]{2,1,0:T(8,128)(2,1)S(1)} %reorder.1.refs_0_.inv, bf16[48,4096]{1,0:T(8,128)(2,1)S(1)} %get-tuple-element.60.refs_1_, ...), custom_call_target="tpu_custom_call" | custom-call | tf_op jit(solution)/shard_map/level2_rows144/pallas_call | solution.py:221
  80.3 1.8 %level1_rows96.1.refs_2_ = bf16[96,4096]{1,0:T(8,128)(2,1)S(1)} custom-call(s32[640]{0:T(1024)S(1)} %concatenate.3.meta, bf16[4,256,256]{2,1,0:T(8,128)(2,1)S(1)} %reorder.1.refs_0_.inv, bf16[256,4096]{1,0:T(8,128)(2,1)S(1)} %get-tuple-element.69.refs_1_, bf16[128,4096]{1,0:T(8,128)(2,1)S(1)} %get-tuple-element.58.refs_4_.refs_2_, ...), custom_call_target="tpu_custom_call" | custom-call | tf_op jit(solution)/shard_map/level1_rows96/pallas_call | solution.py:221
  82.2 1.6 %level0_rows64.1.refs_2_ = bf16[64,4096]{1,0:T(8,128)(2,1)S(1)} custom-call(s32[640]{0:T(1024)S(1)} %concatenate.3.meta, bf16[4,256,256]{2,1,0:T(8,128)(2,1)S(1)} %reorder.1.refs_0_.inv, bf16[256,4096]{1,0:T(8,128)(2,1)S(1)} %get-tuple-element.66.refs_1_, bf16[64,4096]{1,0:T(8,128)(2,1)S(1)} %get-tuple-element.53.refs_2_, ...), custom_call_target="tpu_custom_call" | custom-call | tf_op jit(solution)/shard_map/level0_rows64/pallas_call | solution.py:221
  83.8 1.3 collective-permute-start.12
  85.1 2.3 %collective-permute-start.16 = (bf16[48,4096]{1,0:T(8,128)(2,1)S(1)}, bf16[48,4096]{1,0:T(8,128)(2,1)S(1)}, u32[]{:S(2)}, u32[]{:S(2)}) collective-permute-start(bf16[48,4096]{1,0:T(8,128)(2,1)S(1)} %get-tuple-element.64.refs_1_), channel_id=1, source_target_pairs={{0,2},{1,3},{2,0},{3,1},{4,6},{5,7},{6,4},{7,5},{8,10},{9,11},{10,... | collective-permute-start | bytes 1179656 | tf_op jit(solution)/shard_map/ppermute | solution.py:28
  87.4 1.6 %level1_rows64.2 = (bf16[32,4096]{1,0:T(8,128)(2,1)S(1)}, bf16[32,4096]{1,0:T(8,128)(2,1)S(1)}) custom-call(s32[640]{0:T(1024)S(1)} %concatenate.3.meta, bf16[4,256,256]{2,1,0:T(8,128)(2,1)S(1)} %reorder.1.refs_0_.inv, bf16[256,4096]{1,0:T(8,128)(2,1)S(1)} %get-tuple-element.69.refs_1_, bf16[64,4096]{1,0:T(8,128)(2,1)S(1)} %get-tuple-element.54.refs_2_, ...), custom_call_target="tpu_custom_call" | custom-call | tf_op jit(solution)/shard_map/level1_rows64/pallas_call | solution.py:221
  91.0 2.1 %level2_rows160.1.refs_8_ = bf16[160,4096]{1,0:T(8,128)(2,1)S(1)} custom-call(s32[640]{0:T(1024)S(1)} %concatenate.3.meta, bf16[4,256,256]{2,1,0:T(8,128)(2,1)S(1)} %reorder.1.refs_0_.inv, bf16[256,4096]{1,0:T(8,128)(2,1)S(1)} %get-tuple-element.68.refs_1_, bf16[96,4096]{1,0:T(8,128)(2,1)S(1)} %level1_rows96.1.refs_2_, ...), custom_call_target="tpu_custom_call" | custom-call | tf_op jit(solution)/shard_map/level2_rows160/pallas_call | solution.py:221
  93.1 12.7 %collective-permute-done.16.refs_7_ = bf16[48,4096]{1,0:T(8,128)(2,1)S(1)} collective-permute-done((bf16[48,4096]{1,0:T(8,128)(2,1)S(1)}, bf16[48,4096]{1,0:T(8,128)(2,1)S(1)}, u32[]{:S(2)}, u32[]{:S(2)}) %collective-permute-start.16) | collective-permute-done | bytes 393248 | tf_op jit(solution)/shard_map/ppermute | solution.py:28
  105.8 4.6 %collective-permute-done.12.refs_3_ = bf16[64,4096]{1,0:T(8,128)(2,1)S(1)} collective-permute-done((bf16[64,4096]{1,0:T(8,128)(2,1)S(1)}, bf16[64,4096]{1,0:T(8,128)(2,1)S(1)}, u32[]{:S(2)}, u32[]{:S(2)}) %collective-permute-start.12) | collective-permute-done | bytes 524320 | tf_op jit(solution)/shard_map/ppermute | solution.py:28
  110.4 1.6 %level1_rows64.3.refs_2_ = bf16[64,4096]{1,0:T(8,128)(2,1)S(1)} custom-call(s32[640]{0:T(1024)S(1)} %concatenate.3.meta, bf16[4,256,256]{2,1,0:T(8,128)(2,1)S(1)} %reorder.1.refs_0_.inv, bf16[256,4096]{1,0:T(8,128)(2,1)S(1)} %get-tuple-element.69.refs_1_, bf16[64,4096]{1,0:T(8,128)(2,1)S(1)} %level0_rows64.1.refs_2_, ...), custom_call_target="tpu_custom_call" | custom-call | flops 1500000000 | tf_op jit(solution)/shard_map/level1_rows64/pallas_call | solution.py:221
  112.1 1.9 %collective-permute-done.17.refs_3_ = bf16[64,4096]{1,0:T(8,128)(2,1)S(1)} collective-permute-done((bf16[64,4096]{1,0:T(8,128)(2,1)S(1)}, bf16[64,4096]{1,0:T(8,128)(2,1)S(1)}, u32[]{:S(2)}, u32[]{:S(2)}) %collective-permute-start.17) | collective-permute-done | bytes 524320 | tf_op jit(solution)/shard_map/ppermute | solution.py:28
  114.0 1.6 %level2_rows64.1.refs_2_ = bf16[64,4096]{1,0:T(8,128)(2,1)S(1)} custom-call(s32[640]{0:T(1024)S(1)} %concatenate.3.meta, bf16[4,256,256]{2,1,0:T(8,128)(2,1)S(1)} %reorder.1.refs_0_.inv, bf16[256,4096]{1,0:T(8,128)(2,1)S(1)} %get-tuple-element.68.refs_1_, bf16[64,4096]{1,0:T(8,128)(2,1)S(1)} %level1_rows64.3.refs_2_, ...), custom_call_target="tpu_custom_call" | custom-call | tf_op jit(solution)/shard_map/level2_rows64/pallas_call | solution.py:221
  116.2 7.9 %collective-permute-done.18.refs_4_ = bf16[32,4096]{1,0:T(8,128)(2,1)S(1)} collective-permute-done((bf16[32,4096]{1,0:T(8,128)(2,1)S(1)}, bf16[32,4096]{1,0:T(8,128)(2,1)S(1)}, u32[]{:S(2)}, u32[]{:S(2)}) %collective-permute-start.18) | collective-permute-done | bytes 262176 | tf_op jit(solution)/shard_map/ppermute | solution.py:28
  124.1 1.5 %collective-permute-done.20.refs_6_ = bf16[32,4096]{1,0:T(8,128)(2,1)S(1)} collective-permute-done((bf16[32,4096]{1,0:T(8,128)(2,1)S(1)}, bf16[32,4096]{1,0:T(8,128)(2,1)S(1)}, u32[]{:S(2)}, u32[]{:S(2)}) %collective-permute-start.20) | collective-permute-done | bytes 262176 | tf_op jit(solution)/shard_map/ppermute | solution.py:28
  125.6 10.7 %collective-permute-done.21.refs_9_ = bf16[160,4096]{1,0:T(8,128)(2,1)S(1)} collective-permute-done((bf16[160,4096]{1,0:T(8,128)(2,1)S(1)}, bf16[160,4096]{1,0:T(8,128)(2,1)S(1)}, u32[]{:S(2)}, u32[]{:S(2)}) %collective-permute-start.21) | collective-permute-done | bytes 1310752 | tf_op jit(solution)/shard_map/ppermute | solution.py:28
  136.3 5.4 %level3_rows192.1 = (bf16[256,4096]{1,0:T(8,128)(2,1)}, bf16[256,4096]{1,0:T(8,128)(2,1)S(1)}) custom-call(s32[640]{0:T(1024)S(1)} %concatenate.3.meta, bf16[4,256,256]{2,1,0:T(8,128)(2,1)S(1)} %reorder.1.refs_0_.inv, bf16[48,4096]{1,0:T(8,128)(2,1)S(1)} %get-tuple-element.64.refs_1_, bf16[96,4096]{1,0:T(8,128)(2,1)S(1)} %get-tuple-element.65.refs_2_, ...), custom_call_target="tpu_custom_call" | custom-call | tf_op jit(solution)/shard_map/level3_rows192/pallas_call | solution.py:221
  141.7 5.3 %collective-permute-done.22.refs_3_ = bf16[64,4096]{1,0:T(8,128)(2,1)S(1)} collective-permute-done((bf16[64,4096]{1,0:T(8,128)(2,1)S(1)}, bf16[64,4096]{1,0:T(8,128)(2,1)S(1)}, u32[]{:S(2)}, u32[]{:S(2)}) %collective-permute-start.22) | collective-permute-done | bytes 524320 | tf_op jit(solution)/shard_map/ppermute | solution.py:28
  147.0 2.4 %level3_rows64.1 = bf16[256,4096]{1,0:T(8,128)(2,1)} custom-call(s32[640]{0:T(1024)S(1)} %concatenate.3.meta, bf16[4,256,256]{2,1,0:T(8,128)(2,1)S(1)} %reorder.1.refs_0_.inv, bf16[256,4096]{1,0:T(8,128)(2,1)S(1)} %get-tuple-element.82.refs_1_, bf16[64,4096]{1,0:T(8,128)(2,1)S(1)} %level2_rows64.1.refs_2_, ...), custom_call_target="tpu_custom_call", output_to_operand_aliasing={{}: (5, {})} | custom-call | tf_op jit(solution)/shard_map/level3_rows64/pallas_call | solution.py:221
  (46 shorter events, 8.3 us)
Async XLA Ops:
  0.0 35.8 %copy-start.1 = (s32[4,2,32]{2,1,0:T(2,128)S(1)}, s32[4,2,32]{2,1,0:T(2,128)}, u32[]{:S(2)}) copy-start(s32[4,2,32]{2,1,0:T(2,128)} %param.7) | copy-start | bytes 3076
  0.0 35.9 %copy-start.3 = (s32[4,32]{1,0:T(4,128)S(1)}, s32[4,32]{1,0:T(4,128)}, u32[]{:S(2)}) copy-start(s32[4,32]{1,0:T(4,128)} %param.8) | copy-start | bytes 1540
  0.0 35.9 %copy-start.2 = (s32[4,32]{1,0:T(4,128)S(1)}, s32[4,32]{1,0:T(4,128)}, u32[]{:S(2)}) copy-start(s32[4,32]{1,0:T(4,128)} %param.9) | copy-start | bytes 1540
  1.2 38.4 %collective-permute-start.3 = (bf16[80,4096]{1,0:T(8,128)(2,1)S(1)}, bf16[80,4096]{1,0:T(8,128)(2,1)S(1)}, u32[]{:S(2)}, u32[]{:S(2)}) collective-permute-start(bf16[80,4096]{1,0:T(8,128)(2,1)S(1)} %slice.87.refs_1_), channel_id=1, source_target_pairs={{0,16},{8,24},{16,0},{24,8},{1,17},{9,25},{17,1},{25,9},{2,18},{10... | collective-permute-start | bytes 1966088 | tf_op jit(solution)/shard_map/ppermute | solution.py:28
  4.2 31.1 %collective-permute-start.1 = (bf16[80,4096]{1,0:T(8,128)(2,1)S(1)}, bf16[80,4096]{1,0:T(8,128)(2,1)S(1)}, u32[]{:S(2)}, u32[]{:S(2)}) collective-permute-start(bf16[80,4096]{1,0:T(8,128)(2,1)S(1)} %slice.87.refs_1_), channel_id=1, source_target_pairs={{0,4},{1,5},{2,6},{3,7},{4,0},{5,1},{6,2},{7,3},{8,12},{9,13},{10,... | collective-permute-start | bytes 1966088 | tf_op jit(solution)/shard_map/ppermute | solution.py:28
  8.1 30.0 %collective-permute-start = (bf16[64,4096]{1,0:T(8,128)(2,1)S(1)}, bf16[64,4096]{1,0:T(8,128)(2,1)}, u32[]{:S(2)}, u32[]{:S(2)}) collective-permute-start(bf16[64,4096]{1,0:T(8,128)(2,1)S(1)} %get-tuple-element.85.refs_5_), channel_id=1, source_target_pairs={{0,16},{8,24},{16,0},{24,8},{1,17},{9,25},{17,1},{25,9},{2,18},{10... | collective-permute-start | bytes 1572872 | tf_op jit(solution)/shard_map/ppermute | solution.py:28
  9.7 29.9 %collective-permute-start.4 = (bf16[48,4096]{1,0:T(8,128)(2,1)S(1)}, bf16[48,4096]{1,0:T(8,128)(2,1)}, u32[]{:S(2)}, u32[]{:S(2)}) collective-permute-start(bf16[48,4096]{1,0:T(8,128)(2,1)S(1)} %slice.90.refs_2_), channel_id=1, source_target_pairs={{0,16},{8,24},{16,0},{24,8},{1,17},{9,25},{17,1},{25,9},{2,18},{10... | collective-permute-start | bytes 1179656 | tf_op jit(solution)/shard_map/ppermute | solution.py:28
  35.3 19.7 %collective-permute-start.5 = (bf16[80,4096]{1,0:T(8,128)(2,1)S(1)}, bf16[80,4096]{1,0:T(8,128)(2,1)}, u32[]{:S(2)}, u32[]{:S(2)}) collective-permute-start(bf16[80,4096]{1,0:T(8,128)(2,1)S(1)} %collective-permute-done.1.refs_0_), channel_id=1, source_target_pairs={{0,16},{8,24},{16,0},{24,8},{1,17},{9,25},{17,1},{25,9},{2,18},{10... | collective-permute-start | bytes 1966088 | tf_op jit(solution)/shard_map/ppermute | solution.py:28
  35.8 19.2 %collective-permute-start.2 = (bf16[48,4096]{1,0:T(8,128)(2,1)S(1)}, bf16[48,4096]{1,0:T(8,128)(2,1)}, u32[]{:S(2)}, u32[]{:S(2)}) collective-permute-start(bf16[48,4096]{1,0:T(8,128)(2,1)S(1)} %slice.90.refs_2_), channel_id=1, source_target_pairs={{0,4},{1,5},{2,6},{3,7},{4,0},{5,1},{6,2},{7,3},{8,12},{9,13},{10,... | collective-permute-start | bytes 1179656 | tf_op jit(solution)/shard_map/ppermute | solution.py:28
  36.1 1.0 copy-start
  55.0 9.5 %collective-permute-start.6 = (bf16[48,4096]{1,0:T(8,128)(2,1)}, bf16[48,4096]{1,0:T(8,128)(2,1)S(1)}, u32[]{:S(2)}, u32[]{:S(2)}) collective-permute-start(bf16[48,4096]{1,0:T(8,128)(2,1)} %collective-permute-done.2.refs_1_), channel_id=1, source_target_pairs={{0,16},{8,24},{16,0},{24,8},{1,17},{9,25},{17,1},{25,9},{2,18},{10... | collective-permute-start | bytes 1179656 | tf_op jit(solution)/shard_map/ppermute | solution.py:28
  56.6 23.7 %collective-permute-start.8 = (bf16[64,4096]{1,0:T(8,128)(2,1)S(1)}, bf16[64,4096]{1,0:T(8,128)(2,1)S(1)}, u32[]{:S(2)}, u32[]{:S(2)}) collective-permute-start(bf16[64,4096]{1,0:T(8,128)(2,1)S(1)} %get-tuple-element.54.refs_2_), channel_id=1, source_target_pairs={{0,4},{1,5},{2,6},{3,7},{4,0},{5,1},{6,2},{7,3},{8,12},{9,13},{10,... | collective-permute-start | bytes 1572872 | tf_op jit(solution)/shard_map/ppermute | solution.py:28
  64.5 15.8 %collective-permute-start.7 = (bf16[64,4096]{1,0:T(8,128)(2,1)S(1)}, bf16[64,4096]{1,0:T(8,128)(2,1)S(1)}, u32[]{:S(2)}, u32[]{:S(2)}) collective-permute-start(bf16[64,4096]{1,0:T(8,128)(2,1)S(1)} %get-tuple-element.53.refs_2_), channel_id=1, source_target_pairs={{0,16},{8,24},{16,0},{24,8},{1,17},{9,25},{17,1},{25,9},{2,18},{10... | collective-permute-start | bytes 1572872 | tf_op jit(solution)/shard_map/ppermute | solution.py:28
  73.7 2.7 %collective-permute-start.10 = (bf16[48,4096]{1,0:T(8,128)(2,1)S(1)}, bf16[48,4096]{1,0:T(8,128)(2,1)S(1)}, u32[]{:S(2)}, u32[]{:S(2)}) collective-permute-start(bf16[48,4096]{1,0:T(8,128)(2,1)S(1)} %get-tuple-element.61.refs_2_), channel_id=1, source_target_pairs={{0,8},{8,0},{16,24},{24,16},{1,9},{9,1},{17,25},{25,17},{2,10},{10... | collective-permute-start | bytes 1179656 | tf_op jit(solution)/shard_map/ppermute | solution.py:28
  73.8 2.7 %collective-permute-start.9 = (bf16[48,4096]{1,0:T(8,128)(2,1)S(1)}, bf16[48,4096]{1,0:T(8,128)(2,1)S(1)}, u32[]{:S(2)}, u32[]{:S(2)}) collective-permute-start(bf16[48,4096]{1,0:T(8,128)(2,1)S(1)} %get-tuple-element.60.refs_1_), channel_id=1, source_target_pairs={{0,8},{8,0},{16,24},{24,16},{1,9},{9,1},{17,25},{25,17},{2,10},{10... | collective-permute-start | bytes 1179656 | tf_op jit(solution)/shard_map/ppermute | solution.py:28
  74.3 2.1 %collective-permute-start.11 = (bf16[32,4096]{1,0:T(8,128)(2,1)S(1)}, bf16[32,4096]{1,0:T(8,128)(2,1)S(1)}, u32[]{:S(2)}, u32[]{:S(2)}) collective-permute-start(bf16[32,4096]{1,0:T(8,128)(2,1)S(1)} %get-tuple-element.62.refs_3_), channel_id=1, source_target_pairs={{0,8},{8,0},{16,24},{24,16},{1,9},{9,1},{17,25},{25,17},{2,10},{10... | collective-permute-start | bytes 786440 | tf_op jit(solution)/shard_map/ppermute | solution.py:28
  82.1 8.9 %collective-permute-start.13 = (bf16[96,4096]{1,0:T(8,128)(2,1)S(1)}, bf16[96,4096]{1,0:T(8,128)(2,1)S(1)}, u32[]{:S(2)}, u32[]{:S(2)}) collective-permute-start(bf16[96,4096]{1,0:T(8,128)(2,1)S(1)} %level1_rows96.1.refs_2_), channel_id=1, source_target_pairs={{0,8},{8,0},{16,24},{24,16},{1,9},{9,1},{17,25},{25,17},{2,10},{10... | collective-permute-start | bytes 2359304 | tf_op jit(solution)/shard_map/ppermute | solution.py:28
  83.8 26.6 %collective-permute-start.12 = (bf16[64,4096]{1,0:T(8,128)(2,1)S(1)}, bf16[64,4096]{1,0:T(8,128)(2,1)S(1)}, u32[]{:S(2)}, u32[]{:S(2)}) collective-permute-start(bf16[64,4096]{1,0:T(8,128)(2,1)S(1)} %level0_rows64.1.refs_2_), channel_id=1, source_target_pairs={{0,4},{1,5},{2,6},{3,7},{4,0},{5,1},{6,2},{7,3},{8,12},{9,13},{10,... | collective-permute-start | bytes 1572872 | tf_op jit(solution)/shard_map/ppermute | solution.py:28
  85.1 20.7 %collective-permute-start.16 = (bf16[48,4096]{1,0:T(8,128)(2,1)S(1)}, bf16[48,4096]{1,0:T(8,128)(2,1)S(1)}, u32[]{:S(2)}, u32[]{:S(2)}) collective-permute-start(bf16[48,4096]{1,0:T(8,128)(2,1)S(1)} %get-tuple-element.64.refs_1_), channel_id=1, source_target_pairs={{0,2},{1,3},{2,0},{3,1},{4,6},{5,7},{6,4},{7,5},{8,10},{9,11},{10,... | collective-permute-start | bytes 1179656 | tf_op jit(solution)/shard_map/ppermute | solution.py:28
  89.0 1.6 %collective-permute-start.14 = (bf16[32,4096]{1,0:T(8,128)(2,1)S(1)}, bf16[32,4096]{1,0:T(8,128)(2,1)S(1)}, u32[]{:S(2)}, u32[]{:S(2)}) collective-permute-start(bf16[32,4096]{1,0:T(8,128)(2,1)S(1)} %get-tuple-element.75.refs_4_), channel_id=1, source_target_pairs={{0,8},{8,0},{16,24},{24,16},{1,9},{9,1},{17,25},{25,17},{2,10},{10... | collective-permute-start | bytes 786440 | tf_op jit(solution)/shard_map/ppermute | solution.py:28
  89.1 1.9 %collective-permute-start.15 = (bf16[32,4096]{1,0:T(8,128)(2,1)S(1)}, bf16[32,4096]{1,0:T(8,128)(2,1)S(1)}, u32[]{:S(2)}, u32[]{:S(2)}) collective-permute-start(bf16[32,4096]{1,0:T(8,128)(2,1)S(1)} %get-tuple-element.76.refs_6_), channel_id=1, source_target_pairs={{0,8},{8,0},{16,24},{24,16},{1,9},{9,1},{17,25},{25,17},{2,10},{10... | collective-permute-start | bytes 786440 | tf_op jit(solution)/shard_map/ppermute | solution.py:28
  93.0 43.3 %collective-permute-start.21 = (bf16[160,4096]{1,0:T(8,128)(2,1)S(1)}, bf16[160,4096]{1,0:T(8,128)(2,1)S(1)}, u32[]{:S(2)}, u32[]{:S(2)}) collective-permute-start(bf16[160,4096]{1,0:T(8,128)(2,1)S(1)} %level2_rows160.1.refs_8_), channel_id=1, source_target_pairs={{0,2},{1,3},{2,0},{3,1},{4,6},{5,7},{6,4},{7,5},{8,10},{9,11},{10,... | collective-permute-start | bytes 3932168 | tf_op jit(solution)/shard_map/ppermute | solution.py:28
  112.0 2.0 %collective-permute-start.17 = (bf16[64,4096]{1,0:T(8,128)(2,1)S(1)}, bf16[64,4096]{1,0:T(8,128)(2,1)S(1)}, u32[]{:S(2)}, u32[]{:S(2)}) collective-permute-start(bf16[64,4096]{1,0:T(8,128)(2,1)S(1)} %level1_rows64.3.refs_2_), channel_id=1, source_target_pairs={{0,8},{8,0},{16,24},{24,16},{1,9},{9,1},{17,25},{25,17},{2,10},{10... | collective-permute-start | bytes 1572872 | tf_op jit(solution)/shard_map/ppermute | solution.py:28
  115.6 8.4 %collective-permute-start.18 = (bf16[32,4096]{1,0:T(8,128)(2,1)S(1)}, bf16[32,4096]{1,0:T(8,128)(2,1)S(1)}, u32[]{:S(2)}, u32[]{:S(2)}) collective-permute-start(bf16[32,4096]{1,0:T(8,128)(2,1)S(1)} %slice.91.refs_3_), channel_id=1, source_target_pairs={{0,16},{8,24},{16,0},{24,8},{1,17},{9,25},{17,1},{25,9},{2,18},{10... | collective-permute-start | bytes 786440 | tf_op jit(solution)/shard_map/ppermute | solution.py:28
  116.2 30.8 %collective-permute-start.22 = (bf16[64,4096]{1,0:T(8,128)(2,1)S(1)}, bf16[64,4096]{1,0:T(8,128)(2,1)S(1)}, u32[]{:S(2)}, u32[]{:S(2)}) collective-permute-start(bf16[64,4096]{1,0:T(8,128)(2,1)S(1)} %level2_rows64.1.refs_2_), channel_id=1, source_target_pairs={{0,2},{1,3},{2,0},{3,1},{4,6},{5,7},{6,4},{7,5},{8,10},{9,11},{10,... | collective-permute-start | bytes 1572872 | tf_op jit(solution)/shard_map/ppermute | solution.py:28
  116.2 7.9 %collective-permute-start.19 = (bf16[32,4096]{1,0:T(8,128)(2,1)S(1)}, bf16[32,4096]{1,0:T(8,128)(2,1)S(1)}, u32[]{:S(2)}, u32[]{:S(2)}) collective-permute-start(bf16[32,4096]{1,0:T(8,128)(2,1)S(1)} %slice.91.refs_3_), channel_id=1, source_target_pairs={{0,8},{8,0},{16,24},{24,16},{1,9},{9,1},{17,25},{25,17},{2,10},{10... | collective-permute-start | bytes 786440 | tf_op jit(solution)/shard_map/ppermute | solution.py:28
  124.1 1.5 %collective-permute-start.20 = (bf16[32,4096]{1,0:T(8,128)(2,1)S(1)}, bf16[32,4096]{1,0:T(8,128)(2,1)S(1)}, u32[]{:S(2)}, u32[]{:S(2)}) collective-permute-start(bf16[32,4096]{1,0:T(8,128)(2,1)S(1)} %collective-permute-done.18.refs_4_), channel_id=1, source_target_pairs={{0,8},{8,0},{16,24},{24,16},{1,9},{9,1},{17,25},{25,17},{2,10},{10... | collective-permute-start | bytes 786440 | tf_op jit(solution)/shard_map/ppermute | solution.py:28

commit v7 on v6

--- a/solution.py
+++ b/solution.py
@@ -157,15 +157,16 @@
     )
 
 
-def two_level_kernel(meta, inv, *refs, blocks, counts, first_outs, second_outs):
+def two_level_kernel(meta, inv, *refs, blocks, counts, first_outs, second_outs, pairs):
     n = len(counts)
-    ours, theirs, near, far, far_x = refs[:n], refs[n : 2 * n], *refs[2 * n : 2 * n + 3]
-    outs, panel, other_panel, merged = refs[2 * n + 3 : -3], *refs[-3:]
+    ours, theirs, near, near_x = refs[:n], refs[n : 2 * n], *refs[2 * n : 2 * n + 2]
+    outs, panel, other_panel, merged, far, far_x = refs[2 * n + 2 : -5], *refs[-5:]
     stacks = tuple([(ref, 0, count) for ref, count in zip(group, counts)] for group in (ours, theirs))
-    made = list(zip((far, far_x), first_outs))
-    eliminate(meta, inv, other_panel, merged, stacks, [], made, 0, blocks)
+    eliminate(meta, inv, other_panel, merged, stacks, [], list(zip((far, far_x), first_outs)), 0, blocks)
+    held = ((near, far), (near_x, far_x))
     top = tuple([(ref, 0, ref.shape[0])] for ref in (near, far))
-    eliminate(meta, inv, panel, merged, top, [], list(zip(outs, second_outs)), 1, blocks)
+    stacked = [tuple([(ref, low, rows)] for ref in held[i]) for i, low, rows in pairs]
+    eliminate(meta, inv, panel, merged, top, stacked, list(zip(outs, second_outs)), 1, blocks)
 
 
 def run_level(level, meta, held, outs, pairs=(), top=None, keeps=False, part=None, cost=0):
@@ -232,9 +233,9 @@
     )(meta, *arrays, *hidden)
 
 
-def run_two_levels(meta, inv, ours, theirs, near, first_outs, second_outs):
+def run_two_levels(meta, inv, ours, theirs, near, near_x, first_outs, second_outs, pairs):
     width, size = near.shape[1], inv.shape[1]
-    rows = [sum(job[2] for job in dest) for dest in (*first_outs, *second_outs)] + [size]
+    rows = [sum(job[2] for job in dest) for dest in second_outs] + [size]
     vmem = pl.BlockSpec(memory_space=pltpu.VMEM)
     kernel = functools.partial(
         two_level_kernel,
@@ -242,17 +243,23 @@
         counts=tuple(x.shape[0] for x in ours),
         first_outs=first_outs,
         second_outs=second_outs,
+        pairs=pairs,
     )
     return pl.pallas_call(
         kernel,
         out_shape=[jax.ShapeDtypeStruct((n, width), BF16) for n in rows],
-        in_specs=[pl.BlockSpec(memory_space=pltpu.SMEM)] + [vmem] * (2 + 2 * len(ours)),
+        in_specs=[pl.BlockSpec(memory_space=pltpu.SMEM)] + [vmem] * (3 + 2 * len(ours)),
         out_specs=[vmem] * len(rows),
-        scratch_shapes=[pltpu.VMEM((size, width), BF16), pltpu.VMEM((size, width), F32)],
+        scratch_shapes=[
+            pltpu.VMEM((size, width), BF16),
+            pltpu.VMEM((size, width), F32),
+            pltpu.VMEM(near.shape, BF16),
+            pltpu.VMEM(near_x.shape, BF16),
+        ],
         compiler_params=pltpu.CompilerParams(vmem_limit_bytes=30 * 2**20),
         cost_estimate=pl.CostEstimate(flops=0, bytes_accessed=0, transcendentals=0),
         name="level0_level1",
-    )(meta, inv, *ours, *theirs, near)
+    )(meta, inv, *ours, *theirs, near, near_x)
 
 
 def reorder(meta, pivot_inverse):
@@ -331,19 +338,19 @@
     after_z1 = trade(after_1, 1)
     first_z2, first_yz1 = after(first_z2, first_yz1)
     first_yz2 = trade(first_z2, 0)
-    rest_2, first_yz2 = after(rest_2, first_yz2)
-    rest_y2 = trade(rest_2, 0)
-
     e, y, z, yz = (("top", low, eighth) for low in range(0, size, quarter))
     jobs = [[e, (*y[:2], share)], [("top", quarter + share, share), z], [yz]]
-    far, far_x, *head, panel_1 = run_two_levels(
+    jobs.append([(0, 0, eighth), (1, 0, quarter)])
+    *head, next_0, panel_1 = run_two_levels(
         meta,
         inv,
         (first_z1, first_z2),
         (first_yz1, first_yz2),
         near,
+        near_x,
         (tuple(tops), (("top", quarter, quarter),)),
         jobs,
+        ((0, eighth, eighth), (1, 0, quarter)),
     )
     head_c = [trade(x, 2) for x in head]
 
@@ -356,27 +363,16 @@
         top=tuple(sum((rows_of(x) for x in group), []) for group in (head, head_c)),
         keeps=True,
     )
-    rest_y2, after_z1, far_x, lead = after(rest_y2, after_z1, far_x, lead)
-    after_2 = chunk(0, panel_0, rest_2, rest_y2, cost=0)
-    after_z2 = trade(after_2, 1)
-    (next_0,) = run_level(
-        1,
-        meta,
-        (inv, panel_1),
-        [[(0, 0, eighth), (1, 0, quarter)]],
-        pairs=[
-            ([(near, eighth, eighth)], [(far, eighth, eighth)]),
-            (rows_of(near_x), rows_of(far_x)),
-        ],
-    )
     lead_w = trade(lead, 3)
-    after_z1, after_2 = after(after_z1, after_2)
+    after_z1, rest_2, lead = after(after_z1, rest_2, lead)
+    rest_y2 = trade(rest_2, 0)
     next_1 = run_level(
         1,
         meta,
         (inv, panel_1),
         [[(0, 0, eighth)], [(0, eighth, eighth)]],
         pairs=[(rows_of(after_1), rows_of(after_z1))],
+        cost=10**9,
     )
     next_1 = [next_0, *next_1]
     (last_1,) = run_level(
@@ -386,17 +382,18 @@
         [[(i, 0, x.shape[0]) for i, x in enumerate(next_1)]],
         pairs=[(rows_of(x), rows_of(trade(x, 2))) for x in next_1],
     )
+    rest_y2, lead_w, last_1 = after(rest_y2, lead_w, last_1)
+    after_2 = chunk(0, panel_0, rest_2, rest_y2, cost=3 * 10**9)
+    after_z2 = trade(after_2, 1)
     last_w1 = trade(last_1, 3)
-    after_z2, last_1, lead_w = after(after_z2, last_1, lead_w)
-    next_2 = chunk(1, panel_1, after_2, after_z2, cost=15 * 10**8)
-    last_2 = chunk(2, panel_2, next_2, trade(next_2, 2))
-    last_w2 = trade(last_2, 3)
-    lead_w, last_2 = after(lead_w, last_2)
     tops_w = lead_w[:eighth]
     tops_wc = trade(tops_w, 2)
     tops_wy = trade(tops_w, 0)
+    after_z2, tops_wy = after(after_z2, tops_wy)
     tops_wyc = trade(tops_wy, 2)
-
+    next_2 = chunk(1, panel_1, after_2, after_z2, cost=0)
+    last_2 = chunk(2, panel_2, next_2, trade(next_2, 2))
+    last_w2 = trade(last_2, 3)
     more = lead.shape[0] - eighth
     tops = [(lead, 0, share), (others, 0, share), (lead, share, share)]
     tops += [(others, share * i, share) for i in range(1, 6)]
@@ -411,6 +408,7 @@
         pairs=[([(lead, eighth, more)], [(lead_w, eighth, more)]), (rows_of(last_1), rows_of(last_w1))],
         keeps=True,
         part=(all_rows, 0, None),
+        cost=5 * 10**9,
     )
     return chunk(3, panel_3, last_2, last_w2, part=(all_rows, all_rows // quarter - 1, out))
 

time: 150 us -> 157 us (1.047)
  local copies, waits for them, and re-layouts: 4.65 us -> 9.75 us
  starting transfers between devices: 17.5 us -> 21.3 us
  waiting for transfers between devices: 92 us -> 90.3 us
    ppermute x23, starting transfers between devices: 17.5 us -> 21.3 us  [trade(): lax.ppermute(block, axis, [(i, i ^ flip) for i in range(lax.axis_size(axi...]
    add x4, local copies, waits for them, and re-layouts: 0.02 us -> 2.13 us  [make_meta(): jnp.zeros((blocks,), jnp.int32) + shift]
    pallas_call x10 -> x9, Pallas kernels: 26.5 us -> 24.8 us  [run_level(): pl.pallas_call(kernel, grid=(1,) if part is not None else (), out_shape=s...]
    ppermute x23, waiting for transfers between devices: 92 us -> 90.3 us  [trade(): lax.ppermute(block, axis, [(i, i ^ flip) for i in range(lax.axis_size(axi...]
  transfers between devices with their start and end apart: 23 -> 23, of which waited for: 15 -> 13; matrix products, arithmetic and copies ran while one was open for 2% -> 6% of each run, Pallas kernels for 21% -> 20%
where the time goes in v7:
time: 157 us; the launch traced here: 156 us
  waiting for transfers between devices  90.3 us (58%)
  Pallas kernels  33.6 us (21%)
  starting transfers between devices  21.3 us (14%)
  local copies, waits for them, and re-layouts  9.75 us (6%)
    ppermute x23, waiting for transfers between devices, trade(): lax.ppermute(block, axis, [(i, i ^ flip) for i in range(lax.axis_size(axi...  90.3 us
    pallas_call x9, Pallas kernels, run_level(): pl.pallas_call(kernel, grid=(1,) if part is not None else (), out_shape=s...  24.8 us
    ppermute x23, starting transfers between devices, trade(): lax.ppermute(block, axis, [(i, i ^ flip) for i in range(lax.axis_size(axi...  21.3 us
    pallas_call x1, Pallas kernels, run_two_levels(): pl.pallas_call(kernel, out_shape=[jax.ShapeDtypeStruct((n, width), BF16)...  7.97 us
  transfers between devices with their start and end apart: 23, of which 13 were waited for; matrix products, arithmetic and copies ran while one was open for 6% of the time, Pallas kernels for 20%

profile of v7, /device:TPU:0, one launch (start us, length us, event | category | flops | bytes accessed | tf_op | source)
XLA Modules:
  0.0 156.3 jit_solution(11747855534262482715)
XLA Ops:
  0.0 1.1 slice.87.refs_1_
  1.1 3.0 %collective-permute-start.2 = (bf16[80,4096]{1,0:T(8,128)(2,1)S(1)}, bf16[80,4096]{1,0:T(8,128)(2,1)S(1)}, u32[]{:S(2)}, u32[]{:S(2)}) collective-permute-start(bf16[80,4096]{1,0:T(8,128)(2,1)S(1)} %slice.87.refs_1_), channel_id=1, source_target_pairs={{0,16},{8,24},{16,0},{24,8},{1,17},{9,25},{17,1},{25,9},{2,18},{10... | collective-permute-start | bytes 1966088 | tf_op jit(solution)/shard_map/ppermute | solution.py:28
  4.2 2.6 %collective-permute-start = (bf16[80,4096]{1,0:T(8,128)(2,1)S(1)}, bf16[80,4096]{1,0:T(8,128)(2,1)S(1)}, u32[]{:S(2)}, u32[]{:S(2)}) collective-permute-start(bf16[80,4096]{1,0:T(8,128)(2,1)S(1)} %slice.87.refs_1_), channel_id=1, source_target_pairs={{0,4},{1,5},{2,6},{3,7},{4,0},{5,1},{6,2},{7,3},{8,12},{9,13},{10,... | collective-permute-start | bytes 1966088 | tf_op jit(solution)/shard_map/ppermute | solution.py:28
  6.8 2.1 %fusion.8 = (bf16[64,4096]{1,0:T(8,128)(2,1)}, bf16[64,4096]{1,0:T(8,128)(2,1)S(1)}) fusion(bf16[256,4096]{1,0:T(8,128)(2,1)} %param.5), kind=kLoop, calls=%fused_computation.24 | loop fusion | bytes 2097152 | tf_op jit(solution)/shard_map/slice | solution.py:317
  10.4 1.6 %collective-permute-start.3 = (bf16[48,4096]{1,0:T(8,128)(2,1)S(1)}, bf16[48,4096]{1,0:T(8,128)(2,1)}, u32[]{:S(2)}, u32[]{:S(2)}) collective-permute-start(bf16[48,4096]{1,0:T(8,128)(2,1)S(1)} %slice.88.refs_2_), channel_id=1, source_target_pairs={{0,16},{8,24},{16,0},{24,8},{1,17},{9,25},{17,1},{25,9},{2,18},{10... | collective-permute-start | bytes 1179656 | tf_op jit(solution)/shard_map/ppermute | solution.py:28
  12.0 23.4 %collective-permute-done.refs_0_ = bf16[80,4096]{1,0:T(8,128)(2,1)S(1)} collective-permute-done((bf16[80,4096]{1,0:T(8,128)(2,1)S(1)}, bf16[80,4096]{1,0:T(8,128)(2,1)S(1)}, u32[]{:S(2)}, u32[]{:S(2)}) %collective-permute-start) | collective-permute-done | bytes 655392 | tf_op jit(solution)/shard_map/ppermute | solution.py:28
  36.9 1.5 slice_bitcast_fusion
  41.4 1.0 copy-done
  43.4 4.8 %level0_rows256.1 = (bf16[128,4096]{1,0:T(8,128)(2,1)S(1)}, bf16[64,4096]{1,0:T(8,128)(2,1)S(1)}, bf16[64,4096]{1,0:T(8,128)(2,1)S(1)}, bf16[256,4096]{1,0:T(8,128)(2,1)S(1)}) custom-call(s32[640]{0:T(1024)S(1)} %concatenate.3.meta, bf16[4,256,256]{2,1,0:T(8,128)(2,1)S(1)} %reorder.1.refs_0_.inv, bf16[80,4096]{1,0:T(8,128)(2,1)S(1)} %slice.87.refs_1_, ...), custom_call_target="tpu_custom_call" | custom-call | tf_op jit(solution)/shard_map/level0_rows256/pallas_call | solution.py:222
  48.2 7.3 %collective-permute-done.1.refs_1_ = bf16[48,4096]{1,0:T(8,128)(2,1)} collective-permute-done((bf16[48,4096]{1,0:T(8,128)(2,1)S(1)}, bf16[48,4096]{1,0:T(8,128)(2,1)}, u32[]{:S(2)}, u32[]{:S(2)}) %collective-permute-start.1) | collective-permute-done | bytes 393248 | tf_op jit(solution)/shard_map/ppermute | solution.py:28
  55.5 1.5 collective-permute-start.7
  57.1 7.7 %collective-permute-done.7.refs_3_ = bf16[48,4096]{1,0:T(8,128)(2,1)S(1)} collective-permute-done((bf16[48,4096]{1,0:T(8,128)(2,1)}, bf16[48,4096]{1,0:T(8,128)(2,1)S(1)}, u32[]{:S(2)}, u32[]{:S(2)}) %collective-permute-start.7) | collective-permute-done | bytes 393248 | tf_op jit(solution)/shard_map/ppermute | solution.py:28
  64.8 8.0 %level0_level1.1 = (bf16[48,4096]{1,0:T(8,128)(2,1)S(1)}, bf16[48,4096]{1,0:T(8,128)(2,1)S(1)}, bf16[32,4096]{1,0:T(8,128)(2,1)S(1)}, bf16[96,4096]{1,0:T(8,128)(2,1)S(1)}, bf16[256,4096]{1,0:T(8,128)(2,1)S(1)}) custom-call(s32[640]{0:T(1024)S(1)} %concatenate.3.meta, bf16[4,256,256]{2,1,0:T(8,128)(2,1)S(1)} %reorder.1.refs_0_.inv, ...), custom_call_target="tpu_custom_call" | custom-call | tf_op jit(solution)/shard_map/level0_level1/pallas_call | solution.py:248
  73.8 1.6 %collective-permute-done.10.refs_6_ = bf16[32,4096]{1,0:T(8,128)(2,1)S(1)} collective-permute-done((bf16[32,4096]{1,0:T(8,128)(2,1)S(1)}, bf16[32,4096]{1,0:T(8,128)(2,1)S(1)}, u32[]{:S(2)}, u32[]{:S(2)}) %collective-permute-start.10) | collective-permute-done | bytes 262176 | tf_op jit(solution)/shard_map/ppermute | solution.py:28
  75.5 3.7 %level2_rows144.1 = (bf16[48,4096]{1,0:T(8,128)(2,1)S(1)}, bf16[96,4096]{1,0:T(8,128)(2,1)S(1)}, bf16[256,4096]{1,0:T(8,128)(2,1)S(1)}) custom-call(s32[640]{0:T(1024)S(1)} %concatenate.3.meta, bf16[4,256,256]{2,1,0:T(8,128)(2,1)S(1)} %reorder.1.refs_0_.inv, bf16[48,4096]{1,0:T(8,128)(2,1)S(1)} %get-tuple-element.52.refs_1_, ...), custom_call_target="tpu_custom_call" | custom-call | tf_op jit(solution)/shard_map/level2_rows144/pallas_call | solution.py:222
  79.2 1.6 %collective-permute-done.5.refs_3_ = bf16[64,4096]{1,0:T(8,128)(2,1)S(1)} collective-permute-done((bf16[64,4096]{1,0:T(8,128)(2,1)S(1)}, bf16[64,4096]{1,0:T(8,128)(2,1)S(1)}, u32[]{:S(2)}, u32[]{:S(2)}) %collective-permute-start.5) | collective-permute-done | bytes 524320 | tf_op jit(solution)/shard_map/ppermute | solution.py:28
  81.3 1.6 %level1_rows64.2 = (bf16[32,4096]{1,0:T(8,128)(2,1)S(1)}, bf16[32,4096]{1,0:T(8,128)(2,1)S(1)}) custom-call(s32[640]{0:T(1024)S(1)} %concatenate.3.meta, bf16[4,256,256]{2,1,0:T(8,128)(2,1)S(1)} %reorder.1.refs_0_.inv, bf16[256,4096]{1,0:T(8,128)(2,1)S(1)} %get-tuple-element.61.refs_1_, bf16[64,4096]{1,0:T(8,128)(2,1)S(1)} %get-tuple-element.44.refs_2_, ...), custom_call_target="tpu_custom_call" | custom-call | flops 1000000000 | tf_op jit(solution)/shard_map/level1_rows64/pallas_call | solution.py:222
  84.8 2.1 %level2_rows160.1.refs_8_ = bf16[160,4096]{1,0:T(8,128)(2,1)S(1)} custom-call(s32[640]{0:T(1024)S(1)} %concatenate.3.meta, bf16[4,256,256]{2,1,0:T(8,128)(2,1)S(1)} %reorder.1.refs_0_.inv, bf16[256,4096]{1,0:T(8,128)(2,1)S(1)} %get-tuple-element.59.refs_1_, bf16[96,4096]{1,0:T(8,128)(2,1)S(1)} %get-tuple-element.60.refs_2_, ...), custom_call_target="tpu_custom_call" | custom-call | tf_op jit(solution)/shard_map/level2_rows160/pallas_call | solution.py:222
  86.9 4.8 %collective-permute-done.12.refs_7_ = bf16[48,4096]{1,0:T(8,128)(2,1)S(1)} collective-permute-done((bf16[48,4096]{1,0:T(8,128)(2,1)S(1)}, bf16[48,4096]{1,0:T(8,128)(2,1)S(1)}, u32[]{:S(2)}, u32[]{:S(2)}) %collective-permute-start.12) | collective-permute-done | bytes 393248 | tf_op jit(solution)/shard_map/ppermute | solution.py:28
  91.7 2.3 %collective-permute-done.11.refs_3_ = bf16[64,4096]{1,0:T(8,128)(2,1)S(1)} collective-permute-done((bf16[64,4096]{1,0:T(8,128)(2,1)S(1)}, bf16[64,4096]{1,0:T(8,128)(2,1)S(1)}, u32[]{:S(2)}, u32[]{:S(2)}) %collective-permute-start.11) | collective-permute-done | bytes 524320 | tf_op jit(solution)/shard_map/ppermute | solution.py:28
  94.0 1.6 %level0_rows64.1.refs_2_ = bf16[64,4096]{1,0:T(8,128)(2,1)S(1)} custom-call(s32[640]{0:T(1024)S(1)} %concatenate.3.meta, bf16[4,256,256]{2,1,0:T(8,128)(2,1)S(1)} %reorder.1.refs_0_.inv, bf16[256,4096]{1,0:T(8,128)(2,1)S(1)} %get-tuple-element.66.refs_1_, bf16[64,4096]{1,0:T(8,128)(2,1)S(1)} %copy-done.1, bf16[64,4096]{1,0:T(8,128)(2,1)S(1)} %collective-permute-done.11.refs_3_), custom_call_target="tpu_custom_call" | custom-call | flops 3000000000 | tf_op jit(solution)/shard_map/level0_rows64/pallas_call | solution.py:222
  95.7 3.0 %collective-permute-start.16 = (bf16[64,4096]{1,0:T(8,128)(2,1)S(1)}, bf16[64,4096]{1,0:T(8,128)(2,1)S(1)}, u32[]{:S(2)}, u32[]{:S(2)}) collective-permute-start(bf16[64,4096]{1,0:T(8,128)(2,1)S(1)} %level0_rows64.1.refs_2_), channel_id=1, source_target_pairs={{0,4},{1,5},{2,6},{3,7},{4,0},{5,1},{6,2},{7,3},{8,12},{9,13},{10,... | collective-permute-start | bytes 1572872 | tf_op jit(solution)/shard_map/ppermute | solution.py:28
  98.7 1.6 %collective-permute-start.17 = (bf16[32,4096]{1,0:T(8,128)(2,1)S(1)}, bf16[32,4096]{1,0:T(8,128)(2,1)S(1)}, u32[]{:S(2)}, u32[]{:S(2)}) collective-permute-start(bf16[32,4096]{1,0:T(8,128)(2,1)S(1)} %slice.91.refs_3_), channel_id=1, source_target_pairs={{0,16},{8,24},{16,0},{24,8},{1,17},{9,25},{17,1},{25,9},{2,18},{10... | collective-permute-start | bytes 786440 | tf_op jit(solution)/shard_map/ppermute | solution.py:28
  100.3 5.4 %collective-permute-done.17.refs_4_ = bf16[32,4096]{1,0:T(8,128)(2,1)S(1)} collective-permute-done((bf16[32,4096]{1,0:T(8,128)(2,1)S(1)}, bf16[32,4096]{1,0:T(8,128)(2,1)S(1)}, u32[]{:S(2)}, u32[]{:S(2)}) %collective-permute-start.17) | collective-permute-done | bytes 262176 | tf_op jit(solution)/shard_map/ppermute | solution.py:28
  105.6 26.6 %collective-permute-done.16.refs_3_ = bf16[64,4096]{1,0:T(8,128)(2,1)S(1)} collective-permute-done((bf16[64,4096]{1,0:T(8,128)(2,1)S(1)}, bf16[64,4096]{1,0:T(8,128)(2,1)S(1)}, u32[]{:S(2)}, u32[]{:S(2)}) %collective-permute-start.16) | collective-permute-done | bytes 524320 | tf_op jit(solution)/shard_map/ppermute | solution.py:28
  132.3 1.6 %level1_rows64.3.refs_2_ = bf16[64,4096]{1,0:T(8,128)(2,1)S(1)} custom-call(s32[640]{0:T(1024)S(1)} %concatenate.3.meta, bf16[4,256,256]{2,1,0:T(8,128)(2,1)S(1)} %reorder.1.refs_0_.inv, bf16[256,4096]{1,0:T(8,128)(2,1)S(1)} %get-tuple-element.61.refs_1_, bf16[64,4096]{1,0:T(8,128)(2,1)S(1)} %level0_rows64.1.refs_2_, ...), custom_call_target="tpu_custom_call" | custom-call | tf_op jit(solution)/shard_map/level1_rows64/pallas_call | solution.py:222
  134.5 1.3 collective-permute-done.21.refs_3_
  135.9 1.6 %level2_rows64.1.refs_2_ = bf16[64,4096]{1,0:T(8,128)(2,1)S(1)} custom-call(s32[640]{0:T(1024)S(1)} %concatenate.3.meta, bf16[4,256,256]{2,1,0:T(8,128)(2,1)S(1)} %reorder.1.refs_0_.inv, bf16[256,4096]{1,0:T(8,128)(2,1)S(1)} %get-tuple-element.59.refs_1_, bf16[64,4096]{1,0:T(8,128)(2,1)S(1)} %level1_rows64.3.refs_2_, ...), custom_call_target="tpu_custom_call" | custom-call | tf_op jit(solution)/shard_map/level2_rows64/pallas_call | solution.py:222
  137.5 4.2 %collective-permute-start.22 = (bf16[64,4096]{1,0:T(8,128)(2,1)S(1)}, bf16[64,4096]{1,0:T(8,128)(2,1)S(1)}, u32[]{:S(2)}, u32[]{:S(2)}) collective-permute-start(bf16[64,4096]{1,0:T(8,128)(2,1)S(1)} %level2_rows64.1.refs_2_), channel_id=1, source_target_pairs={{0,2},{1,3},{2,0},{3,1},{4,6},{5,7},{6,4},{7,5},{8,10},{9,11},{10,... | collective-permute-start | bytes 1572872 | tf_op jit(solution)/shard_map/ppermute | solution.py:28
  141.7 5.4 %level3_rows192.1 = (bf16[256,4096]{1,0:T(8,128)(2,1)}, bf16[256,4096]{1,0:T(8,128)(2,1)S(1)}) custom-call(s32[640]{0:T(1024)S(1)} %concatenate.3.meta, bf16[4,256,256]{2,1,0:T(8,128)(2,1)S(1)} %reorder.1.refs_0_.inv, bf16[48,4096]{1,0:T(8,128)(2,1)S(1)} %get-tuple-element.56.refs_1_, bf16[96,4096]{1,0:T(8,128)(2,1)S(1)} %get-tuple-element.57.refs_2_, ...), custom_call_target="tpu_custom_call" | custom-call | flops 5000000000 | tf_op jit(solution)/shard_map/level3_rows192/pallas_call | solution.py:222
  147.1 6.8 %collective-permute-done.22.refs_3_ = bf16[64,4096]{1,0:T(8,128)(2,1)S(1)} collective-permute-done((bf16[64,4096]{1,0:T(8,128)(2,1)S(1)}, bf16[64,4096]{1,0:T(8,128)(2,1)S(1)}, u32[]{:S(2)}, u32[]{:S(2)}) %collective-permute-start.22) | collective-permute-done | bytes 524320 | tf_op jit(solution)/shard_map/ppermute | solution.py:28
  153.9 2.4 %level3_rows64.1 = bf16[256,4096]{1,0:T(8,128)(2,1)} custom-call(s32[640]{0:T(1024)S(1)} %concatenate.3.meta, bf16[4,256,256]{2,1,0:T(8,128)(2,1)S(1)} %reorder.1.refs_0_.inv, bf16[256,4096]{1,0:T(8,128)(2,1)S(1)} %get-tuple-element.70.refs_1_, bf16[64,4096]{1,0:T(8,128)(2,1)S(1)} %level2_rows64.1.refs_2_, ...), custom_call_target="tpu_custom_call", output_to_operand_aliasing={{}: (5, {})} | custom-call | tf_op jit(solution)/shard_map/level3_rows64/pallas_call | solution.py:222
  (43 shorter events, 11.2 us)
Async XLA Ops:
  0.0 35.8 %copy-start.2 = (s32[4,2,32]{2,1,0:T(2,128)S(1)}, s32[4,2,32]{2,1,0:T(2,128)}, u32[]{:S(2)}) copy-start(s32[4,2,32]{2,1,0:T(2,128)} %param.7) | copy-start | bytes 3076
  1.1 42.2 %collective-permute-start.2 = (bf16[80,4096]{1,0:T(8,128)(2,1)S(1)}, bf16[80,4096]{1,0:T(8,128)(2,1)S(1)}, u32[]{:S(2)}, u32[]{:S(2)}) collective-permute-start(bf16[80,4096]{1,0:T(8,128)(2,1)S(1)} %slice.87.refs_1_), channel_id=1, source_target_pairs={{0,16},{8,24},{16,0},{24,8},{1,17},{9,25},{17,1},{25,9},{2,18},{10... | collective-permute-start | bytes 1966088 | tf_op jit(solution)/shard_map/ppermute | solution.py:28
  4.2 31.1 %collective-permute-start = (bf16[80,4096]{1,0:T(8,128)(2,1)S(1)}, bf16[80,4096]{1,0:T(8,128)(2,1)S(1)}, u32[]{:S(2)}, u32[]{:S(2)}) collective-permute-start(bf16[80,4096]{1,0:T(8,128)(2,1)S(1)} %slice.87.refs_1_), channel_id=1, source_target_pairs={{0,4},{1,5},{2,6},{3,7},{4,0},{5,1},{6,2},{7,3},{8,12},{9,13},{10,... | collective-permute-start | bytes 1966088 | tf_op jit(solution)/shard_map/ppermute | solution.py:28
  8.8 34.5 %collective-permute-start.4 = (bf16[64,4096]{1,0:T(8,128)(2,1)S(1)}, bf16[64,4096]{1,0:T(8,128)(2,1)}, u32[]{:S(2)}, u32[]{:S(2)}) collective-permute-start(bf16[64,4096]{1,0:T(8,128)(2,1)S(1)} %get-tuple-element.74.refs_5_), channel_id=1, source_target_pairs={{0,16},{8,24},{16,0},{24,8},{1,17},{9,25},{17,1},{25,9},{2,18},{10... | collective-permute-start | bytes 1572872 | tf_op jit(solution)/shard_map/ppermute | solution.py:28
  10.4 33.0 %collective-permute-start.3 = (bf16[48,4096]{1,0:T(8,128)(2,1)S(1)}, bf16[48,4096]{1,0:T(8,128)(2,1)}, u32[]{:S(2)}, u32[]{:S(2)}) collective-permute-start(bf16[48,4096]{1,0:T(8,128)(2,1)S(1)} %slice.88.refs_2_), channel_id=1, source_target_pairs={{0,16},{8,24},{16,0},{24,8},{1,17},{9,25},{17,1},{25,9},{2,18},{10... | collective-permute-start | bytes 1179656 | tf_op jit(solution)/shard_map/ppermute | solution.py:28
  35.3 20.2 %collective-permute-start.6 = (bf16[80,4096]{1,0:T(8,128)(2,1)S(1)}, bf16[80,4096]{1,0:T(8,128)(2,1)S(1)}, u32[]{:S(2)}, u32[]{:S(2)}) collective-permute-start(bf16[80,4096]{1,0:T(8,128)(2,1)S(1)} %collective-permute-done.refs_0_), channel_id=1, source_target_pairs={{0,16},{8,24},{16,0},{24,8},{1,17},{9,25},{17,1},{25,9},{2,18},{10... | collective-permute-start | bytes 1966088 | tf_op jit(solution)/shard_map/ppermute | solution.py:28
  36.4 19.1 %collective-permute-start.1 = (bf16[48,4096]{1,0:T(8,128)(2,1)S(1)}, bf16[48,4096]{1,0:T(8,128)(2,1)}, u32[]{:S(2)}, u32[]{:S(2)}) collective-permute-start(bf16[48,4096]{1,0:T(8,128)(2,1)S(1)} %slice.88.refs_2_), channel_id=1, source_target_pairs={{0,4},{1,5},{2,6},{3,7},{4,0},{5,1},{6,2},{7,3},{8,12},{9,13},{10,... | collective-permute-start | bytes 1179656 | tf_op jit(solution)/shard_map/ppermute | solution.py:28
  41.4 1.0 copy-start
  55.5 9.2 %collective-permute-start.7 = (bf16[48,4096]{1,0:T(8,128)(2,1)}, bf16[48,4096]{1,0:T(8,128)(2,1)S(1)}, u32[]{:S(2)}, u32[]{:S(2)}) collective-permute-start(bf16[48,4096]{1,0:T(8,128)(2,1)} %collective-permute-done.1.refs_1_), channel_id=1, source_target_pairs={{0,16},{8,24},{16,0},{24,8},{1,17},{9,25},{17,1},{25,9},{2,18},{10... | collective-permute-start | bytes 1179656 | tf_op jit(solution)/shard_map/ppermute | solution.py:28
  57.1 23.7 %collective-permute-start.5 = (bf16[64,4096]{1,0:T(8,128)(2,1)S(1)}, bf16[64,4096]{1,0:T(8,128)(2,1)S(1)}, u32[]{:S(2)}, u32[]{:S(2)}) collective-permute-start(bf16[64,4096]{1,0:T(8,128)(2,1)S(1)} %get-tuple-element.44.refs_2_), channel_id=1, source_target_pairs={{0,4},{1,5},{2,6},{3,7},{4,0},{5,1},{6,2},{7,3},{8,12},{9,13},{10,... | collective-permute-start | bytes 1572872 | tf_op jit(solution)/shard_map/ppermute | solution.py:28
  72.7 8.0 %copy-start.1 = (bf16[64,4096]{1,0:T(8,128)(2,1)S(1)}, bf16[64,4096]{1,0:T(8,128)(2,1)}, u32[]{:S(2)}) copy-start(bf16[64,4096]{1,0:T(8,128)(2,1)} %get-tuple-element.58.refs_2_) | copy-start | bytes 1572868
  72.8 2.7 %collective-permute-start.8 = (bf16[48,4096]{1,0:T(8,128)(2,1)S(1)}, bf16[48,4096]{1,0:T(8,128)(2,1)S(1)}, u32[]{:S(2)}, u32[]{:S(2)}) collective-permute-start(bf16[48,4096]{1,0:T(8,128)(2,1)S(1)} %get-tuple-element.52.refs_1_), channel_id=1, source_target_pairs={{0,8},{8,0},{16,24},{24,16},{1,9},{9,1},{17,25},{25,17},{2,10},{10... | collective-permute-start | bytes 1179656 | tf_op jit(solution)/shard_map/ppermute | solution.py:28
  72.8 2.7 %collective-permute-start.9 = (bf16[48,4096]{1,0:T(8,128)(2,1)S(1)}, bf16[48,4096]{1,0:T(8,128)(2,1)S(1)}, u32[]{:S(2)}, u32[]{:S(2)}) collective-permute-start(bf16[48,4096]{1,0:T(8,128)(2,1)S(1)} %get-tuple-element.53.refs_2_), channel_id=1, source_target_pairs={{0,8},{8,0},{16,24},{24,16},{1,9},{9,1},{17,25},{25,17},{2,10},{10... | collective-permute-start | bytes 1179656 | tf_op jit(solution)/shard_map/ppermute | solution.py:28
  73.3 2.1 %collective-permute-start.10 = (bf16[32,4096]{1,0:T(8,128)(2,1)S(1)}, bf16[32,4096]{1,0:T(8,128)(2,1)S(1)}, u32[]{:S(2)}, u32[]{:S(2)}) collective-permute-start(bf16[32,4096]{1,0:T(8,128)(2,1)S(1)} %get-tuple-element.54.refs_3_), channel_id=1, source_target_pairs={{0,8},{8,0},{16,24},{24,16},{1,9},{9,1},{17,25},{25,17},{2,10},{10... | collective-permute-start | bytes 786440 | tf_op jit(solution)/shard_map/ppermute | solution.py:28
  73.4 11.4 %collective-permute-start.13 = (bf16[96,4096]{1,0:T(8,128)(2,1)S(1)}, bf16[96,4096]{1,0:T(8,128)(2,1)S(1)}, u32[]{:S(2)}, u32[]{:S(2)}) collective-permute-start(bf16[96,4096]{1,0:T(8,128)(2,1)S(1)} %get-tuple-element.60.refs_2_), channel_id=1, source_target_pairs={{0,8},{8,0},{16,24},{24,16},{1,9},{9,1},{17,25},{25,17},{2,10},{10... | collective-permute-start | bytes 2359304 | tf_op jit(solution)/shard_map/ppermute | solution.py:28
  80.8 13.3 %collective-permute-start.11 = (bf16[64,4096]{1,0:T(8,128)(2,1)S(1)}, bf16[64,4096]{1,0:T(8,128)(2,1)S(1)}, u32[]{:S(2)}, u32[]{:S(2)}) collective-permute-start(bf16[64,4096]{1,0:T(8,128)(2,1)S(1)} %copy-done.1), channel_id=1, source_target_pairs={{0,16},{8,24},{16,0},{24,8},{1,17},{9,25},{17,1},{25,9},{2,18},{10... | collective-permute-start | bytes 1572872 | tf_op jit(solution)/shard_map/ppermute | solution.py:28
  81.2 10.5 %collective-permute-start.12 = (bf16[48,4096]{1,0:T(8,128)(2,1)S(1)}, bf16[48,4096]{1,0:T(8,128)(2,1)S(1)}, u32[]{:S(2)}, u32[]{:S(2)}) collective-permute-start(bf16[48,4096]{1,0:T(8,128)(2,1)S(1)} %get-tuple-element.56.refs_1_), channel_id=1, source_target_pairs={{0,2},{1,3},{2,0},{3,1},{4,6},{5,7},{6,4},{7,5},{8,10},{9,11},{10,... | collective-permute-start | bytes 1179656 | tf_op jit(solution)/shard_map/ppermute | solution.py:28
  82.9 1.6 %collective-permute-start.14 = (bf16[32,4096]{1,0:T(8,128)(2,1)S(1)}, bf16[32,4096]{1,0:T(8,128)(2,1)S(1)}, u32[]{:S(2)}, u32[]{:S(2)}) collective-permute-start(bf16[32,4096]{1,0:T(8,128)(2,1)S(1)} %get-tuple-element.63.refs_4_), channel_id=1, source_target_pairs={{0,8},{8,0},{16,24},{24,16},{1,9},{9,1},{17,25},{25,17},{2,10},{10... | collective-permute-start | bytes 786440 | tf_op jit(solution)/shard_map/ppermute | solution.py:28
  82.9 1.9 %collective-permute-start.15 = (bf16[32,4096]{1,0:T(8,128)(2,1)S(1)}, bf16[32,4096]{1,0:T(8,128)(2,1)S(1)}, u32[]{:S(2)}, u32[]{:S(2)}) collective-permute-start(bf16[32,4096]{1,0:T(8,128)(2,1)S(1)} %get-tuple-element.64.refs_6_), channel_id=1, source_target_pairs={{0,8},{8,0},{16,24},{24,16},{1,9},{9,1},{17,25},{25,17},{2,10},{10... | collective-permute-start | bytes 786440 | tf_op jit(solution)/shard_map/ppermute | solution.py:28
  94.0 47.6 %collective-permute-start.20 = (bf16[160,4096]{1,0:T(8,128)(2,1)S(1)}, bf16[160,4096]{1,0:T(8,128)(2,1)S(1)}, u32[]{:S(2)}, u32[]{:S(2)}) collective-permute-start(bf16[160,4096]{1,0:T(8,128)(2,1)S(1)} %level2_rows160.1.refs_8_), channel_id=1, source_target_pairs={{0,2},{1,3},{2,0},{3,1},{4,6},{5,7},{6,4},{7,5},{8,10},{9,11},{10,... | collective-permute-start | bytes 3932168 | tf_op jit(solution)/shard_map/ppermute | solution.py:28
  95.7 36.6 %collective-permute-start.16 = (bf16[64,4096]{1,0:T(8,128)(2,1)S(1)}, bf16[64,4096]{1,0:T(8,128)(2,1)S(1)}, u32[]{:S(2)}, u32[]{:S(2)}) collective-permute-start(bf16[64,4096]{1,0:T(8,128)(2,1)S(1)} %level0_rows64.1.refs_2_), channel_id=1, source_target_pairs={{0,4},{1,5},{2,6},{3,7},{4,0},{5,1},{6,2},{7,3},{8,12},{9,13},{10,... | collective-permute-start | bytes 1572872 | tf_op jit(solution)/shard_map/ppermute | solution.py:28
  98.7 7.0 %collective-permute-start.17 = (bf16[32,4096]{1,0:T(8,128)(2,1)S(1)}, bf16[32,4096]{1,0:T(8,128)(2,1)S(1)}, u32[]{:S(2)}, u32[]{:S(2)}) collective-permute-start(bf16[32,4096]{1,0:T(8,128)(2,1)S(1)} %slice.91.refs_3_), channel_id=1, source_target_pairs={{0,16},{8,24},{16,0},{24,8},{1,17},{9,25},{17,1},{25,9},{2,18},{10... | collective-permute-start | bytes 786440 | tf_op jit(solution)/shard_map/ppermute | solution.py:28
  133.9 2.0 %collective-permute-start.21 = (bf16[64,4096]{1,0:T(8,128)(2,1)S(1)}, bf16[64,4096]{1,0:T(8,128)(2,1)S(1)}, u32[]{:S(2)}, u32[]{:S(2)}) collective-permute-start(bf16[64,4096]{1,0:T(8,128)(2,1)S(1)} %level1_rows64.3.refs_2_), channel_id=1, source_target_pairs={{0,8},{8,0},{16,24},{24,16},{1,9},{9,1},{17,25},{25,17},{2,10},{10... | collective-permute-start | bytes 1572872 | tf_op jit(solution)/shard_map/ppermute | solution.py:28
  134.0 7.7 %collective-permute-start.18 = (bf16[32,4096]{1,0:T(8,128)(2,1)S(1)}, bf16[32,4096]{1,0:T(8,128)(2,1)S(1)}, u32[]{:S(2)}, u32[]{:S(2)}) collective-permute-start(bf16[32,4096]{1,0:T(8,128)(2,1)S(1)} %slice.91.refs_3_), channel_id=1, source_target_pairs={{0,8},{8,0},{16,24},{24,16},{1,9},{9,1},{17,25},{25,17},{2,10},{10... | collective-permute-start | bytes 786440 | tf_op jit(solution)/shard_map/ppermute | solution.py:28
  134.5 7.2 %collective-permute-start.19 = (bf16[32,4096]{1,0:T(8,128)(2,1)S(1)}, bf16[32,4096]{1,0:T(8,128)(2,1)S(1)}, u32[]{:S(2)}, u32[]{:S(2)}) collective-permute-start(bf16[32,4096]{1,0:T(8,128)(2,1)S(1)} %collective-permute-done.17.refs_4_), channel_id=1, source_target_pairs={{0,8},{8,0},{16,24},{24,16},{1,9},{9,1},{17,25},{25,17},{2,10},{10... | collective-permute-start | bytes 786440 | tf_op jit(solution)/shard_map/ppermute | solution.py:28
  137.5 16.4 %collective-permute-start.22 = (bf16[64,4096]{1,0:T(8,128)(2,1)S(1)}, bf16[64,4096]{1,0:T(8,128)(2,1)S(1)}, u32[]{:S(2)}, u32[]{:S(2)}) collective-permute-start(bf16[64,4096]{1,0:T(8,128)(2,1)S(1)} %level2_rows64.1.refs_2_), channel_id=1, source_target_pairs={{0,2},{1,3},{2,0},{3,1},{4,6},{5,7},{6,4},{7,5},{8,10},{9,11},{10,... | collective-permute-start | bytes 1572872 | tf_op jit(solution)/shard_map/ppermute | solution.py:28

commit v8 on v7

--- a/solution.py
+++ b/solution.py
@@ -338,6 +338,9 @@
     after_z1 = trade(after_1, 1)
     first_z2, first_yz1 = after(first_z2, first_yz1)
     first_yz2 = trade(first_z2, 0)
+    rest_2, first_yz2 = after(rest_2, first_yz2)
+    rest_y2 = trade(rest_2, 0)
+
     e, y, z, yz = (("top", low, eighth) for low in range(0, size, quarter))
     jobs = [[e, (*y[:2], share)], [("top", quarter + share, share), z], [yz]]
     jobs.append([(0, 0, eighth), (1, 0, quarter)])
@@ -364,34 +367,34 @@
         keeps=True,
     )
     lead_w = trade(lead, 3)
-    after_z1, rest_2, lead = after(after_z1, rest_2, lead)
-    rest_y2 = trade(rest_2, 0)
+    after_z1, rest_y2, lead = after(after_z1, rest_y2, lead)
     next_1 = run_level(
         1,
         meta,
         (inv, panel_1),
         [[(0, 0, eighth)], [(0, eighth, eighth)]],
         pairs=[(rows_of(after_1), rows_of(after_z1))],
-        cost=10**9,
+        cost=10**10,
     )
     next_1 = [next_0, *next_1]
+    next_c1 = [trade(x, 2) for x in next_1]
+    after_2 = chunk(0, panel_0, rest_2, rest_y2, cost=0)
+    after_z2 = trade(after_2, 1)
+    next_c1[0], after_2 = after(next_c1[0], after_2)
     (last_1,) = run_level(
         2,
         meta,
         (inv, panel_2),
         [[(i, 0, x.shape[0]) for i, x in enumerate(next_1)]],
-        pairs=[(rows_of(x), rows_of(trade(x, 2))) for x in next_1],
-    )
-    rest_y2, lead_w, last_1 = after(rest_y2, lead_w, last_1)
-    after_2 = chunk(0, panel_0, rest_2, rest_y2, cost=3 * 10**9)
-    after_z2 = trade(after_2, 1)
+        pairs=[(rows_of(x), rows_of(y)) for x, y in zip(next_1, next_c1)],
+    )
     last_w1 = trade(last_1, 3)
     tops_w = lead_w[:eighth]
     tops_wc = trade(tops_w, 2)
     tops_wy = trade(tops_w, 0)
     after_z2, tops_wy = after(after_z2, tops_wy)
     tops_wyc = trade(tops_wy, 2)
-    next_2 = chunk(1, panel_1, after_2, after_z2, cost=0)
+    next_2 = chunk(1, panel_1, after_2, after_z2, cost=5 * 10**9)
     last_2 = chunk(2, panel_2, next_2, trade(next_2, 2))
     last_w2 = trade(last_2, 3)
     more = lead.shape[0] - eighth
@@ -408,7 +411,7 @@
         pairs=[([(lead, eighth, more)], [(lead_w, eighth, more)]), (rows_of(last_1), rows_of(last_w1))],
         keeps=True,
         part=(all_rows, 0, None),
-        cost=5 * 10**9,
+        cost=5 * 10**10,
     )
     return chunk(3, panel_3, last_2, last_w2, part=(all_rows, all_rows // quarter - 1, out))
 

time: 157 us -> 145 us (0.924)
  local copies, waits for them, and re-layouts: 9.75 us -> 4.65 us
  starting transfers between devices: 21.3 us -> 18.1 us
  waiting for transfers between devices: 90.3 us -> 88.2 us
    ppermute x23, starting transfers between devices: 21.3 us -> 18.1 us  [trade(): lax.ppermute(block, axis, [(i, i ^ flip) for i in range(lax.axis_size(axi...]
    ppermute x23, waiting for transfers between devices: 90.3 us -> 88.2 us  [trade(): lax.ppermute(block, axis, [(i, i ^ flip) for i in range(lax.axis_size(axi...]
    add x4, local copies, waits for them, and re-layouts: 2.13 us -> 0.02 us  [make_meta(): jnp.zeros((blocks,), jnp.int32) + shift]
  transfers between devices with their start and end apart: 23 -> 23, of which waited for: 13 -> 11; matrix products, arithmetic and copies ran while one was open for 6% -> 2% of each run, Pallas kernels for 20% -> 22%
where the time goes in v8:
time: 145 us
  waiting for transfers between devices  88.2 us (61%)
  Pallas kernels  33.8 us (23%)
  starting transfers between devices  18.1 us (12%)
  local copies, waits for them, and re-layouts  4.65 us (3%)
    ppermute x23, waiting for transfers between devices, trade(): lax.ppermute(block, axis, [(i, i ^ flip) for i in range(lax.axis_size(axi...  88.2 us
    pallas_call x9, Pallas kernels, run_level(): pl.pallas_call(kernel, grid=(1,) if part is not None else (), out_shape=s...  25 us
    ppermute x23, starting transfers between devices, trade(): lax.ppermute(block, axis, [(i, i ^ flip) for i in range(lax.axis_size(axi...  18.1 us
    pallas_call x1, Pallas kernels, run_two_levels(): pl.pallas_call(kernel, out_shape=[jax.ShapeDtypeStruct((n, width), BF16)...  7.96 us
  transfers between devices with their start and end apart: 23, of which 11 were waited for; matrix products, arithmetic and copies ran while one was open for 2% of the time, Pallas kernels for 22%

profile of v8, /device:TPU:0, one launch (start us, length us, event | category | flops | bytes accessed | tf_op | source)
XLA Modules:
  0.0 145.0 jit_solution(9387403036415108222)
XLA Ops:
  0.0 1.2 slice.87.refs_1_
  1.2 3.0 %collective-permute-start.2 = (bf16[80,4096]{1,0:T(8,128)(2,1)S(1)}, bf16[80,4096]{1,0:T(8,128)(2,1)}, u32[]{:S(2)}, u32[]{:S(2)}) collective-permute-start(bf16[80,4096]{1,0:T(8,128)(2,1)S(1)} %slice.87.refs_1_), channel_id=1, source_target_pairs={{0,16},{8,24},{16,0},{24,8},{1,17},{9,25},{17,1},{25,9},{2,18},{10... | collective-permute-start | bytes 1966088 | tf_op jit(solution)/shard_map/ppermute | solution.py:28
  4.2 2.6 %collective-permute-start = (bf16[80,4096]{1,0:T(8,128)(2,1)S(1)}, bf16[80,4096]{1,0:T(8,128)(2,1)S(1)}, u32[]{:S(2)}, u32[]{:S(2)}) collective-permute-start(bf16[80,4096]{1,0:T(8,128)(2,1)S(1)} %slice.87.refs_1_), channel_id=1, source_target_pairs={{0,4},{1,5},{2,6},{3,7},{4,0},{5,1},{6,2},{7,3},{8,12},{9,13},{10,... | collective-permute-start | bytes 1966088 | tf_op jit(solution)/shard_map/ppermute | solution.py:28
  6.8 1.3 fusion.8
  8.6 1.0 slice.88.refs_2_
  9.7 1.6 %collective-permute-start.3 = (bf16[48,4096]{1,0:T(8,128)(2,1)S(1)}, bf16[48,4096]{1,0:T(8,128)(2,1)}, u32[]{:S(2)}, u32[]{:S(2)}) collective-permute-start(bf16[48,4096]{1,0:T(8,128)(2,1)S(1)} %slice.88.refs_2_), channel_id=1, source_target_pairs={{0,16},{8,24},{16,0},{24,8},{1,17},{9,25},{17,1},{25,9},{2,18},{10... | collective-permute-start | bytes 1179656 | tf_op jit(solution)/shard_map/ppermute | solution.py:28
  11.3 24.1 %collective-permute-done.refs_0_ = bf16[80,4096]{1,0:T(8,128)(2,1)S(1)} collective-permute-done((bf16[80,4096]{1,0:T(8,128)(2,1)S(1)}, bf16[80,4096]{1,0:T(8,128)(2,1)S(1)}, u32[]{:S(2)}, u32[]{:S(2)}) %collective-permute-start) | collective-permute-done | bytes 655392 | tf_op jit(solution)/shard_map/ppermute | solution.py:28
  36.1 1.0 copy-done
  37.2 0.9 reorder.1.refs_0_.inv
  38.1 1.4 collective-permute-done.3.refs_4_
  39.5 5.0 %level0_rows256.1 = (bf16[128,4096]{1,0:T(8,128)(2,1)S(1)}, bf16[64,4096]{1,0:T(8,128)(2,1)S(1)}, bf16[64,4096]{1,0:T(8,128)(2,1)S(1)}, bf16[256,4096]{1,0:T(8,128)(2,1)S(1)}) custom-call(s32[640]{0:T(1024)S(1)} %concatenate.3.meta, bf16[4,256,256]{2,1,0:T(8,128)(2,1)S(1)} %reorder.1.refs_0_.inv, bf16[80,4096]{1,0:T(8,128)(2,1)S(1)} %slice.87.refs_1_, ...), custom_call_target="tpu_custom_call" | custom-call | tf_op jit(solution)/shard_map/level0_rows256/pallas_call | solution.py:222
  44.5 10.5 %collective-permute-done.1.refs_1_ = bf16[48,4096]{1,0:T(8,128)(2,1)} collective-permute-done((bf16[48,4096]{1,0:T(8,128)(2,1)S(1)}, bf16[48,4096]{1,0:T(8,128)(2,1)}, u32[]{:S(2)}, u32[]{:S(2)}) %collective-permute-start.1) | collective-permute-done | bytes 393248 | tf_op jit(solution)/shard_map/ppermute | solution.py:28
  55.0 1.5 %collective-permute-start.7 = (bf16[48,4096]{1,0:T(8,128)(2,1)}, bf16[48,4096]{1,0:T(8,128)(2,1)S(1)}, u32[]{:S(2)}, u32[]{:S(2)}) collective-permute-start(bf16[48,4096]{1,0:T(8,128)(2,1)} %collective-permute-done.1.refs_1_), channel_id=1, source_target_pairs={{0,16},{8,24},{16,0},{24,8},{1,17},{9,25},{17,1},{25,9},{2,18},{10... | collective-permute-start | bytes 1179656 | tf_op jit(solution)/shard_map/ppermute | solution.py:28
  57.0 7.6 %collective-permute-done.7.refs_3_ = bf16[48,4096]{1,0:T(8,128)(2,1)S(1)} collective-permute-done((bf16[48,4096]{1,0:T(8,128)(2,1)}, bf16[48,4096]{1,0:T(8,128)(2,1)S(1)}, u32[]{:S(2)}, u32[]{:S(2)}) %collective-permute-start.7) | collective-permute-done | bytes 393248 | tf_op jit(solution)/shard_map/ppermute | solution.py:28
  64.5 1.5 %collective-permute-start.8 = (bf16[64,4096]{1,0:T(8,128)(2,1)S(1)}, bf16[64,4096]{1,0:T(8,128)(2,1)S(1)}, u32[]{:S(2)}, u32[]{:S(2)}) collective-permute-start(bf16[64,4096]{1,0:T(8,128)(2,1)S(1)} %get-tuple-element.49.refs_2_), channel_id=1, source_target_pairs={{0,16},{8,24},{16,0},{24,8},{1,17},{9,25},{17,1},{25,9},{2,18},{10... | collective-permute-start | bytes 1572872 | tf_op jit(solution)/shard_map/ppermute | solution.py:28
  66.1 8.0 %level0_level1.1 = (bf16[48,4096]{1,0:T(8,128)(2,1)S(1)}, bf16[48,4096]{1,0:T(8,128)(2,1)S(1)}, bf16[32,4096]{1,0:T(8,128)(2,1)S(1)}, bf16[96,4096]{1,0:T(8,128)(2,1)S(1)}, bf16[256,4096]{1,0:T(8,128)(2,1)S(1)}) custom-call(s32[640]{0:T(1024)S(1)} %concatenate.3.meta, bf16[4,256,256]{2,1,0:T(8,128)(2,1)S(1)} %reorder.1.refs_0_.inv, ...), custom_call_target="tpu_custom_call" | custom-call | tf_op jit(solution)/shard_map/level0_level1/pallas_call | solution.py:248
  74.7 2.1 %collective-permute-done.11.refs_6_ = bf16[32,4096]{1,0:T(8,128)(2,1)S(1)} collective-permute-done((bf16[32,4096]{1,0:T(8,128)(2,1)S(1)}, bf16[32,4096]{1,0:T(8,128)(2,1)S(1)}, u32[]{:S(2)}, u32[]{:S(2)}) %collective-permute-start.11) | collective-permute-done | bytes 262176 | tf_op jit(solution)/shard_map/ppermute | solution.py:28
  76.9 3.7 %level2_rows144.1 = (bf16[48,4096]{1,0:T(8,128)(2,1)S(1)}, bf16[96,4096]{1,0:T(8,128)(2,1)S(1)}, bf16[256,4096]{1,0:T(8,128)(2,1)S(1)}) custom-call(s32[640]{0:T(1024)S(1)} %concatenate.3.meta, bf16[4,256,256]{2,1,0:T(8,128)(2,1)S(1)} %reorder.1.refs_0_.inv, bf16[48,4096]{1,0:T(8,128)(2,1)S(1)} %get-tuple-element.55.refs_1_, ...), custom_call_target="tpu_custom_call" | custom-call | tf_op jit(solution)/shard_map/level2_rows144/pallas_call | solution.py:222
  80.8 1.6 %level1_rows64.2 = (bf16[32,4096]{1,0:T(8,128)(2,1)S(1)}, bf16[32,4096]{1,0:T(8,128)(2,1)S(1)}) custom-call(s32[640]{0:T(1024)S(1)} %concatenate.3.meta, bf16[4,256,256]{2,1,0:T(8,128)(2,1)S(1)} %reorder.1.refs_0_.inv, bf16[256,4096]{1,0:T(8,128)(2,1)S(1)} %get-tuple-element.67.refs_1_, bf16[64,4096]{1,0:T(8,128)(2,1)S(1)} %get-tuple-element.45.refs_2_, ...), custom_call_target="tpu_custom_call" | custom-call | flops 10000000000 | tf_op jit(solution)/shard_map/level1_rows64/pallas_call | solution.py:222
  83.0 1.6 %level0_rows64.1.refs_2_ = bf16[64,4096]{1,0:T(8,128)(2,1)S(1)} custom-call(s32[640]{0:T(1024)S(1)} %concatenate.3.meta, bf16[4,256,256]{2,1,0:T(8,128)(2,1)S(1)} %reorder.1.refs_0_.inv, bf16[256,4096]{1,0:T(8,128)(2,1)S(1)} %get-tuple-element.61.refs_1_, bf16[64,4096]{1,0:T(8,128)(2,1)S(1)} %get-tuple-element.49.refs_2_, ...), custom_call_target="tpu_custom_call" | custom-call | tf_op jit(solution)/shard_map/level0_rows64/pallas_call | solution.py:222
  84.6 3.5 %collective-permute-start.13 = (bf16[64,4096]{1,0:T(8,128)(2,1)S(1)}, bf16[64,4096]{1,0:T(8,128)(2,1)S(1)}, u32[]{:S(2)}, u32[]{:S(2)}) collective-permute-start(bf16[64,4096]{1,0:T(8,128)(2,1)S(1)} %level0_rows64.1.refs_2_), channel_id=1, source_target_pairs={{0,4},{1,5},{2,6},{3,7},{4,0},{5,1},{6,2},{7,3},{8,12},{9,13},{10,... | collective-permute-start | bytes 1572872 | tf_op jit(solution)/shard_map/ppermute | solution.py:28
  88.1 2.1 %level2_rows160.1.refs_8_ = bf16[160,4096]{1,0:T(8,128)(2,1)S(1)} custom-call(s32[640]{0:T(1024)S(1)} %concatenate.3.meta, bf16[4,256,256]{2,1,0:T(8,128)(2,1)S(1)} %reorder.1.refs_0_.inv, bf16[256,4096]{1,0:T(8,128)(2,1)S(1)} %get-tuple-element.64.refs_1_, bf16[96,4096]{1,0:T(8,128)(2,1)S(1)} %get-tuple-element.65.refs_2_, ...), custom_call_target="tpu_custom_call" | custom-call | tf_op jit(solution)/shard_map/level2_rows160/pallas_call | solution.py:222
  90.2 6.7 %collective-permute-done.12.refs_7_ = bf16[48,4096]{1,0:T(8,128)(2,1)S(1)} collective-permute-done((bf16[48,4096]{1,0:T(8,128)(2,1)S(1)}, bf16[48,4096]{1,0:T(8,128)(2,1)S(1)}, u32[]{:S(2)}, u32[]{:S(2)}) %collective-permute-start.12) | collective-permute-done | bytes 393248 | tf_op jit(solution)/shard_map/ppermute | solution.py:28
  97.5 6.7 %collective-permute-done.14.refs_4_ = bf16[32,4096]{1,0:T(8,128)(2,1)S(1)} collective-permute-done((bf16[32,4096]{1,0:T(8,128)(2,1)S(1)}, bf16[32,4096]{1,0:T(8,128)(2,1)S(1)}, u32[]{:S(2)}, u32[]{:S(2)}) %collective-permute-start.14) | collective-permute-done | bytes 262176 | tf_op jit(solution)/shard_map/ppermute | solution.py:28
  104.3 7.4 %collective-permute-done.13.refs_3_ = bf16[64,4096]{1,0:T(8,128)(2,1)S(1)} collective-permute-done((bf16[64,4096]{1,0:T(8,128)(2,1)S(1)}, bf16[64,4096]{1,0:T(8,128)(2,1)S(1)}, u32[]{:S(2)}, u32[]{:S(2)}) %collective-permute-start.13) | collective-permute-done | bytes 524320 | tf_op jit(solution)/shard_map/ppermute | solution.py:28
  111.6 1.6 %level1_rows64.3.refs_2_ = bf16[64,4096]{1,0:T(8,128)(2,1)S(1)} custom-call(s32[640]{0:T(1024)S(1)} %concatenate.3.meta, bf16[4,256,256]{2,1,0:T(8,128)(2,1)S(1)} %reorder.1.refs_0_.inv, bf16[256,4096]{1,0:T(8,128)(2,1)S(1)} %get-tuple-element.67.refs_1_, bf16[64,4096]{1,0:T(8,128)(2,1)S(1)} %level0_rows64.1.refs_2_, ...), custom_call_target="tpu_custom_call" | custom-call | flops 5000000000 | tf_op jit(solution)/shard_map/level1_rows64/pallas_call | solution.py:222
  113.9 1.3 collective-permute-done.21.refs_3_
  115.2 1.6 %level2_rows64.1.refs_2_ = bf16[64,4096]{1,0:T(8,128)(2,1)S(1)} custom-call(s32[640]{0:T(1024)S(1)} %concatenate.3.meta, bf16[4,256,256]{2,1,0:T(8,128)(2,1)S(1)} %reorder.1.refs_0_.inv, bf16[256,4096]{1,0:T(8,128)(2,1)S(1)} %get-tuple-element.64.refs_1_, bf16[64,4096]{1,0:T(8,128)(2,1)S(1)} %level1_rows64.3.refs_2_, ...), custom_call_target="tpu_custom_call" | custom-call | tf_op jit(solution)/shard_map/level2_rows64/pallas_call | solution.py:222
  116.9 15.0 %collective-permute-done.20.refs_9_ = bf16[160,4096]{1,0:T(8,128)(2,1)S(1)} collective-permute-done((bf16[160,4096]{1,0:T(8,128)(2,1)S(1)}, bf16[160,4096]{1,0:T(8,128)(2,1)S(1)}, u32[]{:S(2)}, u32[]{:S(2)}) %collective-permute-start.20) | collective-permute-done | bytes 1310752 | tf_op jit(solution)/shard_map/ppermute | solution.py:28
  132.0 5.4 %level3_rows192.1 = (bf16[256,4096]{1,0:T(8,128)(2,1)}, bf16[256,4096]{1,0:T(8,128)(2,1)S(1)}) custom-call(s32[640]{0:T(1024)S(1)} %concatenate.3.meta, bf16[4,256,256]{2,1,0:T(8,128)(2,1)S(1)} %reorder.1.refs_0_.inv, bf16[48,4096]{1,0:T(8,128)(2,1)S(1)} %get-tuple-element.59.refs_1_, bf16[96,4096]{1,0:T(8,128)(2,1)S(1)} %get-tuple-element.60.refs_2_, ...), custom_call_target="tpu_custom_call" | custom-call | flops 49999998976 | tf_op jit(solution)/shard_map/level3_rows192/pallas_call | solution.py:222
  137.4 5.3 %collective-permute-done.22.refs_3_ = bf16[64,4096]{1,0:T(8,128)(2,1)S(1)} collective-permute-done((bf16[64,4096]{1,0:T(8,128)(2,1)S(1)}, bf16[64,4096]{1,0:T(8,128)(2,1)S(1)}, u32[]{:S(2)}, u32[]{:S(2)}) %collective-permute-start.22) | collective-permute-done | bytes 524320 | tf_op jit(solution)/shard_map/ppermute | solution.py:28
  142.6 2.4 %level3_rows64.1 = bf16[256,4096]{1,0:T(8,128)(2,1)} custom-call(s32[640]{0:T(1024)S(1)} %concatenate.3.meta, bf16[4,256,256]{2,1,0:T(8,128)(2,1)S(1)} %reorder.1.refs_0_.inv, bf16[256,4096]{1,0:T(8,128)(2,1)S(1)} %get-tuple-element.71.refs_1_, bf16[64,4096]{1,0:T(8,128)(2,1)S(1)} %level2_rows64.1.refs_2_, ...), custom_call_target="tpu_custom_call", output_to_operand_aliasing={{}: (5, {})} | custom-call | tf_op jit(solution)/shard_map/level3_rows64/pallas_call | solution.py:222
  (45 shorter events, 4.5 us)
Async XLA Ops:
  0.0 35.8 %copy-start.1 = (s32[4,2,32]{2,1,0:T(2,128)S(1)}, s32[4,2,32]{2,1,0:T(2,128)}, u32[]{:S(2)}) copy-start(s32[4,2,32]{2,1,0:T(2,128)} %param.7) | copy-start | bytes 3076
  0.0 35.9 %copy-start.3 = (s32[4,32]{1,0:T(4,128)S(1)}, s32[4,32]{1,0:T(4,128)}, u32[]{:S(2)}) copy-start(s32[4,32]{1,0:T(4,128)} %param.8) | copy-start | bytes 1540
  0.0 35.9 %copy-start.2 = (s32[4,32]{1,0:T(4,128)S(1)}, s32[4,32]{1,0:T(4,128)}, u32[]{:S(2)}) copy-start(s32[4,32]{1,0:T(4,128)} %param.9) | copy-start | bytes 1540
  1.2 38.4 %collective-permute-start.2 = (bf16[80,4096]{1,0:T(8,128)(2,1)S(1)}, bf16[80,4096]{1,0:T(8,128)(2,1)}, u32[]{:S(2)}, u32[]{:S(2)}) collective-permute-start(bf16[80,4096]{1,0:T(8,128)(2,1)S(1)} %slice.87.refs_1_), channel_id=1, source_target_pairs={{0,16},{8,24},{16,0},{24,8},{1,17},{9,25},{17,1},{25,9},{2,18},{10... | collective-permute-start | bytes 1966088 | tf_op jit(solution)/shard_map/ppermute | solution.py:28
  4.2 31.1 %collective-permute-start = (bf16[80,4096]{1,0:T(8,128)(2,1)S(1)}, bf16[80,4096]{1,0:T(8,128)(2,1)S(1)}, u32[]{:S(2)}, u32[]{:S(2)}) collective-permute-start(bf16[80,4096]{1,0:T(8,128)(2,1)S(1)} %slice.87.refs_1_), channel_id=1, source_target_pairs={{0,4},{1,5},{2,6},{3,7},{4,0},{5,1},{6,2},{7,3},{8,12},{9,13},{10,... | collective-permute-start | bytes 1966088 | tf_op jit(solution)/shard_map/ppermute | solution.py:28
  8.1 30.0 %collective-permute-start.4 = (bf16[64,4096]{1,0:T(8,128)(2,1)S(1)}, bf16[64,4096]{1,0:T(8,128)(2,1)}, u32[]{:S(2)}, u32[]{:S(2)}) collective-permute-start(bf16[64,4096]{1,0:T(8,128)(2,1)S(1)} %get-tuple-element.76.refs_5_), channel_id=1, source_target_pairs={{0,16},{8,24},{16,0},{24,8},{1,17},{9,25},{17,1},{25,9},{2,18},{10... | collective-permute-start | bytes 1572872 | tf_op jit(solution)/shard_map/ppermute | solution.py:28
  9.7 29.9 %collective-permute-start.3 = (bf16[48,4096]{1,0:T(8,128)(2,1)S(1)}, bf16[48,4096]{1,0:T(8,128)(2,1)}, u32[]{:S(2)}, u32[]{:S(2)}) collective-permute-start(bf16[48,4096]{1,0:T(8,128)(2,1)S(1)} %slice.88.refs_2_), channel_id=1, source_target_pairs={{0,16},{8,24},{16,0},{24,8},{1,17},{9,25},{17,1},{25,9},{2,18},{10... | collective-permute-start | bytes 1179656 | tf_op jit(solution)/shard_map/ppermute | solution.py:28
  35.3 19.7 %collective-permute-start.6 = (bf16[80,4096]{1,0:T(8,128)(2,1)S(1)}, bf16[80,4096]{1,0:T(8,128)(2,1)S(1)}, u32[]{:S(2)}, u32[]{:S(2)}) collective-permute-start(bf16[80,4096]{1,0:T(8,128)(2,1)S(1)} %collective-permute-done.refs_0_), channel_id=1, source_target_pairs={{0,16},{8,24},{16,0},{24,8},{1,17},{9,25},{17,1},{25,9},{2,18},{10... | collective-permute-start | bytes 1966088 | tf_op jit(solution)/shard_map/ppermute | solution.py:28
  35.8 19.2 %collective-permute-start.1 = (bf16[48,4096]{1,0:T(8,128)(2,1)S(1)}, bf16[48,4096]{1,0:T(8,128)(2,1)}, u32[]{:S(2)}, u32[]{:S(2)}) collective-permute-start(bf16[48,4096]{1,0:T(8,128)(2,1)S(1)} %slice.88.refs_2_), channel_id=1, source_target_pairs={{0,4},{1,5},{2,6},{3,7},{4,0},{5,1},{6,2},{7,3},{8,12},{9,13},{10,... | collective-permute-start | bytes 1179656 | tf_op jit(solution)/shard_map/ppermute | solution.py:28
  36.1 1.0 copy-start
  55.0 9.5 %collective-permute-start.7 = (bf16[48,4096]{1,0:T(8,128)(2,1)}, bf16[48,4096]{1,0:T(8,128)(2,1)S(1)}, u32[]{:S(2)}, u32[]{:S(2)}) collective-permute-start(bf16[48,4096]{1,0:T(8,128)(2,1)} %collective-permute-done.1.refs_1_), channel_id=1, source_target_pairs={{0,16},{8,24},{16,0},{24,8},{1,17},{9,25},{17,1},{25,9},{2,18},{10... | collective-permute-start | bytes 1179656 | tf_op jit(solution)/shard_map/ppermute | solution.py:28
  56.6 24.2 %collective-permute-start.5 = (bf16[64,4096]{1,0:T(8,128)(2,1)S(1)}, bf16[64,4096]{1,0:T(8,128)(2,1)S(1)}, u32[]{:S(2)}, u32[]{:S(2)}) collective-permute-start(bf16[64,4096]{1,0:T(8,128)(2,1)S(1)} %get-tuple-element.45.refs_2_), channel_id=1, source_target_pairs={{0,4},{1,5},{2,6},{3,7},{4,0},{5,1},{6,2},{7,3},{8,12},{9,13},{10,... | collective-permute-start | bytes 1572872 | tf_op jit(solution)/shard_map/ppermute | solution.py:28
  64.5 16.2 %collective-permute-start.8 = (bf16[64,4096]{1,0:T(8,128)(2,1)S(1)}, bf16[64,4096]{1,0:T(8,128)(2,1)S(1)}, u32[]{:S(2)}, u32[]{:S(2)}) collective-permute-start(bf16[64,4096]{1,0:T(8,128)(2,1)S(1)} %get-tuple-element.49.refs_2_), channel_id=1, source_target_pairs={{0,16},{8,24},{16,0},{24,8},{1,17},{9,25},{17,1},{25,9},{2,18},{10... | collective-permute-start | bytes 1572872 | tf_op jit(solution)/shard_map/ppermute | solution.py:28
  74.1 2.9 %collective-permute-start.10 = (bf16[48,4096]{1,0:T(8,128)(2,1)S(1)}, bf16[48,4096]{1,0:T(8,128)(2,1)S(1)}, u32[]{:S(2)}, u32[]{:S(2)}) collective-permute-start(bf16[48,4096]{1,0:T(8,128)(2,1)S(1)} %get-tuple-element.56.refs_2_), channel_id=1, source_target_pairs={{0,8},{8,0},{16,24},{24,16},{1,9},{9,1},{17,25},{25,17},{2,10},{10... | collective-permute-start | bytes 1179656 | tf_op jit(solution)/shard_map/ppermute | solution.py:28
  74.1 2.8 %collective-permute-start.9 = (bf16[48,4096]{1,0:T(8,128)(2,1)S(1)}, bf16[48,4096]{1,0:T(8,128)(2,1)S(1)}, u32[]{:S(2)}, u32[]{:S(2)}) collective-permute-start(bf16[48,4096]{1,0:T(8,128)(2,1)S(1)} %get-tuple-element.55.refs_1_), channel_id=1, source_target_pairs={{0,8},{8,0},{16,24},{24,16},{1,9},{9,1},{17,25},{25,17},{2,10},{10... | collective-permute-start | bytes 1179656 | tf_op jit(solution)/shard_map/ppermute | solution.py:28
  74.6 2.1 %collective-permute-start.11 = (bf16[32,4096]{1,0:T(8,128)(2,1)S(1)}, bf16[32,4096]{1,0:T(8,128)(2,1)S(1)}, u32[]{:S(2)}, u32[]{:S(2)}) collective-permute-start(bf16[32,4096]{1,0:T(8,128)(2,1)S(1)} %get-tuple-element.57.refs_3_), channel_id=1, source_target_pairs={{0,8},{8,0},{16,24},{24,16},{1,9},{9,1},{17,25},{25,17},{2,10},{10... | collective-permute-start | bytes 786440 | tf_op jit(solution)/shard_map/ppermute | solution.py:28
  76.8 11.3 %collective-permute-start.17 = (bf16[96,4096]{1,0:T(8,128)(2,1)S(1)}, bf16[96,4096]{1,0:T(8,128)(2,1)S(1)}, u32[]{:S(2)}, u32[]{:S(2)}) collective-permute-start(bf16[96,4096]{1,0:T(8,128)(2,1)S(1)} %get-tuple-element.65.refs_2_), channel_id=1, source_target_pairs={{0,8},{8,0},{16,24},{24,16},{1,9},{9,1},{17,25},{25,17},{2,10},{10... | collective-permute-start | bytes 2359304 | tf_op jit(solution)/shard_map/ppermute | solution.py:28
  80.6 16.3 %collective-permute-start.12 = (bf16[48,4096]{1,0:T(8,128)(2,1)S(1)}, bf16[48,4096]{1,0:T(8,128)(2,1)S(1)}, u32[]{:S(2)}, u32[]{:S(2)}) collective-permute-start(bf16[48,4096]{1,0:T(8,128)(2,1)S(1)} %get-tuple-element.59.refs_1_), channel_id=1, source_target_pairs={{0,2},{1,3},{2,0},{3,1},{4,6},{5,7},{6,4},{7,5},{8,10},{9,11},{10,... | collective-permute-start | bytes 1179656 | tf_op jit(solution)/shard_map/ppermute | solution.py:28
  82.4 5.7 %collective-permute-start.18 = (bf16[32,4096]{1,0:T(8,128)(2,1)S(1)}, bf16[32,4096]{1,0:T(8,128)(2,1)S(1)}, u32[]{:S(2)}, u32[]{:S(2)}) collective-permute-start(bf16[32,4096]{1,0:T(8,128)(2,1)S(1)} %get-tuple-element.69.refs_4_), channel_id=1, source_target_pairs={{0,8},{8,0},{16,24},{24,16},{1,9},{9,1},{17,25},{25,17},{2,10},{10... | collective-permute-start | bytes 786440 | tf_op jit(solution)/shard_map/ppermute | solution.py:28
  82.8 5.3 %collective-permute-start.19 = (bf16[32,4096]{1,0:T(8,128)(2,1)S(1)}, bf16[32,4096]{1,0:T(8,128)(2,1)S(1)}, u32[]{:S(2)}, u32[]{:S(2)}) collective-permute-start(bf16[32,4096]{1,0:T(8,128)(2,1)S(1)} %get-tuple-element.70.refs_6_), channel_id=1, source_target_pairs={{0,8},{8,0},{16,24},{24,16},{1,9},{9,1},{17,25},{25,17},{2,10},{10... | collective-permute-start | bytes 786440 | tf_op jit(solution)/shard_map/ppermute | solution.py:28
  84.6 27.0 %collective-permute-start.13 = (bf16[64,4096]{1,0:T(8,128)(2,1)S(1)}, bf16[64,4096]{1,0:T(8,128)(2,1)S(1)}, u32[]{:S(2)}, u32[]{:S(2)}) collective-permute-start(bf16[64,4096]{1,0:T(8,128)(2,1)S(1)} %level0_rows64.1.refs_2_), channel_id=1, source_target_pairs={{0,4},{1,5},{2,6},{3,7},{4,0},{5,1},{6,2},{7,3},{8,12},{9,13},{10,... | collective-permute-start | bytes 1572872 | tf_op jit(solution)/shard_map/ppermute | solution.py:28
  90.1 41.8 %collective-permute-start.20 = (bf16[160,4096]{1,0:T(8,128)(2,1)S(1)}, bf16[160,4096]{1,0:T(8,128)(2,1)S(1)}, u32[]{:S(2)}, u32[]{:S(2)}) collective-permute-start(bf16[160,4096]{1,0:T(8,128)(2,1)S(1)} %level2_rows160.1.refs_8_), channel_id=1, source_target_pairs={{0,2},{1,3},{2,0},{3,1},{4,6},{5,7},{6,4},{7,5},{8,10},{9,11},{10,... | collective-permute-start | bytes 3932168 | tf_op jit(solution)/shard_map/ppermute | solution.py:28
  97.0 7.3 %collective-permute-start.14 = (bf16[32,4096]{1,0:T(8,128)(2,1)S(1)}, bf16[32,4096]{1,0:T(8,128)(2,1)S(1)}, u32[]{:S(2)}, u32[]{:S(2)}) collective-permute-start(bf16[32,4096]{1,0:T(8,128)(2,1)S(1)} %slice.92.refs_3_), channel_id=1, source_target_pairs={{0,16},{8,24},{16,0},{24,8},{1,17},{9,25},{17,1},{25,9},{2,18},{10... | collective-permute-start | bytes 786440 | tf_op jit(solution)/shard_map/ppermute | solution.py:28
  113.2 2.0 %collective-permute-start.21 = (bf16[64,4096]{1,0:T(8,128)(2,1)S(1)}, bf16[64,4096]{1,0:T(8,128)(2,1)S(1)}, u32[]{:S(2)}, u32[]{:S(2)}) collective-permute-start(bf16[64,4096]{1,0:T(8,128)(2,1)S(1)} %level1_rows64.3.refs_2_), channel_id=1, source_target_pairs={{0,8},{8,0},{16,24},{24,16},{1,9},{9,1},{17,25},{25,17},{2,10},{10... | collective-permute-start | bytes 1572872 | tf_op jit(solution)/shard_map/ppermute | solution.py:28
  113.3 3.6 %collective-permute-start.15 = (bf16[32,4096]{1,0:T(8,128)(2,1)S(1)}, bf16[32,4096]{1,0:T(8,128)(2,1)S(1)}, u32[]{:S(2)}, u32[]{:S(2)}) collective-permute-start(bf16[32,4096]{1,0:T(8,128)(2,1)S(1)} %slice.92.refs_3_), channel_id=1, source_target_pairs={{0,8},{8,0},{16,24},{24,16},{1,9},{9,1},{17,25},{25,17},{2,10},{10... | collective-permute-start | bytes 786440 | tf_op jit(solution)/shard_map/ppermute | solution.py:28
  113.8 3.1 %collective-permute-start.16 = (bf16[32,4096]{1,0:T(8,128)(2,1)S(1)}, bf16[32,4096]{1,0:T(8,128)(2,1)S(1)}, u32[]{:S(2)}, u32[]{:S(2)}) collective-permute-start(bf16[32,4096]{1,0:T(8,128)(2,1)S(1)} %collective-permute-done.14.refs_4_), channel_id=1, source_target_pairs={{0,8},{8,0},{16,24},{24,16},{1,9},{9,1},{17,25},{25,17},{2,10},{10... | collective-permute-start | bytes 786440 | tf_op jit(solution)/shard_map/ppermute | solution.py:28
  116.8 25.8 %collective-permute-start.22 = (bf16[64,4096]{1,0:T(8,128)(2,1)S(1)}, bf16[64,4096]{1,0:T(8,128)(2,1)S(1)}, u32[]{:S(2)}, u32[]{:S(2)}) collective-permute-start(bf16[64,4096]{1,0:T(8,128)(2,1)S(1)} %level2_rows64.1.refs_2_), channel_id=1, source_target_pairs={{0,2},{1,3},{2,0},{3,1},{4,6},{5,7},{6,4},{7,5},{8,10},{9,11},{10,... | collective-permute-start | bytes 1572872 | tf_op jit(solution)/shard_map/ppermute | solution.py:28

commit v9 on v8

--- a/solution.py
+++ b/solution.py
@@ -82,9 +82,17 @@
     def order(j):
         return meta[base + j]
 
+    jobs = [job for _, dest in outs for job in dest]
     if top is not None:
         a, b = top
         half = sum(count for _, _, count in a)
+        kept = [(start, start + rows) for source, start, rows in jobs if source == "top"]
+
+        def keep(value, first, rows, j):
+            for low, high in kept:
+                low, high = max(low, first), min(high, first + rows)
+                if low < high:
+                    merged[pl.ds(low, high - low), at(j)] = value[low - first : high - first]
 
         def merge_block(j, carry):
             other = order(j)
@@ -93,14 +101,13 @@
             for start, rows in segments(a, b):
                 from_a = read(a, start, rows, j) + read(b, start, rows, other)
                 from_b = read(b, start, rows, j) + read(a, start, rows, other)
-                low, high = pl.ds(start, rows), pl.ds(half + start, rows)
-                merged[low, at(j)] = from_a
-                merged[high, at(j)] = from_b
-                panel[low, at(j)] = (from_a * keep_a).astype(BF16)
-                panel[high, at(j)] = (from_b * keep_b).astype(BF16)
+                keep(from_a, start, rows, j)
+                keep(from_b, half + start, rows, j)
+                panel[pl.ds(start, rows), at(j)] = (from_a * keep_a).astype(BF16)
+                panel[pl.ds(half + start, rows), at(j)] = (from_b * keep_b).astype(BF16)
             return carry
 
-        lax.fori_loop(0, blocks, merge_block, 0, unroll=4)
+        lax.fori_loop(0, blocks, merge_block, 0, unroll=8)
 
     def columns(job, j):
         source, start, rows = job
@@ -109,7 +116,6 @@
         a, b = pairs[source]
         return read(a, start, rows, j) + read(b, start, rows, order(j))
 
-    jobs = [job for _, dest in outs for job in dest]
     pivots = [meta[base + 3 * blocks + i] for i in range(inv.shape[1] // BLOCK)]
     coupling = jnp.concatenate(
         [jnp.concatenate([columns(job, p) for p in pivots], axis=1).astype(BF16) for job in jobs],
@@ -133,7 +139,7 @@
                 done += rows
         return carry
 
-    lax.fori_loop(0, width // TILE, finish_tile, 0, unroll=4)
+    lax.fori_loop(0, width // TILE, finish_tile, 0, unroll=8)
 
 
 def level_kernel(meta, *refs, level, blocks, n_in, top, pairs, outs, n_hidden):

time: 145 us -> 144 us (level)
  Pallas kernels: 33.8 us -> 30.3 us
  waiting for transfers between devices: 88.2 us -> 90.6 us
    pallas_call x9, Pallas kernels: 25 us -> 22.4 us  [run_level(): pl.pallas_call(kernel, grid=(1,) if part is not None else (), out_shape=s...]
    ppermute x23, waiting for transfers between devices: 88.2 us -> 90.6 us  [trade(): lax.ppermute(block, axis, [(i, i ^ flip) for i in range(lax.axis_size(axi...]
  transfers between devices with their start and end apart: 23 -> 23, of which waited for: 11 -> 12; matrix products, arithmetic and copies ran while one was open for 2% -> 2% of each run, Pallas kernels for 22% -> 20%
where the time goes in v9:
time: 144 us; the launch traced here: 143 us
  waiting for transfers between devices  90.6 us (63%)
  Pallas kernels  30.3 us (21%)
  starting transfers between devices  17.5 us (12%)
  local copies, waits for them, and re-layouts  4.65 us (3%)
    ppermute x23, waiting for transfers between devices, trade(): lax.ppermute(block, axis, [(i, i ^ flip) for i in range(lax.axis_size(axi...  90.6 us
    pallas_call x9, Pallas kernels, run_level(): pl.pallas_call(kernel, grid=(1,) if part is not None else (), out_shape=s...  22.4 us
    ppermute x23, starting transfers between devices, trade(): lax.ppermute(block, axis, [(i, i ^ flip) for i in range(lax.axis_size(axi...  17.5 us
    pallas_call x1, Pallas kernels, run_two_levels(): pl.pallas_call(kernel, out_shape=[jax.ShapeDtypeStruct((n, width), BF16)...  7 us
  transfers between devices with their start and end apart: 23, of which 12 were waited for; matrix products, arithmetic and copies ran while one was open for 2% of the time, Pallas kernels for 20%

profile of v9, /device:TPU:0, one launch (start us, length us, event | category | flops | bytes accessed | tf_op | source)
XLA Modules:
  0.0 143.4 jit_solution(7133500858099361900)
XLA Ops:
  0.0 1.2 slice.87.refs_1_
  1.2 3.0 %collective-permute-start.2 = (bf16[80,4096]{1,0:T(8,128)(2,1)S(1)}, bf16[80,4096]{1,0:T(8,128)(2,1)}, u32[]{:S(2)}, u32[]{:S(2)}) collective-permute-start(bf16[80,4096]{1,0:T(8,128)(2,1)S(1)} %slice.87.refs_1_), channel_id=1, source_target_pairs={{0,16},{8,24},{16,0},{24,8},{1,17},{9,25},{17,1},{25,9},{2,18},{10... | collective-permute-start | bytes 1966088 | tf_op jit(solution)/shard_map/ppermute | solution.py:28
  4.2 2.6 %collective-permute-start = (bf16[80,4096]{1,0:T(8,128)(2,1)S(1)}, bf16[80,4096]{1,0:T(8,128)(2,1)S(1)}, u32[]{:S(2)}, u32[]{:S(2)}) collective-permute-start(bf16[80,4096]{1,0:T(8,128)(2,1)S(1)} %slice.87.refs_1_), channel_id=1, source_target_pairs={{0,4},{1,5},{2,6},{3,7},{4,0},{5,1},{6,2},{7,3},{8,12},{9,13},{10,... | collective-permute-start | bytes 1966088 | tf_op jit(solution)/shard_map/ppermute | solution.py:28
  6.8 1.3 fusion.8
  8.6 1.0 slice.88.refs_2_
  9.7 1.6 %collective-permute-start.3 = (bf16[48,4096]{1,0:T(8,128)(2,1)S(1)}, bf16[48,4096]{1,0:T(8,128)(2,1)}, u32[]{:S(2)}, u32[]{:S(2)}) collective-permute-start(bf16[48,4096]{1,0:T(8,128)(2,1)S(1)} %slice.88.refs_2_), channel_id=1, source_target_pairs={{0,16},{8,24},{16,0},{24,8},{1,17},{9,25},{17,1},{25,9},{2,18},{10... | collective-permute-start | bytes 1179656 | tf_op jit(solution)/shard_map/ppermute | solution.py:28
  11.3 24.1 %collective-permute-done.refs_0_ = bf16[80,4096]{1,0:T(8,128)(2,1)S(1)} collective-permute-done((bf16[80,4096]{1,0:T(8,128)(2,1)S(1)}, bf16[80,4096]{1,0:T(8,128)(2,1)S(1)}, u32[]{:S(2)}, u32[]{:S(2)}) %collective-permute-start) | collective-permute-done | bytes 655392 | tf_op jit(solution)/shard_map/ppermute | solution.py:28
  36.1 1.0 copy-done
  38.1 1.4 %collective-permute-done.3.refs_4_ = bf16[48,4096]{1,0:T(8,128)(2,1)} collective-permute-done((bf16[48,4096]{1,0:T(8,128)(2,1)S(1)}, bf16[48,4096]{1,0:T(8,128)(2,1)}, u32[]{:S(2)}, u32[]{:S(2)}) %collective-permute-start.3) | collective-permute-done | bytes 393248 | tf_op jit(solution)/shard_map/ppermute | solution.py:28
  39.5 4.7 %level0_rows256.1 = (bf16[128,4096]{1,0:T(8,128)(2,1)S(1)}, bf16[64,4096]{1,0:T(8,128)(2,1)S(1)}, bf16[64,4096]{1,0:T(8,128)(2,1)S(1)}, bf16[256,4096]{1,0:T(8,128)(2,1)S(1)}) custom-call(s32[640]{0:T(1024)S(1)} %concatenate.3.meta, bf16[4,256,256]{2,1,0:T(8,128)(2,1)S(1)} %reorder.1.refs_0_.inv, bf16[80,4096]{1,0:T(8,128)(2,1)S(1)} %slice.87.refs_1_, ...), custom_call_target="tpu_custom_call" | custom-call | tf_op jit(solution)/shard_map/level0_rows256/pallas_call | solution.py:228
  44.2 10.8 %collective-permute-done.1.refs_1_ = bf16[48,4096]{1,0:T(8,128)(2,1)} collective-permute-done((bf16[48,4096]{1,0:T(8,128)(2,1)S(1)}, bf16[48,4096]{1,0:T(8,128)(2,1)}, u32[]{:S(2)}, u32[]{:S(2)}) %collective-permute-start.1) | collective-permute-done | bytes 393248 | tf_op jit(solution)/shard_map/ppermute | solution.py:28
  55.0 1.5 %collective-permute-start.7 = (bf16[48,4096]{1,0:T(8,128)(2,1)}, bf16[48,4096]{1,0:T(8,128)(2,1)S(1)}, u32[]{:S(2)}, u32[]{:S(2)}) collective-permute-start(bf16[48,4096]{1,0:T(8,128)(2,1)} %collective-permute-done.1.refs_1_), channel_id=1, source_target_pairs={{0,16},{8,24},{16,0},{24,8},{1,17},{9,25},{17,1},{25,9},{2,18},{10... | collective-permute-start | bytes 1179656 | tf_op jit(solution)/shard_map/ppermute | solution.py:28
  57.0 7.6 %collective-permute-done.7.refs_3_ = bf16[48,4096]{1,0:T(8,128)(2,1)S(1)} collective-permute-done((bf16[48,4096]{1,0:T(8,128)(2,1)}, bf16[48,4096]{1,0:T(8,128)(2,1)S(1)}, u32[]{:S(2)}, u32[]{:S(2)}) %collective-permute-start.7) | collective-permute-done | bytes 393248 | tf_op jit(solution)/shard_map/ppermute | solution.py:28
  64.5 1.5 %collective-permute-start.8 = (bf16[64,4096]{1,0:T(8,128)(2,1)S(1)}, bf16[64,4096]{1,0:T(8,128)(2,1)S(1)}, u32[]{:S(2)}, u32[]{:S(2)}) collective-permute-start(bf16[64,4096]{1,0:T(8,128)(2,1)S(1)} %get-tuple-element.49.refs_2_), channel_id=1, source_target_pairs={{0,16},{8,24},{16,0},{24,8},{1,17},{9,25},{17,1},{25,9},{2,18},{10... | collective-permute-start | bytes 1572872 | tf_op jit(solution)/shard_map/ppermute | solution.py:28
  66.1 7.0 %level0_level1.1 = (bf16[48,4096]{1,0:T(8,128)(2,1)S(1)}, bf16[48,4096]{1,0:T(8,128)(2,1)S(1)}, bf16[32,4096]{1,0:T(8,128)(2,1)S(1)}, bf16[96,4096]{1,0:T(8,128)(2,1)S(1)}, bf16[256,4096]{1,0:T(8,128)(2,1)S(1)}) custom-call(s32[640]{0:T(1024)S(1)} %concatenate.3.meta, bf16[4,256,256]{2,1,0:T(8,128)(2,1)S(1)} %reorder.1.refs_0_.inv, ...), custom_call_target="tpu_custom_call" | custom-call | tf_op jit(solution)/shard_map/level0_level1/pallas_call | solution.py:254
  73.7 2.1 %collective-permute-done.11.refs_6_ = bf16[32,4096]{1,0:T(8,128)(2,1)S(1)} collective-permute-done((bf16[32,4096]{1,0:T(8,128)(2,1)S(1)}, bf16[32,4096]{1,0:T(8,128)(2,1)S(1)}, u32[]{:S(2)}, u32[]{:S(2)}) %collective-permute-start.11) | collective-permute-done | bytes 262176 | tf_op jit(solution)/shard_map/ppermute | solution.py:28
  76.0 3.2 %level2_rows144.1 = (bf16[48,4096]{1,0:T(8,128)(2,1)S(1)}, bf16[96,4096]{1,0:T(8,128)(2,1)S(1)}, bf16[256,4096]{1,0:T(8,128)(2,1)S(1)}) custom-call(s32[640]{0:T(1024)S(1)} %concatenate.3.meta, bf16[4,256,256]{2,1,0:T(8,128)(2,1)S(1)} %reorder.1.refs_0_.inv, bf16[48,4096]{1,0:T(8,128)(2,1)S(1)} %get-tuple-element.55.refs_1_, ...), custom_call_target="tpu_custom_call" | custom-call | tf_op jit(solution)/shard_map/level2_rows144/pallas_call | solution.py:228
  79.3 1.0 collective-permute-done.5.refs_3_
  80.3 1.4 level1_rows64.2
  82.3 1.4 level0_rows64.1.refs_2_
  83.7 2.5 %collective-permute-start.13 = (bf16[64,4096]{1,0:T(8,128)(2,1)S(1)}, bf16[64,4096]{1,0:T(8,128)(2,1)S(1)}, u32[]{:S(2)}, u32[]{:S(2)}) collective-permute-start(bf16[64,4096]{1,0:T(8,128)(2,1)S(1)} %level0_rows64.1.refs_2_), channel_id=1, source_target_pairs={{0,4},{1,5},{2,6},{3,7},{4,0},{5,1},{6,2},{7,3},{8,12},{9,13},{10,... | collective-permute-start | bytes 1572872 | tf_op jit(solution)/shard_map/ppermute | solution.py:28
  86.2 2.1 %level2_rows160.1.refs_8_ = bf16[160,4096]{1,0:T(8,128)(2,1)S(1)} custom-call(s32[640]{0:T(1024)S(1)} %concatenate.3.meta, bf16[4,256,256]{2,1,0:T(8,128)(2,1)S(1)} %reorder.1.refs_0_.inv, bf16[256,4096]{1,0:T(8,128)(2,1)S(1)} %get-tuple-element.64.refs_1_, bf16[96,4096]{1,0:T(8,128)(2,1)S(1)} %get-tuple-element.65.refs_2_, ...), custom_call_target="tpu_custom_call" | custom-call | tf_op jit(solution)/shard_map/level2_rows160/pallas_call | solution.py:228
  88.7 7.0 %collective-permute-done.12.refs_7_ = bf16[48,4096]{1,0:T(8,128)(2,1)S(1)} collective-permute-done((bf16[48,4096]{1,0:T(8,128)(2,1)S(1)}, bf16[48,4096]{1,0:T(8,128)(2,1)S(1)}, u32[]{:S(2)}, u32[]{:S(2)}) %collective-permute-start.12) | collective-permute-done | bytes 393248 | tf_op jit(solution)/shard_map/ppermute | solution.py:28
  96.3 6.7 %collective-permute-done.14.refs_4_ = bf16[32,4096]{1,0:T(8,128)(2,1)S(1)} collective-permute-done((bf16[32,4096]{1,0:T(8,128)(2,1)S(1)}, bf16[32,4096]{1,0:T(8,128)(2,1)S(1)}, u32[]{:S(2)}, u32[]{:S(2)}) %collective-permute-start.14) | collective-permute-done | bytes 262176 | tf_op jit(solution)/shard_map/ppermute | solution.py:28
  103.0 7.0 %collective-permute-done.13.refs_3_ = bf16[64,4096]{1,0:T(8,128)(2,1)S(1)} collective-permute-done((bf16[64,4096]{1,0:T(8,128)(2,1)S(1)}, bf16[64,4096]{1,0:T(8,128)(2,1)S(1)}, u32[]{:S(2)}, u32[]{:S(2)}) %collective-permute-start.13) | collective-permute-done | bytes 524320 | tf_op jit(solution)/shard_map/ppermute | solution.py:28
  110.0 1.4 level1_rows64.3.refs_2_
  112.0 1.3 collective-permute-done.21.refs_3_
  113.4 1.4 level2_rows64.1.refs_2_
  114.9 15.6 %collective-permute-done.20.refs_9_ = bf16[160,4096]{1,0:T(8,128)(2,1)S(1)} collective-permute-done((bf16[160,4096]{1,0:T(8,128)(2,1)S(1)}, bf16[160,4096]{1,0:T(8,128)(2,1)S(1)}, u32[]{:S(2)}, u32[]{:S(2)}) %collective-permute-start.20) | collective-permute-done | bytes 1310752 | tf_op jit(solution)/shard_map/ppermute | solution.py:28
  130.5 4.7 %level3_rows192.1 = (bf16[256,4096]{1,0:T(8,128)(2,1)}, bf16[256,4096]{1,0:T(8,128)(2,1)S(1)}) custom-call(s32[640]{0:T(1024)S(1)} %concatenate.3.meta, bf16[4,256,256]{2,1,0:T(8,128)(2,1)S(1)} %reorder.1.refs_0_.inv, bf16[48,4096]{1,0:T(8,128)(2,1)S(1)} %get-tuple-element.59.refs_1_, bf16[96,4096]{1,0:T(8,128)(2,1)S(1)} %get-tuple-element.60.refs_2_, ...), custom_call_target="tpu_custom_call" | custom-call | flops 49999998976 | tf_op jit(solution)/shard_map/level3_rows192/pallas_call | solution.py:228
  135.2 6.0 %collective-permute-done.22.refs_3_ = bf16[64,4096]{1,0:T(8,128)(2,1)S(1)} collective-permute-done((bf16[64,4096]{1,0:T(8,128)(2,1)S(1)}, bf16[64,4096]{1,0:T(8,128)(2,1)S(1)}, u32[]{:S(2)}, u32[]{:S(2)}) %collective-permute-start.22) | collective-permute-done | bytes 524320 | tf_op jit(solution)/shard_map/ppermute | solution.py:28
  141.2 2.2 %level3_rows64.1 = bf16[256,4096]{1,0:T(8,128)(2,1)} custom-call(s32[640]{0:T(1024)S(1)} %concatenate.3.meta, bf16[4,256,256]{2,1,0:T(8,128)(2,1)S(1)} %reorder.1.refs_0_.inv, bf16[256,4096]{1,0:T(8,128)(2,1)S(1)} %get-tuple-element.71.refs_1_, bf16[64,4096]{1,0:T(8,128)(2,1)S(1)} %level2_rows64.1.refs_2_, ...), custom_call_target="tpu_custom_call", output_to_operand_aliasing={{}: (5, {})} | custom-call | tf_op jit(solution)/shard_map/level3_rows64/pallas_call | solution.py:228
  (45 shorter events, 5.8 us)
Async XLA Ops:
  0.0 35.8 %copy-start.1 = (s32[4,2,32]{2,1,0:T(2,128)S(1)}, s32[4,2,32]{2,1,0:T(2,128)}, u32[]{:S(2)}) copy-start(s32[4,2,32]{2,1,0:T(2,128)} %param.7) | copy-start | bytes 3076
  0.0 35.9 %copy-start.3 = (s32[4,32]{1,0:T(4,128)S(1)}, s32[4,32]{1,0:T(4,128)}, u32[]{:S(2)}) copy-start(s32[4,32]{1,0:T(4,128)} %param.8) | copy-start | bytes 1540
  0.0 35.9 %copy-start.2 = (s32[4,32]{1,0:T(4,128)S(1)}, s32[4,32]{1,0:T(4,128)}, u32[]{:S(2)}) copy-start(s32[4,32]{1,0:T(4,128)} %param.9) | copy-start | bytes 1540
  1.2 38.4 %collective-permute-start.2 = (bf16[80,4096]{1,0:T(8,128)(2,1)S(1)}, bf16[80,4096]{1,0:T(8,128)(2,1)}, u32[]{:S(2)}, u32[]{:S(2)}) collective-permute-start(bf16[80,4096]{1,0:T(8,128)(2,1)S(1)} %slice.87.refs_1_), channel_id=1, source_target_pairs={{0,16},{8,24},{16,0},{24,8},{1,17},{9,25},{17,1},{25,9},{2,18},{10... | collective-permute-start | bytes 1966088 | tf_op jit(solution)/shard_map/ppermute | solution.py:28
  4.2 31.1 %collective-permute-start = (bf16[80,4096]{1,0:T(8,128)(2,1)S(1)}, bf16[80,4096]{1,0:T(8,128)(2,1)S(1)}, u32[]{:S(2)}, u32[]{:S(2)}) collective-permute-start(bf16[80,4096]{1,0:T(8,128)(2,1)S(1)} %slice.87.refs_1_), channel_id=1, source_target_pairs={{0,4},{1,5},{2,6},{3,7},{4,0},{5,1},{6,2},{7,3},{8,12},{9,13},{10,... | collective-permute-start | bytes 1966088 | tf_op jit(solution)/shard_map/ppermute | solution.py:28
  8.1 30.0 %collective-permute-start.4 = (bf16[64,4096]{1,0:T(8,128)(2,1)S(1)}, bf16[64,4096]{1,0:T(8,128)(2,1)}, u32[]{:S(2)}, u32[]{:S(2)}) collective-permute-start(bf16[64,4096]{1,0:T(8,128)(2,1)S(1)} %get-tuple-element.76.refs_5_), channel_id=1, source_target_pairs={{0,16},{8,24},{16,0},{24,8},{1,17},{9,25},{17,1},{25,9},{2,18},{10... | collective-permute-start | bytes 1572872 | tf_op jit(solution)/shard_map/ppermute | solution.py:28
  9.7 29.9 %collective-permute-start.3 = (bf16[48,4096]{1,0:T(8,128)(2,1)S(1)}, bf16[48,4096]{1,0:T(8,128)(2,1)}, u32[]{:S(2)}, u32[]{:S(2)}) collective-permute-start(bf16[48,4096]{1,0:T(8,128)(2,1)S(1)} %slice.88.refs_2_), channel_id=1, source_target_pairs={{0,16},{8,24},{16,0},{24,8},{1,17},{9,25},{17,1},{25,9},{2,18},{10... | collective-permute-start | bytes 1179656 | tf_op jit(solution)/shard_map/ppermute | solution.py:28
  35.3 19.7 %collective-permute-start.6 = (bf16[80,4096]{1,0:T(8,128)(2,1)S(1)}, bf16[80,4096]{1,0:T(8,128)(2,1)S(1)}, u32[]{:S(2)}, u32[]{:S(2)}) collective-permute-start(bf16[80,4096]{1,0:T(8,128)(2,1)S(1)} %collective-permute-done.refs_0_), channel_id=1, source_target_pairs={{0,16},{8,24},{16,0},{24,8},{1,17},{9,25},{17,1},{25,9},{2,18},{10... | collective-permute-start | bytes 1966088 | tf_op jit(solution)/shard_map/ppermute | solution.py:28
  35.8 19.2 %collective-permute-start.1 = (bf16[48,4096]{1,0:T(8,128)(2,1)S(1)}, bf16[48,4096]{1,0:T(8,128)(2,1)}, u32[]{:S(2)}, u32[]{:S(2)}) collective-permute-start(bf16[48,4096]{1,0:T(8,128)(2,1)S(1)} %slice.88.refs_2_), channel_id=1, source_target_pairs={{0,4},{1,5},{2,6},{3,7},{4,0},{5,1},{6,2},{7,3},{8,12},{9,13},{10,... | collective-permute-start | bytes 1179656 | tf_op jit(solution)/shard_map/ppermute | solution.py:28
  36.1 1.0 copy-start
  55.0 9.5 %collective-permute-start.7 = (bf16[48,4096]{1,0:T(8,128)(2,1)}, bf16[48,4096]{1,0:T(8,128)(2,1)S(1)}, u32[]{:S(2)}, u32[]{:S(2)}) collective-permute-start(bf16[48,4096]{1,0:T(8,128)(2,1)} %collective-permute-done.1.refs_1_), channel_id=1, source_target_pairs={{0,16},{8,24},{16,0},{24,8},{1,17},{9,25},{17,1},{25,9},{2,18},{10... | collective-permute-start | bytes 1179656 | tf_op jit(solution)/shard_map/ppermute | solution.py:28
  56.6 23.7 %collective-permute-start.5 = (bf16[64,4096]{1,0:T(8,128)(2,1)S(1)}, bf16[64,4096]{1,0:T(8,128)(2,1)S(1)}, u32[]{:S(2)}, u32[]{:S(2)}) collective-permute-start(bf16[64,4096]{1,0:T(8,128)(2,1)S(1)} %get-tuple-element.45.refs_2_), channel_id=1, source_target_pairs={{0,4},{1,5},{2,6},{3,7},{4,0},{5,1},{6,2},{7,3},{8,12},{9,13},{10,... | collective-permute-start | bytes 1572872 | tf_op jit(solution)/shard_map/ppermute | solution.py:28
  64.5 15.8 %collective-permute-start.8 = (bf16[64,4096]{1,0:T(8,128)(2,1)S(1)}, bf16[64,4096]{1,0:T(8,128)(2,1)S(1)}, u32[]{:S(2)}, u32[]{:S(2)}) collective-permute-start(bf16[64,4096]{1,0:T(8,128)(2,1)S(1)} %get-tuple-element.49.refs_2_), channel_id=1, source_target_pairs={{0,16},{8,24},{16,0},{24,8},{1,17},{9,25},{17,1},{25,9},{2,18},{10... | collective-permute-start | bytes 1572872 | tf_op jit(solution)/shard_map/ppermute | solution.py:28
  73.1 2.9 %collective-permute-start.10 = (bf16[48,4096]{1,0:T(8,128)(2,1)S(1)}, bf16[48,4096]{1,0:T(8,128)(2,1)S(1)}, u32[]{:S(2)}, u32[]{:S(2)}) collective-permute-start(bf16[48,4096]{1,0:T(8,128)(2,1)S(1)} %get-tuple-element.56.refs_2_), channel_id=1, source_target_pairs={{0,8},{8,0},{16,24},{24,16},{1,9},{9,1},{17,25},{25,17},{2,10},{10... | collective-permute-start | bytes 1179656 | tf_op jit(solution)/shard_map/ppermute | solution.py:28
  73.2 2.8 %collective-permute-start.9 = (bf16[48,4096]{1,0:T(8,128)(2,1)S(1)}, bf16[48,4096]{1,0:T(8,128)(2,1)S(1)}, u32[]{:S(2)}, u32[]{:S(2)}) collective-permute-start(bf16[48,4096]{1,0:T(8,128)(2,1)S(1)} %get-tuple-element.55.refs_1_), channel_id=1, source_target_pairs={{0,8},{8,0},{16,24},{24,16},{1,9},{9,1},{17,25},{25,17},{2,10},{10... | collective-permute-start | bytes 1179656 | tf_op jit(solution)/shard_map/ppermute | solution.py:28
  73.7 2.1 %collective-permute-start.11 = (bf16[32,4096]{1,0:T(8,128)(2,1)S(1)}, bf16[32,4096]{1,0:T(8,128)(2,1)S(1)}, u32[]{:S(2)}, u32[]{:S(2)}) collective-permute-start(bf16[32,4096]{1,0:T(8,128)(2,1)S(1)} %get-tuple-element.57.refs_3_), channel_id=1, source_target_pairs={{0,8},{8,0},{16,24},{24,16},{1,9},{9,1},{17,25},{25,17},{2,10},{10... | collective-permute-start | bytes 786440 | tf_op jit(solution)/shard_map/ppermute | solution.py:28
  75.8 10.4 %collective-permute-start.17 = (bf16[96,4096]{1,0:T(8,128)(2,1)S(1)}, bf16[96,4096]{1,0:T(8,128)(2,1)S(1)}, u32[]{:S(2)}, u32[]{:S(2)}) collective-permute-start(bf16[96,4096]{1,0:T(8,128)(2,1)S(1)} %get-tuple-element.65.refs_2_), channel_id=1, source_target_pairs={{0,8},{8,0},{16,24},{24,16},{1,9},{9,1},{17,25},{25,17},{2,10},{10... | collective-permute-start | bytes 2359304 | tf_op jit(solution)/shard_map/ppermute | solution.py:28
  79.2 16.5 %collective-permute-start.12 = (bf16[48,4096]{1,0:T(8,128)(2,1)S(1)}, bf16[48,4096]{1,0:T(8,128)(2,1)S(1)}, u32[]{:S(2)}, u32[]{:S(2)}) collective-permute-start(bf16[48,4096]{1,0:T(8,128)(2,1)S(1)} %get-tuple-element.59.refs_1_), channel_id=1, source_target_pairs={{0,2},{1,3},{2,0},{3,1},{4,6},{5,7},{6,4},{7,5},{8,10},{9,11},{10,... | collective-permute-start | bytes 1179656 | tf_op jit(solution)/shard_map/ppermute | solution.py:28
  81.7 4.5 %collective-permute-start.18 = (bf16[32,4096]{1,0:T(8,128)(2,1)S(1)}, bf16[32,4096]{1,0:T(8,128)(2,1)S(1)}, u32[]{:S(2)}, u32[]{:S(2)}) collective-permute-start(bf16[32,4096]{1,0:T(8,128)(2,1)S(1)} %get-tuple-element.69.refs_4_), channel_id=1, source_target_pairs={{0,8},{8,0},{16,24},{24,16},{1,9},{9,1},{17,25},{25,17},{2,10},{10... | collective-permute-start | bytes 786440 | tf_op jit(solution)/shard_map/ppermute | solution.py:28
  81.8 4.4 %collective-permute-start.19 = (bf16[32,4096]{1,0:T(8,128)(2,1)S(1)}, bf16[32,4096]{1,0:T(8,128)(2,1)S(1)}, u32[]{:S(2)}, u32[]{:S(2)}) collective-permute-start(bf16[32,4096]{1,0:T(8,128)(2,1)S(1)} %get-tuple-element.70.refs_6_), channel_id=1, source_target_pairs={{0,8},{8,0},{16,24},{24,16},{1,9},{9,1},{17,25},{25,17},{2,10},{10... | collective-permute-start | bytes 786440 | tf_op jit(solution)/shard_map/ppermute | solution.py:28
  83.7 26.3 %collective-permute-start.13 = (bf16[64,4096]{1,0:T(8,128)(2,1)S(1)}, bf16[64,4096]{1,0:T(8,128)(2,1)S(1)}, u32[]{:S(2)}, u32[]{:S(2)}) collective-permute-start(bf16[64,4096]{1,0:T(8,128)(2,1)S(1)} %level0_rows64.1.refs_2_), channel_id=1, source_target_pairs={{0,4},{1,5},{2,6},{3,7},{4,0},{5,1},{6,2},{7,3},{8,12},{9,13},{10,... | collective-permute-start | bytes 1572872 | tf_op jit(solution)/shard_map/ppermute | solution.py:28
  88.3 42.2 %collective-permute-start.20 = (bf16[160,4096]{1,0:T(8,128)(2,1)S(1)}, bf16[160,4096]{1,0:T(8,128)(2,1)S(1)}, u32[]{:S(2)}, u32[]{:S(2)}) collective-permute-start(bf16[160,4096]{1,0:T(8,128)(2,1)S(1)} %level2_rows160.1.refs_8_), channel_id=1, source_target_pairs={{0,2},{1,3},{2,0},{3,1},{4,6},{5,7},{6,4},{7,5},{8,10},{9,11},{10,... | collective-permute-start | bytes 3932168 | tf_op jit(solution)/shard_map/ppermute | solution.py:28
  95.7 7.3 %collective-permute-start.14 = (bf16[32,4096]{1,0:T(8,128)(2,1)S(1)}, bf16[32,4096]{1,0:T(8,128)(2,1)S(1)}, u32[]{:S(2)}, u32[]{:S(2)}) collective-permute-start(bf16[32,4096]{1,0:T(8,128)(2,1)S(1)} %slice.92.refs_3_), channel_id=1, source_target_pairs={{0,16},{8,24},{16,0},{24,8},{1,17},{9,25},{17,1},{25,9},{2,18},{10... | collective-permute-start | bytes 786440 | tf_op jit(solution)/shard_map/ppermute | solution.py:28
  111.4 2.0 %collective-permute-start.21 = (bf16[64,4096]{1,0:T(8,128)(2,1)S(1)}, bf16[64,4096]{1,0:T(8,128)(2,1)S(1)}, u32[]{:S(2)}, u32[]{:S(2)}) collective-permute-start(bf16[64,4096]{1,0:T(8,128)(2,1)S(1)} %level1_rows64.3.refs_2_), channel_id=1, source_target_pairs={{0,8},{8,0},{16,24},{24,16},{1,9},{9,1},{17,25},{25,17},{2,10},{10... | collective-permute-start | bytes 1572872 | tf_op jit(solution)/shard_map/ppermute | solution.py:28
  111.5 3.4 %collective-permute-start.15 = (bf16[32,4096]{1,0:T(8,128)(2,1)S(1)}, bf16[32,4096]{1,0:T(8,128)(2,1)S(1)}, u32[]{:S(2)}, u32[]{:S(2)}) collective-permute-start(bf16[32,4096]{1,0:T(8,128)(2,1)S(1)} %slice.92.refs_3_), channel_id=1, source_target_pairs={{0,8},{8,0},{16,24},{24,16},{1,9},{9,1},{17,25},{25,17},{2,10},{10... | collective-permute-start | bytes 786440 | tf_op jit(solution)/shard_map/ppermute | solution.py:28
  112.0 2.9 %collective-permute-start.16 = (bf16[32,4096]{1,0:T(8,128)(2,1)S(1)}, bf16[32,4096]{1,0:T(8,128)(2,1)S(1)}, u32[]{:S(2)}, u32[]{:S(2)}) collective-permute-start(bf16[32,4096]{1,0:T(8,128)(2,1)S(1)} %collective-permute-done.14.refs_4_), channel_id=1, source_target_pairs={{0,8},{8,0},{16,24},{24,16},{1,9},{9,1},{17,25},{25,17},{2,10},{10... | collective-permute-start | bytes 786440 | tf_op jit(solution)/shard_map/ppermute | solution.py:28
  114.8 26.4 %collective-permute-start.22 = (bf16[64,4096]{1,0:T(8,128)(2,1)S(1)}, bf16[64,4096]{1,0:T(8,128)(2,1)S(1)}, u32[]{:S(2)}, u32[]{:S(2)}) collective-permute-start(bf16[64,4096]{1,0:T(8,128)(2,1)S(1)} %level2_rows64.1.refs_2_), channel_id=1, source_target_pairs={{0,2},{1,3},{2,0},{3,1},{4,6},{5,7},{6,4},{7,5},{8,10},{9,11},{10,... | collective-permute-start | bytes 1572872 | tf_op jit(solution)/shard_map/ppermute | solution.py:28

commit v10 on v9

--- a/solution.py
+++ b/solution.py
@@ -107,7 +107,7 @@
                 panel[pl.ds(half + start, rows), at(j)] = (from_b * keep_b).astype(BF16)
             return carry
 
-        lax.fori_loop(0, blocks, merge_block, 0, unroll=8)
+        lax.fori_loop(0, blocks, merge_block, 0, unroll=True)
 
     def columns(job, j):
         source, start, rows = job
@@ -139,7 +139,7 @@
                 done += rows
         return carry
 
-    lax.fori_loop(0, width // TILE, finish_tile, 0, unroll=8)
+    lax.fori_loop(0, width // TILE, finish_tile, 0, unroll=True)
 
 
 def level_kernel(meta, *refs, level, blocks, n_in, top, pairs, outs, n_hidden):

time: 144 us -> 142 us (0.986)
  Pallas kernels: 30.3 us -> 23.1 us
  waiting for transfers between devices: 90.6 us -> 95.9 us
    ppermute x23, waiting for transfers between devices: 90.6 us -> 95.9 us  [trade(): lax.ppermute(block, axis, [(i, i ^ flip) for i in range(lax.axis_size(axi...]
    pallas_call x9, Pallas kernels: 22.4 us -> 17.7 us  [run_level(): pl.pallas_call(kernel, grid=(1,) if part is not None else (), out_shape=s...]
    pallas_call x1, Pallas kernels: 7 us -> 4.45 us  [run_two_levels(): pl.pallas_call(kernel, out_shape=[jax.ShapeDtypeStruct((n, width), BF16)...]
  transfers between devices with their start and end apart: 23 -> 23, of which waited for: 12 -> 13; matrix products, arithmetic and copies ran while one was open for 2% -> 2% of each run, Pallas kernels for 20% -> 15%
where the time goes in v10:
time: 142 us; the launch traced here: 141 us
  waiting for transfers between devices  95.9 us (68%)
  Pallas kernels  23.1 us (16%)
  starting transfers between devices  17.4 us (12%)
  local copies, waits for them, and re-layouts  4.65 us (3%)
    ppermute x23, waiting for transfers between devices, trade(): lax.ppermute(block, axis, [(i, i ^ flip) for i in range(lax.axis_size(axi...  95.9 us
    pallas_call x9, Pallas kernels, run_level(): pl.pallas_call(kernel, grid=(1,) if part is not None else (), out_shape=s...  17.7 us
    ppermute x23, starting transfers between devices, trade(): lax.ppermute(block, axis, [(i, i ^ flip) for i in range(lax.axis_size(axi...  17.4 us
    pallas_call x1, Pallas kernels, run_two_levels(): pl.pallas_call(kernel, out_shape=[jax.ShapeDtypeStruct((n, width), BF16)...  4.45 us
  transfers between devices with their start and end apart: 23, of which 13 were waited for; matrix products, arithmetic and copies ran while one was open for 2% of the time, Pallas kernels for 15%

profile of v10, /device:TPU:0, one launch (start us, length us, event | category | flops | bytes accessed | tf_op | source)
XLA Modules:
  0.0 141.3 jit_solution(16723394291539034933)
XLA Ops:
  0.0 1.2 slice.87.refs_1_
  1.2 3.0 %collective-permute-start.2 = (bf16[80,4096]{1,0:T(8,128)(2,1)S(1)}, bf16[80,4096]{1,0:T(8,128)(2,1)}, u32[]{:S(2)}, u32[]{:S(2)}) collective-permute-start(bf16[80,4096]{1,0:T(8,128)(2,1)S(1)} %slice.87.refs_1_), channel_id=1, source_target_pairs={{0,16},{8,24},{16,0},{24,8},{1,17},{9,25},{17,1},{25,9},{2,18},{10... | collective-permute-start | bytes 1966088 | tf_op jit(solution)/shard_map/ppermute | solution.py:28
  4.2 2.6 %collective-permute-start = (bf16[80,4096]{1,0:T(8,128)(2,1)S(1)}, bf16[80,4096]{1,0:T(8,128)(2,1)S(1)}, u32[]{:S(2)}, u32[]{:S(2)}) collective-permute-start(bf16[80,4096]{1,0:T(8,128)(2,1)S(1)} %slice.87.refs_1_), channel_id=1, source_target_pairs={{0,4},{1,5},{2,6},{3,7},{4,0},{5,1},{6,2},{7,3},{8,12},{9,13},{10,... | collective-permute-start | bytes 1966088 | tf_op jit(solution)/shard_map/ppermute | solution.py:28
  6.8 1.3 fusion.8
  8.6 1.0 slice.88.refs_2_
  9.7 1.6 %collective-permute-start.3 = (bf16[48,4096]{1,0:T(8,128)(2,1)S(1)}, bf16[48,4096]{1,0:T(8,128)(2,1)}, u32[]{:S(2)}, u32[]{:S(2)}) collective-permute-start(bf16[48,4096]{1,0:T(8,128)(2,1)S(1)} %slice.88.refs_2_), channel_id=1, source_target_pairs={{0,16},{8,24},{16,0},{24,8},{1,17},{9,25},{17,1},{25,9},{2,18},{10... | collective-permute-start | bytes 1179656 | tf_op jit(solution)/shard_map/ppermute | solution.py:28
  11.3 24.1 %collective-permute-done.refs_0_ = bf16[80,4096]{1,0:T(8,128)(2,1)S(1)} collective-permute-done((bf16[80,4096]{1,0:T(8,128)(2,1)S(1)}, bf16[80,4096]{1,0:T(8,128)(2,1)S(1)}, u32[]{:S(2)}, u32[]{:S(2)}) %collective-permute-start) | collective-permute-done | bytes 655392 | tf_op jit(solution)/shard_map/ppermute | solution.py:28
  36.1 1.0 copy-done
  38.1 1.4 %collective-permute-done.3.refs_4_ = bf16[48,4096]{1,0:T(8,128)(2,1)} collective-permute-done((bf16[48,4096]{1,0:T(8,128)(2,1)S(1)}, bf16[48,4096]{1,0:T(8,128)(2,1)}, u32[]{:S(2)}, u32[]{:S(2)}) %collective-permute-start.3) | collective-permute-done | bytes 393248 | tf_op jit(solution)/shard_map/ppermute | solution.py:28
  39.5 3.5 %level0_rows256.1 = (bf16[128,4096]{1,0:T(8,128)(2,1)S(1)}, bf16[64,4096]{1,0:T(8,128)(2,1)S(1)}, bf16[64,4096]{1,0:T(8,128)(2,1)S(1)}, bf16[256,4096]{1,0:T(8,128)(2,1)S(1)}) custom-call(s32[640]{0:T(1024)S(1)} %concatenate.3.meta, bf16[4,256,256]{2,1,0:T(8,128)(2,1)S(1)} %reorder.1.refs_0_.inv, bf16[80,4096]{1,0:T(8,128)(2,1)S(1)} %slice.87.refs_1_, ...), custom_call_target="tpu_custom_call" | custom-call | tf_op jit(solution)/shard_map/level0_rows256/pallas_call | solution.py:228
  43.0 12.0 %collective-permute-done.1.refs_1_ = bf16[48,4096]{1,0:T(8,128)(2,1)} collective-permute-done((bf16[48,4096]{1,0:T(8,128)(2,1)S(1)}, bf16[48,4096]{1,0:T(8,128)(2,1)}, u32[]{:S(2)}, u32[]{:S(2)}) %collective-permute-start.1) | collective-permute-done | bytes 393248 | tf_op jit(solution)/shard_map/ppermute | solution.py:28
  55.0 1.5 %collective-permute-start.7 = (bf16[48,4096]{1,0:T(8,128)(2,1)}, bf16[48,4096]{1,0:T(8,128)(2,1)S(1)}, u32[]{:S(2)}, u32[]{:S(2)}) collective-permute-start(bf16[48,4096]{1,0:T(8,128)(2,1)} %collective-permute-done.1.refs_1_), channel_id=1, source_target_pairs={{0,16},{8,24},{16,0},{24,8},{1,17},{9,25},{17,1},{25,9},{2,18},{10... | collective-permute-start | bytes 1179656 | tf_op jit(solution)/shard_map/ppermute | solution.py:28
  57.0 7.6 %collective-permute-done.7.refs_3_ = bf16[48,4096]{1,0:T(8,128)(2,1)S(1)} collective-permute-done((bf16[48,4096]{1,0:T(8,128)(2,1)}, bf16[48,4096]{1,0:T(8,128)(2,1)S(1)}, u32[]{:S(2)}, u32[]{:S(2)}) %collective-permute-start.7) | collective-permute-done | bytes 393248 | tf_op jit(solution)/shard_map/ppermute | solution.py:28
  64.5 1.5 %collective-permute-start.8 = (bf16[64,4096]{1,0:T(8,128)(2,1)S(1)}, bf16[64,4096]{1,0:T(8,128)(2,1)S(1)}, u32[]{:S(2)}, u32[]{:S(2)}) collective-permute-start(bf16[64,4096]{1,0:T(8,128)(2,1)S(1)} %get-tuple-element.49.refs_2_), channel_id=1, source_target_pairs={{0,16},{8,24},{16,0},{24,8},{1,17},{9,25},{17,1},{25,9},{2,18},{10... | collective-permute-start | bytes 1572872 | tf_op jit(solution)/shard_map/ppermute | solution.py:28
  66.1 4.5 %level0_level1.1 = (bf16[48,4096]{1,0:T(8,128)(2,1)S(1)}, bf16[48,4096]{1,0:T(8,128)(2,1)S(1)}, bf16[32,4096]{1,0:T(8,128)(2,1)S(1)}, bf16[96,4096]{1,0:T(8,128)(2,1)S(1)}, bf16[256,4096]{1,0:T(8,128)(2,1)S(1)}) custom-call(s32[640]{0:T(1024)S(1)} %concatenate.3.meta, bf16[4,256,256]{2,1,0:T(8,128)(2,1)S(1)} %reorder.1.refs_0_.inv, ...), custom_call_target="tpu_custom_call" | custom-call | tf_op jit(solution)/shard_map/level0_level1/pallas_call | solution.py:254
  71.2 2.1 %collective-permute-done.11.refs_6_ = bf16[32,4096]{1,0:T(8,128)(2,1)S(1)} collective-permute-done((bf16[32,4096]{1,0:T(8,128)(2,1)S(1)}, bf16[32,4096]{1,0:T(8,128)(2,1)S(1)}, u32[]{:S(2)}, u32[]{:S(2)}) %collective-permute-start.11) | collective-permute-done | bytes 262176 | tf_op jit(solution)/shard_map/ppermute | solution.py:28
  73.4 2.2 %level2_rows144.1 = (bf16[48,4096]{1,0:T(8,128)(2,1)S(1)}, bf16[96,4096]{1,0:T(8,128)(2,1)S(1)}, bf16[256,4096]{1,0:T(8,128)(2,1)S(1)}) custom-call(s32[640]{0:T(1024)S(1)} %concatenate.3.meta, bf16[4,256,256]{2,1,0:T(8,128)(2,1)S(1)} %reorder.1.refs_0_.inv, bf16[48,4096]{1,0:T(8,128)(2,1)S(1)} %get-tuple-element.55.refs_1_, ...), custom_call_target="tpu_custom_call" | custom-call | tf_op jit(solution)/shard_map/level2_rows144/pallas_call | solution.py:228
  75.8 4.6 %collective-permute-done.5.refs_3_ = bf16[64,4096]{1,0:T(8,128)(2,1)S(1)} collective-permute-done((bf16[64,4096]{1,0:T(8,128)(2,1)S(1)}, bf16[64,4096]{1,0:T(8,128)(2,1)S(1)}, u32[]{:S(2)}, u32[]{:S(2)}) %collective-permute-start.5) | collective-permute-done | bytes 524320 | tf_op jit(solution)/shard_map/ppermute | solution.py:28
  80.4 1.2 level1_rows64.2
  82.2 1.2 level0_rows64.1.refs_2_
  83.6 1.5 %level2_rows160.1.refs_8_ = bf16[160,4096]{1,0:T(8,128)(2,1)S(1)} custom-call(s32[640]{0:T(1024)S(1)} %concatenate.3.meta, bf16[4,256,256]{2,1,0:T(8,128)(2,1)S(1)} %reorder.1.refs_0_.inv, bf16[256,4096]{1,0:T(8,128)(2,1)S(1)} %get-tuple-element.64.refs_1_, bf16[96,4096]{1,0:T(8,128)(2,1)S(1)} %get-tuple-element.65.refs_2_, ...), custom_call_target="tpu_custom_call" | custom-call | tf_op jit(solution)/shard_map/level2_rows160/pallas_call | solution.py:228
  85.1 2.8 %collective-permute-start.20 = (bf16[160,4096]{1,0:T(8,128)(2,1)S(1)}, bf16[160,4096]{1,0:T(8,128)(2,1)S(1)}, u32[]{:S(2)}, u32[]{:S(2)}) collective-permute-start(bf16[160,4096]{1,0:T(8,128)(2,1)S(1)} %level2_rows160.1.refs_8_), channel_id=1, source_target_pairs={{0,2},{1,3},{2,0},{3,1},{4,6},{5,7},{6,4},{7,5},{8,10},{9,11},{10,... | collective-permute-start | bytes 3932168 | tf_op jit(solution)/shard_map/ppermute | solution.py:28
  87.9 2.2 %collective-permute-done.12.refs_7_ = bf16[48,4096]{1,0:T(8,128)(2,1)S(1)} collective-permute-done((bf16[48,4096]{1,0:T(8,128)(2,1)S(1)}, bf16[48,4096]{1,0:T(8,128)(2,1)S(1)}, u32[]{:S(2)}, u32[]{:S(2)}) %collective-permute-start.12) | collective-permute-done | bytes 393248 | tf_op jit(solution)/shard_map/ppermute | solution.py:28
  90.7 7.7 %collective-permute-done.14.refs_4_ = bf16[32,4096]{1,0:T(8,128)(2,1)S(1)} collective-permute-done((bf16[32,4096]{1,0:T(8,128)(2,1)S(1)}, bf16[32,4096]{1,0:T(8,128)(2,1)S(1)}, u32[]{:S(2)}, u32[]{:S(2)}) %collective-permute-start.14) | collective-permute-done | bytes 262176 | tf_op jit(solution)/shard_map/ppermute | solution.py:28
  98.4 11.3 %collective-permute-done.13.refs_3_ = bf16[64,4096]{1,0:T(8,128)(2,1)S(1)} collective-permute-done((bf16[64,4096]{1,0:T(8,128)(2,1)S(1)}, bf16[64,4096]{1,0:T(8,128)(2,1)S(1)}, u32[]{:S(2)}, u32[]{:S(2)}) %collective-permute-start.13) | collective-permute-done | bytes 524320 | tf_op jit(solution)/shard_map/ppermute | solution.py:28
  109.7 1.2 level1_rows64.3.refs_2_
  111.6 1.3 collective-permute-done.21.refs_3_
  112.9 1.2 level2_rows64.1.refs_2_
  114.2 13.9 %collective-permute-done.20.refs_9_ = bf16[160,4096]{1,0:T(8,128)(2,1)S(1)} collective-permute-done((bf16[160,4096]{1,0:T(8,128)(2,1)S(1)}, bf16[160,4096]{1,0:T(8,128)(2,1)S(1)}, u32[]{:S(2)}, u32[]{:S(2)}) %collective-permute-start.20) | collective-permute-done | bytes 1310752 | tf_op jit(solution)/shard_map/ppermute | solution.py:28
  128.1 3.6 %level3_rows192.1 = (bf16[256,4096]{1,0:T(8,128)(2,1)}, bf16[256,4096]{1,0:T(8,128)(2,1)S(1)}) custom-call(s32[640]{0:T(1024)S(1)} %concatenate.3.meta, bf16[4,256,256]{2,1,0:T(8,128)(2,1)S(1)} %reorder.1.refs_0_.inv, bf16[48,4096]{1,0:T(8,128)(2,1)S(1)} %get-tuple-element.59.refs_1_, bf16[96,4096]{1,0:T(8,128)(2,1)S(1)} %get-tuple-element.60.refs_2_, ...), custom_call_target="tpu_custom_call" | custom-call | flops 49999998976 | tf_op jit(solution)/shard_map/level3_rows192/pallas_call | solution.py:228
  131.7 7.6 %collective-permute-done.22.refs_3_ = bf16[64,4096]{1,0:T(8,128)(2,1)S(1)} collective-permute-done((bf16[64,4096]{1,0:T(8,128)(2,1)S(1)}, bf16[64,4096]{1,0:T(8,128)(2,1)S(1)}, u32[]{:S(2)}, u32[]{:S(2)}) %collective-permute-start.22) | collective-permute-done | bytes 524320 | tf_op jit(solution)/shard_map/ppermute | solution.py:28
  139.3 2.0 %level3_rows64.1 = bf16[256,4096]{1,0:T(8,128)(2,1)} custom-call(s32[640]{0:T(1024)S(1)} %concatenate.3.meta, bf16[4,256,256]{2,1,0:T(8,128)(2,1)S(1)} %reorder.1.refs_0_.inv, bf16[256,4096]{1,0:T(8,128)(2,1)S(1)} %get-tuple-element.71.refs_1_, bf16[64,4096]{1,0:T(8,128)(2,1)S(1)} %level2_rows64.1.refs_2_, ...), custom_call_target="tpu_custom_call", output_to_operand_aliasing={{}: (5, {})} | custom-call | tf_op jit(solution)/shard_map/level3_rows64/pallas_call | solution.py:228
  (45 shorter events, 5.5 us)
Async XLA Ops:
  0.0 35.8 %copy-start.1 = (s32[4,2,32]{2,1,0:T(2,128)S(1)}, s32[4,2,32]{2,1,0:T(2,128)}, u32[]{:S(2)}) copy-start(s32[4,2,32]{2,1,0:T(2,128)} %param.7) | copy-start | bytes 3076
  0.0 35.9 %copy-start.3 = (s32[4,32]{1,0:T(4,128)S(1)}, s32[4,32]{1,0:T(4,128)}, u32[]{:S(2)}) copy-start(s32[4,32]{1,0:T(4,128)} %param.8) | copy-start | bytes 1540
  0.0 35.9 %copy-start.2 = (s32[4,32]{1,0:T(4,128)S(1)}, s32[4,32]{1,0:T(4,128)}, u32[]{:S(2)}) copy-start(s32[4,32]{1,0:T(4,128)} %param.9) | copy-start | bytes 1540
  1.2 38.4 %collective-permute-start.2 = (bf16[80,4096]{1,0:T(8,128)(2,1)S(1)}, bf16[80,4096]{1,0:T(8,128)(2,1)}, u32[]{:S(2)}, u32[]{:S(2)}) collective-permute-start(bf16[80,4096]{1,0:T(8,128)(2,1)S(1)} %slice.87.refs_1_), channel_id=1, source_target_pairs={{0,16},{8,24},{16,0},{24,8},{1,17},{9,25},{17,1},{25,9},{2,18},{10... | collective-permute-start | bytes 1966088 | tf_op jit(solution)/shard_map/ppermute | solution.py:28
  4.2 31.1 %collective-permute-start = (bf16[80,4096]{1,0:T(8,128)(2,1)S(1)}, bf16[80,4096]{1,0:T(8,128)(2,1)S(1)}, u32[]{:S(2)}, u32[]{:S(2)}) collective-permute-start(bf16[80,4096]{1,0:T(8,128)(2,1)S(1)} %slice.87.refs_1_), channel_id=1, source_target_pairs={{0,4},{1,5},{2,6},{3,7},{4,0},{5,1},{6,2},{7,3},{8,12},{9,13},{10,... | collective-permute-start | bytes 1966088 | tf_op jit(solution)/shard_map/ppermute | solution.py:28
  8.1 30.0 %collective-permute-start.4 = (bf16[64,4096]{1,0:T(8,128)(2,1)S(1)}, bf16[64,4096]{1,0:T(8,128)(2,1)}, u32[]{:S(2)}, u32[]{:S(2)}) collective-permute-start(bf16[64,4096]{1,0:T(8,128)(2,1)S(1)} %get-tuple-element.76.refs_5_), channel_id=1, source_target_pairs={{0,16},{8,24},{16,0},{24,8},{1,17},{9,25},{17,1},{25,9},{2,18},{10... | collective-permute-start | bytes 1572872 | tf_op jit(solution)/shard_map/ppermute | solution.py:28
  9.7 29.9 %collective-permute-start.3 = (bf16[48,4096]{1,0:T(8,128)(2,1)S(1)}, bf16[48,4096]{1,0:T(8,128)(2,1)}, u32[]{:S(2)}, u32[]{:S(2)}) collective-permute-start(bf16[48,4096]{1,0:T(8,128)(2,1)S(1)} %slice.88.refs_2_), channel_id=1, source_target_pairs={{0,16},{8,24},{16,0},{24,8},{1,17},{9,25},{17,1},{25,9},{2,18},{10... | collective-permute-start | bytes 1179656 | tf_op jit(solution)/shard_map/ppermute | solution.py:28
  35.3 19.7 %collective-permute-start.6 = (bf16[80,4096]{1,0:T(8,128)(2,1)S(1)}, bf16[80,4096]{1,0:T(8,128)(2,1)S(1)}, u32[]{:S(2)}, u32[]{:S(2)}) collective-permute-start(bf16[80,4096]{1,0:T(8,128)(2,1)S(1)} %collective-permute-done.refs_0_), channel_id=1, source_target_pairs={{0,16},{8,24},{16,0},{24,8},{1,17},{9,25},{17,1},{25,9},{2,18},{10... | collective-permute-start | bytes 1966088 | tf_op jit(solution)/shard_map/ppermute | solution.py:28
  35.8 19.2 %collective-permute-start.1 = (bf16[48,4096]{1,0:T(8,128)(2,1)S(1)}, bf16[48,4096]{1,0:T(8,128)(2,1)}, u32[]{:S(2)}, u32[]{:S(2)}) collective-permute-start(bf16[48,4096]{1,0:T(8,128)(2,1)S(1)} %slice.88.refs_2_), channel_id=1, source_target_pairs={{0,4},{1,5},{2,6},{3,7},{4,0},{5,1},{6,2},{7,3},{8,12},{9,13},{10,... | collective-permute-start | bytes 1179656 | tf_op jit(solution)/shard_map/ppermute | solution.py:28
  36.1 1.0 copy-start
  55.0 9.5 %collective-permute-start.7 = (bf16[48,4096]{1,0:T(8,128)(2,1)}, bf16[48,4096]{1,0:T(8,128)(2,1)S(1)}, u32[]{:S(2)}, u32[]{:S(2)}) collective-permute-start(bf16[48,4096]{1,0:T(8,128)(2,1)} %collective-permute-done.1.refs_1_), channel_id=1, source_target_pairs={{0,16},{8,24},{16,0},{24,8},{1,17},{9,25},{17,1},{25,9},{2,18},{10... | collective-permute-start | bytes 1179656 | tf_op jit(solution)/shard_map/ppermute | solution.py:28
  56.6 23.8 %collective-permute-start.5 = (bf16[64,4096]{1,0:T(8,128)(2,1)S(1)}, bf16[64,4096]{1,0:T(8,128)(2,1)S(1)}, u32[]{:S(2)}, u32[]{:S(2)}) collective-permute-start(bf16[64,4096]{1,0:T(8,128)(2,1)S(1)} %get-tuple-element.45.refs_2_), channel_id=1, source_target_pairs={{0,4},{1,5},{2,6},{3,7},{4,0},{5,1},{6,2},{7,3},{8,12},{9,13},{10,... | collective-permute-start | bytes 1572872 | tf_op jit(solution)/shard_map/ppermute | solution.py:28
  64.5 15.9 %collective-permute-start.8 = (bf16[64,4096]{1,0:T(8,128)(2,1)S(1)}, bf16[64,4096]{1,0:T(8,128)(2,1)S(1)}, u32[]{:S(2)}, u32[]{:S(2)}) collective-permute-start(bf16[64,4096]{1,0:T(8,128)(2,1)S(1)} %get-tuple-element.49.refs_2_), channel_id=1, source_target_pairs={{0,16},{8,24},{16,0},{24,8},{1,17},{9,25},{17,1},{25,9},{2,18},{10... | collective-permute-start | bytes 1572872 | tf_op jit(solution)/shard_map/ppermute | solution.py:28
  70.5 2.9 %collective-permute-start.10 = (bf16[48,4096]{1,0:T(8,128)(2,1)S(1)}, bf16[48,4096]{1,0:T(8,128)(2,1)S(1)}, u32[]{:S(2)}, u32[]{:S(2)}) collective-permute-start(bf16[48,4096]{1,0:T(8,128)(2,1)S(1)} %get-tuple-element.56.refs_2_), channel_id=1, source_target_pairs={{0,8},{8,0},{16,24},{24,16},{1,9},{9,1},{17,25},{25,17},{2,10},{10... | collective-permute-start | bytes 1179656 | tf_op jit(solution)/shard_map/ppermute | solution.py:28
  70.6 2.8 %collective-permute-start.9 = (bf16[48,4096]{1,0:T(8,128)(2,1)S(1)}, bf16[48,4096]{1,0:T(8,128)(2,1)S(1)}, u32[]{:S(2)}, u32[]{:S(2)}) collective-permute-start(bf16[48,4096]{1,0:T(8,128)(2,1)S(1)} %get-tuple-element.55.refs_1_), channel_id=1, source_target_pairs={{0,8},{8,0},{16,24},{24,16},{1,9},{9,1},{17,25},{25,17},{2,10},{10... | collective-permute-start | bytes 1179656 | tf_op jit(solution)/shard_map/ppermute | solution.py:28
  71.1 2.1 %collective-permute-start.11 = (bf16[32,4096]{1,0:T(8,128)(2,1)S(1)}, bf16[32,4096]{1,0:T(8,128)(2,1)S(1)}, u32[]{:S(2)}, u32[]{:S(2)}) collective-permute-start(bf16[32,4096]{1,0:T(8,128)(2,1)S(1)} %get-tuple-element.57.refs_3_), channel_id=1, source_target_pairs={{0,8},{8,0},{16,24},{24,16},{1,9},{9,1},{17,25},{25,17},{2,10},{10... | collective-permute-start | bytes 786440 | tf_op jit(solution)/shard_map/ppermute | solution.py:28
  73.3 10.3 %collective-permute-start.17 = (bf16[96,4096]{1,0:T(8,128)(2,1)S(1)}, bf16[96,4096]{1,0:T(8,128)(2,1)S(1)}, u32[]{:S(2)}, u32[]{:S(2)}) collective-permute-start(bf16[96,4096]{1,0:T(8,128)(2,1)S(1)} %get-tuple-element.65.refs_2_), channel_id=1, source_target_pairs={{0,8},{8,0},{16,24},{24,16},{1,9},{9,1},{17,25},{25,17},{2,10},{10... | collective-permute-start | bytes 2359304 | tf_op jit(solution)/shard_map/ppermute | solution.py:28
  75.6 14.4 %collective-permute-start.12 = (bf16[48,4096]{1,0:T(8,128)(2,1)S(1)}, bf16[48,4096]{1,0:T(8,128)(2,1)S(1)}, u32[]{:S(2)}, u32[]{:S(2)}) collective-permute-start(bf16[48,4096]{1,0:T(8,128)(2,1)S(1)} %get-tuple-element.59.refs_1_), channel_id=1, source_target_pairs={{0,2},{1,3},{2,0},{3,1},{4,6},{5,7},{6,4},{7,5},{8,10},{9,11},{10,... | collective-permute-start | bytes 1179656 | tf_op jit(solution)/shard_map/ppermute | solution.py:28
  81.7 1.9 %collective-permute-start.18 = (bf16[32,4096]{1,0:T(8,128)(2,1)S(1)}, bf16[32,4096]{1,0:T(8,128)(2,1)S(1)}, u32[]{:S(2)}, u32[]{:S(2)}) collective-permute-start(bf16[32,4096]{1,0:T(8,128)(2,1)S(1)} %get-tuple-element.69.refs_4_), channel_id=1, source_target_pairs={{0,8},{8,0},{16,24},{24,16},{1,9},{9,1},{17,25},{25,17},{2,10},{10... | collective-permute-start | bytes 786440 | tf_op jit(solution)/shard_map/ppermute | solution.py:28
  81.7 1.9 %collective-permute-start.19 = (bf16[32,4096]{1,0:T(8,128)(2,1)S(1)}, bf16[32,4096]{1,0:T(8,128)(2,1)S(1)}, u32[]{:S(2)}, u32[]{:S(2)}) collective-permute-start(bf16[32,4096]{1,0:T(8,128)(2,1)S(1)} %get-tuple-element.70.refs_6_), channel_id=1, source_target_pairs={{0,8},{8,0},{16,24},{24,16},{1,9},{9,1},{17,25},{25,17},{2,10},{10... | collective-permute-start | bytes 786440 | tf_op jit(solution)/shard_map/ppermute | solution.py:28
  83.5 26.2 %collective-permute-start.13 = (bf16[64,4096]{1,0:T(8,128)(2,1)S(1)}, bf16[64,4096]{1,0:T(8,128)(2,1)S(1)}, u32[]{:S(2)}, u32[]{:S(2)}) collective-permute-start(bf16[64,4096]{1,0:T(8,128)(2,1)S(1)} %level0_rows64.1.refs_2_), channel_id=1, source_target_pairs={{0,4},{1,5},{2,6},{3,7},{4,0},{5,1},{6,2},{7,3},{8,12},{9,13},{10,... | collective-permute-start | bytes 1572872 | tf_op jit(solution)/shard_map/ppermute | solution.py:28
  85.1 43.0 %collective-permute-start.20 = (bf16[160,4096]{1,0:T(8,128)(2,1)S(1)}, bf16[160,4096]{1,0:T(8,128)(2,1)S(1)}, u32[]{:S(2)}, u32[]{:S(2)}) collective-permute-start(bf16[160,4096]{1,0:T(8,128)(2,1)S(1)} %level2_rows160.1.refs_8_), channel_id=1, source_target_pairs={{0,2},{1,3},{2,0},{3,1},{4,6},{5,7},{6,4},{7,5},{8,10},{9,11},{10,... | collective-permute-start | bytes 3932168 | tf_op jit(solution)/shard_map/ppermute | solution.py:28
  90.1 8.3 %collective-permute-start.14 = (bf16[32,4096]{1,0:T(8,128)(2,1)S(1)}, bf16[32,4096]{1,0:T(8,128)(2,1)S(1)}, u32[]{:S(2)}, u32[]{:S(2)}) collective-permute-start(bf16[32,4096]{1,0:T(8,128)(2,1)S(1)} %slice.92.refs_3_), channel_id=1, source_target_pairs={{0,16},{8,24},{16,0},{24,8},{1,17},{9,25},{17,1},{25,9},{2,18},{10... | collective-permute-start | bytes 786440 | tf_op jit(solution)/shard_map/ppermute | solution.py:28
  110.9 2.0 %collective-permute-start.21 = (bf16[64,4096]{1,0:T(8,128)(2,1)S(1)}, bf16[64,4096]{1,0:T(8,128)(2,1)S(1)}, u32[]{:S(2)}, u32[]{:S(2)}) collective-permute-start(bf16[64,4096]{1,0:T(8,128)(2,1)S(1)} %level1_rows64.3.refs_2_), channel_id=1, source_target_pairs={{0,8},{8,0},{16,24},{24,16},{1,9},{9,1},{17,25},{25,17},{2,10},{10... | collective-permute-start | bytes 1572872 | tf_op jit(solution)/shard_map/ppermute | solution.py:28
  111.0 3.2 %collective-permute-start.15 = (bf16[32,4096]{1,0:T(8,128)(2,1)S(1)}, bf16[32,4096]{1,0:T(8,128)(2,1)S(1)}, u32[]{:S(2)}, u32[]{:S(2)}) collective-permute-start(bf16[32,4096]{1,0:T(8,128)(2,1)S(1)} %slice.92.refs_3_), channel_id=1, source_target_pairs={{0,8},{8,0},{16,24},{24,16},{1,9},{9,1},{17,25},{25,17},{2,10},{10... | collective-permute-start | bytes 786440 | tf_op jit(solution)/shard_map/ppermute | solution.py:28
  111.5 2.7 %collective-permute-start.16 = (bf16[32,4096]{1,0:T(8,128)(2,1)S(1)}, bf16[32,4096]{1,0:T(8,128)(2,1)S(1)}, u32[]{:S(2)}, u32[]{:S(2)}) collective-permute-start(bf16[32,4096]{1,0:T(8,128)(2,1)S(1)} %collective-permute-done.14.refs_4_), channel_id=1, source_target_pairs={{0,8},{8,0},{16,24},{24,16},{1,9},{9,1},{17,25},{25,17},{2,10},{10... | collective-permute-start | bytes 786440 | tf_op jit(solution)/shard_map/ppermute | solution.py:28
  114.1 25.2 %collective-permute-start.22 = (bf16[64,4096]{1,0:T(8,128)(2,1)S(1)}, bf16[64,4096]{1,0:T(8,128)(2,1)S(1)}, u32[]{:S(2)}, u32[]{:S(2)}) collective-permute-start(bf16[64,4096]{1,0:T(8,128)(2,1)S(1)} %level2_rows64.1.refs_2_), channel_id=1, source_target_pairs={{0,2},{1,3},{2,0},{3,1},{4,6},{5,7},{6,4},{7,5},{8,10},{9,11},{10,... | collective-permute-start | bytes 1572872 | tf_op jit(solution)/shard_map/ppermute | solution.py:28

commit v11 on v10

--- a/solution.py
+++ b/solution.py
@@ -318,10 +318,10 @@
     cut_2 = half + quarter
     begin_1 = schur_slab[:cut_1]
     first_z1 = trade(begin_1, 1)
-    begin_y1 = trade(begin_1, 0)
     slab, begin_1 = after(schur_slab, begin_1)
     begin_2, begin_3, rest_2 = slab[cut_1:half], slab[half:cut_2], slab[cut_2:]
-    begin_y2, begin_y3 = trade(begin_2, 0), trade(begin_3, 0)
+    begin_1, begin_3, rest_2 = after(begin_1, begin_3, rest_2)
+    begin_y1, begin_y2, begin_y3 = (trade(x, 0) for x in (begin_1, begin_2, begin_3))
     inv = reorder(meta, pivot_inverse)
 
     first_yz1 = trade(first_z1, 0)
@@ -348,8 +348,8 @@
     rest_y2 = trade(rest_2, 0)
 
     e, y, z, yz = (("top", low, eighth) for low in range(0, size, quarter))
-    jobs = [[e, (*y[:2], share)], [("top", quarter + share, share), z], [yz]]
-    jobs.append([(0, 0, eighth), (1, 0, quarter)])
+    jobs = [[e, (*y[:2], share)], [("top", quarter + share, share), z], [yz, (0, 0, share)]]
+    jobs.append([(0, share, share), (1, 0, quarter)])
     *head, next_0, panel_1 = run_two_levels(
         meta,
         inv,
@@ -368,8 +368,11 @@
         2,
         meta,
         (inv,),
-        [[tops[0], tops[2], ("top", share, share)], [tops[i] for i in (1, 3, 4, 5, 6, 7)]],
-        top=tuple(sum((rows_of(x) for x in group), []) for group in (head, head_c)),
+        [[tops[0], ("top", share, share), (0, 0, share)], tops[1:]],
+        top=tuple(
+            rows_of(group[0]) + rows_of(group[1]) + [(group[2], 0, eighth)] for group in (head, head_c)
+        ),
+        pairs=[tuple([(group[2], eighth, share)] for group in (head, head_c))],
         keeps=True,
     )
     lead_w = trade(lead, 3)
@@ -395,26 +398,26 @@
         pairs=[(rows_of(x), rows_of(y)) for x, y in zip(next_1, next_c1)],
     )
     last_w1 = trade(last_1, 3)
-    tops_w = lead_w[:eighth]
-    tops_wc = trade(tops_w, 2)
-    tops_wy = trade(tops_w, 0)
-    after_z2, tops_wy = after(after_z2, tops_wy)
-    tops_wyc = trade(tops_wy, 2)
-    next_2 = chunk(1, panel_1, after_2, after_z2, cost=5 * 10**9)
+    first_w = lead_w[:share]
+    first_wy = trade(first_w, 0)
+    first_wz = trade(first_w, 1)
+    after_z2, first_wy = after(after_z2, first_wy)
+    first_wz, after_z2 = after(first_wz, after_z2)
+    first_wyz = trade(first_wz, 0)
+    firsts_w = [first_w, first_wy, first_wz, first_wyz]
+    firsts_w += [trade(x, 2) for x in firsts_w]
+    next_2 = chunk(1, panel_1, after_2, after_z2, cost=3 * 10**9)
     last_2 = chunk(2, panel_2, next_2, trade(next_2, 2))
     last_w2 = trade(last_2, 3)
-    more = lead.shape[0] - eighth
-    tops = [(lead, 0, share), (others, 0, share), (lead, share, share)]
-    tops += [(others, share * i, share) for i in range(1, 6)]
-    tops_other = [(x, low, share) for low in (0, share) for x in (tops_w, tops_wy)]
-    tops_other += [(x, low, share) for low in (0, share) for x in (tops_wc, tops_wyc)]
+    tops = [(lead, 0, share)] + [(others, share * i, share) for i in range(7)]
+    tops_other = [(x, 0, share) for x in firsts_w]
     out, panel_3 = run_level(
         3,
         meta,
         (inv,),
-        [[("top", 0, share), (0, 0, more), (1, 0, last_1.shape[0])]],
+        [[("top", 0, share), (0, 0, eighth), (1, 0, last_1.shape[0])]],
         top=(tops, tops_other),
-        pairs=[([(lead, eighth, more)], [(lead_w, eighth, more)]), (rows_of(last_1), rows_of(last_w1))],
+        pairs=[([(lead, share, eighth)], [(lead_w, share, eighth)]), (rows_of(last_1), rows_of(last_w1))],
         keeps=True,
         part=(all_rows, 0, None),
         cost=5 * 10**10,

time: 142 us -> 152 us (1.070)
  waiting for transfers between devices: 95.9 us -> 102 us
  starting transfers between devices: 17.4 us -> 22 us
    ppermute x23 -> x27, waiting for transfers between devices: 95.9 us -> 102 us  [trade(): lax.ppermute(block, axis, [(i, i ^ flip) for i in range(lax.axis_size(axi...]
    ppermute x23 -> x27, starting transfers between devices: 17.4 us -> 22 us  [trade(): lax.ppermute(block, axis, [(i, i ^ flip) for i in range(lax.axis_size(axi...]
  transfers between devices with their start and end apart: 23 -> 27, of which waited for: 13 -> 17; matrix products, arithmetic and copies ran while one was open for 2% -> 2% of each run, Pallas kernels for 15% -> 14%
where the time goes in v11:
time: 152 us
  waiting for transfers between devices  102 us (67%)
  Pallas kernels  23.2 us (15%)
  starting transfers between devices  22 us (14%)
  local copies, waits for them, and re-layouts  4.64 us (3%)
    ppermute x27, waiting for transfers between devices, trade(): lax.ppermute(block, axis, [(i, i ^ flip) for i in range(lax.axis_size(axi...  102 us
    ppermute x27, starting transfers between devices, trade(): lax.ppermute(block, axis, [(i, i ^ flip) for i in range(lax.axis_size(axi...  22 us
    pallas_call x9, Pallas kernels, run_level(): pl.pallas_call(kernel, grid=(1,) if part is not None else (), out_shape=s...  17.8 us
    pallas_call x1, Pallas kernels, run_two_levels(): pl.pallas_call(kernel, out_shape=[jax.ShapeDtypeStruct((n, width), BF16)...  4.49 us
  transfers between devices with their start and end apart: 27, of which 17 were waited for; matrix products, arithmetic and copies ran while one was open for 2% of the time, Pallas kernels for 14%

profile of v11, /device:TPU:0, one launch (start us, length us, event | category | flops | bytes accessed | tf_op | source)
XLA Modules:
  0.0 152.2 jit_solution(8630335507384732305)
XLA Ops:
  1.2 4.1 %collective-permute-start = (bf16[80,4096]{1,0:T(8,128)(2,1)S(1)}, bf16[80,4096]{1,0:T(8,128)(2,1)S(1)}, u32[]{:S(2)}, u32[]{:S(2)}) collective-permute-start(bf16[80,4096]{1,0:T(8,128)(2,1)S(1)} %slice.87.refs_1_), channel_id=1, source_target_pairs={{0,4},{1,5},{2,6},{3,7},{4,0},{5,1},{6,2},{7,3},{8,12},{9,13},{10,... | collective-permute-start | bytes 1966088 | tf_op jit(solution)/shard_map/ppermute | solution.py:28
  5.3 1.3 fusion.8
  6.6 1.6 %collective-permute-start.4 = (bf16[64,4096]{1,0:T(8,128)(2,1)S(1)}, bf16[64,4096]{1,0:T(8,128)(2,1)}, u32[]{:S(2)}, u32[]{:S(2)}) collective-permute-start(bf16[64,4096]{1,0:T(8,128)(2,1)S(1)} %get-tuple-element.49.refs_5_), channel_id=1, source_target_pairs={{0,16},{8,24},{16,0},{24,8},{1,17},{9,25},{17,1},{25,9},{2,18},{10... | collective-permute-start | bytes 1572872 | tf_op jit(solution)/shard_map/ppermute | solution.py:28
  9.7 1.6 %collective-permute-start.3 = (bf16[48,4096]{1,0:T(8,128)(2,1)S(1)}, bf16[48,4096]{1,0:T(8,128)(2,1)}, u32[]{:S(2)}, u32[]{:S(2)}) collective-permute-start(bf16[48,4096]{1,0:T(8,128)(2,1)S(1)} %slice.88.refs_2_), channel_id=1, source_target_pairs={{0,16},{8,24},{16,0},{24,8},{1,17},{9,25},{17,1},{25,9},{2,18},{10... | collective-permute-start | bytes 1179656 | tf_op jit(solution)/shard_map/ppermute | solution.py:28
  11.3 22.8 %collective-permute-done.refs_0_ = bf16[80,4096]{1,0:T(8,128)(2,1)S(1)} collective-permute-done((bf16[80,4096]{1,0:T(8,128)(2,1)S(1)}, bf16[80,4096]{1,0:T(8,128)(2,1)S(1)}, u32[]{:S(2)}, u32[]{:S(2)}) %collective-permute-start) | collective-permute-done | bytes 655392 | tf_op jit(solution)/shard_map/ppermute | solution.py:28
  34.1 1.6 %collective-permute-start.6 = (bf16[80,4096]{1,0:T(8,128)(2,1)S(1)}, bf16[80,4096]{1,0:T(8,128)(2,1)S(1)}, u32[]{:S(2)}, u32[]{:S(2)}) collective-permute-start(bf16[80,4096]{1,0:T(8,128)(2,1)S(1)} %collective-permute-done.refs_0_), channel_id=1, source_target_pairs={{0,16},{8,24},{16,0},{24,8},{1,17},{9,25},{17,1},{25,9},{2,18},{10... | collective-permute-start | bytes 1966088 | tf_op jit(solution)/shard_map/ppermute | solution.py:28
  37.9 6.1 %collective-permute-done.3.refs_4_ = bf16[48,4096]{1,0:T(8,128)(2,1)} collective-permute-done((bf16[48,4096]{1,0:T(8,128)(2,1)S(1)}, bf16[48,4096]{1,0:T(8,128)(2,1)}, u32[]{:S(2)}, u32[]{:S(2)}) %collective-permute-start.3) | collective-permute-done | bytes 393248 | tf_op jit(solution)/shard_map/ppermute | solution.py:28
  44.0 3.5 %level0_rows256.1 = (bf16[128,4096]{1,0:T(8,128)(2,1)S(1)}, bf16[64,4096]{1,0:T(8,128)(2,1)S(1)}, bf16[64,4096]{1,0:T(8,128)(2,1)S(1)}, bf16[256,4096]{1,0:T(8,128)(2,1)S(1)}) custom-call(s32[640]{0:T(1024)S(1)} %concatenate.3.meta, bf16[4,256,256]{2,1,0:T(8,128)(2,1)S(1)} %reorder.1.refs_0_.inv, bf16[80,4096]{1,0:T(8,128)(2,1)S(1)} %slice.87.refs_1_, ...), custom_call_target="tpu_custom_call" | custom-call | tf_op jit(solution)/shard_map/level0_rows256/pallas_call | solution.py:228
  47.6 7.3 %collective-permute-done.1.refs_1_ = bf16[48,4096]{1,0:T(8,128)(2,1)} collective-permute-done((bf16[48,4096]{1,0:T(8,128)(2,1)S(1)}, bf16[48,4096]{1,0:T(8,128)(2,1)}, u32[]{:S(2)}, u32[]{:S(2)}) %collective-permute-start.1) | collective-permute-done | bytes 393248 | tf_op jit(solution)/shard_map/ppermute | solution.py:28
  54.9 1.6 %collective-permute-done.6.refs_2_ = bf16[80,4096]{1,0:T(8,128)(2,1)S(1)} collective-permute-done((bf16[80,4096]{1,0:T(8,128)(2,1)S(1)}, bf16[80,4096]{1,0:T(8,128)(2,1)S(1)}, u32[]{:S(2)}, u32[]{:S(2)}) %collective-permute-start.6) | collective-permute-done | bytes 655392 | tf_op jit(solution)/shard_map/ppermute | solution.py:28
  56.5 1.5 collective-permute-start.7
  58.4 8.0 %collective-permute-done.7.refs_3_ = bf16[48,4096]{1,0:T(8,128)(2,1)S(1)} collective-permute-done((bf16[48,4096]{1,0:T(8,128)(2,1)}, bf16[48,4096]{1,0:T(8,128)(2,1)S(1)}, u32[]{:S(2)}, u32[]{:S(2)}) %collective-permute-start.7) | collective-permute-done | bytes 393248 | tf_op jit(solution)/shard_map/ppermute | solution.py:28
  66.4 1.5 collective-permute-start.8
  67.9 4.5 %level0_level1.1 = (bf16[48,4096]{1,0:T(8,128)(2,1)S(1)}, bf16[48,4096]{1,0:T(8,128)(2,1)S(1)}, bf16[48,4096]{1,0:T(8,128)(2,1)S(1)}, bf16[80,4096]{1,0:T(8,128)(2,1)S(1)}, bf16[256,4096]{1,0:T(8,128)(2,1)S(1)}) custom-call(s32[640]{0:T(1024)S(1)} %concatenate.3.meta, bf16[4,256,256]{2,1,0:T(8,128)(2,1)S(1)} %reorder.1.refs_0_.inv, ...), custom_call_target="tpu_custom_call" | custom-call | tf_op jit(solution)/shard_map/level0_level1/pallas_call | solution.py:254
  75.3 2.2 %level2_rows160.1 = (bf16[48,4096]{1,0:T(8,128)(2,1)S(1)}, bf16[112,4096]{1,0:T(8,128)(2,1)S(1)}, bf16[256,4096]{1,0:T(8,128)(2,1)S(1)}) custom-call(s32[640]{0:T(1024)S(1)} %concatenate.3.meta, bf16[4,256,256]{2,1,0:T(8,128)(2,1)S(1)} %reorder.1.refs_0_.inv, bf16[48,4096]{1,0:T(8,128)(2,1)S(1)} %get-tuple-element.63.refs_1_, ...), custom_call_target="tpu_custom_call" | custom-call | tf_op jit(solution)/shard_map/level2_rows160/pallas_call | solution.py:228
  77.6 1.6 %collective-permute-start.12 = (bf16[48,4096]{1,0:T(8,128)(2,1)S(1)}, bf16[48,4096]{1,0:T(8,128)(2,1)S(1)}, u32[]{:S(2)}, u32[]{:S(2)}) collective-permute-start(bf16[48,4096]{1,0:T(8,128)(2,1)S(1)} %get-tuple-element.67.refs_1_), channel_id=1, source_target_pairs={{0,2},{1,3},{2,0},{3,1},{4,6},{5,7},{6,4},{7,5},{8,10},{9,11},{10,... | collective-permute-start | bytes 1179656 | tf_op jit(solution)/shard_map/ppermute | solution.py:28
  79.2 3.3 %collective-permute-done.5.refs_3_ = bf16[64,4096]{1,0:T(8,128)(2,1)S(1)} collective-permute-done((bf16[64,4096]{1,0:T(8,128)(2,1)S(1)}, bf16[64,4096]{1,0:T(8,128)(2,1)S(1)}, u32[]{:S(2)}, u32[]{:S(2)}) %collective-permute-start.5) | collective-permute-done | bytes 524320 | tf_op jit(solution)/shard_map/ppermute | solution.py:28
  82.5 1.2 level0_rows64.1.refs_2_
  83.8 1.3 level1_rows64.2
  87.0 1.4 level2_rows144.1.refs_12_
  88.4 1.8 %collective-permute-start.24 = (bf16[144,4096]{1,0:T(8,128)(2,1)S(1)}, bf16[144,4096]{1,0:T(8,128)(2,1)S(1)}, u32[]{:S(2)}, u32[]{:S(2)}) collective-permute-start(bf16[144,4096]{1,0:T(8,128)(2,1)S(1)} %level2_rows144.1.refs_12_), channel_id=1, source_target_pairs={{0,2},{1,3},{2,0},{3,1},{4,6},{5,7},{6,4},{7,5},{8,10},{9,11},{10,... | collective-permute-start | bytes 3538952 | tf_op jit(solution)/shard_map/ppermute | solution.py:28
  90.3 3.1 %collective-permute-done.12.refs_11_ = bf16[48,4096]{1,0:T(8,128)(2,1)S(1)} collective-permute-done((bf16[48,4096]{1,0:T(8,128)(2,1)S(1)}, bf16[48,4096]{1,0:T(8,128)(2,1)S(1)}, u32[]{:S(2)}, u32[]{:S(2)}) %collective-permute-start.12) | collective-permute-done | bytes 393248 | tf_op jit(solution)/shard_map/ppermute | solution.py:28
  94.7 4.1 %collective-permute-done.14.refs_4_ = bf16[16,4096]{1,0:T(8,128)(2,1)S(1)} collective-permute-done((bf16[16,4096]{1,0:T(8,128)(2,1)S(1)}, bf16[16,4096]{1,0:T(8,128)(2,1)S(1)}, u32[]{:S(2)}, u32[]{:S(2)}) %collective-permute-start.14) | collective-permute-done | bytes 131104 | tf_op jit(solution)/shard_map/ppermute | solution.py:28
  98.8 11.3 %collective-permute-done.13.refs_3_ = bf16[64,4096]{1,0:T(8,128)(2,1)S(1)} collective-permute-done((bf16[64,4096]{1,0:T(8,128)(2,1)S(1)}, bf16[64,4096]{1,0:T(8,128)(2,1)S(1)}, u32[]{:S(2)}, u32[]{:S(2)}) %collective-permute-start.13) | collective-permute-done | bytes 524320 | tf_op jit(solution)/shard_map/ppermute | solution.py:28
  110.1 17.1 %collective-permute-done.15.refs_5_ = bf16[16,4096]{1,0:T(8,128)(2,1)S(1)} collective-permute-done((bf16[16,4096]{1,0:T(8,128)(2,1)S(1)}, bf16[16,4096]{1,0:T(8,128)(2,1)S(1)}, u32[]{:S(2)}, u32[]{:S(2)}) %collective-permute-start.15) | collective-permute-done | bytes 131104 | tf_op jit(solution)/shard_map/ppermute | solution.py:28
  127.3 1.3 level1_rows64.3.refs_2_
  129.7 4.8 %collective-permute-done.16.refs_6_ = bf16[16,4096]{1,0:T(8,128)(2,1)S(1)} collective-permute-done((bf16[16,4096]{1,0:T(8,128)(2,1)S(1)}, bf16[16,4096]{1,0:T(8,128)(2,1)S(1)}, u32[]{:S(2)}, u32[]{:S(2)}) %collective-permute-start.16) | collective-permute-done | bytes 131104 | tf_op jit(solution)/shard_map/ppermute | solution.py:28
  135.0 1.2 level2_rows64.1.refs_2_
  136.3 1.3 collective-permute-start.26
  137.6 3.6 %level3_rows192.1 = (bf16[256,4096]{1,0:T(8,128)(2,1)}, bf16[256,4096]{1,0:T(8,128)(2,1)S(1)}) custom-call(s32[640]{0:T(1024)S(1)} %concatenate.3.meta, bf16[4,256,256]{2,1,0:T(8,128)(2,1)S(1)} %reorder.1.refs_0_.inv, bf16[48,4096]{1,0:T(8,128)(2,1)S(1)} %get-tuple-element.67.refs_1_, bf16[112,4096]{1,0:T(8,128)(2,1)S(1)} %get-tuple-element.68.refs_2_, ...), custom_call_target="tpu_custom_call" | custom-call | flops 49999998976 | tf_op jit(solution)/shard_map/level3_rows192/pallas_call | solution.py:228
  141.2 9.0 %collective-permute-done.26.refs_3_ = bf16[64,4096]{1,0:T(8,128)(2,1)S(1)} collective-permute-done((bf16[64,4096]{1,0:T(8,128)(2,1)S(1)}, bf16[64,4096]{1,0:T(8,128)(2,1)S(1)}, u32[]{:S(2)}, u32[]{:S(2)}) %collective-permute-start.26) | collective-permute-done | bytes 524320 | tf_op jit(solution)/shard_map/ppermute | solution.py:28
  150.2 2.0 %level3_rows64.1 = bf16[256,4096]{1,0:T(8,128)(2,1)} custom-call(s32[640]{0:T(1024)S(1)} %concatenate.3.meta, bf16[4,256,256]{2,1,0:T(8,128)(2,1)S(1)} %reorder.1.refs_0_.inv, bf16[256,4096]{1,0:T(8,128)(2,1)S(1)} %get-tuple-element.81.refs_1_, bf16[64,4096]{1,0:T(8,128)(2,1)S(1)} %level2_rows64.1.refs_2_, ...), custom_call_target="tpu_custom_call", output_to_operand_aliasing={{}: (5, {})} | custom-call | tf_op jit(solution)/shard_map/level3_rows64/pallas_call | solution.py:228
  (53 shorter events, 13.1 us)
Async XLA Ops:
  0.0 35.6 %copy-start.1 = (s32[4,2,32]{2,1,0:T(2,128)S(1)}, s32[4,2,32]{2,1,0:T(2,128)}, u32[]{:S(2)}) copy-start(s32[4,2,32]{2,1,0:T(2,128)} %param.7) | copy-start | bytes 3076
  0.0 35.8 %copy-start.3 = (s32[4,32]{1,0:T(4,128)S(1)}, s32[4,32]{1,0:T(4,128)}, u32[]{:S(2)}) copy-start(s32[4,32]{1,0:T(4,128)} %param.8) | copy-start | bytes 1540
  0.0 35.8 %copy-start.2 = (s32[4,32]{1,0:T(4,128)S(1)}, s32[4,32]{1,0:T(4,128)}, u32[]{:S(2)}) copy-start(s32[4,32]{1,0:T(4,128)} %param.9) | copy-start | bytes 1540
  1.2 32.9 %collective-permute-start = (bf16[80,4096]{1,0:T(8,128)(2,1)S(1)}, bf16[80,4096]{1,0:T(8,128)(2,1)S(1)}, u32[]{:S(2)}, u32[]{:S(2)}) collective-permute-start(bf16[80,4096]{1,0:T(8,128)(2,1)S(1)} %slice.87.refs_1_), channel_id=1, source_target_pairs={{0,4},{1,5},{2,6},{3,7},{4,0},{5,1},{6,2},{7,3},{8,12},{9,13},{10,... | collective-permute-start | bytes 1966088 | tf_op jit(solution)/shard_map/ppermute | solution.py:28
  6.6 31.4 %collective-permute-start.4 = (bf16[64,4096]{1,0:T(8,128)(2,1)S(1)}, bf16[64,4096]{1,0:T(8,128)(2,1)}, u32[]{:S(2)}, u32[]{:S(2)}) collective-permute-start(bf16[64,4096]{1,0:T(8,128)(2,1)S(1)} %get-tuple-element.49.refs_5_), channel_id=1, source_target_pairs={{0,16},{8,24},{16,0},{24,8},{1,17},{9,25},{17,1},{25,9},{2,18},{10... | collective-permute-start | bytes 1572872 | tf_op jit(solution)/shard_map/ppermute | solution.py:28
  8.1 35.9 %collective-permute-start.2 = (bf16[80,4096]{1,0:T(8,128)(2,1)S(1)}, bf16[80,4096]{1,0:T(8,128)(2,1)}, u32[]{:S(2)}, u32[]{:S(2)}) collective-permute-start(bf16[80,4096]{1,0:T(8,128)(2,1)S(1)} %slice.87.refs_1_), channel_id=1, source_target_pairs={{0,16},{8,24},{16,0},{24,8},{1,17},{9,25},{17,1},{25,9},{2,18},{10... | collective-permute-start | bytes 1966088 | tf_op jit(solution)/shard_map/ppermute | solution.py:28
  9.7 34.4 %collective-permute-start.3 = (bf16[48,4096]{1,0:T(8,128)(2,1)S(1)}, bf16[48,4096]{1,0:T(8,128)(2,1)}, u32[]{:S(2)}, u32[]{:S(2)}) collective-permute-start(bf16[48,4096]{1,0:T(8,128)(2,1)S(1)} %slice.88.refs_2_), channel_id=1, source_target_pairs={{0,16},{8,24},{16,0},{24,8},{1,17},{9,25},{17,1},{25,9},{2,18},{10... | collective-permute-start | bytes 1179656 | tf_op jit(solution)/shard_map/ppermute | solution.py:28
  34.1 22.5 %collective-permute-start.6 = (bf16[80,4096]{1,0:T(8,128)(2,1)S(1)}, bf16[80,4096]{1,0:T(8,128)(2,1)S(1)}, u32[]{:S(2)}, u32[]{:S(2)}) collective-permute-start(bf16[80,4096]{1,0:T(8,128)(2,1)S(1)} %collective-permute-done.refs_0_), channel_id=1, source_target_pairs={{0,16},{8,24},{16,0},{24,8},{1,17},{9,25},{17,1},{25,9},{2,18},{10... | collective-permute-start | bytes 1966088 | tf_op jit(solution)/shard_map/ppermute | solution.py:28
  35.7 19.2 %collective-permute-start.1 = (bf16[48,4096]{1,0:T(8,128)(2,1)S(1)}, bf16[48,4096]{1,0:T(8,128)(2,1)}, u32[]{:S(2)}, u32[]{:S(2)}) collective-permute-start(bf16[48,4096]{1,0:T(8,128)(2,1)S(1)} %slice.88.refs_2_), channel_id=1, source_target_pairs={{0,4},{1,5},{2,6},{3,7},{4,0},{5,1},{6,2},{7,3},{8,12},{9,13},{10,... | collective-permute-start | bytes 1179656 | tf_op jit(solution)/shard_map/ppermute | solution.py:28
  35.9 1.0 copy-start
  56.5 9.9 %collective-permute-start.7 = (bf16[48,4096]{1,0:T(8,128)(2,1)}, bf16[48,4096]{1,0:T(8,128)(2,1)S(1)}, u32[]{:S(2)}, u32[]{:S(2)}) collective-permute-start(bf16[48,4096]{1,0:T(8,128)(2,1)} %collective-permute-done.1.refs_1_), channel_id=1, source_target_pairs={{0,16},{8,24},{16,0},{24,8},{1,17},{9,25},{17,1},{25,9},{2,18},{10... | collective-permute-start | bytes 1179656 | tf_op jit(solution)/shard_map/ppermute | solution.py:28
  58.0 24.4 %collective-permute-start.5 = (bf16[64,4096]{1,0:T(8,128)(2,1)S(1)}, bf16[64,4096]{1,0:T(8,128)(2,1)S(1)}, u32[]{:S(2)}, u32[]{:S(2)}) collective-permute-start(bf16[64,4096]{1,0:T(8,128)(2,1)S(1)} %get-tuple-element.53.refs_2_), channel_id=1, source_target_pairs={{0,4},{1,5},{2,6},{3,7},{4,0},{5,1},{6,2},{7,3},{8,12},{9,13},{10,... | collective-permute-start | bytes 1572872 | tf_op jit(solution)/shard_map/ppermute | solution.py:28
  66.4 16.1 %collective-permute-start.8 = (bf16[64,4096]{1,0:T(8,128)(2,1)S(1)}, bf16[64,4096]{1,0:T(8,128)(2,1)S(1)}, u32[]{:S(2)}, u32[]{:S(2)}) collective-permute-start(bf16[64,4096]{1,0:T(8,128)(2,1)S(1)} %get-tuple-element.57.refs_2_), channel_id=1, source_target_pairs={{0,16},{8,24},{16,0},{24,8},{1,17},{9,25},{17,1},{25,9},{2,18},{10... | collective-permute-start | bytes 1572872 | tf_op jit(solution)/shard_map/ppermute | solution.py:28
  72.4 1.8 %collective-permute-start.10 = (bf16[48,4096]{1,0:T(8,128)(2,1)S(1)}, bf16[48,4096]{1,0:T(8,128)(2,1)S(1)}, u32[]{:S(2)}, u32[]{:S(2)}) collective-permute-start(bf16[48,4096]{1,0:T(8,128)(2,1)S(1)} %get-tuple-element.64.refs_2_), channel_id=1, source_target_pairs={{0,8},{8,0},{16,24},{24,16},{1,9},{9,1},{17,25},{25,17},{2,10},{10... | collective-permute-start | bytes 1179656 | tf_op jit(solution)/shard_map/ppermute | solution.py:28
  72.5 2.3 %collective-permute-start.11 = (bf16[48,4096]{1,0:T(8,128)(2,1)S(1)}, bf16[48,4096]{1,0:T(8,128)(2,1)S(1)}, u32[]{:S(2)}, u32[]{:S(2)}) collective-permute-start(bf16[48,4096]{1,0:T(8,128)(2,1)S(1)} %get-tuple-element.65.refs_3_), channel_id=1, source_target_pairs={{0,8},{8,0},{16,24},{24,16},{1,9},{9,1},{17,25},{25,17},{2,10},{10... | collective-permute-start | bytes 1179656 | tf_op jit(solution)/shard_map/ppermute | solution.py:28
  73.0 2.3 %collective-permute-start.9 = (bf16[48,4096]{1,0:T(8,128)(2,1)S(1)}, bf16[48,4096]{1,0:T(8,128)(2,1)S(1)}, u32[]{:S(2)}, u32[]{:S(2)}) collective-permute-start(bf16[48,4096]{1,0:T(8,128)(2,1)S(1)} %get-tuple-element.63.refs_1_), channel_id=1, source_target_pairs={{0,8},{8,0},{16,24},{24,16},{1,9},{9,1},{17,25},{25,17},{2,10},{10... | collective-permute-start | bytes 1179656 | tf_op jit(solution)/shard_map/ppermute | solution.py:28
  74.2 11.4 %collective-permute-start.21 = (bf16[80,4096]{1,0:T(8,128)(2,1)S(1)}, bf16[80,4096]{1,0:T(8,128)(2,1)S(1)}, u32[]{:S(2)}, u32[]{:S(2)}) collective-permute-start(bf16[80,4096]{1,0:T(8,128)(2,1)S(1)} %get-tuple-element.75.refs_2_), channel_id=1, source_target_pairs={{0,8},{8,0},{16,24},{24,16},{1,9},{9,1},{17,25},{25,17},{2,10},{10... | collective-permute-start | bytes 1966088 | tf_op jit(solution)/shard_map/ppermute | solution.py:28
  77.6 15.8 %collective-permute-start.12 = (bf16[48,4096]{1,0:T(8,128)(2,1)S(1)}, bf16[48,4096]{1,0:T(8,128)(2,1)S(1)}, u32[]{:S(2)}, u32[]{:S(2)}) collective-permute-start(bf16[48,4096]{1,0:T(8,128)(2,1)S(1)} %get-tuple-element.67.refs_1_), channel_id=1, source_target_pairs={{0,2},{1,3},{2,0},{3,1},{4,6},{5,7},{6,4},{7,5},{8,10},{9,11},{10,... | collective-permute-start | bytes 1179656 | tf_op jit(solution)/shard_map/ppermute | solution.py:28
  83.7 26.4 %collective-permute-start.13 = (bf16[64,4096]{1,0:T(8,128)(2,1)S(1)}, bf16[64,4096]{1,0:T(8,128)(2,1)S(1)}, u32[]{:S(2)}, u32[]{:S(2)}) collective-permute-start(bf16[64,4096]{1,0:T(8,128)(2,1)S(1)} %level0_rows64.1.refs_2_), channel_id=1, source_target_pairs={{0,4},{1,5},{2,6},{3,7},{4,0},{5,1},{6,2},{7,3},{8,12},{9,13},{10,... | collective-permute-start | bytes 1572872 | tf_op jit(solution)/shard_map/ppermute | solution.py:28
  85.0 1.6 %collective-permute-start.22 = (bf16[32,4096]{1,0:T(8,128)(2,1)S(1)}, bf16[32,4096]{1,0:T(8,128)(2,1)S(1)}, u32[]{:S(2)}, u32[]{:S(2)}) collective-permute-start(bf16[32,4096]{1,0:T(8,128)(2,1)S(1)} %get-tuple-element.79.refs_4_), channel_id=1, source_target_pairs={{0,8},{8,0},{16,24},{24,16},{1,9},{9,1},{17,25},{25,17},{2,10},{10... | collective-permute-start | bytes 786440 | tf_op jit(solution)/shard_map/ppermute | solution.py:28
  85.1 1.9 %collective-permute-start.23 = (bf16[32,4096]{1,0:T(8,128)(2,1)S(1)}, bf16[32,4096]{1,0:T(8,128)(2,1)S(1)}, u32[]{:S(2)}, u32[]{:S(2)}) collective-permute-start(bf16[32,4096]{1,0:T(8,128)(2,1)S(1)} %get-tuple-element.80.refs_6_), channel_id=1, source_target_pairs={{0,8},{8,0},{16,24},{24,16},{1,9},{9,1},{17,25},{25,17},{2,10},{10... | collective-permute-start | bytes 786440 | tf_op jit(solution)/shard_map/ppermute | solution.py:28
  88.4 49.1 %collective-permute-start.24 = (bf16[144,4096]{1,0:T(8,128)(2,1)S(1)}, bf16[144,4096]{1,0:T(8,128)(2,1)S(1)}, u32[]{:S(2)}, u32[]{:S(2)}) collective-permute-start(bf16[144,4096]{1,0:T(8,128)(2,1)S(1)} %level2_rows144.1.refs_12_), channel_id=1, source_target_pairs={{0,2},{1,3},{2,0},{3,1},{4,6},{5,7},{6,4},{7,5},{8,10},{9,11},{10,... | collective-permute-start | bytes 3538952 | tf_op jit(solution)/shard_map/ppermute | solution.py:28
  93.4 5.4 %collective-permute-start.14 = (bf16[16,4096]{1,0:T(8,128)(2,1)S(1)}, bf16[16,4096]{1,0:T(8,128)(2,1)S(1)}, u32[]{:S(2)}, u32[]{:S(2)}) collective-permute-start(bf16[16,4096]{1,0:T(8,128)(2,1)S(1)} %slice.92.refs_3_), channel_id=1, source_target_pairs={{0,16},{8,24},{16,0},{24,8},{1,17},{9,25},{17,1},{25,9},{2,18},{10... | collective-permute-start | bytes 393224 | tf_op jit(solution)/shard_map/ppermute | solution.py:28
  94.3 33.0 %collective-permute-start.15 = (bf16[16,4096]{1,0:T(8,128)(2,1)S(1)}, bf16[16,4096]{1,0:T(8,128)(2,1)S(1)}, u32[]{:S(2)}, u32[]{:S(2)}) collective-permute-start(bf16[16,4096]{1,0:T(8,128)(2,1)S(1)} %slice.92.refs_3_), channel_id=1, source_target_pairs={{0,4},{1,5},{2,6},{3,7},{4,0},{5,1},{6,2},{7,3},{8,12},{9,13},{10,... | collective-permute-start | bytes 393224 | tf_op jit(solution)/shard_map/ppermute | solution.py:28
  128.5 6.0 %collective-permute-start.25 = (bf16[64,4096]{1,0:T(8,128)(2,1)S(1)}, bf16[64,4096]{1,0:T(8,128)(2,1)S(1)}, u32[]{:S(2)}, u32[]{:S(2)}) collective-permute-start(bf16[64,4096]{1,0:T(8,128)(2,1)S(1)} %level1_rows64.3.refs_2_), channel_id=1, source_target_pairs={{0,8},{8,0},{16,24},{24,16},{1,9},{9,1},{17,25},{25,17},{2,10},{10... | collective-permute-start | bytes 1572872 | tf_op jit(solution)/shard_map/ppermute | solution.py:28
  128.6 5.9 %collective-permute-start.16 = (bf16[16,4096]{1,0:T(8,128)(2,1)S(1)}, bf16[16,4096]{1,0:T(8,128)(2,1)S(1)}, u32[]{:S(2)}, u32[]{:S(2)}) collective-permute-start(bf16[16,4096]{1,0:T(8,128)(2,1)S(1)} %collective-permute-done.15.refs_5_), channel_id=1, source_target_pairs={{0,16},{8,24},{16,0},{24,8},{1,17},{9,25},{17,1},{25,9},{2,18},{10... | collective-permute-start | bytes 393224 | tf_op jit(solution)/shard_map/ppermute | solution.py:28
  129.2 7.1 %collective-permute-start.17 = (bf16[16,4096]{1,0:T(8,128)(2,1)S(1)}, bf16[16,4096]{1,0:T(8,128)(2,1)S(1)}, u32[]{:S(2)}, u32[]{:S(2)}) collective-permute-start(bf16[16,4096]{1,0:T(8,128)(2,1)S(1)} %slice.92.refs_3_), channel_id=1, source_target_pairs={{0,8},{8,0},{16,24},{24,16},{1,9},{9,1},{17,25},{25,17},{2,10},{10... | collective-permute-start | bytes 393224 | tf_op jit(solution)/shard_map/ppermute | solution.py:28
  129.3 8.2 %collective-permute-start.19 = (bf16[16,4096]{1,0:T(8,128)(2,1)S(1)}, bf16[16,4096]{1,0:T(8,128)(2,1)S(1)}, u32[]{:S(2)}, u32[]{:S(2)}) collective-permute-start(bf16[16,4096]{1,0:T(8,128)(2,1)S(1)} %collective-permute-done.15.refs_5_), channel_id=1, source_target_pairs={{0,8},{8,0},{16,24},{24,16},{1,9},{9,1},{17,25},{25,17},{2,10},{10... | collective-permute-start | bytes 393224 | tf_op jit(solution)/shard_map/ppermute | solution.py:28
  134.5 3.1 %collective-permute-start.18 = (bf16[16,4096]{1,0:T(8,128)(2,1)S(1)}, bf16[16,4096]{1,0:T(8,128)(2,1)S(1)}, u32[]{:S(2)}, u32[]{:S(2)}) collective-permute-start(bf16[16,4096]{1,0:T(8,128)(2,1)S(1)} %collective-permute-done.14.refs_4_), channel_id=1, source_target_pairs={{0,8},{8,0},{16,24},{24,16},{1,9},{9,1},{17,25},{25,17},{2,10},{10... | collective-permute-start | bytes 393224 | tf_op jit(solution)/shard_map/ppermute | solution.py:28
  134.5 3.1 %collective-permute-start.20 = (bf16[16,4096]{1,0:T(8,128)(2,1)S(1)}, bf16[16,4096]{1,0:T(8,128)(2,1)S(1)}, u32[]{:S(2)}, u32[]{:S(2)}) collective-permute-start(bf16[16,4096]{1,0:T(8,128)(2,1)S(1)} %collective-permute-done.16.refs_6_), channel_id=1, source_target_pairs={{0,8},{8,0},{16,24},{24,16},{1,9},{9,1},{17,25},{25,17},{2,10},{10... | collective-permute-start | bytes 393224 | tf_op jit(solution)/shard_map/ppermute | solution.py:28
  136.3 13.9 %collective-permute-start.26 = (bf16[64,4096]{1,0:T(8,128)(2,1)S(1)}, bf16[64,4096]{1,0:T(8,128)(2,1)S(1)}, u32[]{:S(2)}, u32[]{:S(2)}) collective-permute-start(bf16[64,4096]{1,0:T(8,128)(2,1)S(1)} %level2_rows64.1.refs_2_), channel_id=1, source_target_pairs={{0,2},{1,3},{2,0},{3,1},{4,6},{5,7},{6,4},{7,5},{8,10},{9,11},{10,... | collective-permute-start | bytes 1572872 | tf_op jit(solution)/shard_map/ppermute | solution.py:28

commit v12 on v10

--- a/solution.py
+++ b/solution.py
@@ -268,7 +268,7 @@
     )(meta, inv, *ours, *theirs, near, near_x)
 
 
-def reorder(meta, pivot_inverse):
+def reorder(meta, pivot_inverse, cost=0):
     step = meta.shape[0] // LEVELS
     return pl.pallas_call(
         functools.partial(reorder_kernel, step=step),
@@ -276,7 +276,7 @@
         in_specs=[pl.BlockSpec(memory_space=pltpu.SMEM), pl.BlockSpec(memory_space=pltpu.VMEM)],
         out_specs=pl.BlockSpec(memory_space=pltpu.VMEM),
         compiler_params=pltpu.CompilerParams(vmem_limit_bytes=30 * 2**20),
-        cost_estimate=pl.CostEstimate(flops=0, bytes_accessed=0, transcendentals=0),
+        cost_estimate=pl.CostEstimate(flops=cost, bytes_accessed=0, transcendentals=0),
         name="reorder",
     )(meta, pivot_inverse)
 
@@ -322,7 +322,8 @@
     slab, begin_1 = after(schur_slab, begin_1)
     begin_2, begin_3, rest_2 = slab[cut_1:half], slab[half:cut_2], slab[cut_2:]
     begin_y2, begin_y3 = trade(begin_2, 0), trade(begin_3, 0)
-    inv = reorder(meta, pivot_inverse)
+    pivot_inverse, first_z1 = after(pivot_inverse, first_z1)
+    inv = reorder(meta, pivot_inverse, cost=10**9)
 
     first_yz1 = trade(first_z1, 0)
     first_2, first_z1 = after(begin_2, first_z1)

time: 142 us -> 142 us (level)
  starting transfers between devices: 17.4 us -> 19 us
    ppermute x23, starting transfers between devices: 17.4 us -> 19 us  [trade(): lax.ppermute(block, axis, [(i, i ^ flip) for i in range(lax.axis_size(axi...]
  transfers between devices with their start and end apart: 23 -> 23, of which waited for: 13 -> 14; matrix products, arithmetic and copies ran while one was open for 2% -> 2% of each run, Pallas kernels for 15% -> 15%
where the time goes in v12:
time: 142 us
  waiting for transfers between devices  95 us (67%)
  Pallas kernels  23.2 us (16%)
  starting transfers between devices  19 us (13%)
  local copies, waits for them, and re-layouts  4.65 us (3%)
    ppermute x23, waiting for transfers between devices, trade(): lax.ppermute(block, axis, [(i, i ^ flip) for i in range(lax.axis_size(axi...  95 us
    ppermute x23, starting transfers between devices, trade(): lax.ppermute(block, axis, [(i, i ^ flip) for i in range(lax.axis_size(axi...  19 us
    pallas_call x9, Pallas kernels, run_level(): pl.pallas_call(kernel, grid=(1,) if part is not None else (), out_shape=s...  17.8 us
    pallas_call x1, Pallas kernels, run_two_levels(): pl.pallas_call(kernel, out_shape=[jax.ShapeDtypeStruct((n, width), BF16)...  4.45 us
  transfers between devices with their start and end apart: 23, of which 14 were waited for; matrix products, arithmetic and copies ran while one was open for 2% of the time, Pallas kernels for 15%

profile of v12, /device:TPU:0, one launch (start us, length us, event | category | flops | bytes accessed | tf_op | source)
XLA Modules:
  0.0 142.1 jit_solution(4101252492269133446)
XLA Ops:
  0.0 1.2 slice.87.refs_1_
  1.2 4.1 %collective-permute-start = (bf16[80,4096]{1,0:T(8,128)(2,1)S(1)}, bf16[80,4096]{1,0:T(8,128)(2,1)S(1)}, u32[]{:S(2)}, u32[]{:S(2)}) collective-permute-start(bf16[80,4096]{1,0:T(8,128)(2,1)S(1)} %slice.87.refs_1_), channel_id=1, source_target_pairs={{0,4},{1,5},{2,6},{3,7},{4,0},{5,1},{6,2},{7,3},{8,12},{9,13},{10,... | collective-permute-start | bytes 1966088 | tf_op jit(solution)/shard_map/ppermute | solution.py:28
  5.3 1.5 %collective-permute-start.2 = (bf16[80,4096]{1,0:T(8,128)(2,1)S(1)}, bf16[80,4096]{1,0:T(8,128)(2,1)}, u32[]{:S(2)}, u32[]{:S(2)}) collective-permute-start(bf16[80,4096]{1,0:T(8,128)(2,1)S(1)} %slice.87.refs_1_), channel_id=1, source_target_pairs={{0,16},{8,24},{16,0},{24,8},{1,17},{9,25},{17,1},{25,9},{2,18},{10... | collective-permute-start | bytes 1966088 | tf_op jit(solution)/shard_map/ppermute | solution.py:28
  6.8 1.3 fusion.8
  9.7 1.6 %collective-permute-start.3 = (bf16[48,4096]{1,0:T(8,128)(2,1)S(1)}, bf16[48,4096]{1,0:T(8,128)(2,1)}, u32[]{:S(2)}, u32[]{:S(2)}) collective-permute-start(bf16[48,4096]{1,0:T(8,128)(2,1)S(1)} %slice.88.refs_2_), channel_id=1, source_target_pairs={{0,16},{8,24},{16,0},{24,8},{1,17},{9,25},{17,1},{25,9},{2,18},{10... | collective-permute-start | bytes 1179656 | tf_op jit(solution)/shard_map/ppermute | solution.py:28
  11.3 22.8 %collective-permute-done.refs_0_ = bf16[80,4096]{1,0:T(8,128)(2,1)S(1)} collective-permute-done((bf16[80,4096]{1,0:T(8,128)(2,1)S(1)}, bf16[80,4096]{1,0:T(8,128)(2,1)S(1)}, u32[]{:S(2)}, u32[]{:S(2)}) %collective-permute-start) | collective-permute-done | bytes 655392 | tf_op jit(solution)/shard_map/ppermute | solution.py:28
  34.1 1.6 %collective-permute-start.6 = (bf16[80,4096]{1,0:T(8,128)(2,1)S(1)}, bf16[80,4096]{1,0:T(8,128)(2,1)S(1)}, u32[]{:S(2)}, u32[]{:S(2)}) collective-permute-start(bf16[80,4096]{1,0:T(8,128)(2,1)S(1)} %collective-permute-done.refs_0_), channel_id=1, source_target_pairs={{0,16},{8,24},{16,0},{24,8},{1,17},{9,25},{17,1},{25,9},{2,18},{10... | collective-permute-start | bytes 1966088 | tf_op jit(solution)/shard_map/ppermute | solution.py:28
  37.9 4.8 %collective-permute-done.3.refs_4_ = bf16[48,4096]{1,0:T(8,128)(2,1)} collective-permute-done((bf16[48,4096]{1,0:T(8,128)(2,1)S(1)}, bf16[48,4096]{1,0:T(8,128)(2,1)}, u32[]{:S(2)}, u32[]{:S(2)}) %collective-permute-start.3) | collective-permute-done | bytes 393248 | tf_op jit(solution)/shard_map/ppermute | solution.py:28
  42.7 3.5 %level0_rows256.1 = (bf16[128,4096]{1,0:T(8,128)(2,1)S(1)}, bf16[64,4096]{1,0:T(8,128)(2,1)S(1)}, bf16[64,4096]{1,0:T(8,128)(2,1)S(1)}, bf16[256,4096]{1,0:T(8,128)(2,1)S(1)}) custom-call(s32[640]{0:T(1024)S(1)} %concatenate.3.meta, bf16[4,256,256]{2,1,0:T(8,128)(2,1)S(1)} %reorder.1.refs_0_.inv, bf16[80,4096]{1,0:T(8,128)(2,1)S(1)} %slice.87.refs_1_, ...), custom_call_target="tpu_custom_call" | custom-call | tf_op jit(solution)/shard_map/level0_rows256/pallas_call | solution.py:228
  46.3 8.6 %collective-permute-done.1.refs_1_ = bf16[48,4096]{1,0:T(8,128)(2,1)} collective-permute-done((bf16[48,4096]{1,0:T(8,128)(2,1)S(1)}, bf16[48,4096]{1,0:T(8,128)(2,1)}, u32[]{:S(2)}, u32[]{:S(2)}) %collective-permute-start.1) | collective-permute-done | bytes 393248 | tf_op jit(solution)/shard_map/ppermute | solution.py:28
  55.2 1.5 %collective-permute-start.7 = (bf16[48,4096]{1,0:T(8,128)(2,1)}, bf16[48,4096]{1,0:T(8,128)(2,1)S(1)}, u32[]{:S(2)}, u32[]{:S(2)}) collective-permute-start(bf16[48,4096]{1,0:T(8,128)(2,1)} %collective-permute-done.1.refs_1_), channel_id=1, source_target_pairs={{0,16},{8,24},{16,0},{24,8},{1,17},{9,25},{17,1},{25,9},{2,18},{10... | collective-permute-start | bytes 1179656 | tf_op jit(solution)/shard_map/ppermute | solution.py:28
  57.1 8.1 %collective-permute-done.7.refs_3_ = bf16[48,4096]{1,0:T(8,128)(2,1)S(1)} collective-permute-done((bf16[48,4096]{1,0:T(8,128)(2,1)}, bf16[48,4096]{1,0:T(8,128)(2,1)S(1)}, u32[]{:S(2)}, u32[]{:S(2)}) %collective-permute-start.7) | collective-permute-done | bytes 393248 | tf_op jit(solution)/shard_map/ppermute | solution.py:28
  65.2 1.5 %collective-permute-start.8 = (bf16[64,4096]{1,0:T(8,128)(2,1)S(1)}, bf16[64,4096]{1,0:T(8,128)(2,1)S(1)}, u32[]{:S(2)}, u32[]{:S(2)}) collective-permute-start(bf16[64,4096]{1,0:T(8,128)(2,1)S(1)} %get-tuple-element.53.refs_2_), channel_id=1, source_target_pairs={{0,16},{8,24},{16,0},{24,8},{1,17},{9,25},{17,1},{25,9},{2,18},{10... | collective-permute-start | bytes 1572872 | tf_op jit(solution)/shard_map/ppermute | solution.py:28
  66.7 4.5 %level0_level1.1 = (bf16[48,4096]{1,0:T(8,128)(2,1)S(1)}, bf16[48,4096]{1,0:T(8,128)(2,1)S(1)}, bf16[32,4096]{1,0:T(8,128)(2,1)S(1)}, bf16[96,4096]{1,0:T(8,128)(2,1)S(1)}, bf16[256,4096]{1,0:T(8,128)(2,1)S(1)}) custom-call(s32[640]{0:T(1024)S(1)} %concatenate.3.meta, bf16[4,256,256]{2,1,0:T(8,128)(2,1)S(1)} %reorder.1.refs_0_.inv, ...), custom_call_target="tpu_custom_call" | custom-call | tf_op jit(solution)/shard_map/level0_level1/pallas_call | solution.py:254
  71.8 2.1 %collective-permute-done.11.refs_6_ = bf16[32,4096]{1,0:T(8,128)(2,1)S(1)} collective-permute-done((bf16[32,4096]{1,0:T(8,128)(2,1)S(1)}, bf16[32,4096]{1,0:T(8,128)(2,1)S(1)}, u32[]{:S(2)}, u32[]{:S(2)}) %collective-permute-start.11) | collective-permute-done | bytes 262176 | tf_op jit(solution)/shard_map/ppermute | solution.py:28
  74.0 2.2 %level2_rows144.1 = (bf16[48,4096]{1,0:T(8,128)(2,1)S(1)}, bf16[96,4096]{1,0:T(8,128)(2,1)S(1)}, bf16[256,4096]{1,0:T(8,128)(2,1)S(1)}) custom-call(s32[640]{0:T(1024)S(1)} %concatenate.3.meta, bf16[4,256,256]{2,1,0:T(8,128)(2,1)S(1)} %reorder.1.refs_0_.inv, bf16[48,4096]{1,0:T(8,128)(2,1)S(1)} %get-tuple-element.59.refs_1_, ...), custom_call_target="tpu_custom_call" | custom-call | tf_op jit(solution)/shard_map/level2_rows144/pallas_call | solution.py:228
  76.2 1.5 %collective-permute-start.12 = (bf16[48,4096]{1,0:T(8,128)(2,1)S(1)}, bf16[48,4096]{1,0:T(8,128)(2,1)S(1)}, u32[]{:S(2)}, u32[]{:S(2)}) collective-permute-start(bf16[48,4096]{1,0:T(8,128)(2,1)S(1)} %get-tuple-element.63.refs_1_), channel_id=1, source_target_pairs={{0,2},{1,3},{2,0},{3,1},{4,6},{5,7},{6,4},{7,5},{8,10},{9,11},{10,... | collective-permute-start | bytes 1179656 | tf_op jit(solution)/shard_map/ppermute | solution.py:28
  77.8 3.5 %collective-permute-done.5.refs_3_ = bf16[64,4096]{1,0:T(8,128)(2,1)S(1)} collective-permute-done((bf16[64,4096]{1,0:T(8,128)(2,1)S(1)}, bf16[64,4096]{1,0:T(8,128)(2,1)S(1)}, u32[]{:S(2)}, u32[]{:S(2)}) %collective-permute-start.5) | collective-permute-done | bytes 524320 | tf_op jit(solution)/shard_map/ppermute | solution.py:28
  81.2 1.2 level1_rows64.2
  83.1 1.2 level0_rows64.1.refs_2_
  84.5 1.5 %level2_rows160.1.refs_8_ = bf16[160,4096]{1,0:T(8,128)(2,1)S(1)} custom-call(s32[640]{0:T(1024)S(1)} %concatenate.3.meta, bf16[4,256,256]{2,1,0:T(8,128)(2,1)S(1)} %reorder.1.refs_0_.inv, bf16[256,4096]{1,0:T(8,128)(2,1)S(1)} %get-tuple-element.68.refs_1_, bf16[96,4096]{1,0:T(8,128)(2,1)S(1)} %get-tuple-element.69.refs_2_, ...), custom_call_target="tpu_custom_call" | custom-call | tf_op jit(solution)/shard_map/level2_rows160/pallas_call | solution.py:228
  86.0 1.7 %collective-permute-start.20 = (bf16[160,4096]{1,0:T(8,128)(2,1)S(1)}, bf16[160,4096]{1,0:T(8,128)(2,1)S(1)}, u32[]{:S(2)}, u32[]{:S(2)}) collective-permute-start(bf16[160,4096]{1,0:T(8,128)(2,1)S(1)} %level2_rows160.1.refs_8_), channel_id=1, source_target_pairs={{0,2},{1,3},{2,0},{3,1},{4,6},{5,7},{6,4},{7,5},{8,10},{9,11},{10,... | collective-permute-start | bytes 3932168 | tf_op jit(solution)/shard_map/ppermute | solution.py:28
  87.7 2.1 %collective-permute-done.12.refs_7_ = bf16[48,4096]{1,0:T(8,128)(2,1)S(1)} collective-permute-done((bf16[48,4096]{1,0:T(8,128)(2,1)S(1)}, bf16[48,4096]{1,0:T(8,128)(2,1)S(1)}, u32[]{:S(2)}, u32[]{:S(2)}) %collective-permute-start.12) | collective-permute-done | bytes 393248 | tf_op jit(solution)/shard_map/ppermute | solution.py:28
  90.6 7.5 %collective-permute-done.14.refs_4_ = bf16[32,4096]{1,0:T(8,128)(2,1)S(1)} collective-permute-done((bf16[32,4096]{1,0:T(8,128)(2,1)S(1)}, bf16[32,4096]{1,0:T(8,128)(2,1)S(1)}, u32[]{:S(2)}, u32[]{:S(2)}) %collective-permute-start.14) | collective-permute-done | bytes 262176 | tf_op jit(solution)/shard_map/ppermute | solution.py:28
  98.0 11.9 %collective-permute-done.13.refs_3_ = bf16[64,4096]{1,0:T(8,128)(2,1)S(1)} collective-permute-done((bf16[64,4096]{1,0:T(8,128)(2,1)S(1)}, bf16[64,4096]{1,0:T(8,128)(2,1)S(1)}, u32[]{:S(2)}, u32[]{:S(2)}) %collective-permute-start.13) | collective-permute-done | bytes 524320 | tf_op jit(solution)/shard_map/ppermute | solution.py:28
  110.0 1.2 level1_rows64.3.refs_2_
  111.9 1.3 collective-permute-done.21.refs_3_
  113.2 1.2 level2_rows64.1.refs_2_
  114.5 14.4 %collective-permute-done.20.refs_9_ = bf16[160,4096]{1,0:T(8,128)(2,1)S(1)} collective-permute-done((bf16[160,4096]{1,0:T(8,128)(2,1)S(1)}, bf16[160,4096]{1,0:T(8,128)(2,1)S(1)}, u32[]{:S(2)}, u32[]{:S(2)}) %collective-permute-start.20) | collective-permute-done | bytes 1310752 | tf_op jit(solution)/shard_map/ppermute | solution.py:28
  128.9 3.6 %level3_rows192.1 = (bf16[256,4096]{1,0:T(8,128)(2,1)}, bf16[256,4096]{1,0:T(8,128)(2,1)S(1)}) custom-call(s32[640]{0:T(1024)S(1)} %concatenate.3.meta, bf16[4,256,256]{2,1,0:T(8,128)(2,1)S(1)} %reorder.1.refs_0_.inv, bf16[48,4096]{1,0:T(8,128)(2,1)S(1)} %get-tuple-element.63.refs_1_, bf16[96,4096]{1,0:T(8,128)(2,1)S(1)} %get-tuple-element.64.refs_2_, ...), custom_call_target="tpu_custom_call" | custom-call | flops 49999998976 | tf_op jit(solution)/shard_map/level3_rows192/pallas_call | solution.py:228
  132.5 7.6 %collective-permute-done.22.refs_3_ = bf16[64,4096]{1,0:T(8,128)(2,1)S(1)} collective-permute-done((bf16[64,4096]{1,0:T(8,128)(2,1)S(1)}, bf16[64,4096]{1,0:T(8,128)(2,1)S(1)}, u32[]{:S(2)}, u32[]{:S(2)}) %collective-permute-start.22) | collective-permute-done | bytes 524320 | tf_op jit(solution)/shard_map/ppermute | solution.py:28
  140.1 2.0 %level3_rows64.1 = bf16[256,4096]{1,0:T(8,128)(2,1)} custom-call(s32[640]{0:T(1024)S(1)} %concatenate.3.meta, bf16[4,256,256]{2,1,0:T(8,128)(2,1)S(1)} %reorder.1.refs_0_.inv, bf16[256,4096]{1,0:T(8,128)(2,1)S(1)} %get-tuple-element.75.refs_1_, bf16[64,4096]{1,0:T(8,128)(2,1)S(1)} %level2_rows64.1.refs_2_, ...), custom_call_target="tpu_custom_call", output_to_operand_aliasing={{}: (5, {})} | custom-call | tf_op jit(solution)/shard_map/level3_rows64/pallas_call | solution.py:228
  (45 shorter events, 7.5 us)
Async XLA Ops:
  0.0 35.6 %copy-start.1 = (s32[4,2,32]{2,1,0:T(2,128)S(1)}, s32[4,2,32]{2,1,0:T(2,128)}, u32[]{:S(2)}) copy-start(s32[4,2,32]{2,1,0:T(2,128)} %param.7) | copy-start | bytes 3076
  0.0 35.8 %copy-start.3 = (s32[4,32]{1,0:T(4,128)S(1)}, s32[4,32]{1,0:T(4,128)}, u32[]{:S(2)}) copy-start(s32[4,32]{1,0:T(4,128)} %param.8) | copy-start | bytes 1540
  0.0 35.8 %copy-start.2 = (s32[4,32]{1,0:T(4,128)S(1)}, s32[4,32]{1,0:T(4,128)}, u32[]{:S(2)}) copy-start(s32[4,32]{1,0:T(4,128)} %param.9) | copy-start | bytes 1540
  1.2 32.9 %collective-permute-start = (bf16[80,4096]{1,0:T(8,128)(2,1)S(1)}, bf16[80,4096]{1,0:T(8,128)(2,1)S(1)}, u32[]{:S(2)}, u32[]{:S(2)}) collective-permute-start(bf16[80,4096]{1,0:T(8,128)(2,1)S(1)} %slice.87.refs_1_), channel_id=1, source_target_pairs={{0,4},{1,5},{2,6},{3,7},{4,0},{5,1},{6,2},{7,3},{8,12},{9,13},{10,... | collective-permute-start | bytes 1966088 | tf_op jit(solution)/shard_map/ppermute | solution.py:28
  5.3 37.4 %collective-permute-start.2 = (bf16[80,4096]{1,0:T(8,128)(2,1)S(1)}, bf16[80,4096]{1,0:T(8,128)(2,1)}, u32[]{:S(2)}, u32[]{:S(2)}) collective-permute-start(bf16[80,4096]{1,0:T(8,128)(2,1)S(1)} %slice.87.refs_1_), channel_id=1, source_target_pairs={{0,16},{8,24},{16,0},{24,8},{1,17},{9,25},{17,1},{25,9},{2,18},{10... | collective-permute-start | bytes 1966088 | tf_op jit(solution)/shard_map/ppermute | solution.py:28
  8.1 27.9 %collective-permute-start.4 = (bf16[64,4096]{1,0:T(8,128)(2,1)S(1)}, bf16[64,4096]{1,0:T(8,128)(2,1)}, u32[]{:S(2)}, u32[]{:S(2)}) collective-permute-start(bf16[64,4096]{1,0:T(8,128)(2,1)S(1)} %get-tuple-element.80.refs_5_), channel_id=1, source_target_pairs={{0,16},{8,24},{16,0},{24,8},{1,17},{9,25},{17,1},{25,9},{2,18},{10... | collective-permute-start | bytes 1572872 | tf_op jit(solution)/shard_map/ppermute | solution.py:28
  9.7 33.0 %collective-permute-start.3 = (bf16[48,4096]{1,0:T(8,128)(2,1)S(1)}, bf16[48,4096]{1,0:T(8,128)(2,1)}, u32[]{:S(2)}, u32[]{:S(2)}) collective-permute-start(bf16[48,4096]{1,0:T(8,128)(2,1)S(1)} %slice.88.refs_2_), channel_id=1, source_target_pairs={{0,16},{8,24},{16,0},{24,8},{1,17},{9,25},{17,1},{25,9},{2,18},{10... | collective-permute-start | bytes 1179656 | tf_op jit(solution)/shard_map/ppermute | solution.py:28
  34.1 21.1 %collective-permute-start.6 = (bf16[80,4096]{1,0:T(8,128)(2,1)S(1)}, bf16[80,4096]{1,0:T(8,128)(2,1)S(1)}, u32[]{:S(2)}, u32[]{:S(2)}) collective-permute-start(bf16[80,4096]{1,0:T(8,128)(2,1)S(1)} %collective-permute-done.refs_0_), channel_id=1, source_target_pairs={{0,16},{8,24},{16,0},{24,8},{1,17},{9,25},{17,1},{25,9},{2,18},{10... | collective-permute-start | bytes 1966088 | tf_op jit(solution)/shard_map/ppermute | solution.py:28
  35.6 19.2 %collective-permute-start.1 = (bf16[48,4096]{1,0:T(8,128)(2,1)S(1)}, bf16[48,4096]{1,0:T(8,128)(2,1)}, u32[]{:S(2)}, u32[]{:S(2)}) collective-permute-start(bf16[48,4096]{1,0:T(8,128)(2,1)S(1)} %slice.88.refs_2_), channel_id=1, source_target_pairs={{0,4},{1,5},{2,6},{3,7},{4,0},{5,1},{6,2},{7,3},{8,12},{9,13},{10,... | collective-permute-start | bytes 1179656 | tf_op jit(solution)/shard_map/ppermute | solution.py:28
  35.9 1.0 copy-start
  55.2 10.0 %collective-permute-start.7 = (bf16[48,4096]{1,0:T(8,128)(2,1)}, bf16[48,4096]{1,0:T(8,128)(2,1)S(1)}, u32[]{:S(2)}, u32[]{:S(2)}) collective-permute-start(bf16[48,4096]{1,0:T(8,128)(2,1)} %collective-permute-done.1.refs_1_), channel_id=1, source_target_pairs={{0,16},{8,24},{16,0},{24,8},{1,17},{9,25},{17,1},{25,9},{2,18},{10... | collective-permute-start | bytes 1179656 | tf_op jit(solution)/shard_map/ppermute | solution.py:28
  56.7 24.5 %collective-permute-start.5 = (bf16[64,4096]{1,0:T(8,128)(2,1)S(1)}, bf16[64,4096]{1,0:T(8,128)(2,1)S(1)}, u32[]{:S(2)}, u32[]{:S(2)}) collective-permute-start(bf16[64,4096]{1,0:T(8,128)(2,1)S(1)} %get-tuple-element.49.refs_2_), channel_id=1, source_target_pairs={{0,4},{1,5},{2,6},{3,7},{4,0},{5,1},{6,2},{7,3},{8,12},{9,13},{10,... | collective-permute-start | bytes 1572872 | tf_op jit(solution)/shard_map/ppermute | solution.py:28
  65.2 16.1 %collective-permute-start.8 = (bf16[64,4096]{1,0:T(8,128)(2,1)S(1)}, bf16[64,4096]{1,0:T(8,128)(2,1)S(1)}, u32[]{:S(2)}, u32[]{:S(2)}) collective-permute-start(bf16[64,4096]{1,0:T(8,128)(2,1)S(1)} %get-tuple-element.53.refs_2_), channel_id=1, source_target_pairs={{0,16},{8,24},{16,0},{24,8},{1,17},{9,25},{17,1},{25,9},{2,18},{10... | collective-permute-start | bytes 1572872 | tf_op jit(solution)/shard_map/ppermute | solution.py:28
  71.1 2.9 %collective-permute-start.10 = (bf16[48,4096]{1,0:T(8,128)(2,1)S(1)}, bf16[48,4096]{1,0:T(8,128)(2,1)S(1)}, u32[]{:S(2)}, u32[]{:S(2)}) collective-permute-start(bf16[48,4096]{1,0:T(8,128)(2,1)S(1)} %get-tuple-element.60.refs_2_), channel_id=1, source_target_pairs={{0,8},{8,0},{16,24},{24,16},{1,9},{9,1},{17,25},{25,17},{2,10},{10... | collective-permute-start | bytes 1179656 | tf_op jit(solution)/shard_map/ppermute | solution.py:28
  71.2 2.8 %collective-permute-start.9 = (bf16[48,4096]{1,0:T(8,128)(2,1)S(1)}, bf16[48,4096]{1,0:T(8,128)(2,1)S(1)}, u32[]{:S(2)}, u32[]{:S(2)}) collective-permute-start(bf16[48,4096]{1,0:T(8,128)(2,1)S(1)} %get-tuple-element.59.refs_1_), channel_id=1, source_target_pairs={{0,8},{8,0},{16,24},{24,16},{1,9},{9,1},{17,25},{25,17},{2,10},{10... | collective-permute-start | bytes 1179656 | tf_op jit(solution)/shard_map/ppermute | solution.py:28
  71.7 2.1 %collective-permute-start.11 = (bf16[32,4096]{1,0:T(8,128)(2,1)S(1)}, bf16[32,4096]{1,0:T(8,128)(2,1)S(1)}, u32[]{:S(2)}, u32[]{:S(2)}) collective-permute-start(bf16[32,4096]{1,0:T(8,128)(2,1)S(1)} %get-tuple-element.61.refs_3_), channel_id=1, source_target_pairs={{0,8},{8,0},{16,24},{24,16},{1,9},{9,1},{17,25},{25,17},{2,10},{10... | collective-permute-start | bytes 786440 | tf_op jit(solution)/shard_map/ppermute | solution.py:28
  73.9 10.5 %collective-permute-start.17 = (bf16[96,4096]{1,0:T(8,128)(2,1)S(1)}, bf16[96,4096]{1,0:T(8,128)(2,1)S(1)}, u32[]{:S(2)}, u32[]{:S(2)}) collective-permute-start(bf16[96,4096]{1,0:T(8,128)(2,1)S(1)} %get-tuple-element.69.refs_2_), channel_id=1, source_target_pairs={{0,8},{8,0},{16,24},{24,16},{1,9},{9,1},{17,25},{25,17},{2,10},{10... | collective-permute-start | bytes 2359304 | tf_op jit(solution)/shard_map/ppermute | solution.py:28
  76.2 13.5 %collective-permute-start.12 = (bf16[48,4096]{1,0:T(8,128)(2,1)S(1)}, bf16[48,4096]{1,0:T(8,128)(2,1)S(1)}, u32[]{:S(2)}, u32[]{:S(2)}) collective-permute-start(bf16[48,4096]{1,0:T(8,128)(2,1)S(1)} %get-tuple-element.63.refs_1_), channel_id=1, source_target_pairs={{0,2},{1,3},{2,0},{3,1},{4,6},{5,7},{6,4},{7,5},{8,10},{9,11},{10,... | collective-permute-start | bytes 1179656 | tf_op jit(solution)/shard_map/ppermute | solution.py:28
  82.5 1.9 %collective-permute-start.18 = (bf16[32,4096]{1,0:T(8,128)(2,1)S(1)}, bf16[32,4096]{1,0:T(8,128)(2,1)S(1)}, u32[]{:S(2)}, u32[]{:S(2)}) collective-permute-start(bf16[32,4096]{1,0:T(8,128)(2,1)S(1)} %get-tuple-element.73.refs_4_), channel_id=1, source_target_pairs={{0,8},{8,0},{16,24},{24,16},{1,9},{9,1},{17,25},{25,17},{2,10},{10... | collective-permute-start | bytes 786440 | tf_op jit(solution)/shard_map/ppermute | solution.py:28
  82.6 1.9 %collective-permute-start.19 = (bf16[32,4096]{1,0:T(8,128)(2,1)S(1)}, bf16[32,4096]{1,0:T(8,128)(2,1)S(1)}, u32[]{:S(2)}, u32[]{:S(2)}) collective-permute-start(bf16[32,4096]{1,0:T(8,128)(2,1)S(1)} %get-tuple-element.74.refs_6_), channel_id=1, source_target_pairs={{0,8},{8,0},{16,24},{24,16},{1,9},{9,1},{17,25},{25,17},{2,10},{10... | collective-permute-start | bytes 786440 | tf_op jit(solution)/shard_map/ppermute | solution.py:28
  84.3 25.7 %collective-permute-start.13 = (bf16[64,4096]{1,0:T(8,128)(2,1)S(1)}, bf16[64,4096]{1,0:T(8,128)(2,1)S(1)}, u32[]{:S(2)}, u32[]{:S(2)}) collective-permute-start(bf16[64,4096]{1,0:T(8,128)(2,1)S(1)} %level0_rows64.1.refs_2_), channel_id=1, source_target_pairs={{0,4},{1,5},{2,6},{3,7},{4,0},{5,1},{6,2},{7,3},{8,12},{9,13},{10,... | collective-permute-start | bytes 1572872 | tf_op jit(solution)/shard_map/ppermute | solution.py:28
  86.0 43.0 %collective-permute-start.20 = (bf16[160,4096]{1,0:T(8,128)(2,1)S(1)}, bf16[160,4096]{1,0:T(8,128)(2,1)S(1)}, u32[]{:S(2)}, u32[]{:S(2)}) collective-permute-start(bf16[160,4096]{1,0:T(8,128)(2,1)S(1)} %level2_rows160.1.refs_8_), channel_id=1, source_target_pairs={{0,2},{1,3},{2,0},{3,1},{4,6},{5,7},{6,4},{7,5},{8,10},{9,11},{10,... | collective-permute-start | bytes 3932168 | tf_op jit(solution)/shard_map/ppermute | solution.py:28
  89.8 8.3 %collective-permute-start.14 = (bf16[32,4096]{1,0:T(8,128)(2,1)S(1)}, bf16[32,4096]{1,0:T(8,128)(2,1)S(1)}, u32[]{:S(2)}, u32[]{:S(2)}) collective-permute-start(bf16[32,4096]{1,0:T(8,128)(2,1)S(1)} %slice.92.refs_3_), channel_id=1, source_target_pairs={{0,16},{8,24},{16,0},{24,8},{1,17},{9,25},{17,1},{25,9},{2,18},{10... | collective-permute-start | bytes 786440 | tf_op jit(solution)/shard_map/ppermute | solution.py:28
  111.2 2.0 %collective-permute-start.21 = (bf16[64,4096]{1,0:T(8,128)(2,1)S(1)}, bf16[64,4096]{1,0:T(8,128)(2,1)S(1)}, u32[]{:S(2)}, u32[]{:S(2)}) collective-permute-start(bf16[64,4096]{1,0:T(8,128)(2,1)S(1)} %level1_rows64.3.refs_2_), channel_id=1, source_target_pairs={{0,8},{8,0},{16,24},{24,16},{1,9},{9,1},{17,25},{25,17},{2,10},{10... | collective-permute-start | bytes 1572872 | tf_op jit(solution)/shard_map/ppermute | solution.py:28
  111.3 3.2 %collective-permute-start.15 = (bf16[32,4096]{1,0:T(8,128)(2,1)S(1)}, bf16[32,4096]{1,0:T(8,128)(2,1)S(1)}, u32[]{:S(2)}, u32[]{:S(2)}) collective-permute-start(bf16[32,4096]{1,0:T(8,128)(2,1)S(1)} %slice.92.refs_3_), channel_id=1, source_target_pairs={{0,8},{8,0},{16,24},{24,16},{1,9},{9,1},{17,25},{25,17},{2,10},{10... | collective-permute-start | bytes 786440 | tf_op jit(solution)/shard_map/ppermute | solution.py:28
  111.8 2.7 %collective-permute-start.16 = (bf16[32,4096]{1,0:T(8,128)(2,1)S(1)}, bf16[32,4096]{1,0:T(8,128)(2,1)S(1)}, u32[]{:S(2)}, u32[]{:S(2)}) collective-permute-start(bf16[32,4096]{1,0:T(8,128)(2,1)S(1)} %collective-permute-done.14.refs_4_), channel_id=1, source_target_pairs={{0,8},{8,0},{16,24},{24,16},{1,9},{9,1},{17,25},{25,17},{2,10},{10... | collective-permute-start | bytes 786440 | tf_op jit(solution)/shard_map/ppermute | solution.py:28
  114.4 25.7 %collective-permute-start.22 = (bf16[64,4096]{1,0:T(8,128)(2,1)S(1)}, bf16[64,4096]{1,0:T(8,128)(2,1)S(1)}, u32[]{:S(2)}, u32[]{:S(2)}) collective-permute-start(bf16[64,4096]{1,0:T(8,128)(2,1)S(1)} %level2_rows64.1.refs_2_), channel_id=1, source_target_pairs={{0,2},{1,3},{2,0},{3,1},{4,6},{5,7},{6,4},{7,5},{8,10},{9,11},{10,... | collective-permute-start | bytes 1572872 | tf_op jit(solution)/shard_map/ppermute | solution.py:28

commit v13 on v10

--- a/solution.py
+++ b/solution.py
@@ -348,8 +348,8 @@
     rest_y2 = trade(rest_2, 0)
 
     e, y, z, yz = (("top", low, eighth) for low in range(0, size, quarter))
-    jobs = [[e, (*y[:2], share)], [("top", quarter + share, share), z], [yz]]
-    jobs.append([(0, 0, eighth), (1, 0, quarter)])
+    jobs = [[e, (*y[:2], share)], [("top", quarter + share, share), z], [yz, (0, 0, share)]]
+    jobs.append([(0, share, share), (1, 0, quarter)])
     *head, next_0, panel_1 = run_two_levels(
         meta,
         inv,
@@ -364,15 +364,18 @@
     head_c = [trade(x, 2) for x in head]
 
     tops = [("top", low, share) for low in range(0, size, eighth)]
-    lead, others, panel_2 = run_level(
+    first, lead, others, panel_2 = run_level(
         2,
         meta,
         (inv,),
-        [[tops[0], tops[2], ("top", share, share)], [tops[i] for i in (1, 3, 4, 5, 6, 7)]],
-        top=tuple(sum((rows_of(x) for x in group), []) for group in (head, head_c)),
+        [[tops[0]], [("top", share, share), (0, 0, share)], tops[1:]],
+        top=tuple(
+            rows_of(group[0]) + rows_of(group[1]) + [(group[2], 0, eighth)] for group in (head, head_c)
+        ),
+        pairs=[tuple([(group[2], eighth, share)] for group in (head, head_c))],
         keeps=True,
     )
-    lead_w = trade(lead, 3)
+    first_w, lead_w = trade(first, 3), trade(lead, 3)
     after_z1, rest_y2, lead = after(after_z1, rest_y2, lead)
     next_1 = run_level(
         1,
@@ -395,26 +398,25 @@
         pairs=[(rows_of(x), rows_of(y)) for x, y in zip(next_1, next_c1)],
     )
     last_w1 = trade(last_1, 3)
-    tops_w = lead_w[:eighth]
+    first_wz = trade(first_w, 1)
+    after_z2, first_wz, lead_w = after(after_z2, first_wz, lead_w)
+    tops_w = jnp.concatenate([first_w, first_wz], axis=0)
     tops_wc = trade(tops_w, 2)
     tops_wy = trade(tops_w, 0)
-    after_z2, tops_wy = after(after_z2, tops_wy)
     tops_wyc = trade(tops_wy, 2)
     next_2 = chunk(1, panel_1, after_2, after_z2, cost=5 * 10**9)
     last_2 = chunk(2, panel_2, next_2, trade(next_2, 2))
     last_w2 = trade(last_2, 3)
-    more = lead.shape[0] - eighth
-    tops = [(lead, 0, share), (others, 0, share), (lead, share, share)]
-    tops += [(others, share * i, share) for i in range(1, 6)]
+    tops = [(first, 0, share)] + [(others, share * i, share) for i in range(7)]
     tops_other = [(x, low, share) for low in (0, share) for x in (tops_w, tops_wy)]
     tops_other += [(x, low, share) for low in (0, share) for x in (tops_wc, tops_wyc)]
     out, panel_3 = run_level(
         3,
         meta,
         (inv,),
-        [[("top", 0, share), (0, 0, more), (1, 0, last_1.shape[0])]],
+        [[("top", 0, share), (0, 0, eighth), (1, 0, last_1.shape[0])]],
         top=(tops, tops_other),
-        pairs=[([(lead, eighth, more)], [(lead_w, eighth, more)]), (rows_of(last_1), rows_of(last_w1))],
+        pairs=[(rows_of(lead), rows_of(lead_w)), (rows_of(last_1), rows_of(last_w1))],
         keeps=True,
         part=(all_rows, 0, None),
         cost=5 * 10**10,

time: 142 us -> 142 us (level)
  waiting for transfers between devices: 95.9 us -> 93.1 us
  starting transfers between devices: 17.4 us -> 20.2 us
    ppermute x23 -> x25, starting transfers between devices: 17.4 us -> 20.2 us  [trade(): lax.ppermute(block, axis, [(i, i ^ flip) for i in range(lax.axis_size(axi...]
    ppermute x23 -> x25, waiting for transfers between devices: 95.9 us -> 93.1 us  [trade(): lax.ppermute(block, axis, [(i, i ^ flip) for i in range(lax.axis_size(axi...]
  transfers between devices with their start and end apart: 23 -> 25, of which waited for: 13 -> 15; matrix products, arithmetic and copies ran while one was open for 2% -> 2% of each run, Pallas kernels for 15% -> 15%
where the time goes in v13:
time: 142 us; the launch traced here: 141 us
  waiting for transfers between devices  93.1 us (66%)
  Pallas kernels  23.1 us (16%)
  starting transfers between devices  20.2 us (14%)
  local copies, waits for them, and re-layouts  4.65 us (3%)
    ppermute x25, waiting for transfers between devices, trade(): lax.ppermute(block, axis, [(i, i ^ flip) for i in range(lax.axis_size(axi...  93.1 us
    ppermute x25, starting transfers between devices, trade(): lax.ppermute(block, axis, [(i, i ^ flip) for i in range(lax.axis_size(axi...  20.2 us
    pallas_call x9, Pallas kernels, run_level(): pl.pallas_call(kernel, grid=(1,) if part is not None else (), out_shape=s...  17.7 us
    pallas_call x1, Pallas kernels, run_two_levels(): pl.pallas_call(kernel, out_shape=[jax.ShapeDtypeStruct((n, width), BF16)...  4.48 us
  transfers between devices with their start and end apart: 25, of which 15 were waited for; matrix products, arithmetic and copies ran while one was open for 2% of the time, Pallas kernels for 15%

profile of v13, /device:TPU:0, one launch (start us, length us, event | category | flops | bytes accessed | tf_op | source)
XLA Modules:
  0.0 141.3 jit_solution(1758927046049028265)
XLA Ops:
  0.0 1.2 slice.84.refs_1_
  1.2 3.0 %collective-permute-start.2 = (bf16[80,4096]{1,0:T(8,128)(2,1)S(1)}, bf16[80,4096]{1,0:T(8,128)(2,1)}, u32[]{:S(2)}, u32[]{:S(2)}) collective-permute-start(bf16[80,4096]{1,0:T(8,128)(2,1)S(1)} %slice.84.refs_1_), channel_id=1, source_target_pairs={{0,16},{8,24},{16,0},{24,8},{1,17},{9,25},{17,1},{25,9},{2,18},{10... | collective-permute-start | bytes 1966088 | tf_op jit(solution)/shard_map/ppermute | solution.py:28
  4.2 2.6 %collective-permute-start = (bf16[80,4096]{1,0:T(8,128)(2,1)S(1)}, bf16[80,4096]{1,0:T(8,128)(2,1)S(1)}, u32[]{:S(2)}, u32[]{:S(2)}) collective-permute-start(bf16[80,4096]{1,0:T(8,128)(2,1)S(1)} %slice.84.refs_1_), channel_id=1, source_target_pairs={{0,4},{1,5},{2,6},{3,7},{4,0},{5,1},{6,2},{7,3},{8,12},{9,13},{10,... | collective-permute-start | bytes 1966088 | tf_op jit(solution)/shard_map/ppermute | solution.py:28
  6.8 1.3 fusion.8
  9.7 1.6 %collective-permute-start.3 = (bf16[48,4096]{1,0:T(8,128)(2,1)S(1)}, bf16[48,4096]{1,0:T(8,128)(2,1)}, u32[]{:S(2)}, u32[]{:S(2)}) collective-permute-start(bf16[48,4096]{1,0:T(8,128)(2,1)S(1)} %slice.85.refs_2_), channel_id=1, source_target_pairs={{0,16},{8,24},{16,0},{24,8},{1,17},{9,25},{17,1},{25,9},{2,18},{10... | collective-permute-start | bytes 1179656 | tf_op jit(solution)/shard_map/ppermute | solution.py:28
  11.3 24.1 %collective-permute-done.refs_0_ = bf16[80,4096]{1,0:T(8,128)(2,1)S(1)} collective-permute-done((bf16[80,4096]{1,0:T(8,128)(2,1)S(1)}, bf16[80,4096]{1,0:T(8,128)(2,1)S(1)}, u32[]{:S(2)}, u32[]{:S(2)}) %collective-permute-start) | collective-permute-done | bytes 655392 | tf_op jit(solution)/shard_map/ppermute | solution.py:28
  36.1 1.0 copy-done
  38.1 1.4 %collective-permute-done.3.refs_4_ = bf16[48,4096]{1,0:T(8,128)(2,1)} collective-permute-done((bf16[48,4096]{1,0:T(8,128)(2,1)S(1)}, bf16[48,4096]{1,0:T(8,128)(2,1)}, u32[]{:S(2)}, u32[]{:S(2)}) %collective-permute-start.3) | collective-permute-done | bytes 393248 | tf_op jit(solution)/shard_map/ppermute | solution.py:28
  39.5 3.5 %level0_rows256.1 = (bf16[128,4096]{1,0:T(8,128)(2,1)S(1)}, bf16[64,4096]{1,0:T(8,128)(2,1)S(1)}, bf16[64,4096]{1,0:T(8,128)(2,1)S(1)}, bf16[256,4096]{1,0:T(8,128)(2,1)S(1)}) custom-call(s32[640]{0:T(1024)S(1)} %concatenate.6.meta, bf16[4,256,256]{2,1,0:T(8,128)(2,1)S(1)} %reorder.1.refs_0_.inv, bf16[80,4096]{1,0:T(8,128)(2,1)S(1)} %slice.84.refs_1_, ...), custom_call_target="tpu_custom_call" | custom-call | tf_op jit(solution)/shard_map/level0_rows256/pallas_call | solution.py:228
  43.0 12.0 %collective-permute-done.1.refs_1_ = bf16[48,4096]{1,0:T(8,128)(2,1)} collective-permute-done((bf16[48,4096]{1,0:T(8,128)(2,1)S(1)}, bf16[48,4096]{1,0:T(8,128)(2,1)}, u32[]{:S(2)}, u32[]{:S(2)}) %collective-permute-start.1) | collective-permute-done | bytes 393248 | tf_op jit(solution)/shard_map/ppermute | solution.py:28
  55.0 1.5 %collective-permute-start.6 = (bf16[48,4096]{1,0:T(8,128)(2,1)}, bf16[48,4096]{1,0:T(8,128)(2,1)S(1)}, u32[]{:S(2)}, u32[]{:S(2)}) collective-permute-start(bf16[48,4096]{1,0:T(8,128)(2,1)} %collective-permute-done.1.refs_1_), channel_id=1, source_target_pairs={{0,16},{8,24},{16,0},{24,8},{1,17},{9,25},{17,1},{25,9},{2,18},{10... | collective-permute-start | bytes 1179656 | tf_op jit(solution)/shard_map/ppermute | solution.py:28
  57.0 7.6 %collective-permute-done.6.refs_3_ = bf16[48,4096]{1,0:T(8,128)(2,1)S(1)} collective-permute-done((bf16[48,4096]{1,0:T(8,128)(2,1)}, bf16[48,4096]{1,0:T(8,128)(2,1)S(1)}, u32[]{:S(2)}, u32[]{:S(2)}) %collective-permute-start.6) | collective-permute-done | bytes 393248 | tf_op jit(solution)/shard_map/ppermute | solution.py:28
  64.5 1.5 %collective-permute-start.12 = (bf16[64,4096]{1,0:T(8,128)(2,1)S(1)}, bf16[64,4096]{1,0:T(8,128)(2,1)S(1)}, u32[]{:S(2)}, u32[]{:S(2)}) collective-permute-start(bf16[64,4096]{1,0:T(8,128)(2,1)S(1)} %get-tuple-element.61.refs_2_), channel_id=1, source_target_pairs={{0,16},{8,24},{16,0},{24,8},{1,17},{9,25},{17,1},{25,9},{2,18},{10... | collective-permute-start | bytes 1572872 | tf_op jit(solution)/shard_map/ppermute | solution.py:28
  66.1 4.5 %level0_level1.1 = (bf16[48,4096]{1,0:T(8,128)(2,1)S(1)}, bf16[48,4096]{1,0:T(8,128)(2,1)S(1)}, bf16[48,4096]{1,0:T(8,128)(2,1)S(1)}, bf16[80,4096]{1,0:T(8,128)(2,1)S(1)}, bf16[256,4096]{1,0:T(8,128)(2,1)S(1)}) custom-call(s32[640]{0:T(1024)S(1)} %concatenate.6.meta, bf16[4,256,256]{2,1,0:T(8,128)(2,1)S(1)} %reorder.1.refs_0_.inv, ...), custom_call_target="tpu_custom_call" | custom-call | tf_op jit(solution)/shard_map/level0_level1/pallas_call | solution.py:254
  71.2 1.1 collective-permute-done.7.refs_4_
  73.5 2.2 %level2_rows160.1 = (bf16[16,4096]{1,0:T(8,128)(2,1)S(1)}, bf16[32,4096]{1,0:T(8,128)(2,1)S(1)}, bf16[112,4096]{1,0:T(8,128)(2,1)S(1)}, bf16[256,4096]{1,0:T(8,128)(2,1)S(1)}) custom-call(s32[640]{0:T(1024)S(1)} %concatenate.6.meta, bf16[4,256,256]{2,1,0:T(8,128)(2,1)S(1)} %reorder.1.refs_0_.inv, bf16[48,4096]{1,0:T(8,128)(2,1)S(1)} %get-tuple-element.55.refs_1_, ...), custom_call_target="tpu_custom_call" | custom-call | tf_op jit(solution)/shard_map/level2_rows160/pallas_call | solution.py:228
  75.9 1.9 %collective-permute-start.15 = (bf16[32,4096]{1,0:T(8,128)(2,1)S(1)}, bf16[32,4096]{1,0:T(8,128)(2,1)S(1)}, u32[]{:S(2)}, u32[]{:S(2)}) collective-permute-start(bf16[32,4096]{1,0:T(8,128)(2,1)S(1)} %get-tuple-element.66.refs_7_), channel_id=1, source_target_pairs={{0,2},{1,3},{2,0},{3,1},{4,6},{5,7},{6,4},{7,5},{8,10},{9,11},{10,... | collective-permute-start | bytes 786440 | tf_op jit(solution)/shard_map/ppermute | solution.py:28
  77.8 2.6 %collective-permute-done.11.refs_3_ = bf16[64,4096]{1,0:T(8,128)(2,1)S(1)} collective-permute-done((bf16[64,4096]{1,0:T(8,128)(2,1)S(1)}, bf16[64,4096]{1,0:T(8,128)(2,1)S(1)}, u32[]{:S(2)}, u32[]{:S(2)}) %collective-permute-start.11) | collective-permute-done | bytes 524320 | tf_op jit(solution)/shard_map/ppermute | solution.py:28
  80.4 1.2 level0_rows64.1.refs_2_
  81.7 1.2 level1_rows64.2
  83.5 2.9 %collective-permute-start.14 = (bf16[16,4096]{1,0:T(8,128)(2,1)S(1)}, bf16[16,4096]{1,0:T(8,128)(2,1)S(1)}, u32[]{:S(2)}, u32[]{:S(2)}) collective-permute-start(bf16[16,4096]{1,0:T(8,128)(2,1)S(1)} %collective-permute-done.10), channel_id=1, source_target_pairs={{0,4},{1,5},{2,6},{3,7},{4,0},{5,1},{6,2},{7,3},{8,12},{9,13},{10,... | collective-permute-start | bytes 393224 | tf_op jit(solution)/shard_map/ppermute | solution.py:28
  86.5 1.4 %level2_rows144.1.refs_9_ = bf16[144,4096]{1,0:T(8,128)(2,1)S(1)} custom-call(s32[640]{0:T(1024)S(1)} %concatenate.6.meta, bf16[4,256,256]{2,1,0:T(8,128)(2,1)S(1)} %reorder.1.refs_0_.inv, bf16[256,4096]{1,0:T(8,128)(2,1)S(1)} %get-tuple-element.68.refs_1_, bf16[80,4096]{1,0:T(8,128)(2,1)S(1)} %get-tuple-element.69.refs_2_, ...), custom_call_target="tpu_custom_call" | custom-call | tf_op jit(solution)/shard_map/level2_rows144/pallas_call | solution.py:228
  87.9 1.3 collective-permute-start.22
  89.2 3.3 %collective-permute-done.15.refs_8_ = bf16[32,4096]{1,0:T(8,128)(2,1)S(1)} collective-permute-done((bf16[32,4096]{1,0:T(8,128)(2,1)S(1)}, bf16[32,4096]{1,0:T(8,128)(2,1)S(1)}, u32[]{:S(2)}, u32[]{:S(2)}) %collective-permute-start.15) | collective-permute-done | bytes 262176 | tf_op jit(solution)/shard_map/ppermute | solution.py:28
  92.5 20.3 %collective-permute-done.14 = bf16[16,4096]{1,0:T(8,128)(2,1)S(1)} collective-permute-done((bf16[16,4096]{1,0:T(8,128)(2,1)S(1)}, bf16[16,4096]{1,0:T(8,128)(2,1)S(1)}, u32[]{:S(2)}, u32[]{:S(2)}) %collective-permute-start.14) | collective-permute-done | bytes 131104 | tf_op jit(solution)/shard_map/ppermute | solution.py:28
  112.8 1.2 level1_rows64.3.refs_2_
  114.8 8.1 %collective-permute-done.16.refs_4_ = bf16[32,4096]{1,0:T(8,128)(2,1)S(1)} collective-permute-done((bf16[32,4096]{1,0:T(8,128)(2,1)S(1)}, bf16[32,4096]{1,0:T(8,128)(2,1)S(1)}, u32[]{:S(2)}, u32[]{:S(2)}) %collective-permute-start.16) | collective-permute-done | bytes 262176 | tf_op jit(solution)/shard_map/ppermute | solution.py:28
  122.9 1.2 level2_rows64.1.refs_2_
  124.4 3.7 %collective-permute-done.22.refs_10_ = bf16[144,4096]{1,0:T(8,128)(2,1)S(1)} collective-permute-done((bf16[144,4096]{1,0:T(8,128)(2,1)S(1)}, bf16[144,4096]{1,0:T(8,128)(2,1)S(1)}, u32[]{:S(2)}, u32[]{:S(2)}) %collective-permute-start.22) | collective-permute-done | bytes 1179680 | tf_op jit(solution)/shard_map/ppermute | solution.py:28
  128.1 3.6 %level3_rows192.1 = (bf16[256,4096]{1,0:T(8,128)(2,1)}, bf16[256,4096]{1,0:T(8,128)(2,1)S(1)}) custom-call(s32[640]{0:T(1024)S(1)} %concatenate.6.meta, bf16[4,256,256]{2,1,0:T(8,128)(2,1)S(1)} %reorder.1.refs_0_.inv, bf16[16,4096]{1,0:T(8,128)(2,1)S(1)} %get-tuple-element.58.refs_1_, bf16[112,4096]{1,0:T(8,128)(2,1)S(1)} %get-tuple-element.59.refs_2_, ...), custom_call_target="tpu_custom_call" | custom-call | flops 49999998976 | tf_op jit(solution)/shard_map/level3_rows192/pallas_call | solution.py:228
  131.7 7.6 %collective-permute-done.24.refs_3_ = bf16[64,4096]{1,0:T(8,128)(2,1)S(1)} collective-permute-done((bf16[64,4096]{1,0:T(8,128)(2,1)S(1)}, bf16[64,4096]{1,0:T(8,128)(2,1)S(1)}, u32[]{:S(2)}, u32[]{:S(2)}) %collective-permute-start.24) | collective-permute-done | bytes 524320 | tf_op jit(solution)/shard_map/ppermute | solution.py:28
  139.3 2.0 %level3_rows64.1 = bf16[256,4096]{1,0:T(8,128)(2,1)} custom-call(s32[640]{0:T(1024)S(1)} %concatenate.6.meta, bf16[4,256,256]{2,1,0:T(8,128)(2,1)S(1)} %reorder.1.refs_0_.inv, bf16[256,4096]{1,0:T(8,128)(2,1)S(1)} %get-tuple-element.75.refs_1_, bf16[64,4096]{1,0:T(8,128)(2,1)S(1)} %level2_rows64.1.refs_2_, ...), custom_call_target="tpu_custom_call", output_to_operand_aliasing={{}: (5, {})} | custom-call | tf_op jit(solution)/shard_map/level3_rows64/pallas_call | solution.py:228
  (50 shorter events, 7.2 us)
Async XLA Ops:
  0.0 35.8 %copy-start.1 = (s32[4,2,32]{2,1,0:T(2,128)S(1)}, s32[4,2,32]{2,1,0:T(2,128)}, u32[]{:S(2)}) copy-start(s32[4,2,32]{2,1,0:T(2,128)} %param.7) | copy-start | bytes 3076
  0.0 35.9 %copy-start.3 = (s32[4,32]{1,0:T(4,128)S(1)}, s32[4,32]{1,0:T(4,128)}, u32[]{:S(2)}) copy-start(s32[4,32]{1,0:T(4,128)} %param.8) | copy-start | bytes 1540
  0.0 35.9 %copy-start.2 = (s32[4,32]{1,0:T(4,128)S(1)}, s32[4,32]{1,0:T(4,128)}, u32[]{:S(2)}) copy-start(s32[4,32]{1,0:T(4,128)} %param.9) | copy-start | bytes 1540
  1.2 38.4 %collective-permute-start.2 = (bf16[80,4096]{1,0:T(8,128)(2,1)S(1)}, bf16[80,4096]{1,0:T(8,128)(2,1)}, u32[]{:S(2)}, u32[]{:S(2)}) collective-permute-start(bf16[80,4096]{1,0:T(8,128)(2,1)S(1)} %slice.84.refs_1_), channel_id=1, source_target_pairs={{0,16},{8,24},{16,0},{24,8},{1,17},{9,25},{17,1},{25,9},{2,18},{10... | collective-permute-start | bytes 1966088 | tf_op jit(solution)/shard_map/ppermute | solution.py:28
  4.2 31.1 %collective-permute-start = (bf16[80,4096]{1,0:T(8,128)(2,1)S(1)}, bf16[80,4096]{1,0:T(8,128)(2,1)S(1)}, u32[]{:S(2)}, u32[]{:S(2)}) collective-permute-start(bf16[80,4096]{1,0:T(8,128)(2,1)S(1)} %slice.84.refs_1_), channel_id=1, source_target_pairs={{0,4},{1,5},{2,6},{3,7},{4,0},{5,1},{6,2},{7,3},{8,12},{9,13},{10,... | collective-permute-start | bytes 1966088 | tf_op jit(solution)/shard_map/ppermute | solution.py:28
  8.1 30.0 %collective-permute-start.4 = (bf16[64,4096]{1,0:T(8,128)(2,1)S(1)}, bf16[64,4096]{1,0:T(8,128)(2,1)}, u32[]{:S(2)}, u32[]{:S(2)}) collective-permute-start(bf16[64,4096]{1,0:T(8,128)(2,1)S(1)} %get-tuple-element.80.refs_5_), channel_id=1, source_target_pairs={{0,16},{8,24},{16,0},{24,8},{1,17},{9,25},{17,1},{25,9},{2,18},{10... | collective-permute-start | bytes 1572872 | tf_op jit(solution)/shard_map/ppermute | solution.py:28
  9.7 29.9 %collective-permute-start.3 = (bf16[48,4096]{1,0:T(8,128)(2,1)S(1)}, bf16[48,4096]{1,0:T(8,128)(2,1)}, u32[]{:S(2)}, u32[]{:S(2)}) collective-permute-start(bf16[48,4096]{1,0:T(8,128)(2,1)S(1)} %slice.85.refs_2_), channel_id=1, source_target_pairs={{0,16},{8,24},{16,0},{24,8},{1,17},{9,25},{17,1},{25,9},{2,18},{10... | collective-permute-start | bytes 1179656 | tf_op jit(solution)/shard_map/ppermute | solution.py:28
  35.3 19.7 %collective-permute-start.5 = (bf16[80,4096]{1,0:T(8,128)(2,1)S(1)}, bf16[80,4096]{1,0:T(8,128)(2,1)S(1)}, u32[]{:S(2)}, u32[]{:S(2)}) collective-permute-start(bf16[80,4096]{1,0:T(8,128)(2,1)S(1)} %collective-permute-done.refs_0_), channel_id=1, source_target_pairs={{0,16},{8,24},{16,0},{24,8},{1,17},{9,25},{17,1},{25,9},{2,18},{10... | collective-permute-start | bytes 1966088 | tf_op jit(solution)/shard_map/ppermute | solution.py:28
  35.8 19.2 %collective-permute-start.1 = (bf16[48,4096]{1,0:T(8,128)(2,1)S(1)}, bf16[48,4096]{1,0:T(8,128)(2,1)}, u32[]{:S(2)}, u32[]{:S(2)}) collective-permute-start(bf16[48,4096]{1,0:T(8,128)(2,1)S(1)} %slice.85.refs_2_), channel_id=1, source_target_pairs={{0,4},{1,5},{2,6},{3,7},{4,0},{5,1},{6,2},{7,3},{8,12},{9,13},{10,... | collective-permute-start | bytes 1179656 | tf_op jit(solution)/shard_map/ppermute | solution.py:28
  36.1 1.0 copy-start
  55.0 9.5 %collective-permute-start.6 = (bf16[48,4096]{1,0:T(8,128)(2,1)}, bf16[48,4096]{1,0:T(8,128)(2,1)S(1)}, u32[]{:S(2)}, u32[]{:S(2)}) collective-permute-start(bf16[48,4096]{1,0:T(8,128)(2,1)} %collective-permute-done.1.refs_1_), channel_id=1, source_target_pairs={{0,16},{8,24},{16,0},{24,8},{1,17},{9,25},{17,1},{25,9},{2,18},{10... | collective-permute-start | bytes 1179656 | tf_op jit(solution)/shard_map/ppermute | solution.py:28
  56.6 23.8 %collective-permute-start.11 = (bf16[64,4096]{1,0:T(8,128)(2,1)S(1)}, bf16[64,4096]{1,0:T(8,128)(2,1)S(1)}, u32[]{:S(2)}, u32[]{:S(2)}) collective-permute-start(bf16[64,4096]{1,0:T(8,128)(2,1)S(1)} %get-tuple-element.62.refs_2_), channel_id=1, source_target_pairs={{0,4},{1,5},{2,6},{3,7},{4,0},{5,1},{6,2},{7,3},{8,12},{9,13},{10,... | collective-permute-start | bytes 1572872 | tf_op jit(solution)/shard_map/ppermute | solution.py:28
  64.5 15.9 %collective-permute-start.12 = (bf16[64,4096]{1,0:T(8,128)(2,1)S(1)}, bf16[64,4096]{1,0:T(8,128)(2,1)S(1)}, u32[]{:S(2)}, u32[]{:S(2)}) collective-permute-start(bf16[64,4096]{1,0:T(8,128)(2,1)S(1)} %get-tuple-element.61.refs_2_), channel_id=1, source_target_pairs={{0,16},{8,24},{16,0},{24,8},{1,17},{9,25},{17,1},{25,9},{2,18},{10... | collective-permute-start | bytes 1572872 | tf_op jit(solution)/shard_map/ppermute | solution.py:28
  70.6 1.8 %collective-permute-start.7 = (bf16[48,4096]{1,0:T(8,128)(2,1)S(1)}, bf16[48,4096]{1,0:T(8,128)(2,1)S(1)}, u32[]{:S(2)}, u32[]{:S(2)}) collective-permute-start(bf16[48,4096]{1,0:T(8,128)(2,1)S(1)} %get-tuple-element.55.refs_1_), channel_id=1, source_target_pairs={{0,8},{8,0},{16,24},{24,16},{1,9},{9,1},{17,25},{25,17},{2,10},{10... | collective-permute-start | bytes 1179656 | tf_op jit(solution)/shard_map/ppermute | solution.py:28
  70.7 2.3 %collective-permute-start.8 = (bf16[48,4096]{1,0:T(8,128)(2,1)S(1)}, bf16[48,4096]{1,0:T(8,128)(2,1)S(1)}, u32[]{:S(2)}, u32[]{:S(2)}) collective-permute-start(bf16[48,4096]{1,0:T(8,128)(2,1)S(1)} %get-tuple-element.56.refs_2_), channel_id=1, source_target_pairs={{0,8},{8,0},{16,24},{24,16},{1,9},{9,1},{17,25},{25,17},{2,10},{10... | collective-permute-start | bytes 1179656 | tf_op jit(solution)/shard_map/ppermute | solution.py:28
  71.1 2.3 %collective-permute-start.9 = (bf16[48,4096]{1,0:T(8,128)(2,1)S(1)}, bf16[48,4096]{1,0:T(8,128)(2,1)S(1)}, u32[]{:S(2)}, u32[]{:S(2)}) collective-permute-start(bf16[48,4096]{1,0:T(8,128)(2,1)S(1)} %get-tuple-element.57.refs_3_), channel_id=1, source_target_pairs={{0,8},{8,0},{16,24},{24,16},{1,9},{9,1},{17,25},{25,17},{2,10},{10... | collective-permute-start | bytes 1179656 | tf_op jit(solution)/shard_map/ppermute | solution.py:28
  72.4 11.2 %collective-permute-start.19 = (bf16[80,4096]{1,0:T(8,128)(2,1)S(1)}, bf16[80,4096]{1,0:T(8,128)(2,1)S(1)}, u32[]{:S(2)}, u32[]{:S(2)}) collective-permute-start(bf16[80,4096]{1,0:T(8,128)(2,1)S(1)} %get-tuple-element.69.refs_2_), channel_id=1, source_target_pairs={{0,8},{8,0},{16,24},{24,16},{1,9},{9,1},{17,25},{25,17},{2,10},{10... | collective-permute-start | bytes 1966088 | tf_op jit(solution)/shard_map/ppermute | solution.py:28
  75.7 7.5 %collective-permute-start.10 = (bf16[16,4096]{1,0:T(8,128)(2,1)S(1)}, bf16[16,4096]{1,0:T(8,128)(2,1)S(1)}, u32[]{:S(2)}, u32[]{:S(2)}) collective-permute-start(bf16[16,4096]{1,0:T(8,128)(2,1)S(1)} %get-tuple-element.58.refs_1_), channel_id=1, source_target_pairs={{0,2},{1,3},{2,0},{3,1},{4,6},{5,7},{6,4},{7,5},{8,10},{9,11},{10,... | collective-permute-start | bytes 393224 | tf_op jit(solution)/shard_map/ppermute | solution.py:28
  75.9 16.6 %collective-permute-start.15 = (bf16[32,4096]{1,0:T(8,128)(2,1)S(1)}, bf16[32,4096]{1,0:T(8,128)(2,1)S(1)}, u32[]{:S(2)}, u32[]{:S(2)}) collective-permute-start(bf16[32,4096]{1,0:T(8,128)(2,1)S(1)} %get-tuple-element.66.refs_7_), channel_id=1, source_target_pairs={{0,2},{1,3},{2,0},{3,1},{4,6},{5,7},{6,4},{7,5},{8,10},{9,11},{10,... | collective-permute-start | bytes 786440 | tf_op jit(solution)/shard_map/ppermute | solution.py:28
  81.7 31.1 %collective-permute-start.13 = (bf16[64,4096]{1,0:T(8,128)(2,1)S(1)}, bf16[64,4096]{1,0:T(8,128)(2,1)S(1)}, u32[]{:S(2)}, u32[]{:S(2)}) collective-permute-start(bf16[64,4096]{1,0:T(8,128)(2,1)S(1)} %level0_rows64.1.refs_2_), channel_id=1, source_target_pairs={{0,4},{1,5},{2,6},{3,7},{4,0},{5,1},{6,2},{7,3},{8,12},{9,13},{10,... | collective-permute-start | bytes 1572872 | tf_op jit(solution)/shard_map/ppermute | solution.py:28
  83.0 3.5 %collective-permute-start.20 = (bf16[32,4096]{1,0:T(8,128)(2,1)S(1)}, bf16[32,4096]{1,0:T(8,128)(2,1)S(1)}, u32[]{:S(2)}, u32[]{:S(2)}) collective-permute-start(bf16[32,4096]{1,0:T(8,128)(2,1)S(1)} %get-tuple-element.73.refs_4_), channel_id=1, source_target_pairs={{0,8},{8,0},{16,24},{24,16},{1,9},{9,1},{17,25},{25,17},{2,10},{10... | collective-permute-start | bytes 786440 | tf_op jit(solution)/shard_map/ppermute | solution.py:28
  83.2 3.3 %collective-permute-start.21 = (bf16[32,4096]{1,0:T(8,128)(2,1)S(1)}, bf16[32,4096]{1,0:T(8,128)(2,1)S(1)}, u32[]{:S(2)}, u32[]{:S(2)}) collective-permute-start(bf16[32,4096]{1,0:T(8,128)(2,1)S(1)} %get-tuple-element.74.refs_6_), channel_id=1, source_target_pairs={{0,8},{8,0},{16,24},{24,16},{1,9},{9,1},{17,25},{25,17},{2,10},{10... | collective-permute-start | bytes 786440 | tf_op jit(solution)/shard_map/ppermute | solution.py:28
  83.5 29.2 %collective-permute-start.14 = (bf16[16,4096]{1,0:T(8,128)(2,1)S(1)}, bf16[16,4096]{1,0:T(8,128)(2,1)S(1)}, u32[]{:S(2)}, u32[]{:S(2)}) collective-permute-start(bf16[16,4096]{1,0:T(8,128)(2,1)S(1)} %collective-permute-done.10), channel_id=1, source_target_pairs={{0,4},{1,5},{2,6},{3,7},{4,0},{5,1},{6,2},{7,3},{8,12},{9,13},{10,... | collective-permute-start | bytes 393224 | tf_op jit(solution)/shard_map/ppermute | solution.py:28
  87.9 40.2 %collective-permute-start.22 = (bf16[144,4096]{1,0:T(8,128)(2,1)S(1)}, bf16[144,4096]{1,0:T(8,128)(2,1)S(1)}, u32[]{:S(2)}, u32[]{:S(2)}) collective-permute-start(bf16[144,4096]{1,0:T(8,128)(2,1)S(1)} %level2_rows144.1.refs_9_), channel_id=1, source_target_pairs={{0,2},{1,3},{2,0},{3,1},{4,6},{5,7},{6,4},{7,5},{8,10},{9,11},{10,... | collective-permute-start | bytes 3538952 | tf_op jit(solution)/shard_map/ppermute | solution.py:28
  114.0 8.9 %collective-permute-start.23 = (bf16[64,4096]{1,0:T(8,128)(2,1)S(1)}, bf16[64,4096]{1,0:T(8,128)(2,1)S(1)}, u32[]{:S(2)}, u32[]{:S(2)}) collective-permute-start(bf16[64,4096]{1,0:T(8,128)(2,1)S(1)} %level1_rows64.3.refs_2_), channel_id=1, source_target_pairs={{0,8},{8,0},{16,24},{24,16},{1,9},{9,1},{17,25},{25,17},{2,10},{10... | collective-permute-start | bytes 1572872 | tf_op jit(solution)/shard_map/ppermute | solution.py:28
  114.1 8.8 %collective-permute-start.16 = (bf16[32,4096]{1,0:T(8,128)(2,1)S(1)}, bf16[32,4096]{1,0:T(8,128)(2,1)S(1)}, u32[]{:S(2)}, u32[]{:S(2)}) collective-permute-start(bf16[32,4096]{1,0:T(8,128)(2,1)S(1)} %constant_dynamic-update-slice_fusion.refs_3_), channel_id=1, source_target_pairs={{0,16},{8,24},{16,0},{24,8},{1,17},{9,25},{17,1},{25,9},{2,18},{10... | collective-permute-start | bytes 786440 | tf_op jit(solution)/shard_map/ppermute | solution.py:28
  114.6 9.6 %collective-permute-start.17 = (bf16[32,4096]{1,0:T(8,128)(2,1)S(1)}, bf16[32,4096]{1,0:T(8,128)(2,1)S(1)}, u32[]{:S(2)}, u32[]{:S(2)}) collective-permute-start(bf16[32,4096]{1,0:T(8,128)(2,1)S(1)} %constant_dynamic-update-slice_fusion.refs_3_), channel_id=1, source_target_pairs={{0,8},{8,0},{16,24},{24,16},{1,9},{9,1},{17,25},{25,17},{2,10},{10... | collective-permute-start | bytes 786440 | tf_op jit(solution)/shard_map/ppermute | solution.py:28
  122.9 1.5 %collective-permute-start.18 = (bf16[32,4096]{1,0:T(8,128)(2,1)S(1)}, bf16[32,4096]{1,0:T(8,128)(2,1)S(1)}, u32[]{:S(2)}, u32[]{:S(2)}) collective-permute-start(bf16[32,4096]{1,0:T(8,128)(2,1)S(1)} %collective-permute-done.16.refs_4_), channel_id=1, source_target_pairs={{0,8},{8,0},{16,24},{24,16},{1,9},{9,1},{17,25},{25,17},{2,10},{10... | collective-permute-start | bytes 786440 | tf_op jit(solution)/shard_map/ppermute | solution.py:28
  124.1 15.2 %collective-permute-start.24 = (bf16[64,4096]{1,0:T(8,128)(2,1)S(1)}, bf16[64,4096]{1,0:T(8,128)(2,1)S(1)}, u32[]{:S(2)}, u32[]{:S(2)}) collective-permute-start(bf16[64,4096]{1,0:T(8,128)(2,1)S(1)} %level2_rows64.1.refs_2_), channel_id=1, source_target_pairs={{0,2},{1,3},{2,0},{3,1},{4,6},{5,7},{6,4},{7,5},{8,10},{9,11},{10,... | collective-permute-start | bytes 1572872 | tf_op jit(solution)/shard_map/ppermute | solution.py:28

commit v14 on v13

--- a/solution.py
+++ b/solution.py
@@ -68,11 +68,13 @@
         out[level] = jnp.dot(inv[level], swap, preferred_element_type=F32).astype(BF16)
 
 
-def eliminate(meta, inv, panel, merged, top, pairs, outs, level, blocks):
+def eliminate(meta, inv, panel, merged, top, pairs, outs, level, blocks, flush=None):
     width = blocks * BLOCK
     base = level * meta.shape[0] // LEVELS
 
     def at(j):
+        if isinstance(j, int):
+            return pl.ds(j * BLOCK, BLOCK)
         return pl.ds(pl.multiple_of(j * BLOCK, BLOCK), BLOCK)
 
     def read(pieces, start, rows, j):
@@ -124,7 +126,7 @@
     weights = jnp.dot(coupling, inv[level], preferred_element_type=F32).astype(BF16)
 
     def finish_tile(t, carry):
-        lanes = pl.ds(pl.multiple_of(t * TILE, TILE), TILE)
+        lanes = pl.ds(t * TILE, TILE)
         update = jnp.dot(weights, panel[:, lanes], preferred_element_type=F32)
         done = 0
         for out, dest in outs:
@@ -139,7 +141,10 @@
                 done += rows
         return carry
 
-    lax.fori_loop(0, width // TILE, finish_tile, 0, unroll=True)
+    for t in range(width // TILE):
+        finish_tile(t, 0)
+        if flush is not None:
+            flush(t)
 
 
 def level_kernel(meta, *refs, level, blocks, n_in, top, pairs, outs, n_hidden):
@@ -173,6 +178,46 @@
     top = tuple([(ref, 0, ref.shape[0])] for ref in (near, far))
     stacked = [tuple([(ref, low, rows)] for ref in held[i]) for i, low, rows in pairs]
     eliminate(meta, inv, panel, merged, top, stacked, list(zip(outs, second_outs)), 1, blocks)
+
+
+def last_kernel(meta, inv, panel, own, other, old, out, made, sems, *, level, blocks, first):
+    del old
+    rows, width = own.shape
+    quarter = width // sems.shape[0]
+    copies = [
+        pltpu.make_async_copy(
+            made.at[:, pl.ds(i * quarter, quarter)],
+            out.at[pl.ds(first, rows), pl.ds(i * quarter, quarter)],
+            sems.at[i],
+        )
+        for i in range(sems.shape[0])
+    ]
+
+    def flush(t):
+        if (t + 1) * TILE % quarter == 0:
+            copies[t * TILE // quarter].start()
+
+    pair = ([(own, 0, rows)], [(other, 0, rows)])
+    eliminate(meta, inv, panel, None, None, [pair], [(made, [(0, 0, rows)])], level, blocks, flush)
+    for copy in copies:
+        copy.wait()
+
+
+def run_last(level, meta, inv, panel, own, other, first, old):
+    rows, width = own.shape
+    vmem = pl.BlockSpec(memory_space=pltpu.VMEM)
+    kernel = functools.partial(last_kernel, level=level, blocks=width // BLOCK, first=first)
+    return pl.pallas_call(
+        kernel,
+        out_shape=jax.ShapeDtypeStruct(old.shape, BF16),
+        in_specs=[pl.BlockSpec(memory_space=pltpu.SMEM)] + [vmem] * 4 + [pl.BlockSpec(memory_space=pl.ANY)],
+        out_specs=pl.BlockSpec(memory_space=pl.ANY),
+        scratch_shapes=[pltpu.VMEM((rows, width), BF16), pltpu.SemaphoreType.DMA((4,))],
+        input_output_aliases={5: 0},
+        compiler_params=pltpu.CompilerParams(vmem_limit_bytes=30 * 2**20),
+        cost_estimate=pl.CostEstimate(flops=0, bytes_accessed=0, transcendentals=0),
+        name="last_rows",
+    )(meta, inv, panel, own, other, old)
 
 
 def run_level(level, meta, held, outs, pairs=(), top=None, keeps=False, part=None, cost=0):
@@ -421,7 +466,7 @@
         part=(all_rows, 0, None),
         cost=5 * 10**10,
     )
-    return chunk(3, panel_3, last_2, last_w2, part=(all_rows, all_rows // quarter - 1, out))
+    return run_last(3, meta, inv, panel_3, last_2, last_w2, all_rows - quarter, out)
 
 
 def solution(mesh):

time: 142 us -> 142 us (level)
    pallas_call x9 -> x8, Pallas kernels: 17.7 us -> 15.7 us  [run_level(): pl.pallas_call(kernel, grid=(1,) if part is not None else (), out_shape=s...]
    pallas_call x0 -> x1, Pallas kernels: none -> 1.92 us  [run_last(): pl.pallas_call(kernel, out_shape=jax.ShapeDtypeStruct(old.shape, BF16), i...]
where the time goes in v14:
time: 142 us; the launch traced here: 141 us
  waiting for transfers between devices  93.1 us (66%)
  Pallas kernels  23 us (16%)
  starting transfers between devices  20.2 us (14%)
  local copies, waits for them, and re-layouts  4.65 us (3%)
    ppermute x25, waiting for transfers between devices, trade(): lax.ppermute(block, axis, [(i, i ^ flip) for i in range(lax.axis_size(axi...  93.1 us
    ppermute x25, starting transfers between devices, trade(): lax.ppermute(block, axis, [(i, i ^ flip) for i in range(lax.axis_size(axi...  20.2 us
    pallas_call x8, Pallas kernels, run_level(): pl.pallas_call(kernel, grid=(1,) if part is not None else (), out_shape=s...  15.7 us
    pallas_call x1, Pallas kernels, run_two_levels(): pl.pallas_call(kernel, out_shape=[jax.ShapeDtypeStruct((n, width), BF16)...  4.48 us
  transfers between devices with their start and end apart: 25, of which 15 were waited for; matrix products, arithmetic and copies ran while one was open for 2% of the time, Pallas kernels for 15%

profile of v14, /device:TPU:0, one launch (start us, length us, event | category | flops | bytes accessed | tf_op | source)
XLA Modules:
  0.0 141.2 jit_solution(12557322681974192723)
XLA Ops:
  0.0 1.2 slice.84.refs_1_
  1.2 3.0 %collective-permute-start.2 = (bf16[80,4096]{1,0:T(8,128)(2,1)S(1)}, bf16[80,4096]{1,0:T(8,128)(2,1)}, u32[]{:S(2)}, u32[]{:S(2)}) collective-permute-start(bf16[80,4096]{1,0:T(8,128)(2,1)S(1)} %slice.84.refs_1_), channel_id=1, source_target_pairs={{0,16},{8,24},{16,0},{24,8},{1,17},{9,25},{17,1},{25,9},{2,18},{10... | collective-permute-start | bytes 1966088 | tf_op jit(solution)/shard_map/ppermute | solution.py:28
  4.2 2.6 %collective-permute-start = (bf16[80,4096]{1,0:T(8,128)(2,1)S(1)}, bf16[80,4096]{1,0:T(8,128)(2,1)S(1)}, u32[]{:S(2)}, u32[]{:S(2)}) collective-permute-start(bf16[80,4096]{1,0:T(8,128)(2,1)S(1)} %slice.84.refs_1_), channel_id=1, source_target_pairs={{0,4},{1,5},{2,6},{3,7},{4,0},{5,1},{6,2},{7,3},{8,12},{9,13},{10,... | collective-permute-start | bytes 1966088 | tf_op jit(solution)/shard_map/ppermute | solution.py:28
  6.8 1.3 fusion.8
  9.7 1.6 %collective-permute-start.3 = (bf16[48,4096]{1,0:T(8,128)(2,1)S(1)}, bf16[48,4096]{1,0:T(8,128)(2,1)}, u32[]{:S(2)}, u32[]{:S(2)}) collective-permute-start(bf16[48,4096]{1,0:T(8,128)(2,1)S(1)} %slice.85.refs_2_), channel_id=1, source_target_pairs={{0,16},{8,24},{16,0},{24,8},{1,17},{9,25},{17,1},{25,9},{2,18},{10... | collective-permute-start | bytes 1179656 | tf_op jit(solution)/shard_map/ppermute | solution.py:28
  11.3 24.1 %collective-permute-done.refs_0_ = bf16[80,4096]{1,0:T(8,128)(2,1)S(1)} collective-permute-done((bf16[80,4096]{1,0:T(8,128)(2,1)S(1)}, bf16[80,4096]{1,0:T(8,128)(2,1)S(1)}, u32[]{:S(2)}, u32[]{:S(2)}) %collective-permute-start) | collective-permute-done | bytes 655392 | tf_op jit(solution)/shard_map/ppermute | solution.py:28
  36.1 1.0 copy-done
  38.1 1.4 %collective-permute-done.3.refs_4_ = bf16[48,4096]{1,0:T(8,128)(2,1)} collective-permute-done((bf16[48,4096]{1,0:T(8,128)(2,1)S(1)}, bf16[48,4096]{1,0:T(8,128)(2,1)}, u32[]{:S(2)}, u32[]{:S(2)}) %collective-permute-start.3) | collective-permute-done | bytes 393248 | tf_op jit(solution)/shard_map/ppermute | solution.py:28
  39.5 3.5 %level0_rows256.1 = (bf16[128,4096]{1,0:T(8,128)(2,1)S(1)}, bf16[64,4096]{1,0:T(8,128)(2,1)S(1)}, bf16[64,4096]{1,0:T(8,128)(2,1)S(1)}, bf16[256,4096]{1,0:T(8,128)(2,1)S(1)}) custom-call(s32[640]{0:T(1024)S(1)} %concatenate.6.meta, bf16[4,256,256]{2,1,0:T(8,128)(2,1)S(1)} %reorder.1.refs_0_.inv, bf16[80,4096]{1,0:T(8,128)(2,1)S(1)} %slice.84.refs_1_, ...), custom_call_target="tpu_custom_call" | custom-call | tf_op jit(solution)/shard_map/level0_rows256/pallas_call | solution.py:273
  43.0 12.0 %collective-permute-done.1.refs_1_ = bf16[48,4096]{1,0:T(8,128)(2,1)} collective-permute-done((bf16[48,4096]{1,0:T(8,128)(2,1)S(1)}, bf16[48,4096]{1,0:T(8,128)(2,1)}, u32[]{:S(2)}, u32[]{:S(2)}) %collective-permute-start.1) | collective-permute-done | bytes 393248 | tf_op jit(solution)/shard_map/ppermute | solution.py:28
  55.0 1.5 %collective-permute-start.6 = (bf16[48,4096]{1,0:T(8,128)(2,1)}, bf16[48,4096]{1,0:T(8,128)(2,1)S(1)}, u32[]{:S(2)}, u32[]{:S(2)}) collective-permute-start(bf16[48,4096]{1,0:T(8,128)(2,1)} %collective-permute-done.1.refs_1_), channel_id=1, source_target_pairs={{0,16},{8,24},{16,0},{24,8},{1,17},{9,25},{17,1},{25,9},{2,18},{10... | collective-permute-start | bytes 1179656 | tf_op jit(solution)/shard_map/ppermute | solution.py:28
  57.0 7.6 %collective-permute-done.6.refs_3_ = bf16[48,4096]{1,0:T(8,128)(2,1)S(1)} collective-permute-done((bf16[48,4096]{1,0:T(8,128)(2,1)}, bf16[48,4096]{1,0:T(8,128)(2,1)S(1)}, u32[]{:S(2)}, u32[]{:S(2)}) %collective-permute-start.6) | collective-permute-done | bytes 393248 | tf_op jit(solution)/shard_map/ppermute | solution.py:28
  64.5 1.5 %collective-permute-start.12 = (bf16[64,4096]{1,0:T(8,128)(2,1)S(1)}, bf16[64,4096]{1,0:T(8,128)(2,1)S(1)}, u32[]{:S(2)}, u32[]{:S(2)}) collective-permute-start(bf16[64,4096]{1,0:T(8,128)(2,1)S(1)} %get-tuple-element.61.refs_2_), channel_id=1, source_target_pairs={{0,16},{8,24},{16,0},{24,8},{1,17},{9,25},{17,1},{25,9},{2,18},{10... | collective-permute-start | bytes 1572872 | tf_op jit(solution)/shard_map/ppermute | solution.py:28
  66.1 4.5 %level0_level1.1 = (bf16[48,4096]{1,0:T(8,128)(2,1)S(1)}, bf16[48,4096]{1,0:T(8,128)(2,1)S(1)}, bf16[48,4096]{1,0:T(8,128)(2,1)S(1)}, bf16[80,4096]{1,0:T(8,128)(2,1)S(1)}, bf16[256,4096]{1,0:T(8,128)(2,1)S(1)}) custom-call(s32[640]{0:T(1024)S(1)} %concatenate.6.meta, bf16[4,256,256]{2,1,0:T(8,128)(2,1)S(1)} %reorder.1.refs_0_.inv, ...), custom_call_target="tpu_custom_call" | custom-call | tf_op jit(solution)/shard_map/level0_level1/pallas_call | solution.py:299
  71.2 1.1 collective-permute-done.7.refs_4_
  73.5 2.2 %level2_rows160.1 = (bf16[16,4096]{1,0:T(8,128)(2,1)S(1)}, bf16[32,4096]{1,0:T(8,128)(2,1)S(1)}, bf16[112,4096]{1,0:T(8,128)(2,1)S(1)}, bf16[256,4096]{1,0:T(8,128)(2,1)S(1)}) custom-call(s32[640]{0:T(1024)S(1)} %concatenate.6.meta, bf16[4,256,256]{2,1,0:T(8,128)(2,1)S(1)} %reorder.1.refs_0_.inv, bf16[48,4096]{1,0:T(8,128)(2,1)S(1)} %get-tuple-element.55.refs_1_, ...), custom_call_target="tpu_custom_call" | custom-call | tf_op jit(solution)/shard_map/level2_rows160/pallas_call | solution.py:273
  75.9 1.9 %collective-permute-start.15 = (bf16[32,4096]{1,0:T(8,128)(2,1)S(1)}, bf16[32,4096]{1,0:T(8,128)(2,1)S(1)}, u32[]{:S(2)}, u32[]{:S(2)}) collective-permute-start(bf16[32,4096]{1,0:T(8,128)(2,1)S(1)} %get-tuple-element.66.refs_7_), channel_id=1, source_target_pairs={{0,2},{1,3},{2,0},{3,1},{4,6},{5,7},{6,4},{7,5},{8,10},{9,11},{10,... | collective-permute-start | bytes 786440 | tf_op jit(solution)/shard_map/ppermute | solution.py:28
  77.8 2.6 %collective-permute-done.11.refs_3_ = bf16[64,4096]{1,0:T(8,128)(2,1)S(1)} collective-permute-done((bf16[64,4096]{1,0:T(8,128)(2,1)S(1)}, bf16[64,4096]{1,0:T(8,128)(2,1)S(1)}, u32[]{:S(2)}, u32[]{:S(2)}) %collective-permute-start.11) | collective-permute-done | bytes 524320 | tf_op jit(solution)/shard_map/ppermute | solution.py:28
  80.4 1.2 level0_rows64.1.refs_2_
  81.7 1.2 level1_rows64.2
  83.5 2.9 %collective-permute-start.14 = (bf16[16,4096]{1,0:T(8,128)(2,1)S(1)}, bf16[16,4096]{1,0:T(8,128)(2,1)S(1)}, u32[]{:S(2)}, u32[]{:S(2)}) collective-permute-start(bf16[16,4096]{1,0:T(8,128)(2,1)S(1)} %collective-permute-done.10), channel_id=1, source_target_pairs={{0,4},{1,5},{2,6},{3,7},{4,0},{5,1},{6,2},{7,3},{8,12},{9,13},{10,... | collective-permute-start | bytes 393224 | tf_op jit(solution)/shard_map/ppermute | solution.py:28
  86.5 1.4 level2_rows144.1.refs_9_
  87.9 1.3 collective-permute-start.22
  89.2 3.3 %collective-permute-done.15.refs_8_ = bf16[32,4096]{1,0:T(8,128)(2,1)S(1)} collective-permute-done((bf16[32,4096]{1,0:T(8,128)(2,1)S(1)}, bf16[32,4096]{1,0:T(8,128)(2,1)S(1)}, u32[]{:S(2)}, u32[]{:S(2)}) %collective-permute-start.15) | collective-permute-done | bytes 262176 | tf_op jit(solution)/shard_map/ppermute | solution.py:28
  92.5 20.3 %collective-permute-done.14 = bf16[16,4096]{1,0:T(8,128)(2,1)S(1)} collective-permute-done((bf16[16,4096]{1,0:T(8,128)(2,1)S(1)}, bf16[16,4096]{1,0:T(8,128)(2,1)S(1)}, u32[]{:S(2)}, u32[]{:S(2)}) %collective-permute-start.14) | collective-permute-done | bytes 131104 | tf_op jit(solution)/shard_map/ppermute | solution.py:28
  112.8 1.2 level1_rows64.3.refs_2_
  114.8 8.1 %collective-permute-done.16.refs_4_ = bf16[32,4096]{1,0:T(8,128)(2,1)S(1)} collective-permute-done((bf16[32,4096]{1,0:T(8,128)(2,1)S(1)}, bf16[32,4096]{1,0:T(8,128)(2,1)S(1)}, u32[]{:S(2)}, u32[]{:S(2)}) %collective-permute-start.16) | collective-permute-done | bytes 262176 | tf_op jit(solution)/shard_map/ppermute | solution.py:28
  122.9 1.2 level2_rows64.1.own
  124.4 3.7 %collective-permute-done.22.refs_10_ = bf16[144,4096]{1,0:T(8,128)(2,1)S(1)} collective-permute-done((bf16[144,4096]{1,0:T(8,128)(2,1)S(1)}, bf16[144,4096]{1,0:T(8,128)(2,1)S(1)}, u32[]{:S(2)}, u32[]{:S(2)}) %collective-permute-start.22) | collective-permute-done | bytes 1179680 | tf_op jit(solution)/shard_map/ppermute | solution.py:28
  128.1 3.6 %level3_rows192.1 = (bf16[256,4096]{1,0:T(8,128)(2,1)}, bf16[256,4096]{1,0:T(8,128)(2,1)S(1)}) custom-call(s32[640]{0:T(1024)S(1)} %concatenate.6.meta, bf16[4,256,256]{2,1,0:T(8,128)(2,1)S(1)} %reorder.1.refs_0_.inv, bf16[16,4096]{1,0:T(8,128)(2,1)S(1)} %get-tuple-element.58.refs_1_, bf16[112,4096]{1,0:T(8,128)(2,1)S(1)} %get-tuple-element.59.refs_2_, ...), custom_call_target="tpu_custom_call" | custom-call | flops 49999998976 | tf_op jit(solution)/shard_map/level3_rows192/pallas_call | solution.py:273
  131.7 7.6 %collective-permute-done.24.other = bf16[64,4096]{1,0:T(8,128)(2,1)S(1)} collective-permute-done((bf16[64,4096]{1,0:T(8,128)(2,1)S(1)}, bf16[64,4096]{1,0:T(8,128)(2,1)S(1)}, u32[]{:S(2)}, u32[]{:S(2)}) %collective-permute-start.24) | collective-permute-done | bytes 524320 | tf_op jit(solution)/shard_map/ppermute | solution.py:28
  139.3 1.9 %last_rows.1 = bf16[256,4096]{1,0:T(8,128)(2,1)} custom-call(s32[640]{0:T(1024)S(1)} %concatenate.6.meta, bf16[4,256,256]{2,1,0:T(8,128)(2,1)S(1)} %reorder.1.refs_0_.inv, bf16[256,4096]{1,0:T(8,128)(2,1)S(1)} %get-tuple-element.75.panel, bf16[64,4096]{1,0:T(8,128)(2,1)S(1)} %level2_rows64.1.own, ...), custom_call_target="tpu_custom_call", output_to_operand_aliasing={{}: (5, {})} | custom-call | tf_op jit(solution)/shard_map/last_rows/pallas_call | solution.py:210
  (50 shorter events, 7.2 us)
Async XLA Ops:
  0.0 35.8 %copy-start.1 = (s32[4,2,32]{2,1,0:T(2,128)S(1)}, s32[4,2,32]{2,1,0:T(2,128)}, u32[]{:S(2)}) copy-start(s32[4,2,32]{2,1,0:T(2,128)} %param.7) | copy-start | bytes 3076
  0.0 35.9 %copy-start.3 = (s32[4,32]{1,0:T(4,128)S(1)}, s32[4,32]{1,0:T(4,128)}, u32[]{:S(2)}) copy-start(s32[4,32]{1,0:T(4,128)} %param.8) | copy-start | bytes 1540
  0.0 35.9 %copy-start.2 = (s32[4,32]{1,0:T(4,128)S(1)}, s32[4,32]{1,0:T(4,128)}, u32[]{:S(2)}) copy-start(s32[4,32]{1,0:T(4,128)} %param.9) | copy-start | bytes 1540
  1.2 38.4 %collective-permute-start.2 = (bf16[80,4096]{1,0:T(8,128)(2,1)S(1)}, bf16[80,4096]{1,0:T(8,128)(2,1)}, u32[]{:S(2)}, u32[]{:S(2)}) collective-permute-start(bf16[80,4096]{1,0:T(8,128)(2,1)S(1)} %slice.84.refs_1_), channel_id=1, source_target_pairs={{0,16},{8,24},{16,0},{24,8},{1,17},{9,25},{17,1},{25,9},{2,18},{10... | collective-permute-start | bytes 1966088 | tf_op jit(solution)/shard_map/ppermute | solution.py:28
  4.2 31.1 %collective-permute-start = (bf16[80,4096]{1,0:T(8,128)(2,1)S(1)}, bf16[80,4096]{1,0:T(8,128)(2,1)S(1)}, u32[]{:S(2)}, u32[]{:S(2)}) collective-permute-start(bf16[80,4096]{1,0:T(8,128)(2,1)S(1)} %slice.84.refs_1_), channel_id=1, source_target_pairs={{0,4},{1,5},{2,6},{3,7},{4,0},{5,1},{6,2},{7,3},{8,12},{9,13},{10,... | collective-permute-start | bytes 1966088 | tf_op jit(solution)/shard_map/ppermute | solution.py:28
  8.1 30.0 %collective-permute-start.4 = (bf16[64,4096]{1,0:T(8,128)(2,1)S(1)}, bf16[64,4096]{1,0:T(8,128)(2,1)}, u32[]{:S(2)}, u32[]{:S(2)}) collective-permute-start(bf16[64,4096]{1,0:T(8,128)(2,1)S(1)} %get-tuple-element.80.refs_5_), channel_id=1, source_target_pairs={{0,16},{8,24},{16,0},{24,8},{1,17},{9,25},{17,1},{25,9},{2,18},{10... | collective-permute-start | bytes 1572872 | tf_op jit(solution)/shard_map/ppermute | solution.py:28
  9.7 29.9 %collective-permute-start.3 = (bf16[48,4096]{1,0:T(8,128)(2,1)S(1)}, bf16[48,4096]{1,0:T(8,128)(2,1)}, u32[]{:S(2)}, u32[]{:S(2)}) collective-permute-start(bf16[48,4096]{1,0:T(8,128)(2,1)S(1)} %slice.85.refs_2_), channel_id=1, source_target_pairs={{0,16},{8,24},{16,0},{24,8},{1,17},{9,25},{17,1},{25,9},{2,18},{10... | collective-permute-start | bytes 1179656 | tf_op jit(solution)/shard_map/ppermute | solution.py:28
  35.3 19.7 %collective-permute-start.5 = (bf16[80,4096]{1,0:T(8,128)(2,1)S(1)}, bf16[80,4096]{1,0:T(8,128)(2,1)S(1)}, u32[]{:S(2)}, u32[]{:S(2)}) collective-permute-start(bf16[80,4096]{1,0:T(8,128)(2,1)S(1)} %collective-permute-done.refs_0_), channel_id=1, source_target_pairs={{0,16},{8,24},{16,0},{24,8},{1,17},{9,25},{17,1},{25,9},{2,18},{10... | collective-permute-start | bytes 1966088 | tf_op jit(solution)/shard_map/ppermute | solution.py:28
  35.8 19.2 %collective-permute-start.1 = (bf16[48,4096]{1,0:T(8,128)(2,1)S(1)}, bf16[48,4096]{1,0:T(8,128)(2,1)}, u32[]{:S(2)}, u32[]{:S(2)}) collective-permute-start(bf16[48,4096]{1,0:T(8,128)(2,1)S(1)} %slice.85.refs_2_), channel_id=1, source_target_pairs={{0,4},{1,5},{2,6},{3,7},{4,0},{5,1},{6,2},{7,3},{8,12},{9,13},{10,... | collective-permute-start | bytes 1179656 | tf_op jit(solution)/shard_map/ppermute | solution.py:28
  36.1 1.0 copy-start
  55.0 9.5 %collective-permute-start.6 = (bf16[48,4096]{1,0:T(8,128)(2,1)}, bf16[48,4096]{1,0:T(8,128)(2,1)S(1)}, u32[]{:S(2)}, u32[]{:S(2)}) collective-permute-start(bf16[48,4096]{1,0:T(8,128)(2,1)} %collective-permute-done.1.refs_1_), channel_id=1, source_target_pairs={{0,16},{8,24},{16,0},{24,8},{1,17},{9,25},{17,1},{25,9},{2,18},{10... | collective-permute-start | bytes 1179656 | tf_op jit(solution)/shard_map/ppermute | solution.py:28
  56.6 23.8 %collective-permute-start.11 = (bf16[64,4096]{1,0:T(8,128)(2,1)S(1)}, bf16[64,4096]{1,0:T(8,128)(2,1)S(1)}, u32[]{:S(2)}, u32[]{:S(2)}) collective-permute-start(bf16[64,4096]{1,0:T(8,128)(2,1)S(1)} %get-tuple-element.62.refs_2_), channel_id=1, source_target_pairs={{0,4},{1,5},{2,6},{3,7},{4,0},{5,1},{6,2},{7,3},{8,12},{9,13},{10,... | collective-permute-start | bytes 1572872 | tf_op jit(solution)/shard_map/ppermute | solution.py:28
  64.5 15.9 %collective-permute-start.12 = (bf16[64,4096]{1,0:T(8,128)(2,1)S(1)}, bf16[64,4096]{1,0:T(8,128)(2,1)S(1)}, u32[]{:S(2)}, u32[]{:S(2)}) collective-permute-start(bf16[64,4096]{1,0:T(8,128)(2,1)S(1)} %get-tuple-element.61.refs_2_), channel_id=1, source_target_pairs={{0,16},{8,24},{16,0},{24,8},{1,17},{9,25},{17,1},{25,9},{2,18},{10... | collective-permute-start | bytes 1572872 | tf_op jit(solution)/shard_map/ppermute | solution.py:28
  70.6 1.8 %collective-permute-start.7 = (bf16[48,4096]{1,0:T(8,128)(2,1)S(1)}, bf16[48,4096]{1,0:T(8,128)(2,1)S(1)}, u32[]{:S(2)}, u32[]{:S(2)}) collective-permute-start(bf16[48,4096]{1,0:T(8,128)(2,1)S(1)} %get-tuple-element.55.refs_1_), channel_id=1, source_target_pairs={{0,8},{8,0},{16,24},{24,16},{1,9},{9,1},{17,25},{25,17},{2,10},{10... | collective-permute-start | bytes 1179656 | tf_op jit(solution)/shard_map/ppermute | solution.py:28
  70.7 2.3 %collective-permute-start.8 = (bf16[48,4096]{1,0:T(8,128)(2,1)S(1)}, bf16[48,4096]{1,0:T(8,128)(2,1)S(1)}, u32[]{:S(2)}, u32[]{:S(2)}) collective-permute-start(bf16[48,4096]{1,0:T(8,128)(2,1)S(1)} %get-tuple-element.56.refs_2_), channel_id=1, source_target_pairs={{0,8},{8,0},{16,24},{24,16},{1,9},{9,1},{17,25},{25,17},{2,10},{10... | collective-permute-start | bytes 1179656 | tf_op jit(solution)/shard_map/ppermute | solution.py:28
  71.1 2.3 %collective-permute-start.9 = (bf16[48,4096]{1,0:T(8,128)(2,1)S(1)}, bf16[48,4096]{1,0:T(8,128)(2,1)S(1)}, u32[]{:S(2)}, u32[]{:S(2)}) collective-permute-start(bf16[48,4096]{1,0:T(8,128)(2,1)S(1)} %get-tuple-element.57.refs_3_), channel_id=1, source_target_pairs={{0,8},{8,0},{16,24},{24,16},{1,9},{9,1},{17,25},{25,17},{2,10},{10... | collective-permute-start | bytes 1179656 | tf_op jit(solution)/shard_map/ppermute | solution.py:28
  72.4 11.2 %collective-permute-start.19 = (bf16[80,4096]{1,0:T(8,128)(2,1)S(1)}, bf16[80,4096]{1,0:T(8,128)(2,1)S(1)}, u32[]{:S(2)}, u32[]{:S(2)}) collective-permute-start(bf16[80,4096]{1,0:T(8,128)(2,1)S(1)} %get-tuple-element.69.refs_2_), channel_id=1, source_target_pairs={{0,8},{8,0},{16,24},{24,16},{1,9},{9,1},{17,25},{25,17},{2,10},{10... | collective-permute-start | bytes 1966088 | tf_op jit(solution)/shard_map/ppermute | solution.py:28
  75.7 7.5 %collective-permute-start.10 = (bf16[16,4096]{1,0:T(8,128)(2,1)S(1)}, bf16[16,4096]{1,0:T(8,128)(2,1)S(1)}, u32[]{:S(2)}, u32[]{:S(2)}) collective-permute-start(bf16[16,4096]{1,0:T(8,128)(2,1)S(1)} %get-tuple-element.58.refs_1_), channel_id=1, source_target_pairs={{0,2},{1,3},{2,0},{3,1},{4,6},{5,7},{6,4},{7,5},{8,10},{9,11},{10,... | collective-permute-start | bytes 393224 | tf_op jit(solution)/shard_map/ppermute | solution.py:28
  75.9 16.6 %collective-permute-start.15 = (bf16[32,4096]{1,0:T(8,128)(2,1)S(1)}, bf16[32,4096]{1,0:T(8,128)(2,1)S(1)}, u32[]{:S(2)}, u32[]{:S(2)}) collective-permute-start(bf16[32,4096]{1,0:T(8,128)(2,1)S(1)} %get-tuple-element.66.refs_7_), channel_id=1, source_target_pairs={{0,2},{1,3},{2,0},{3,1},{4,6},{5,7},{6,4},{7,5},{8,10},{9,11},{10,... | collective-permute-start | bytes 786440 | tf_op jit(solution)/shard_map/ppermute | solution.py:28
  81.6 31.1 %collective-permute-start.13 = (bf16[64,4096]{1,0:T(8,128)(2,1)S(1)}, bf16[64,4096]{1,0:T(8,128)(2,1)S(1)}, u32[]{:S(2)}, u32[]{:S(2)}) collective-permute-start(bf16[64,4096]{1,0:T(8,128)(2,1)S(1)} %level0_rows64.1.refs_2_), channel_id=1, source_target_pairs={{0,4},{1,5},{2,6},{3,7},{4,0},{5,1},{6,2},{7,3},{8,12},{9,13},{10,... | collective-permute-start | bytes 1572872 | tf_op jit(solution)/shard_map/ppermute | solution.py:28
  83.0 3.5 %collective-permute-start.20 = (bf16[32,4096]{1,0:T(8,128)(2,1)S(1)}, bf16[32,4096]{1,0:T(8,128)(2,1)S(1)}, u32[]{:S(2)}, u32[]{:S(2)}) collective-permute-start(bf16[32,4096]{1,0:T(8,128)(2,1)S(1)} %get-tuple-element.73.refs_4_), channel_id=1, source_target_pairs={{0,8},{8,0},{16,24},{24,16},{1,9},{9,1},{17,25},{25,17},{2,10},{10... | collective-permute-start | bytes 786440 | tf_op jit(solution)/shard_map/ppermute | solution.py:28
  83.2 3.3 %collective-permute-start.21 = (bf16[32,4096]{1,0:T(8,128)(2,1)S(1)}, bf16[32,4096]{1,0:T(8,128)(2,1)S(1)}, u32[]{:S(2)}, u32[]{:S(2)}) collective-permute-start(bf16[32,4096]{1,0:T(8,128)(2,1)S(1)} %get-tuple-element.74.refs_6_), channel_id=1, source_target_pairs={{0,8},{8,0},{16,24},{24,16},{1,9},{9,1},{17,25},{25,17},{2,10},{10... | collective-permute-start | bytes 786440 | tf_op jit(solution)/shard_map/ppermute | solution.py:28
  83.5 29.2 %collective-permute-start.14 = (bf16[16,4096]{1,0:T(8,128)(2,1)S(1)}, bf16[16,4096]{1,0:T(8,128)(2,1)S(1)}, u32[]{:S(2)}, u32[]{:S(2)}) collective-permute-start(bf16[16,4096]{1,0:T(8,128)(2,1)S(1)} %collective-permute-done.10), channel_id=1, source_target_pairs={{0,4},{1,5},{2,6},{3,7},{4,0},{5,1},{6,2},{7,3},{8,12},{9,13},{10,... | collective-permute-start | bytes 393224 | tf_op jit(solution)/shard_map/ppermute | solution.py:28
  87.9 40.2 %collective-permute-start.22 = (bf16[144,4096]{1,0:T(8,128)(2,1)S(1)}, bf16[144,4096]{1,0:T(8,128)(2,1)S(1)}, u32[]{:S(2)}, u32[]{:S(2)}) collective-permute-start(bf16[144,4096]{1,0:T(8,128)(2,1)S(1)} %level2_rows144.1.refs_9_), channel_id=1, source_target_pairs={{0,2},{1,3},{2,0},{3,1},{4,6},{5,7},{6,4},{7,5},{8,10},{9,11},{10,... | collective-permute-start | bytes 3538952 | tf_op jit(solution)/shard_map/ppermute | solution.py:28
  114.0 8.9 %collective-permute-start.23 = (bf16[64,4096]{1,0:T(8,128)(2,1)S(1)}, bf16[64,4096]{1,0:T(8,128)(2,1)S(1)}, u32[]{:S(2)}, u32[]{:S(2)}) collective-permute-start(bf16[64,4096]{1,0:T(8,128)(2,1)S(1)} %level1_rows64.3.refs_2_), channel_id=1, source_target_pairs={{0,8},{8,0},{16,24},{24,16},{1,9},{9,1},{17,25},{25,17},{2,10},{10... | collective-permute-start | bytes 1572872 | tf_op jit(solution)/shard_map/ppermute | solution.py:28
  114.1 8.8 %collective-permute-start.16 = (bf16[32,4096]{1,0:T(8,128)(2,1)S(1)}, bf16[32,4096]{1,0:T(8,128)(2,1)S(1)}, u32[]{:S(2)}, u32[]{:S(2)}) collective-permute-start(bf16[32,4096]{1,0:T(8,128)(2,1)S(1)} %constant_dynamic-update-slice_fusion.refs_3_), channel_id=1, source_target_pairs={{0,16},{8,24},{16,0},{24,8},{1,17},{9,25},{17,1},{25,9},{2,18},{10... | collective-permute-start | bytes 786440 | tf_op jit(solution)/shard_map/ppermute | solution.py:28
  114.6 9.6 %collective-permute-start.17 = (bf16[32,4096]{1,0:T(8,128)(2,1)S(1)}, bf16[32,4096]{1,0:T(8,128)(2,1)S(1)}, u32[]{:S(2)}, u32[]{:S(2)}) collective-permute-start(bf16[32,4096]{1,0:T(8,128)(2,1)S(1)} %constant_dynamic-update-slice_fusion.refs_3_), channel_id=1, source_target_pairs={{0,8},{8,0},{16,24},{24,16},{1,9},{9,1},{17,25},{25,17},{2,10},{10... | collective-permute-start | bytes 786440 | tf_op jit(solution)/shard_map/ppermute | solution.py:28
  122.9 1.5 %collective-permute-start.18 = (bf16[32,4096]{1,0:T(8,128)(2,1)S(1)}, bf16[32,4096]{1,0:T(8,128)(2,1)S(1)}, u32[]{:S(2)}, u32[]{:S(2)}) collective-permute-start(bf16[32,4096]{1,0:T(8,128)(2,1)S(1)} %collective-permute-done.16.refs_4_), channel_id=1, source_target_pairs={{0,8},{8,0},{16,24},{24,16},{1,9},{9,1},{17,25},{25,17},{2,10},{10... | collective-permute-start | bytes 786440 | tf_op jit(solution)/shard_map/ppermute | solution.py:28
  124.1 15.2 %collective-permute-start.24 = (bf16[64,4096]{1,0:T(8,128)(2,1)S(1)}, bf16[64,4096]{1,0:T(8,128)(2,1)S(1)}, u32[]{:S(2)}, u32[]{:S(2)}) collective-permute-start(bf16[64,4096]{1,0:T(8,128)(2,1)S(1)} %level2_rows64.1.own), channel_id=1, source_target_pairs={{0,2},{1,3},{2,0},{3,1},{4,6},{5,7},{6,4},{7,5},{8,10},{9,11},{10,... | collective-permute-start | bytes 1572872 | tf_op jit(solution)/shard_map/ppermute | solution.py:28

commit v15 on v14

--- a/solution.py
+++ b/solution.py
@@ -88,6 +88,28 @@
     if top is not None:
         a, b = top
         half = sum(count for _, _, count in a)
+    pivots = [meta[base + 3 * blocks + i] for i in range(inv.shape[1] // BLOCK)]
+
+    def pivot_columns(job, p):
+        source, start, rows = job
+        own, other = (a, b) if source == "top" else pairs[source]
+        if source == "top" and start >= half:
+            own, other, start = b, a, start - half
+        parts = []
+        for low, count in segments(own, other):
+            first, last = max(low, start), min(low + count, start + rows)
+            if first < last:
+                size = last - first
+                parts.append(read(own, first, size, p) + read(other, first, size, order(p)))
+        return jnp.concatenate(parts, axis=0)
+
+    coupling = jnp.concatenate(
+        [jnp.concatenate([pivot_columns(job, p) for p in pivots], axis=1).astype(BF16) for job in jobs],
+        axis=0,
+    )
+    weights = jnp.dot(coupling, inv[level], preferred_element_type=F32).astype(BF16)
+
+    if top is not None:
         kept = [(start, start + rows) for source, start, rows in jobs if source == "top"]
 
         def keep(value, first, rows, j):
@@ -117,13 +139,6 @@
             return merged[pl.ds(start, rows), at(j)]
         a, b = pairs[source]
         return read(a, start, rows, j) + read(b, start, rows, order(j))
-
-    pivots = [meta[base + 3 * blocks + i] for i in range(inv.shape[1] // BLOCK)]
-    coupling = jnp.concatenate(
-        [jnp.concatenate([columns(job, p) for p in pivots], axis=1).astype(BF16) for job in jobs],
-        axis=0,
-    )
-    weights = jnp.dot(coupling, inv[level], preferred_element_type=F32).astype(BF16)
 
     def finish_tile(t, carry):
         lanes = pl.ds(t * TILE, TILE)

time: 142 us -> 142 us (level)
  no operation moved by 1% of the time
where the time goes in v15:
time: 142 us; the launch traced here: 141 us
  waiting for transfers between devices  93.7 us (66%)
  Pallas kernels  22.4 us (16%)
  starting transfers between devices  20.2 us (14%)
  local copies, waits for them, and re-layouts  4.65 us (3%)
    ppermute x25, waiting for transfers between devices, trade(): lax.ppermute(block, axis, [(i, i ^ flip) for i in range(lax.axis_size(axi...  93.7 us
    ppermute x25, starting transfers between devices, trade(): lax.ppermute(block, axis, [(i, i ^ flip) for i in range(lax.axis_size(axi...  20.2 us
    pallas_call x8, Pallas kernels, run_level(): pl.pallas_call(kernel, grid=(1,) if part is not None else (), out_shape=s...  15.3 us
    pallas_call x1, Pallas kernels, run_two_levels(): pl.pallas_call(kernel, out_shape=[jax.ShapeDtypeStruct((n, width), BF16)...  4.3 us
  transfers between devices with their start and end apart: 25, of which 15 were waited for; matrix products, arithmetic and copies ran while one was open for 2% of the time, Pallas kernels for 15%

profile of v15, /device:TPU:0, one launch (start us, length us, event | category | flops | bytes accessed | tf_op | source)
XLA Modules:
  0.0 141.2 jit_solution(16664299230388743643)
XLA Ops:
  0.0 1.2 slice.84.refs_1_
  1.2 3.0 %collective-permute-start.2 = (bf16[80,4096]{1,0:T(8,128)(2,1)S(1)}, bf16[80,4096]{1,0:T(8,128)(2,1)}, u32[]{:S(2)}, u32[]{:S(2)}) collective-permute-start(bf16[80,4096]{1,0:T(8,128)(2,1)S(1)} %slice.84.refs_1_), channel_id=1, source_target_pairs={{0,16},{8,24},{16,0},{24,8},{1,17},{9,25},{17,1},{25,9},{2,18},{10... | collective-permute-start | bytes 1966088 | tf_op jit(solution)/shard_map/ppermute | solution.py:28
  4.2 2.6 %collective-permute-start = (bf16[80,4096]{1,0:T(8,128)(2,1)S(1)}, bf16[80,4096]{1,0:T(8,128)(2,1)S(1)}, u32[]{:S(2)}, u32[]{:S(2)}) collective-permute-start(bf16[80,4096]{1,0:T(8,128)(2,1)S(1)} %slice.84.refs_1_), channel_id=1, source_target_pairs={{0,4},{1,5},{2,6},{3,7},{4,0},{5,1},{6,2},{7,3},{8,12},{9,13},{10,... | collective-permute-start | bytes 1966088 | tf_op jit(solution)/shard_map/ppermute | solution.py:28
  6.8 1.3 fusion.8
  9.7 1.6 %collective-permute-start.3 = (bf16[48,4096]{1,0:T(8,128)(2,1)S(1)}, bf16[48,4096]{1,0:T(8,128)(2,1)}, u32[]{:S(2)}, u32[]{:S(2)}) collective-permute-start(bf16[48,4096]{1,0:T(8,128)(2,1)S(1)} %slice.85.refs_2_), channel_id=1, source_target_pairs={{0,16},{8,24},{16,0},{24,8},{1,17},{9,25},{17,1},{25,9},{2,18},{10... | collective-permute-start | bytes 1179656 | tf_op jit(solution)/shard_map/ppermute | solution.py:28
  11.3 24.1 %collective-permute-done.refs_0_ = bf16[80,4096]{1,0:T(8,128)(2,1)S(1)} collective-permute-done((bf16[80,4096]{1,0:T(8,128)(2,1)S(1)}, bf16[80,4096]{1,0:T(8,128)(2,1)S(1)}, u32[]{:S(2)}, u32[]{:S(2)}) %collective-permute-start) | collective-permute-done | bytes 655392 | tf_op jit(solution)/shard_map/ppermute | solution.py:28
  36.1 1.0 copy-done
  38.1 1.4 %collective-permute-done.3.refs_4_ = bf16[48,4096]{1,0:T(8,128)(2,1)} collective-permute-done((bf16[48,4096]{1,0:T(8,128)(2,1)S(1)}, bf16[48,4096]{1,0:T(8,128)(2,1)}, u32[]{:S(2)}, u32[]{:S(2)}) %collective-permute-start.3) | collective-permute-done | bytes 393248 | tf_op jit(solution)/shard_map/ppermute | solution.py:28
  39.5 3.2 %level0_rows256.1 = (bf16[128,4096]{1,0:T(8,128)(2,1)S(1)}, bf16[64,4096]{1,0:T(8,128)(2,1)S(1)}, bf16[64,4096]{1,0:T(8,128)(2,1)S(1)}, bf16[256,4096]{1,0:T(8,128)(2,1)S(1)}) custom-call(s32[640]{0:T(1024)S(1)} %concatenate.6.meta, bf16[4,256,256]{2,1,0:T(8,128)(2,1)S(1)} %reorder.1.refs_0_.inv, bf16[80,4096]{1,0:T(8,128)(2,1)S(1)} %slice.84.refs_1_, ...), custom_call_target="tpu_custom_call" | custom-call | tf_op jit(solution)/shard_map/level0_rows256/pallas_call | solution.py:288
  42.7 12.3 %collective-permute-done.1.refs_1_ = bf16[48,4096]{1,0:T(8,128)(2,1)} collective-permute-done((bf16[48,4096]{1,0:T(8,128)(2,1)S(1)}, bf16[48,4096]{1,0:T(8,128)(2,1)}, u32[]{:S(2)}, u32[]{:S(2)}) %collective-permute-start.1) | collective-permute-done | bytes 393248 | tf_op jit(solution)/shard_map/ppermute | solution.py:28
  55.0 1.5 %collective-permute-start.6 = (bf16[48,4096]{1,0:T(8,128)(2,1)}, bf16[48,4096]{1,0:T(8,128)(2,1)S(1)}, u32[]{:S(2)}, u32[]{:S(2)}) collective-permute-start(bf16[48,4096]{1,0:T(8,128)(2,1)} %collective-permute-done.1.refs_1_), channel_id=1, source_target_pairs={{0,16},{8,24},{16,0},{24,8},{1,17},{9,25},{17,1},{25,9},{2,18},{10... | collective-permute-start | bytes 1179656 | tf_op jit(solution)/shard_map/ppermute | solution.py:28
  57.0 7.6 %collective-permute-done.6.refs_3_ = bf16[48,4096]{1,0:T(8,128)(2,1)S(1)} collective-permute-done((bf16[48,4096]{1,0:T(8,128)(2,1)}, bf16[48,4096]{1,0:T(8,128)(2,1)S(1)}, u32[]{:S(2)}, u32[]{:S(2)}) %collective-permute-start.6) | collective-permute-done | bytes 393248 | tf_op jit(solution)/shard_map/ppermute | solution.py:28
  64.5 1.5 %collective-permute-start.12 = (bf16[64,4096]{1,0:T(8,128)(2,1)S(1)}, bf16[64,4096]{1,0:T(8,128)(2,1)S(1)}, u32[]{:S(2)}, u32[]{:S(2)}) collective-permute-start(bf16[64,4096]{1,0:T(8,128)(2,1)S(1)} %get-tuple-element.61.refs_2_), channel_id=1, source_target_pairs={{0,16},{8,24},{16,0},{24,8},{1,17},{9,25},{17,1},{25,9},{2,18},{10... | collective-permute-start | bytes 1572872 | tf_op jit(solution)/shard_map/ppermute | solution.py:28
  66.1 4.3 %level0_level1.1 = (bf16[48,4096]{1,0:T(8,128)(2,1)S(1)}, bf16[48,4096]{1,0:T(8,128)(2,1)S(1)}, bf16[48,4096]{1,0:T(8,128)(2,1)S(1)}, bf16[80,4096]{1,0:T(8,128)(2,1)S(1)}, bf16[256,4096]{1,0:T(8,128)(2,1)S(1)}) custom-call(s32[640]{0:T(1024)S(1)} %concatenate.6.meta, bf16[4,256,256]{2,1,0:T(8,128)(2,1)S(1)} %reorder.1.refs_0_.inv, ...), custom_call_target="tpu_custom_call" | custom-call | tf_op jit(solution)/shard_map/level0_level1/pallas_call | solution.py:314
  71.0 1.1 collective-permute-done.7.refs_4_
  73.3 2.2 %level2_rows160.1 = (bf16[16,4096]{1,0:T(8,128)(2,1)S(1)}, bf16[32,4096]{1,0:T(8,128)(2,1)S(1)}, bf16[112,4096]{1,0:T(8,128)(2,1)S(1)}, bf16[256,4096]{1,0:T(8,128)(2,1)S(1)}) custom-call(s32[640]{0:T(1024)S(1)} %concatenate.6.meta, bf16[4,256,256]{2,1,0:T(8,128)(2,1)S(1)} %reorder.1.refs_0_.inv, bf16[48,4096]{1,0:T(8,128)(2,1)S(1)} %get-tuple-element.55.refs_1_, ...), custom_call_target="tpu_custom_call" | custom-call | tf_op jit(solution)/shard_map/level2_rows160/pallas_call | solution.py:288
  75.7 1.9 %collective-permute-start.15 = (bf16[32,4096]{1,0:T(8,128)(2,1)S(1)}, bf16[32,4096]{1,0:T(8,128)(2,1)S(1)}, u32[]{:S(2)}, u32[]{:S(2)}) collective-permute-start(bf16[32,4096]{1,0:T(8,128)(2,1)S(1)} %get-tuple-element.66.refs_7_), channel_id=1, source_target_pairs={{0,2},{1,3},{2,0},{3,1},{4,6},{5,7},{6,4},{7,5},{8,10},{9,11},{10,... | collective-permute-start | bytes 786440 | tf_op jit(solution)/shard_map/ppermute | solution.py:28
  77.6 2.8 %collective-permute-done.11.refs_3_ = bf16[64,4096]{1,0:T(8,128)(2,1)S(1)} collective-permute-done((bf16[64,4096]{1,0:T(8,128)(2,1)S(1)}, bf16[64,4096]{1,0:T(8,128)(2,1)S(1)}, u32[]{:S(2)}, u32[]{:S(2)}) %collective-permute-start.11) | collective-permute-done | bytes 524320 | tf_op jit(solution)/shard_map/ppermute | solution.py:28
  80.4 1.2 level0_rows64.1.refs_2_
  81.7 1.2 level1_rows64.2
  83.6 2.9 %collective-permute-start.14 = (bf16[16,4096]{1,0:T(8,128)(2,1)S(1)}, bf16[16,4096]{1,0:T(8,128)(2,1)S(1)}, u32[]{:S(2)}, u32[]{:S(2)}) collective-permute-start(bf16[16,4096]{1,0:T(8,128)(2,1)S(1)} %collective-permute-done.10), channel_id=1, source_target_pairs={{0,4},{1,5},{2,6},{3,7},{4,0},{5,1},{6,2},{7,3},{8,12},{9,13},{10,... | collective-permute-start | bytes 393224 | tf_op jit(solution)/shard_map/ppermute | solution.py:28
  86.5 1.4 %level2_rows144.1.refs_9_ = bf16[144,4096]{1,0:T(8,128)(2,1)S(1)} custom-call(s32[640]{0:T(1024)S(1)} %concatenate.6.meta, bf16[4,256,256]{2,1,0:T(8,128)(2,1)S(1)} %reorder.1.refs_0_.inv, bf16[256,4096]{1,0:T(8,128)(2,1)S(1)} %get-tuple-element.68.refs_1_, bf16[80,4096]{1,0:T(8,128)(2,1)S(1)} %get-tuple-element.69.refs_2_, ...), custom_call_target="tpu_custom_call" | custom-call | tf_op jit(solution)/shard_map/level2_rows144/pallas_call | solution.py:288
  87.9 1.3 collective-permute-start.22
  89.2 3.1 %collective-permute-done.15.refs_8_ = bf16[32,4096]{1,0:T(8,128)(2,1)S(1)} collective-permute-done((bf16[32,4096]{1,0:T(8,128)(2,1)S(1)}, bf16[32,4096]{1,0:T(8,128)(2,1)S(1)}, u32[]{:S(2)}, u32[]{:S(2)}) %collective-permute-start.15) | collective-permute-done | bytes 262176 | tf_op jit(solution)/shard_map/ppermute | solution.py:28
  92.3 20.5 %collective-permute-done.14 = bf16[16,4096]{1,0:T(8,128)(2,1)S(1)} collective-permute-done((bf16[16,4096]{1,0:T(8,128)(2,1)S(1)}, bf16[16,4096]{1,0:T(8,128)(2,1)S(1)}, u32[]{:S(2)}, u32[]{:S(2)}) %collective-permute-start.14) | collective-permute-done | bytes 131104 | tf_op jit(solution)/shard_map/ppermute | solution.py:28
  112.8 1.2 level1_rows64.3.refs_2_
  114.8 8.1 %collective-permute-done.16.refs_4_ = bf16[32,4096]{1,0:T(8,128)(2,1)S(1)} collective-permute-done((bf16[32,4096]{1,0:T(8,128)(2,1)S(1)}, bf16[32,4096]{1,0:T(8,128)(2,1)S(1)}, u32[]{:S(2)}, u32[]{:S(2)}) %collective-permute-start.16) | collective-permute-done | bytes 262176 | tf_op jit(solution)/shard_map/ppermute | solution.py:28
  122.9 1.2 level2_rows64.1.own
  124.4 3.7 %collective-permute-done.22.refs_10_ = bf16[144,4096]{1,0:T(8,128)(2,1)S(1)} collective-permute-done((bf16[144,4096]{1,0:T(8,128)(2,1)S(1)}, bf16[144,4096]{1,0:T(8,128)(2,1)S(1)}, u32[]{:S(2)}, u32[]{:S(2)}) %collective-permute-start.22) | collective-permute-done | bytes 1179680 | tf_op jit(solution)/shard_map/ppermute | solution.py:28
  128.1 3.5 %level3_rows192.1 = (bf16[256,4096]{1,0:T(8,128)(2,1)}, bf16[256,4096]{1,0:T(8,128)(2,1)S(1)}) custom-call(s32[640]{0:T(1024)S(1)} %concatenate.6.meta, bf16[4,256,256]{2,1,0:T(8,128)(2,1)S(1)} %reorder.1.refs_0_.inv, bf16[16,4096]{1,0:T(8,128)(2,1)S(1)} %get-tuple-element.58.refs_1_, bf16[112,4096]{1,0:T(8,128)(2,1)S(1)} %get-tuple-element.59.refs_2_, ...), custom_call_target="tpu_custom_call" | custom-call | flops 49999998976 | tf_op jit(solution)/shard_map/level3_rows192/pallas_call | solution.py:288
  131.7 7.6 %collective-permute-done.24.other = bf16[64,4096]{1,0:T(8,128)(2,1)S(1)} collective-permute-done((bf16[64,4096]{1,0:T(8,128)(2,1)S(1)}, bf16[64,4096]{1,0:T(8,128)(2,1)S(1)}, u32[]{:S(2)}, u32[]{:S(2)}) %collective-permute-start.24) | collective-permute-done | bytes 524320 | tf_op jit(solution)/shard_map/ppermute | solution.py:28
  139.3 1.9 %last_rows.1 = bf16[256,4096]{1,0:T(8,128)(2,1)} custom-call(s32[640]{0:T(1024)S(1)} %concatenate.6.meta, bf16[4,256,256]{2,1,0:T(8,128)(2,1)S(1)} %reorder.1.refs_0_.inv, bf16[256,4096]{1,0:T(8,128)(2,1)S(1)} %get-tuple-element.75.panel, bf16[64,4096]{1,0:T(8,128)(2,1)S(1)} %level2_rows64.1.own, ...), custom_call_target="tpu_custom_call", output_to_operand_aliasing={{}: (5, {})} | custom-call | tf_op jit(solution)/shard_map/last_rows/pallas_call | solution.py:225
  (50 shorter events, 7.2 us)
Async XLA Ops:
  0.0 35.8 %copy-start.1 = (s32[4,2,32]{2,1,0:T(2,128)S(1)}, s32[4,2,32]{2,1,0:T(2,128)}, u32[]{:S(2)}) copy-start(s32[4,2,32]{2,1,0:T(2,128)} %param.7) | copy-start | bytes 3076
  0.0 35.9 %copy-start.3 = (s32[4,32]{1,0:T(4,128)S(1)}, s32[4,32]{1,0:T(4,128)}, u32[]{:S(2)}) copy-start(s32[4,32]{1,0:T(4,128)} %param.8) | copy-start | bytes 1540
  0.0 35.9 %copy-start.2 = (s32[4,32]{1,0:T(4,128)S(1)}, s32[4,32]{1,0:T(4,128)}, u32[]{:S(2)}) copy-start(s32[4,32]{1,0:T(4,128)} %param.9) | copy-start | bytes 1540
  1.2 38.4 %collective-permute-start.2 = (bf16[80,4096]{1,0:T(8,128)(2,1)S(1)}, bf16[80,4096]{1,0:T(8,128)(2,1)}, u32[]{:S(2)}, u32[]{:S(2)}) collective-permute-start(bf16[80,4096]{1,0:T(8,128)(2,1)S(1)} %slice.84.refs_1_), channel_id=1, source_target_pairs={{0,16},{8,24},{16,0},{24,8},{1,17},{9,25},{17,1},{25,9},{2,18},{10... | collective-permute-start | bytes 1966088 | tf_op jit(solution)/shard_map/ppermute | solution.py:28
  4.2 31.1 %collective-permute-start = (bf16[80,4096]{1,0:T(8,128)(2,1)S(1)}, bf16[80,4096]{1,0:T(8,128)(2,1)S(1)}, u32[]{:S(2)}, u32[]{:S(2)}) collective-permute-start(bf16[80,4096]{1,0:T(8,128)(2,1)S(1)} %slice.84.refs_1_), channel_id=1, source_target_pairs={{0,4},{1,5},{2,6},{3,7},{4,0},{5,1},{6,2},{7,3},{8,12},{9,13},{10,... | collective-permute-start | bytes 1966088 | tf_op jit(solution)/shard_map/ppermute | solution.py:28
  8.1 30.0 %collective-permute-start.4 = (bf16[64,4096]{1,0:T(8,128)(2,1)S(1)}, bf16[64,4096]{1,0:T(8,128)(2,1)}, u32[]{:S(2)}, u32[]{:S(2)}) collective-permute-start(bf16[64,4096]{1,0:T(8,128)(2,1)S(1)} %get-tuple-element.80.refs_5_), channel_id=1, source_target_pairs={{0,16},{8,24},{16,0},{24,8},{1,17},{9,25},{17,1},{25,9},{2,18},{10... | collective-permute-start | bytes 1572872 | tf_op jit(solution)/shard_map/ppermute | solution.py:28
  9.7 29.9 %collective-permute-start.3 = (bf16[48,4096]{1,0:T(8,128)(2,1)S(1)}, bf16[48,4096]{1,0:T(8,128)(2,1)}, u32[]{:S(2)}, u32[]{:S(2)}) collective-permute-start(bf16[48,4096]{1,0:T(8,128)(2,1)S(1)} %slice.85.refs_2_), channel_id=1, source_target_pairs={{0,16},{8,24},{16,0},{24,8},{1,17},{9,25},{17,1},{25,9},{2,18},{10... | collective-permute-start | bytes 1179656 | tf_op jit(solution)/shard_map/ppermute | solution.py:28
  35.3 19.7 %collective-permute-start.5 = (bf16[80,4096]{1,0:T(8,128)(2,1)S(1)}, bf16[80,4096]{1,0:T(8,128)(2,1)S(1)}, u32[]{:S(2)}, u32[]{:S(2)}) collective-permute-start(bf16[80,4096]{1,0:T(8,128)(2,1)S(1)} %collective-permute-done.refs_0_), channel_id=1, source_target_pairs={{0,16},{8,24},{16,0},{24,8},{1,17},{9,25},{17,1},{25,9},{2,18},{10... | collective-permute-start | bytes 1966088 | tf_op jit(solution)/shard_map/ppermute | solution.py:28
  35.8 19.2 %collective-permute-start.1 = (bf16[48,4096]{1,0:T(8,128)(2,1)S(1)}, bf16[48,4096]{1,0:T(8,128)(2,1)}, u32[]{:S(2)}, u32[]{:S(2)}) collective-permute-start(bf16[48,4096]{1,0:T(8,128)(2,1)S(1)} %slice.85.refs_2_), channel_id=1, source_target_pairs={{0,4},{1,5},{2,6},{3,7},{4,0},{5,1},{6,2},{7,3},{8,12},{9,13},{10,... | collective-permute-start | bytes 1179656 | tf_op jit(solution)/shard_map/ppermute | solution.py:28
  36.1 1.0 copy-start
  55.0 9.5 %collective-permute-start.6 = (bf16[48,4096]{1,0:T(8,128)(2,1)}, bf16[48,4096]{1,0:T(8,128)(2,1)S(1)}, u32[]{:S(2)}, u32[]{:S(2)}) collective-permute-start(bf16[48,4096]{1,0:T(8,128)(2,1)} %collective-permute-done.1.refs_1_), channel_id=1, source_target_pairs={{0,16},{8,24},{16,0},{24,8},{1,17},{9,25},{17,1},{25,9},{2,18},{10... | collective-permute-start | bytes 1179656 | tf_op jit(solution)/shard_map/ppermute | solution.py:28
  56.6 23.8 %collective-permute-start.11 = (bf16[64,4096]{1,0:T(8,128)(2,1)S(1)}, bf16[64,4096]{1,0:T(8,128)(2,1)S(1)}, u32[]{:S(2)}, u32[]{:S(2)}) collective-permute-start(bf16[64,4096]{1,0:T(8,128)(2,1)S(1)} %get-tuple-element.62.refs_2_), channel_id=1, source_target_pairs={{0,4},{1,5},{2,6},{3,7},{4,0},{5,1},{6,2},{7,3},{8,12},{9,13},{10,... | collective-permute-start | bytes 1572872 | tf_op jit(solution)/shard_map/ppermute | solution.py:28
  64.5 15.9 %collective-permute-start.12 = (bf16[64,4096]{1,0:T(8,128)(2,1)S(1)}, bf16[64,4096]{1,0:T(8,128)(2,1)S(1)}, u32[]{:S(2)}, u32[]{:S(2)}) collective-permute-start(bf16[64,4096]{1,0:T(8,128)(2,1)S(1)} %get-tuple-element.61.refs_2_), channel_id=1, source_target_pairs={{0,16},{8,24},{16,0},{24,8},{1,17},{9,25},{17,1},{25,9},{2,18},{10... | collective-permute-start | bytes 1572872 | tf_op jit(solution)/shard_map/ppermute | solution.py:28
  70.4 1.8 %collective-permute-start.7 = (bf16[48,4096]{1,0:T(8,128)(2,1)S(1)}, bf16[48,4096]{1,0:T(8,128)(2,1)S(1)}, u32[]{:S(2)}, u32[]{:S(2)}) collective-permute-start(bf16[48,4096]{1,0:T(8,128)(2,1)S(1)} %get-tuple-element.55.refs_1_), channel_id=1, source_target_pairs={{0,8},{8,0},{16,24},{24,16},{1,9},{9,1},{17,25},{25,17},{2,10},{10... | collective-permute-start | bytes 1179656 | tf_op jit(solution)/shard_map/ppermute | solution.py:28
  70.5 2.3 %collective-permute-start.8 = (bf16[48,4096]{1,0:T(8,128)(2,1)S(1)}, bf16[48,4096]{1,0:T(8,128)(2,1)S(1)}, u32[]{:S(2)}, u32[]{:S(2)}) collective-permute-start(bf16[48,4096]{1,0:T(8,128)(2,1)S(1)} %get-tuple-element.56.refs_2_), channel_id=1, source_target_pairs={{0,8},{8,0},{16,24},{24,16},{1,9},{9,1},{17,25},{25,17},{2,10},{10... | collective-permute-start | bytes 1179656 | tf_op jit(solution)/shard_map/ppermute | solution.py:28
  71.0 2.3 %collective-permute-start.9 = (bf16[48,4096]{1,0:T(8,128)(2,1)S(1)}, bf16[48,4096]{1,0:T(8,128)(2,1)S(1)}, u32[]{:S(2)}, u32[]{:S(2)}) collective-permute-start(bf16[48,4096]{1,0:T(8,128)(2,1)S(1)} %get-tuple-element.57.refs_3_), channel_id=1, source_target_pairs={{0,8},{8,0},{16,24},{24,16},{1,9},{9,1},{17,25},{25,17},{2,10},{10... | collective-permute-start | bytes 1179656 | tf_op jit(solution)/shard_map/ppermute | solution.py:28
  72.2 11.4 %collective-permute-start.19 = (bf16[80,4096]{1,0:T(8,128)(2,1)S(1)}, bf16[80,4096]{1,0:T(8,128)(2,1)S(1)}, u32[]{:S(2)}, u32[]{:S(2)}) collective-permute-start(bf16[80,4096]{1,0:T(8,128)(2,1)S(1)} %get-tuple-element.69.refs_2_), channel_id=1, source_target_pairs={{0,8},{8,0},{16,24},{24,16},{1,9},{9,1},{17,25},{25,17},{2,10},{10... | collective-permute-start | bytes 1966088 | tf_op jit(solution)/shard_map/ppermute | solution.py:28
  75.5 7.7 %collective-permute-start.10 = (bf16[16,4096]{1,0:T(8,128)(2,1)S(1)}, bf16[16,4096]{1,0:T(8,128)(2,1)S(1)}, u32[]{:S(2)}, u32[]{:S(2)}) collective-permute-start(bf16[16,4096]{1,0:T(8,128)(2,1)S(1)} %get-tuple-element.58.refs_1_), channel_id=1, source_target_pairs={{0,2},{1,3},{2,0},{3,1},{4,6},{5,7},{6,4},{7,5},{8,10},{9,11},{10,... | collective-permute-start | bytes 393224 | tf_op jit(solution)/shard_map/ppermute | solution.py:28
  75.7 16.6 %collective-permute-start.15 = (bf16[32,4096]{1,0:T(8,128)(2,1)S(1)}, bf16[32,4096]{1,0:T(8,128)(2,1)S(1)}, u32[]{:S(2)}, u32[]{:S(2)}) collective-permute-start(bf16[32,4096]{1,0:T(8,128)(2,1)S(1)} %get-tuple-element.66.refs_7_), channel_id=1, source_target_pairs={{0,2},{1,3},{2,0},{3,1},{4,6},{5,7},{6,4},{7,5},{8,10},{9,11},{10,... | collective-permute-start | bytes 786440 | tf_op jit(solution)/shard_map/ppermute | solution.py:28
  81.7 31.1 %collective-permute-start.13 = (bf16[64,4096]{1,0:T(8,128)(2,1)S(1)}, bf16[64,4096]{1,0:T(8,128)(2,1)S(1)}, u32[]{:S(2)}, u32[]{:S(2)}) collective-permute-start(bf16[64,4096]{1,0:T(8,128)(2,1)S(1)} %level0_rows64.1.refs_2_), channel_id=1, source_target_pairs={{0,4},{1,5},{2,6},{3,7},{4,0},{5,1},{6,2},{7,3},{8,12},{9,13},{10,... | collective-permute-start | bytes 1572872 | tf_op jit(solution)/shard_map/ppermute | solution.py:28
  83.0 3.5 %collective-permute-start.20 = (bf16[32,4096]{1,0:T(8,128)(2,1)S(1)}, bf16[32,4096]{1,0:T(8,128)(2,1)S(1)}, u32[]{:S(2)}, u32[]{:S(2)}) collective-permute-start(bf16[32,4096]{1,0:T(8,128)(2,1)S(1)} %get-tuple-element.73.refs_4_), channel_id=1, source_target_pairs={{0,8},{8,0},{16,24},{24,16},{1,9},{9,1},{17,25},{25,17},{2,10},{10... | collective-permute-start | bytes 786440 | tf_op jit(solution)/shard_map/ppermute | solution.py:28
  83.2 3.3 %collective-permute-start.21 = (bf16[32,4096]{1,0:T(8,128)(2,1)S(1)}, bf16[32,4096]{1,0:T(8,128)(2,1)S(1)}, u32[]{:S(2)}, u32[]{:S(2)}) collective-permute-start(bf16[32,4096]{1,0:T(8,128)(2,1)S(1)} %get-tuple-element.74.refs_6_), channel_id=1, source_target_pairs={{0,8},{8,0},{16,24},{24,16},{1,9},{9,1},{17,25},{25,17},{2,10},{10... | collective-permute-start | bytes 786440 | tf_op jit(solution)/shard_map/ppermute | solution.py:28
  83.6 29.2 %collective-permute-start.14 = (bf16[16,4096]{1,0:T(8,128)(2,1)S(1)}, bf16[16,4096]{1,0:T(8,128)(2,1)S(1)}, u32[]{:S(2)}, u32[]{:S(2)}) collective-permute-start(bf16[16,4096]{1,0:T(8,128)(2,1)S(1)} %collective-permute-done.10), channel_id=1, source_target_pairs={{0,4},{1,5},{2,6},{3,7},{4,0},{5,1},{6,2},{7,3},{8,12},{9,13},{10,... | collective-permute-start | bytes 393224 | tf_op jit(solution)/shard_map/ppermute | solution.py:28
  87.9 40.2 %collective-permute-start.22 = (bf16[144,4096]{1,0:T(8,128)(2,1)S(1)}, bf16[144,4096]{1,0:T(8,128)(2,1)S(1)}, u32[]{:S(2)}, u32[]{:S(2)}) collective-permute-start(bf16[144,4096]{1,0:T(8,128)(2,1)S(1)} %level2_rows144.1.refs_9_), channel_id=1, source_target_pairs={{0,2},{1,3},{2,0},{3,1},{4,6},{5,7},{6,4},{7,5},{8,10},{9,11},{10,... | collective-permute-start | bytes 3538952 | tf_op jit(solution)/shard_map/ppermute | solution.py:28
  114.0 8.9 %collective-permute-start.23 = (bf16[64,4096]{1,0:T(8,128)(2,1)S(1)}, bf16[64,4096]{1,0:T(8,128)(2,1)S(1)}, u32[]{:S(2)}, u32[]{:S(2)}) collective-permute-start(bf16[64,4096]{1,0:T(8,128)(2,1)S(1)} %level1_rows64.3.refs_2_), channel_id=1, source_target_pairs={{0,8},{8,0},{16,24},{24,16},{1,9},{9,1},{17,25},{25,17},{2,10},{10... | collective-permute-start | bytes 1572872 | tf_op jit(solution)/shard_map/ppermute | solution.py:28
  114.1 8.8 %collective-permute-start.16 = (bf16[32,4096]{1,0:T(8,128)(2,1)S(1)}, bf16[32,4096]{1,0:T(8,128)(2,1)S(1)}, u32[]{:S(2)}, u32[]{:S(2)}) collective-permute-start(bf16[32,4096]{1,0:T(8,128)(2,1)S(1)} %constant_dynamic-update-slice_fusion.refs_3_), channel_id=1, source_target_pairs={{0,16},{8,24},{16,0},{24,8},{1,17},{9,25},{17,1},{25,9},{2,18},{10... | collective-permute-start | bytes 786440 | tf_op jit(solution)/shard_map/ppermute | solution.py:28
  114.6 9.6 %collective-permute-start.17 = (bf16[32,4096]{1,0:T(8,128)(2,1)S(1)}, bf16[32,4096]{1,0:T(8,128)(2,1)S(1)}, u32[]{:S(2)}, u32[]{:S(2)}) collective-permute-start(bf16[32,4096]{1,0:T(8,128)(2,1)S(1)} %constant_dynamic-update-slice_fusion.refs_3_), channel_id=1, source_target_pairs={{0,8},{8,0},{16,24},{24,16},{1,9},{9,1},{17,25},{25,17},{2,10},{10... | collective-permute-start | bytes 786440 | tf_op jit(solution)/shard_map/ppermute | solution.py:28
  122.9 1.5 %collective-permute-start.18 = (bf16[32,4096]{1,0:T(8,128)(2,1)S(1)}, bf16[32,4096]{1,0:T(8,128)(2,1)S(1)}, u32[]{:S(2)}, u32[]{:S(2)}) collective-permute-start(bf16[32,4096]{1,0:T(8,128)(2,1)S(1)} %collective-permute-done.16.refs_4_), channel_id=1, source_target_pairs={{0,8},{8,0},{16,24},{24,16},{1,9},{9,1},{17,25},{25,17},{2,10},{10... | collective-permute-start | bytes 786440 | tf_op jit(solution)/shard_map/ppermute | solution.py:28
  124.1 15.2 %collective-permute-start.24 = (bf16[64,4096]{1,0:T(8,128)(2,1)S(1)}, bf16[64,4096]{1,0:T(8,128)(2,1)S(1)}, u32[]{:S(2)}, u32[]{:S(2)}) collective-permute-start(bf16[64,4096]{1,0:T(8,128)(2,1)S(1)} %level2_rows64.1.own), channel_id=1, source_target_pairs={{0,2},{1,3},{2,0},{3,1},{4,6},{5,7},{6,4},{7,5},{8,10},{9,11},{10,... | collective-permute-start | bytes 1572872 | tf_op jit(solution)/shard_map/ppermute | solution.py:28

commit v16 on v15

--- a/solution.py
+++ b/solution.py
@@ -227,7 +227,7 @@
         out_shape=jax.ShapeDtypeStruct(old.shape, BF16),
         in_specs=[pl.BlockSpec(memory_space=pltpu.SMEM)] + [vmem] * 4 + [pl.BlockSpec(memory_space=pl.ANY)],
         out_specs=pl.BlockSpec(memory_space=pl.ANY),
-        scratch_shapes=[pltpu.VMEM((rows, width), BF16), pltpu.SemaphoreType.DMA((4,))],
+        scratch_shapes=[pltpu.VMEM((rows, width), BF16), pltpu.SemaphoreType.DMA((8,))],
         input_output_aliases={5: 0},
         compiler_params=pltpu.CompilerParams(vmem_limit_bytes=30 * 2**20),
         cost_estimate=pl.CostEstimate(flops=0, bytes_accessed=0, transcendentals=0),

time: 142 us -> 142 us (level)
  no operation moved by 1% of the time
where the time goes in v16:
time: 142 us; the launch traced here: 141 us
  waiting for transfers between devices  93.7 us (66%)
  Pallas kernels  22.5 us (16%)
  starting transfers between devices  20.2 us (14%)
  local copies, waits for them, and re-layouts  4.65 us (3%)
    ppermute x25, waiting for transfers between devices, trade(): lax.ppermute(block, axis, [(i, i ^ flip) for i in range(lax.axis_size(axi...  93.7 us
    ppermute x25, starting transfers between devices, trade(): lax.ppermute(block, axis, [(i, i ^ flip) for i in range(lax.axis_size(axi...  20.2 us
    pallas_call x8, Pallas kernels, run_level(): pl.pallas_call(kernel, grid=(1,) if part is not None else (), out_shape=s...  15.3 us
    pallas_call x1, Pallas kernels, run_two_levels(): pl.pallas_call(kernel, out_shape=[jax.ShapeDtypeStruct((n, width), BF16)...  4.31 us
  transfers between devices with their start and end apart: 25, of which 15 were waited for; matrix products, arithmetic and copies ran while one was open for 2% of the time, Pallas kernels for 15%

profile of v16, /device:TPU:0, one launch (start us, length us, event | category | flops | bytes accessed | tf_op | source)
XLA Modules:
  0.0 141.2 jit_solution(7119502664496401423)
XLA Ops:
  0.0 1.2 slice.84.refs_1_
  1.2 3.0 %collective-permute-start.2 = (bf16[80,4096]{1,0:T(8,128)(2,1)S(1)}, bf16[80,4096]{1,0:T(8,128)(2,1)}, u32[]{:S(2)}, u32[]{:S(2)}) collective-permute-start(bf16[80,4096]{1,0:T(8,128)(2,1)S(1)} %slice.84.refs_1_), channel_id=1, source_target_pairs={{0,16},{8,24},{16,0},{24,8},{1,17},{9,25},{17,1},{25,9},{2,18},{10... | collective-permute-start | bytes 1966088 | tf_op jit(solution)/shard_map/ppermute | solution.py:28
  4.2 2.6 %collective-permute-start = (bf16[80,4096]{1,0:T(8,128)(2,1)S(1)}, bf16[80,4096]{1,0:T(8,128)(2,1)S(1)}, u32[]{:S(2)}, u32[]{:S(2)}) collective-permute-start(bf16[80,4096]{1,0:T(8,128)(2,1)S(1)} %slice.84.refs_1_), channel_id=1, source_target_pairs={{0,4},{1,5},{2,6},{3,7},{4,0},{5,1},{6,2},{7,3},{8,12},{9,13},{10,... | collective-permute-start | bytes 1966088 | tf_op jit(solution)/shard_map/ppermute | solution.py:28
  6.8 1.3 fusion.8
  9.7 1.6 %collective-permute-start.3 = (bf16[48,4096]{1,0:T(8,128)(2,1)S(1)}, bf16[48,4096]{1,0:T(8,128)(2,1)}, u32[]{:S(2)}, u32[]{:S(2)}) collective-permute-start(bf16[48,4096]{1,0:T(8,128)(2,1)S(1)} %slice.85.refs_2_), channel_id=1, source_target_pairs={{0,16},{8,24},{16,0},{24,8},{1,17},{9,25},{17,1},{25,9},{2,18},{10... | collective-permute-start | bytes 1179656 | tf_op jit(solution)/shard_map/ppermute | solution.py:28
  11.3 24.1 %collective-permute-done.refs_0_ = bf16[80,4096]{1,0:T(8,128)(2,1)S(1)} collective-permute-done((bf16[80,4096]{1,0:T(8,128)(2,1)S(1)}, bf16[80,4096]{1,0:T(8,128)(2,1)S(1)}, u32[]{:S(2)}, u32[]{:S(2)}) %collective-permute-start) | collective-permute-done | bytes 655392 | tf_op jit(solution)/shard_map/ppermute | solution.py:28
  36.1 1.0 copy-done
  38.1 1.4 %collective-permute-done.3.refs_4_ = bf16[48,4096]{1,0:T(8,128)(2,1)} collective-permute-done((bf16[48,4096]{1,0:T(8,128)(2,1)S(1)}, bf16[48,4096]{1,0:T(8,128)(2,1)}, u32[]{:S(2)}, u32[]{:S(2)}) %collective-permute-start.3) | collective-permute-done | bytes 393248 | tf_op jit(solution)/shard_map/ppermute | solution.py:28
  39.5 3.2 %level0_rows256.1 = (bf16[128,4096]{1,0:T(8,128)(2,1)S(1)}, bf16[64,4096]{1,0:T(8,128)(2,1)S(1)}, bf16[64,4096]{1,0:T(8,128)(2,1)S(1)}, bf16[256,4096]{1,0:T(8,128)(2,1)S(1)}) custom-call(s32[640]{0:T(1024)S(1)} %concatenate.6.meta, bf16[4,256,256]{2,1,0:T(8,128)(2,1)S(1)} %reorder.1.refs_0_.inv, bf16[80,4096]{1,0:T(8,128)(2,1)S(1)} %slice.84.refs_1_, ...), custom_call_target="tpu_custom_call" | custom-call | tf_op jit(solution)/shard_map/level0_rows256/pallas_call | solution.py:288
  42.7 12.3 %collective-permute-done.1.refs_1_ = bf16[48,4096]{1,0:T(8,128)(2,1)} collective-permute-done((bf16[48,4096]{1,0:T(8,128)(2,1)S(1)}, bf16[48,4096]{1,0:T(8,128)(2,1)}, u32[]{:S(2)}, u32[]{:S(2)}) %collective-permute-start.1) | collective-permute-done | bytes 393248 | tf_op jit(solution)/shard_map/ppermute | solution.py:28
  55.0 1.5 %collective-permute-start.6 = (bf16[48,4096]{1,0:T(8,128)(2,1)}, bf16[48,4096]{1,0:T(8,128)(2,1)S(1)}, u32[]{:S(2)}, u32[]{:S(2)}) collective-permute-start(bf16[48,4096]{1,0:T(8,128)(2,1)} %collective-permute-done.1.refs_1_), channel_id=1, source_target_pairs={{0,16},{8,24},{16,0},{24,8},{1,17},{9,25},{17,1},{25,9},{2,18},{10... | collective-permute-start | bytes 1179656 | tf_op jit(solution)/shard_map/ppermute | solution.py:28
  57.0 7.6 %collective-permute-done.6.refs_3_ = bf16[48,4096]{1,0:T(8,128)(2,1)S(1)} collective-permute-done((bf16[48,4096]{1,0:T(8,128)(2,1)}, bf16[48,4096]{1,0:T(8,128)(2,1)S(1)}, u32[]{:S(2)}, u32[]{:S(2)}) %collective-permute-start.6) | collective-permute-done | bytes 393248 | tf_op jit(solution)/shard_map/ppermute | solution.py:28
  64.5 1.5 %collective-permute-start.12 = (bf16[64,4096]{1,0:T(8,128)(2,1)S(1)}, bf16[64,4096]{1,0:T(8,128)(2,1)S(1)}, u32[]{:S(2)}, u32[]{:S(2)}) collective-permute-start(bf16[64,4096]{1,0:T(8,128)(2,1)S(1)} %get-tuple-element.61.refs_2_), channel_id=1, source_target_pairs={{0,16},{8,24},{16,0},{24,8},{1,17},{9,25},{17,1},{25,9},{2,18},{10... | collective-permute-start | bytes 1572872 | tf_op jit(solution)/shard_map/ppermute | solution.py:28
  66.1 4.3 %level0_level1.1 = (bf16[48,4096]{1,0:T(8,128)(2,1)S(1)}, bf16[48,4096]{1,0:T(8,128)(2,1)S(1)}, bf16[48,4096]{1,0:T(8,128)(2,1)S(1)}, bf16[80,4096]{1,0:T(8,128)(2,1)S(1)}, bf16[256,4096]{1,0:T(8,128)(2,1)S(1)}) custom-call(s32[640]{0:T(1024)S(1)} %concatenate.6.meta, bf16[4,256,256]{2,1,0:T(8,128)(2,1)S(1)} %reorder.1.refs_0_.inv, ...), custom_call_target="tpu_custom_call" | custom-call | tf_op jit(solution)/shard_map/level0_level1/pallas_call | solution.py:314
  71.1 1.1 collective-permute-done.7.refs_4_
  73.3 2.2 %level2_rows160.1 = (bf16[16,4096]{1,0:T(8,128)(2,1)S(1)}, bf16[32,4096]{1,0:T(8,128)(2,1)S(1)}, bf16[112,4096]{1,0:T(8,128)(2,1)S(1)}, bf16[256,4096]{1,0:T(8,128)(2,1)S(1)}) custom-call(s32[640]{0:T(1024)S(1)} %concatenate.6.meta, bf16[4,256,256]{2,1,0:T(8,128)(2,1)S(1)} %reorder.1.refs_0_.inv, bf16[48,4096]{1,0:T(8,128)(2,1)S(1)} %get-tuple-element.55.refs_1_, ...), custom_call_target="tpu_custom_call" | custom-call | tf_op jit(solution)/shard_map/level2_rows160/pallas_call | solution.py:288
  75.7 1.9 %collective-permute-start.15 = (bf16[32,4096]{1,0:T(8,128)(2,1)S(1)}, bf16[32,4096]{1,0:T(8,128)(2,1)S(1)}, u32[]{:S(2)}, u32[]{:S(2)}) collective-permute-start(bf16[32,4096]{1,0:T(8,128)(2,1)S(1)} %get-tuple-element.66.refs_7_), channel_id=1, source_target_pairs={{0,2},{1,3},{2,0},{3,1},{4,6},{5,7},{6,4},{7,5},{8,10},{9,11},{10,... | collective-permute-start | bytes 786440 | tf_op jit(solution)/shard_map/ppermute | solution.py:28
  77.6 2.8 %collective-permute-done.11.refs_3_ = bf16[64,4096]{1,0:T(8,128)(2,1)S(1)} collective-permute-done((bf16[64,4096]{1,0:T(8,128)(2,1)S(1)}, bf16[64,4096]{1,0:T(8,128)(2,1)S(1)}, u32[]{:S(2)}, u32[]{:S(2)}) %collective-permute-start.11) | collective-permute-done | bytes 524320 | tf_op jit(solution)/shard_map/ppermute | solution.py:28
  80.4 1.2 level0_rows64.1.refs_2_
  81.7 1.2 level1_rows64.2
  83.5 2.9 %collective-permute-start.14 = (bf16[16,4096]{1,0:T(8,128)(2,1)S(1)}, bf16[16,4096]{1,0:T(8,128)(2,1)S(1)}, u32[]{:S(2)}, u32[]{:S(2)}) collective-permute-start(bf16[16,4096]{1,0:T(8,128)(2,1)S(1)} %collective-permute-done.10), channel_id=1, source_target_pairs={{0,4},{1,5},{2,6},{3,7},{4,0},{5,1},{6,2},{7,3},{8,12},{9,13},{10,... | collective-permute-start | bytes 393224 | tf_op jit(solution)/shard_map/ppermute | solution.py:28
  86.5 1.4 %level2_rows144.1.refs_9_ = bf16[144,4096]{1,0:T(8,128)(2,1)S(1)} custom-call(s32[640]{0:T(1024)S(1)} %concatenate.6.meta, bf16[4,256,256]{2,1,0:T(8,128)(2,1)S(1)} %reorder.1.refs_0_.inv, bf16[256,4096]{1,0:T(8,128)(2,1)S(1)} %get-tuple-element.68.refs_1_, bf16[80,4096]{1,0:T(8,128)(2,1)S(1)} %get-tuple-element.69.refs_2_, ...), custom_call_target="tpu_custom_call" | custom-call | tf_op jit(solution)/shard_map/level2_rows144/pallas_call | solution.py:288
  87.9 1.3 collective-permute-start.22
  89.2 3.1 %collective-permute-done.15.refs_8_ = bf16[32,4096]{1,0:T(8,128)(2,1)S(1)} collective-permute-done((bf16[32,4096]{1,0:T(8,128)(2,1)S(1)}, bf16[32,4096]{1,0:T(8,128)(2,1)S(1)}, u32[]{:S(2)}, u32[]{:S(2)}) %collective-permute-start.15) | collective-permute-done | bytes 262176 | tf_op jit(solution)/shard_map/ppermute | solution.py:28
  92.3 20.5 %collective-permute-done.14 = bf16[16,4096]{1,0:T(8,128)(2,1)S(1)} collective-permute-done((bf16[16,4096]{1,0:T(8,128)(2,1)S(1)}, bf16[16,4096]{1,0:T(8,128)(2,1)S(1)}, u32[]{:S(2)}, u32[]{:S(2)}) %collective-permute-start.14) | collective-permute-done | bytes 131104 | tf_op jit(solution)/shard_map/ppermute | solution.py:28
  112.8 1.2 level1_rows64.3.refs_2_
  114.8 8.1 %collective-permute-done.16.refs_4_ = bf16[32,4096]{1,0:T(8,128)(2,1)S(1)} collective-permute-done((bf16[32,4096]{1,0:T(8,128)(2,1)S(1)}, bf16[32,4096]{1,0:T(8,128)(2,1)S(1)}, u32[]{:S(2)}, u32[]{:S(2)}) %collective-permute-start.16) | collective-permute-done | bytes 262176 | tf_op jit(solution)/shard_map/ppermute | solution.py:28
  122.9 1.2 level2_rows64.1.own
  124.4 3.7 %collective-permute-done.22.refs_10_ = bf16[144,4096]{1,0:T(8,128)(2,1)S(1)} collective-permute-done((bf16[144,4096]{1,0:T(8,128)(2,1)S(1)}, bf16[144,4096]{1,0:T(8,128)(2,1)S(1)}, u32[]{:S(2)}, u32[]{:S(2)}) %collective-permute-start.22) | collective-permute-done | bytes 1179680 | tf_op jit(solution)/shard_map/ppermute | solution.py:28
  128.1 3.6 %level3_rows192.1 = (bf16[256,4096]{1,0:T(8,128)(2,1)}, bf16[256,4096]{1,0:T(8,128)(2,1)S(1)}) custom-call(s32[640]{0:T(1024)S(1)} %concatenate.6.meta, bf16[4,256,256]{2,1,0:T(8,128)(2,1)S(1)} %reorder.1.refs_0_.inv, bf16[16,4096]{1,0:T(8,128)(2,1)S(1)} %get-tuple-element.58.refs_1_, bf16[112,4096]{1,0:T(8,128)(2,1)S(1)} %get-tuple-element.59.refs_2_, ...), custom_call_target="tpu_custom_call" | custom-call | flops 49999998976 | tf_op jit(solution)/shard_map/level3_rows192/pallas_call | solution.py:288
  131.7 7.6 %collective-permute-done.24.other = bf16[64,4096]{1,0:T(8,128)(2,1)S(1)} collective-permute-done((bf16[64,4096]{1,0:T(8,128)(2,1)S(1)}, bf16[64,4096]{1,0:T(8,128)(2,1)S(1)}, u32[]{:S(2)}, u32[]{:S(2)}) %collective-permute-start.24) | collective-permute-done | bytes 524320 | tf_op jit(solution)/shard_map/ppermute | solution.py:28
  139.3 1.9 %last_rows.1 = bf16[256,4096]{1,0:T(8,128)(2,1)} custom-call(s32[640]{0:T(1024)S(1)} %concatenate.6.meta, bf16[4,256,256]{2,1,0:T(8,128)(2,1)S(1)} %reorder.1.refs_0_.inv, bf16[256,4096]{1,0:T(8,128)(2,1)S(1)} %get-tuple-element.75.panel, bf16[64,4096]{1,0:T(8,128)(2,1)S(1)} %level2_rows64.1.own, ...), custom_call_target="tpu_custom_call", output_to_operand_aliasing={{}: (5, {})} | custom-call | tf_op jit(solution)/shard_map/last_rows/pallas_call | solution.py:225
  (50 shorter events, 7.2 us)
Async XLA Ops:
  0.0 35.8 %copy-start.1 = (s32[4,2,32]{2,1,0:T(2,128)S(1)}, s32[4,2,32]{2,1,0:T(2,128)}, u32[]{:S(2)}) copy-start(s32[4,2,32]{2,1,0:T(2,128)} %param.7) | copy-start | bytes 3076
  0.0 35.9 %copy-start.3 = (s32[4,32]{1,0:T(4,128)S(1)}, s32[4,32]{1,0:T(4,128)}, u32[]{:S(2)}) copy-start(s32[4,32]{1,0:T(4,128)} %param.8) | copy-start | bytes 1540
  0.0 35.9 %copy-start.2 = (s32[4,32]{1,0:T(4,128)S(1)}, s32[4,32]{1,0:T(4,128)}, u32[]{:S(2)}) copy-start(s32[4,32]{1,0:T(4,128)} %param.9) | copy-start | bytes 1540
  1.2 38.4 %collective-permute-start.2 = (bf16[80,4096]{1,0:T(8,128)(2,1)S(1)}, bf16[80,4096]{1,0:T(8,128)(2,1)}, u32[]{:S(2)}, u32[]{:S(2)}) collective-permute-start(bf16[80,4096]{1,0:T(8,128)(2,1)S(1)} %slice.84.refs_1_), channel_id=1, source_target_pairs={{0,16},{8,24},{16,0},{24,8},{1,17},{9,25},{17,1},{25,9},{2,18},{10... | collective-permute-start | bytes 1966088 | tf_op jit(solution)/shard_map/ppermute | solution.py:28
  4.2 31.1 %collective-permute-start = (bf16[80,4096]{1,0:T(8,128)(2,1)S(1)}, bf16[80,4096]{1,0:T(8,128)(2,1)S(1)}, u32[]{:S(2)}, u32[]{:S(2)}) collective-permute-start(bf16[80,4096]{1,0:T(8,128)(2,1)S(1)} %slice.84.refs_1_), channel_id=1, source_target_pairs={{0,4},{1,5},{2,6},{3,7},{4,0},{5,1},{6,2},{7,3},{8,12},{9,13},{10,... | collective-permute-start | bytes 1966088 | tf_op jit(solution)/shard_map/ppermute | solution.py:28
  8.1 30.0 %collective-permute-start.4 = (bf16[64,4096]{1,0:T(8,128)(2,1)S(1)}, bf16[64,4096]{1,0:T(8,128)(2,1)}, u32[]{:S(2)}, u32[]{:S(2)}) collective-permute-start(bf16[64,4096]{1,0:T(8,128)(2,1)S(1)} %get-tuple-element.80.refs_5_), channel_id=1, source_target_pairs={{0,16},{8,24},{16,0},{24,8},{1,17},{9,25},{17,1},{25,9},{2,18},{10... | collective-permute-start | bytes 1572872 | tf_op jit(solution)/shard_map/ppermute | solution.py:28
  9.7 29.9 %collective-permute-start.3 = (bf16[48,4096]{1,0:T(8,128)(2,1)S(1)}, bf16[48,4096]{1,0:T(8,128)(2,1)}, u32[]{:S(2)}, u32[]{:S(2)}) collective-permute-start(bf16[48,4096]{1,0:T(8,128)(2,1)S(1)} %slice.85.refs_2_), channel_id=1, source_target_pairs={{0,16},{8,24},{16,0},{24,8},{1,17},{9,25},{17,1},{25,9},{2,18},{10... | collective-permute-start | bytes 1179656 | tf_op jit(solution)/shard_map/ppermute | solution.py:28
  35.3 19.7 %collective-permute-start.5 = (bf16[80,4096]{1,0:T(8,128)(2,1)S(1)}, bf16[80,4096]{1,0:T(8,128)(2,1)S(1)}, u32[]{:S(2)}, u32[]{:S(2)}) collective-permute-start(bf16[80,4096]{1,0:T(8,128)(2,1)S(1)} %collective-permute-done.refs_0_), channel_id=1, source_target_pairs={{0,16},{8,24},{16,0},{24,8},{1,17},{9,25},{17,1},{25,9},{2,18},{10... | collective-permute-start | bytes 1966088 | tf_op jit(solution)/shard_map/ppermute | solution.py:28
  35.8 19.2 %collective-permute-start.1 = (bf16[48,4096]{1,0:T(8,128)(2,1)S(1)}, bf16[48,4096]{1,0:T(8,128)(2,1)}, u32[]{:S(2)}, u32[]{:S(2)}) collective-permute-start(bf16[48,4096]{1,0:T(8,128)(2,1)S(1)} %slice.85.refs_2_), channel_id=1, source_target_pairs={{0,4},{1,5},{2,6},{3,7},{4,0},{5,1},{6,2},{7,3},{8,12},{9,13},{10,... | collective-permute-start | bytes 1179656 | tf_op jit(solution)/shard_map/ppermute | solution.py:28
  36.1 1.0 copy-start
  55.0 9.5 %collective-permute-start.6 = (bf16[48,4096]{1,0:T(8,128)(2,1)}, bf16[48,4096]{1,0:T(8,128)(2,1)S(1)}, u32[]{:S(2)}, u32[]{:S(2)}) collective-permute-start(bf16[48,4096]{1,0:T(8,128)(2,1)} %collective-permute-done.1.refs_1_), channel_id=1, source_target_pairs={{0,16},{8,24},{16,0},{24,8},{1,17},{9,25},{17,1},{25,9},{2,18},{10... | collective-permute-start | bytes 1179656 | tf_op jit(solution)/shard_map/ppermute | solution.py:28
  56.6 23.8 %collective-permute-start.11 = (bf16[64,4096]{1,0:T(8,128)(2,1)S(1)}, bf16[64,4096]{1,0:T(8,128)(2,1)S(1)}, u32[]{:S(2)}, u32[]{:S(2)}) collective-permute-start(bf16[64,4096]{1,0:T(8,128)(2,1)S(1)} %get-tuple-element.62.refs_2_), channel_id=1, source_target_pairs={{0,4},{1,5},{2,6},{3,7},{4,0},{5,1},{6,2},{7,3},{8,12},{9,13},{10,... | collective-permute-start | bytes 1572872 | tf_op jit(solution)/shard_map/ppermute | solution.py:28
  64.5 15.9 %collective-permute-start.12 = (bf16[64,4096]{1,0:T(8,128)(2,1)S(1)}, bf16[64,4096]{1,0:T(8,128)(2,1)S(1)}, u32[]{:S(2)}, u32[]{:S(2)}) collective-permute-start(bf16[64,4096]{1,0:T(8,128)(2,1)S(1)} %get-tuple-element.61.refs_2_), channel_id=1, source_target_pairs={{0,16},{8,24},{16,0},{24,8},{1,17},{9,25},{17,1},{25,9},{2,18},{10... | collective-permute-start | bytes 1572872 | tf_op jit(solution)/shard_map/ppermute | solution.py:28
  70.4 1.8 %collective-permute-start.7 = (bf16[48,4096]{1,0:T(8,128)(2,1)S(1)}, bf16[48,4096]{1,0:T(8,128)(2,1)S(1)}, u32[]{:S(2)}, u32[]{:S(2)}) collective-permute-start(bf16[48,4096]{1,0:T(8,128)(2,1)S(1)} %get-tuple-element.55.refs_1_), channel_id=1, source_target_pairs={{0,8},{8,0},{16,24},{24,16},{1,9},{9,1},{17,25},{25,17},{2,10},{10... | collective-permute-start | bytes 1179656 | tf_op jit(solution)/shard_map/ppermute | solution.py:28
  70.5 2.3 %collective-permute-start.8 = (bf16[48,4096]{1,0:T(8,128)(2,1)S(1)}, bf16[48,4096]{1,0:T(8,128)(2,1)S(1)}, u32[]{:S(2)}, u32[]{:S(2)}) collective-permute-start(bf16[48,4096]{1,0:T(8,128)(2,1)S(1)} %get-tuple-element.56.refs_2_), channel_id=1, source_target_pairs={{0,8},{8,0},{16,24},{24,16},{1,9},{9,1},{17,25},{25,17},{2,10},{10... | collective-permute-start | bytes 1179656 | tf_op jit(solution)/shard_map/ppermute | solution.py:28
  71.0 2.3 %collective-permute-start.9 = (bf16[48,4096]{1,0:T(8,128)(2,1)S(1)}, bf16[48,4096]{1,0:T(8,128)(2,1)S(1)}, u32[]{:S(2)}, u32[]{:S(2)}) collective-permute-start(bf16[48,4096]{1,0:T(8,128)(2,1)S(1)} %get-tuple-element.57.refs_3_), channel_id=1, source_target_pairs={{0,8},{8,0},{16,24},{24,16},{1,9},{9,1},{17,25},{25,17},{2,10},{10... | collective-permute-start | bytes 1179656 | tf_op jit(solution)/shard_map/ppermute | solution.py:28
  72.2 11.4 %collective-permute-start.19 = (bf16[80,4096]{1,0:T(8,128)(2,1)S(1)}, bf16[80,4096]{1,0:T(8,128)(2,1)S(1)}, u32[]{:S(2)}, u32[]{:S(2)}) collective-permute-start(bf16[80,4096]{1,0:T(8,128)(2,1)S(1)} %get-tuple-element.69.refs_2_), channel_id=1, source_target_pairs={{0,8},{8,0},{16,24},{24,16},{1,9},{9,1},{17,25},{25,17},{2,10},{10... | collective-permute-start | bytes 1966088 | tf_op jit(solution)/shard_map/ppermute | solution.py:28
  75.5 7.7 %collective-permute-start.10 = (bf16[16,4096]{1,0:T(8,128)(2,1)S(1)}, bf16[16,4096]{1,0:T(8,128)(2,1)S(1)}, u32[]{:S(2)}, u32[]{:S(2)}) collective-permute-start(bf16[16,4096]{1,0:T(8,128)(2,1)S(1)} %get-tuple-element.58.refs_1_), channel_id=1, source_target_pairs={{0,2},{1,3},{2,0},{3,1},{4,6},{5,7},{6,4},{7,5},{8,10},{9,11},{10,... | collective-permute-start | bytes 393224 | tf_op jit(solution)/shard_map/ppermute | solution.py:28
  75.7 16.6 %collective-permute-start.15 = (bf16[32,4096]{1,0:T(8,128)(2,1)S(1)}, bf16[32,4096]{1,0:T(8,128)(2,1)S(1)}, u32[]{:S(2)}, u32[]{:S(2)}) collective-permute-start(bf16[32,4096]{1,0:T(8,128)(2,1)S(1)} %get-tuple-element.66.refs_7_), channel_id=1, source_target_pairs={{0,2},{1,3},{2,0},{3,1},{4,6},{5,7},{6,4},{7,5},{8,10},{9,11},{10,... | collective-permute-start | bytes 786440 | tf_op jit(solution)/shard_map/ppermute | solution.py:28
  81.6 31.1 %collective-permute-start.13 = (bf16[64,4096]{1,0:T(8,128)(2,1)S(1)}, bf16[64,4096]{1,0:T(8,128)(2,1)S(1)}, u32[]{:S(2)}, u32[]{:S(2)}) collective-permute-start(bf16[64,4096]{1,0:T(8,128)(2,1)S(1)} %level0_rows64.1.refs_2_), channel_id=1, source_target_pairs={{0,4},{1,5},{2,6},{3,7},{4,0},{5,1},{6,2},{7,3},{8,12},{9,13},{10,... | collective-permute-start | bytes 1572872 | tf_op jit(solution)/shard_map/ppermute | solution.py:28
  83.0 3.5 %collective-permute-start.20 = (bf16[32,4096]{1,0:T(8,128)(2,1)S(1)}, bf16[32,4096]{1,0:T(8,128)(2,1)S(1)}, u32[]{:S(2)}, u32[]{:S(2)}) collective-permute-start(bf16[32,4096]{1,0:T(8,128)(2,1)S(1)} %get-tuple-element.73.refs_4_), channel_id=1, source_target_pairs={{0,8},{8,0},{16,24},{24,16},{1,9},{9,1},{17,25},{25,17},{2,10},{10... | collective-permute-start | bytes 786440 | tf_op jit(solution)/shard_map/ppermute | solution.py:28
  83.2 3.3 %collective-permute-start.21 = (bf16[32,4096]{1,0:T(8,128)(2,1)S(1)}, bf16[32,4096]{1,0:T(8,128)(2,1)S(1)}, u32[]{:S(2)}, u32[]{:S(2)}) collective-permute-start(bf16[32,4096]{1,0:T(8,128)(2,1)S(1)} %get-tuple-element.74.refs_6_), channel_id=1, source_target_pairs={{0,8},{8,0},{16,24},{24,16},{1,9},{9,1},{17,25},{25,17},{2,10},{10... | collective-permute-start | bytes 786440 | tf_op jit(solution)/shard_map/ppermute | solution.py:28
  83.5 29.2 %collective-permute-start.14 = (bf16[16,4096]{1,0:T(8,128)(2,1)S(1)}, bf16[16,4096]{1,0:T(8,128)(2,1)S(1)}, u32[]{:S(2)}, u32[]{:S(2)}) collective-permute-start(bf16[16,4096]{1,0:T(8,128)(2,1)S(1)} %collective-permute-done.10), channel_id=1, source_target_pairs={{0,4},{1,5},{2,6},{3,7},{4,0},{5,1},{6,2},{7,3},{8,12},{9,13},{10,... | collective-permute-start | bytes 393224 | tf_op jit(solution)/shard_map/ppermute | solution.py:28
  87.9 40.2 %collective-permute-start.22 = (bf16[144,4096]{1,0:T(8,128)(2,1)S(1)}, bf16[144,4096]{1,0:T(8,128)(2,1)S(1)}, u32[]{:S(2)}, u32[]{:S(2)}) collective-permute-start(bf16[144,4096]{1,0:T(8,128)(2,1)S(1)} %level2_rows144.1.refs_9_), channel_id=1, source_target_pairs={{0,2},{1,3},{2,0},{3,1},{4,6},{5,7},{6,4},{7,5},{8,10},{9,11},{10,... | collective-permute-start | bytes 3538952 | tf_op jit(solution)/shard_map/ppermute | solution.py:28
  114.0 8.9 %collective-permute-start.23 = (bf16[64,4096]{1,0:T(8,128)(2,1)S(1)}, bf16[64,4096]{1,0:T(8,128)(2,1)S(1)}, u32[]{:S(2)}, u32[]{:S(2)}) collective-permute-start(bf16[64,4096]{1,0:T(8,128)(2,1)S(1)} %level1_rows64.3.refs_2_), channel_id=1, source_target_pairs={{0,8},{8,0},{16,24},{24,16},{1,9},{9,1},{17,25},{25,17},{2,10},{10... | collective-permute-start | bytes 1572872 | tf_op jit(solution)/shard_map/ppermute | solution.py:28
  114.1 8.8 %collective-permute-start.16 = (bf16[32,4096]{1,0:T(8,128)(2,1)S(1)}, bf16[32,4096]{1,0:T(8,128)(2,1)S(1)}, u32[]{:S(2)}, u32[]{:S(2)}) collective-permute-start(bf16[32,4096]{1,0:T(8,128)(2,1)S(1)} %constant_dynamic-update-slice_fusion.refs_3_), channel_id=1, source_target_pairs={{0,16},{8,24},{16,0},{24,8},{1,17},{9,25},{17,1},{25,9},{2,18},{10... | collective-permute-start | bytes 786440 | tf_op jit(solution)/shard_map/ppermute | solution.py:28
  114.6 9.6 %collective-permute-start.17 = (bf16[32,4096]{1,0:T(8,128)(2,1)S(1)}, bf16[32,4096]{1,0:T(8,128)(2,1)S(1)}, u32[]{:S(2)}, u32[]{:S(2)}) collective-permute-start(bf16[32,4096]{1,0:T(8,128)(2,1)S(1)} %constant_dynamic-update-slice_fusion.refs_3_), channel_id=1, source_target_pairs={{0,8},{8,0},{16,24},{24,16},{1,9},{9,1},{17,25},{25,17},{2,10},{10... | collective-permute-start | bytes 786440 | tf_op jit(solution)/shard_map/ppermute | solution.py:28
  122.9 1.5 %collective-permute-start.18 = (bf16[32,4096]{1,0:T(8,128)(2,1)S(1)}, bf16[32,4096]{1,0:T(8,128)(2,1)S(1)}, u32[]{:S(2)}, u32[]{:S(2)}) collective-permute-start(bf16[32,4096]{1,0:T(8,128)(2,1)S(1)} %collective-permute-done.16.refs_4_), channel_id=1, source_target_pairs={{0,8},{8,0},{16,24},{24,16},{1,9},{9,1},{17,25},{25,17},{2,10},{10... | collective-permute-start | bytes 786440 | tf_op jit(solution)/shard_map/ppermute | solution.py:28
  124.1 15.2 %collective-permute-start.24 = (bf16[64,4096]{1,0:T(8,128)(2,1)S(1)}, bf16[64,4096]{1,0:T(8,128)(2,1)S(1)}, u32[]{:S(2)}, u32[]{:S(2)}) collective-permute-start(bf16[64,4096]{1,0:T(8,128)(2,1)S(1)} %level2_rows64.1.own), channel_id=1, source_target_pairs={{0,2},{1,3},{2,0},{3,1},{4,6},{5,7},{6,4},{7,5},{8,10},{9,11},{10,... | collective-permute-start | bytes 1572872 | tf_op jit(solution)/shard_map/ppermute | solution.py:28
